TPU v7x, 256 devices: a whole 4x4x8 slice. The times are simulated.
256 devices in a mesh: step: 32 (over y, z), head: 8 (over x, core).
Axes of the slice: x: 4, y: 4, z: 8, core: 2. Of those that a mesh axis runs over, the one named last changes fastest.
Arguments:
- guesses: float32 [32, 256, 64], P('step', 'head'), may hold values from -6 to 6
- step_ids: int32 [32], P('step'), may hold values from 0 to 63
- step_sizes: float32 [32], P('step'), may hold values from 0.02 to 0.1
- slide: int32 [1], replicated, may hold values from 1 to 31
- offsets: int32 [256, 2], replicated, may hold values from 0 to 7
- mod_table: float32 [64, 3, 3072], replicated, may hold values from -3 to 3
- w_in: bfloat16 [64, 3072], replicated, may hold values from -0.75 to 0.75
- w_qkv: bfloat16 [3072, 9216], P(None, 'head')
- qk_gain: float32 [2, 128], replicated, may hold values from 0.6 to 4.5
- w_out: bfloat16 [3072, 3072], P('head'), may hold values from -0.109375 to 0.109375
- w_fin: bfloat16 [3072, 64], replicated, may hold values from -0.109375 to 0.109375
Outputs:
- slid: float32 [32, 256, 64], P('step', 'head')
All inputs are finite; a program needn't handle non-finite values.
Results may differ from a plain program's by a relative error of at most 0.0033.
Values may be sent and summed in bfloat16 or wider, within the bound.
No kernel may reach another device: no remote copies, remote signals or barrier semaphores. Data moves between devices by JAX's collectives and lax.ppermute only.
A program may use at most 64 MiB of HBM per device.

v0:
```python
import math

import jax
import jax.numpy as jnp
from jax import lax
from jax.sharding import PartitionSpec as P

GRID_W = 16
ROT_DIM = 56
SWEEPS = 2


def carried_in(part, axis, combine, identity):
    place = lax.axis_index(axis)
    gathered = lax.all_gather(part, axis)
    state = jnp.zeros_like(part) + jnp.asarray(identity, part.dtype)

    def one(turn, state):
        return combine(state, lax.dynamic_index_in_dim(gathered, turn, 0, False))

    return lax.fori_loop(0, place, one, state)


def layer_norm(x):
    mean = jnp.mean(x, axis=-1, keepdims=True)
    centered = x - mean
    var = jnp.mean(centered * centered, axis=-1, keepdims=True)
    return centered * lax.rsqrt(var + 1e-06)


def rotary_angles(offsets, count, head_dim):
    index = jnp.arange(count, dtype=jnp.int32)
    rows = (index // GRID_W + offsets[:, 0]).astype(jnp.float32)
    cols = (index % GRID_W + offsets[:, 1]).astype(jnp.float32)
    freq = 10000.0 ** (-jnp.arange(ROT_DIM // 2, dtype=jnp.float32) * 2.0 / ROT_DIM)
    still = jnp.zeros((count, (head_dim - 2 * ROT_DIM) // 2), jnp.float32)
    return jnp.concatenate([still, rows[:, None] * freq, cols[:, None] * freq], axis=1)


def rotate(x, angles):
    count, heads, head_dim = x.shape
    pairs = x.reshape(count, heads, head_dim // 2, 2)
    cosine = jnp.cos(angles)[:, None, :]
    sine = jnp.sin(angles)[:, None, :]
    first = pairs[..., 0]
    second = pairs[..., 1]
    out = jnp.stack([first * cosine - second * sine, first * sine + second * cosine], axis=-1)
    return out.reshape(count, heads, head_dim)


def rms_gain(x, gain):
    return x * lax.rsqrt(jnp.mean(x * x, axis=-1, keepdims=True) + 1e-06) * gain


def modulated(state, w_in, mod):
    embed = jnp.dot(state.astype(jnp.bfloat16), w_in, preferred_element_type=jnp.float32)
    features = (layer_norm(embed) * (1.0 + mod[1]) + mod[0]).astype(jnp.bfloat16)
    return (embed, features)


def local_drift(state, step_id, step_size, angles, mod_table, w_in, w_qkv, qk_gain, w_out, w_fin):
    head_dim = qk_gain.shape[1]
    local_heads = w_qkv.shape[1] // (3 * head_dim)
    mod = lax.dynamic_index_in_dim(mod_table, step_id, 0, keepdims=False)
    embed, features = modulated(state, w_in, mod)
    qkv = jnp.dot(
        lax.all_gather(features, "head", axis=0, tiled=True),
        w_qkv,
        preferred_element_type=jnp.float32,
    )
    total_rows = qkv.shape[0]
    qkv = qkv.reshape(total_rows, local_heads, 3, head_dim)
    query = rotate(rms_gain(qkv[:, :, 0], qk_gain[0]), angles).astype(jnp.bfloat16)
    keys = rotate(rms_gain(qkv[:, :, 1], qk_gain[1]), angles).astype(jnp.bfloat16)
    values = qkv[:, :, 2].astype(jnp.bfloat16)
    scores = jnp.einsum(
        "shd,thd->hst", query, keys, preferred_element_type=jnp.float32
    ) / math.sqrt(head_dim)
    probs = jax.nn.softmax(scores, axis=-1).astype(jnp.bfloat16)
    heads_out = jnp.einsum("hst,thd->shd", probs, values, preferred_element_type=jnp.float32)
    heads_out = heads_out.astype(jnp.bfloat16).reshape(total_rows, local_heads * head_dim)
    attn = lax.psum_scatter(
        jnp.dot(heads_out, w_out, preferred_element_type=jnp.float32).astype(jnp.bfloat16),
        "head",
        scatter_dimension=0,
        tiled=True,
    ).astype(jnp.float32)
    hres = embed + mod[2] * attn
    normed = layer_norm(hres).astype(jnp.bfloat16)
    return step_size * jnp.dot(normed, w_fin, preferred_element_type=jnp.float32)


def local(
    guesses, step_ids, step_sizes, slide, offsets, mod_table, w_in, w_qkv, qk_gain, w_out, w_fin
):
    angles = rotary_angles(offsets, offsets.shape[0], qk_gain.shape[1])
    state = guesses[0]
    position = lax.axis_index("step")
    first = position == 0
    for sweep in range(SWEEPS):
        drift = local_drift(
            state, step_ids[0], step_sizes[0], angles, mod_table, w_in, w_qkv, qk_gain, w_out, w_fin
        )
        start_part = jnp.where(first, state, jnp.zeros_like(state))
        before = carried_in(
            drift + start_part,
            "step",
            lambda earlier, later: earlier + later,
            jnp.zeros_like(state),
        )
        state = before + start_part
    distance = slide[0]
    window = lax.axis_size("step")
    every = lax.all_gather(state[None], "step", axis=0, tiled=True)
    target = jnp.minimum(position + distance, window - 1)
    result = lax.dynamic_index_in_dim(every, target, 0, keepdims=True)
    return result


def solution(mesh):
    in_specs = (
        P("step", "head", None),
        P("step"),
        P("step"),
        P(),
        P(),
        P(),
        P(),
        P(None, "head"),
        P(),
        P("head", None),
        P(),
    )
    out_specs = P("step", "head", None)
    return jax.shard_map(local, mesh=mesh, in_specs=in_specs, out_specs=out_specs, check_vma=False)
```

profile of v0, /device:TPU:32, one launch (start us, length us, event | category | flops | bytes accessed | tf_op | source)
XLA Modules:
  0.0 368.6 jit_solution(15550767939318311933)
XLA Ops:
  7.3 1.3 fusion.33
  8.7 0.2 multiply_reduce_fusion.7
  8.9 1.6 constant_dynamic-slice_fusion
  10.6 0.6 copy-done.13
  11.1 0.8 add_convert_fusion.1
  12.0 0.0 reduce-scatter.3.cloned.1.call-start
  12.1 0.8 mul.337
  12.8 0.7 mul.356
  13.6 0.1 broadcast_multiply_fusion.1
  13.7 1.0 fusion.19
  14.6 27.1 %all-gather.6.cloned.1.call-done = bf16[256,3072]{1,0:T(8,128)(2,1)} async-done(((bf16[32,3072]{1,0:T(8,128)(2,1)}), bf16[256,3072]{1,0:T(8,128)(2,1)}) %all-gather.6.cloned.1.call-update) | async-done | bytes 1572880 | tf_op jit(solution)/shard_map/all_gather | solution.py:67
  41.8 6.4 %fusion.37 = f32[256,1152]{0,1:T(8,128)S(1)} fusion(bf16[256,3072]{1,0:T(8,128)(2,1)} %all-gather.6.cloned.1.call-done, bf16[3072,1152]{1,0:T(8,128)(2,1)} %param.22), kind=kOutput, calls=%fused_computation.108 | convolution fusion | flops 1811939328 | bytes 9830400 | tf_op jit(solution)/shard_map/dot_general | solution.py:66
  48.1 0.9 multiply_reduce_fusion.5
  49.0 0.2 copy-done.11
  49.3 0.2 squeeze.26
  49.5 1.2 squeeze.27
  50.8 1.0 multiply_multiply_fusion.3
  51.8 1.0 multiply_multiply_fusion.2
  52.8 1.8 subtract_convert_fusion.2
  54.6 0.5 pad_maximum_fusion.1
  55.0 0.1 convert_element_type.90
  55.1 1.4 pad_maximum_fusion
  56.5 0.1 convert_element_type.89
  56.6 1.2 convolution_multiply_fusion.1
  57.8 0.4 fusion.34
  58.2 1.9 convolution_convert_fusion.3
  60.1 2.2 convolution_convert_fusion.1
  62.3 0.0 all-gather.8.cloned.1.call-start
  63.1 34.9 %reduce-scatter.3.cloned.1.call-done = bf16[32,3072]{1,0:T(8,128)(2,1)} async-done(((bf16[256,3072]{1,0:T(8,128)(2,1)}), bf16[32,3072]{1,0:T(8,128)(2,1)}) %reduce-scatter.3.cloned.1.call-update) | async-done | bytes 196624 | tf_op jit(solution)/shard_map/reduce_scatter | solution.py:82
  97.9 1.1 fusion.16
  99.1 1.1 multiply_reduce_fusion.4
  100.2 1.2 fusion.7
  101.5 54.0 %all-gather = f32[1024,64]{1,0:T(8,128)} all-gather(f32[32,64]{1,0:T(8,128)S(1)} %fusion.7), channel_id=2, replica_groups=mesh['step'=32,'head'=8] {'step'}, dimensions={0}, use_global_device_ids=true | all-gather | bytes 270336 | tf_op jit(solution)/shard_map/all_gather | solution.py:15
  155.5 0.7 while.20
  155.5 0.7 bitcast_add_fusion.6
  156.2 0.3 fusion.35
  156.5 0.2 multiply_reduce_fusion.3
  156.8 0.8 add_convert_fusion
  157.6 0.2 reduce-scatter.5.cloned.1.call-start
  157.8 42.9 %all-gather.8.cloned.1.call-done = bf16[256,3072]{1,0:T(8,128)(2,1)} async-done(((bf16[32,3072]{1,0:T(8,128)(2,1)}), bf16[256,3072]{1,0:T(8,128)(2,1)}) %all-gather.8.cloned.1.call-update) | async-done | bytes 1572880 | tf_op jit(solution)/shard_map/all_gather | solution.py:67
  200.8 6.4 %fusion.38 = f32[256,1152]{0,1:T(8,128)S(1)} fusion(bf16[256,3072]{1,0:T(8,128)(2,1)} %all-gather.8.cloned.1.call-done, bf16[3072,1152]{1,0:T(8,128)(2,1)} %param.22), kind=kOutput, calls=%fused_computation.109 | convolution fusion | flops 1811939328 | bytes 9830400 | tf_op jit(solution)/shard_map/dot_general | solution.py:66
  207.2 1.5 multiply_reduce_fusion.1
  208.7 0.2 squeeze.52
  208.9 1.3 add_rsqrt_fusion.1
  210.2 1.2 squeeze.53
  211.4 0.7 add_rsqrt_fusion
  212.1 1.0 multiply_multiply_fusion.1
  213.1 1.0 multiply_multiply_fusion
  214.1 1.7 subtract_convert_fusion
  215.8 0.5 pad_maximum_fusion.3
  216.3 0.1 convert_element_type.101
  216.3 1.4 pad_maximum_fusion.2
  217.7 0.1 convert_element_type.100
  217.8 1.2 convolution_multiply_fusion
  219.0 0.4 fusion.36
  219.5 1.9 convolution_convert_fusion.2
  221.4 2.2 convolution_convert_fusion
  224.2 34.9 %reduce-scatter.5.cloned.1.call-done = bf16[32,3072]{1,0:T(8,128)(2,1)} async-done(((bf16[256,3072]{1,0:T(8,128)(2,1)}), bf16[32,3072]{1,0:T(8,128)(2,1)}) %reduce-scatter.5.cloned.1.call-update) | async-done | bytes 196624 | tf_op jit(solution)/shard_map/reduce_scatter | solution.py:82
  259.2 1.1 fusion.17
  260.3 1.1 multiply_reduce_fusion
  261.4 1.2 fusion.6
  262.7 49.4 %all-gather.1 = f32[1024,64]{1,0:T(8,128)S(1)} all-gather(f32[32,64]{1,0:T(8,128)S(1)} %fusion.6), channel_id=3, replica_groups=mesh['step'=32,'head'=8] {'step'}, dimensions={0}, use_global_device_ids=true | all-gather | bytes 270336 | tf_op jit(solution)/shard_map/all_gather | solution.py:15
  312.1 49.4 %all-gather.2 = f32[1024,64]{1,0:T(8,128)S(1)} all-gather(f32[32,64]{1,0:T(8,128)S(1)} %select_add_fusion), channel_id=4, replica_groups=mesh['step'=32,'head'=8] {'step'}, dimensions={0}, use_global_device_ids=true | all-gather | bytes 270336 | tf_op jit(solution)/shard_map/all_gather | solution.py:114
  361.5 0.6 constant_dynamic-slice_fusion.1
  (60 shorter events, 0.3 us)
Async XLA Ops:
  6.5 53.6 %copy-start = (bf16[384,3072]{1,0:T(8,128)(2,1)S(1)}, bf16[384,3072]{1,0:T(8,128)(2,1)}, u32[]{:S(2)}) copy-start(bf16[384,3072]{1,0:T(8,128)(2,1)} %param.24) | copy-start | bytes 7077892
  6.5 5.5 %copy-start.18 = (f32[2,128]{1,0:T(2,128)S(1)}, f32[2,128]{1,0:T(2,128)}, u32[]{:S(2)}) copy-start(f32[2,128]{1,0:T(2,128)} %param.23) | copy-start | bytes 3076
  6.5 7.0 %copy-start.17 = (s32[256,2]{0,1:T(2,128)S(1)}, s32[256,2]{0,1:T(2,128)}, u32[]{:S(2)}) copy-start(s32[256,2]{0,1:T(2,128)} %param.19) | copy-start | bytes 6148
  6.5 35.2 %all-gather.6.cloned.1.call-start = ((), (), s32[]{:S(2)}) async-start(), calls=%async_computation.2 | async-start | bytes 1769472 | tf_op jit(solution)/shard_map/all_gather | solution.py:67
  10.5 0.6 copy-start.13
  10.5 0.6 copy-start.15
  12.0 86.0 %reduce-scatter.3.cloned.1.call-start = ((), (), s32[]{:S(2)}) async-start(), calls=%async_computation.3 | async-start | bytes 1769472 | tf_op jit(solution)/shard_map/reduce_scatter | solution.py:82
  48.1 1.2 copy-start.11
  50.7 2.0 copy-start.6
  50.8 2.0 copy-start.8
  62.3 35.7 %copy-start.4 = (f32[1,1,3072]{2,0,1:T(1,128)S(1)}, f32[1,1,3072]{2,0,1:T(1,128)}, u32[]{:S(2)}) copy-start(f32[1,1,3072]{2,0,1:T(1,128)} %get-tuple-element.75) | copy-start | bytes 36868
  62.3 38.0 %copy-start.2 = (bf16[3072,64]{0,1:T(8,128)(2,1)S(1)}, bf16[3072,64]{0,1:T(8,128)(2,1)}, u32[]{:S(2)}) copy-start(bf16[3072,64]{0,1:T(8,128)(2,1)} %param.25) | copy-start | bytes 1179652
  62.3 138.5 %all-gather.8.cloned.1.call-start = ((), (), s32[]{:S(2)}) async-start(), calls=%async_computation.4 | async-start | bytes 1769472 | tf_op jit(solution)/shard_map/all_gather | solution.py:67
  97.9 58.3 %copy-start.1 = (bf16[64,3072]{1,0:T(8,128)(2,1)S(1)}, bf16[64,3072]{1,0:T(8,128)(2,1)}, u32[]{:S(2)}) copy-start(bf16[64,3072]{1,0:T(8,128)(2,1)} %param.21) | copy-start | bytes 1179652
  101.5 55.3 %copy-start.14 = (f32[1,1,3072]{2,0,1:T(1,128)S(1)}, f32[1,1,3072]{2,0,1:T(1,128)}, u32[]{:S(2)}) copy-start(f32[1,1,3072]{2,0,1:T(1,128)} %copy-done.13) | copy-start | bytes 36868
  101.5 55.3 %copy-start.16 = (f32[1,1,3072]{2,0,1:T(1,128)S(1)}, f32[1,1,3072]{2,0,1:T(1,128)}, u32[]{:S(2)}) copy-start(f32[1,1,3072]{2,0,1:T(1,128)} %copy-done.15) | copy-start | bytes 36868
  157.6 101.6 %reduce-scatter.5.cloned.1.call-start = ((), (), s32[]{:S(2)}) async-start(), calls=%async_computation.5 | async-start | bytes 1769472 | tf_op jit(solution)/shard_map/reduce_scatter | solution.py:82
  207.2 1.5 copy-start.10
  211.4 2.7 copy-start.7
  211.4 2.7 copy-start.9
  223.5 35.7 %copy-start.5 = (f32[1,1,3072]{2,0,1:T(1,128)S(1)}, f32[1,1,3072]{2,0,1:T(1,128)}, u32[]{:S(2)}) copy-start(f32[1,1,3072]{2,0,1:T(1,128)} %get-tuple-element.75) | copy-start | bytes 36868
  223.5 37.9 %copy-start.3 = (bf16[3072,64]{0,1:T(8,128)(2,1)S(1)}, bf16[3072,64]{0,1:T(8,128)(2,1)}, u32[]{:S(2)}) copy-start(bf16[3072,64]{0,1:T(8,128)(2,1)} %param.25) | copy-start | bytes 1179652
  223.5 37.9 %copy-start.12 = (f32[1,32,64]{2,1,0:T(8,128)S(1)}, f32[1,32,64]{2,1,0:T(8,128)}, u32[]{:S(2)}) copy-start(f32[1,32,64]{2,1,0:T(8,128)} %param.15) | copy-start | bytes 24580
Sparse Core Ops, SparseCore 0:
  12.1 29.6 all-gather.5
  62.4 35.4 reduce-scatter.2
  157.7 42.9 all-gather.7
  223.7 35.4 reduce-scatter.4
where the time goes:
time: 372 us; the launch traced here: 369 us
  blocking collectives  153 us (41%)
  waiting for transfers between devices  140 us (38%)
  matrix products  28.2 us (8%)
  other arithmetic  25.5 us (7%)
  between operations  15.7 us (4%)
  local copies, waits for them, and re-layouts  6.27 us (2%)
    all_gather x2, blocking collectives, carried_in(): gathered = lax.all_gather(part, axis)  103 us
    all_gather x2, waiting for transfers between devices, local_drift(): lax.all_gather(features, 'head', axis=0, tiled=True)  70.1 us
    reduce_scatter x2, waiting for transfers between devices, local_drift(): lax.psum_scatter(jnp.dot(heads_out, w_out, preferred_element_type=jnp.flo...  69.8 us
    all_gather x1, blocking collectives, local(): every = lax.all_gather(state[None], 'step', axis=0, tiled=True)  49.4 us
    dot_general x2, matrix products, local_drift(): jnp.dot(lax.all_gather(features, 'head', axis=0, tiled=True), w_qkv, pref...  12.8 us
  transfers between devices with their start and end apart: 4, of which 4 were waited for; matrix products, arithmetic and copies ran while one was open for 1% of the time, Pallas kernels for 0%

commit v1 on v0

v1 whole, which is shorter than its diff:
```python
import math

import jax
import jax.numpy as jnp
import numpy as np
from jax import lax
from jax.experimental import pallas as pl
from jax.experimental.pallas import tpu as pltpu
from jax.sharding import Mesh
from jax.sharding import PartitionSpec as P

NY, NZ, NX, NC = 4, 8, 4, 2
D = 3072
HD = 128
HL = 3
C = 64
S = 256
ROWS = 32
GRID_W = 16
ROT_DIM = 56
EPS = 1e-06
BF = jnp.bfloat16
F32 = jnp.float32
MIB = 1024 * 1024

VM = pl.BlockSpec(memory_space=pltpu.VMEM)
SM = pl.BlockSpec(memory_space=pltpu.SMEM)
ANY = pl.BlockSpec(memory_space=pl.ANY)


def pack(x):
    return jnp.concatenate([x[:16], x[16:]], axis=1)


def unpack(x):
    return jnp.concatenate([x[:, :C], x[:, C:]], axis=0)


def tables(offsets, qk_gain):
    index = jnp.arange(S, dtype=jnp.int32)
    rows = (index // GRID_W + offsets[:, 0]).astype(F32)
    cols = (index % GRID_W + offsets[:, 1]).astype(F32)
    freq = 10000.0 ** (-jnp.arange(ROT_DIM // 2, dtype=F32) * 2.0 / ROT_DIM)
    still = jnp.zeros((S, (HD - 2 * ROT_DIM) // 2), F32)
    angles = jnp.concatenate([still, rows[:, None] * freq, cols[:, None] * freq], axis=1)
    angles = jnp.repeat(angles, 2, axis=1)
    sign = jnp.where(jnp.arange(HD) % 2 == 0, -1.0, 1.0).astype(F32)
    cosine = jnp.cos(angles)
    sine = jnp.sin(angles) * sign
    swapped = qk_gain.reshape(2, HD // 2, 2)[:, :, ::-1].reshape(2, HD)
    whole = jnp.stack(
        [cosine * qk_gain[0], sine * swapped[0], cosine * qk_gain[1], sine * swapped[1]]
    )
    return whole.reshape(4, 8, ROWS, HD)


def block_body(place, chunk_of, tab, w_in, mod, w_qkv, h_out, zs, es, fs, wv, qs, sems):
    my_x, my_c = place[2], place[3]
    copies = []
    for head in range(HL):
        cut = pl.ds(head * 3 * HD, 3 * HD)
        copy = pltpu.make_async_copy(w_qkv.at[:, cut], wv.at[:, cut], sems.at[head])
        copy.start()
        copies.append(copy)
    order = []
    for r in range(8):
        where = ((my_x + r % 4) % 4) * 2 + (my_c + r // 4) % 2
        order.append(where)
        piece = chunk_of(where)
        zs[32 * r : 32 * r + 16, :] = piece[:, :C]
        zs[32 * r + 16 : 32 * r + 32, :] = piece[:, C:]
    z = zs[...]
    for j in range(6):
        cut = slice(j * 512, j * 512 + 512)
        es[:, cut] = jnp.dot(z, w_in[:, cut], preferred_element_type=F32)

    def norm_rows(i, carry):
        at = pl.ds(pl.multiple_of(i * ROWS, ROWS), ROWS)
        e = es[at, :]
        mean = jnp.sum(e, axis=-1, keepdims=True) * (1.0 / D)
        e = e - mean
        var = jnp.sum(e * e, axis=-1, keepdims=True) * (1.0 / D)
        f = e * lax.rsqrt(var + EPS) * (1.0 + mod[1:2, :]) + mod[0:1, :]
        fs[at, :] = f.astype(BF)
        return carry

    lax.fori_loop(0, 8, norm_rows, 0)
    lane = lax.broadcasted_iota(jnp.int32, (ROWS, HD), 1)
    even = lane % 2 == 0

    def turned(x, tc, ts):
        r = lax.rsqrt(jnp.mean(x * x, axis=-1, keepdims=True) + EPS)
        swap = jnp.where(even, pltpu.roll(x, HD - 1, 1), pltpu.roll(x, 1, 1))
        return ((x * tc + swap * ts) * r).astype(BF)

    for head in range(HL):
        copies[head].wait()
        base = head * 3 * HD
        qkv = jnp.dot(fs[...], wv[:, base : base + 3 * HD], preferred_element_type=F32)
        for r in range(8):
            rows = slice(32 * r, 32 * r + 32)
            where = order[r]
            qs[0, rows, :] = turned(qkv[rows, :HD], tab[0, where], tab[1, where])
            qs[1, rows, :] = turned(qkv[rows, HD : 2 * HD], tab[2, where], tab[3, where])
            qs[2, rows, :] = qkv[rows, 2 * HD :].astype(BF)
        scores = lax.dot_general(
            qs[0], qs[1], (((1,), (1,)), ((), ())), preferred_element_type=F32
        )
        top = jnp.max(scores, axis=-1, keepdims=True)
        p = jnp.exp((scores - top) * (1.0 / math.sqrt(HD)))
        p = p / jnp.sum(p, axis=-1, keepdims=True)
        out = jnp.dot(p.astype(BF), qs[2], preferred_element_type=F32)
        h_out[:, head * HD : head * HD + HD] = out.astype(BF)


def first_kernel(place, zg, tab, w_in, mod, w_qkv, h_out, *scratch):
    block_body(place, lambda i: zg[i], tab, w_in, mod, w_qkv, h_out, *scratch)


def second_kernel(place, zg, parts, tab, w_in, mod, w_qkv, h_out, z_out, *scratch):
    start = place[0] * NZ + place[1] == 0

    def chunk_of(i):
        x, c = i // 2, i % 2
        total = parts[0, x, c] + parts[1, x, c] + parts[2, x, c] + parts[3, x, c]
        return jnp.where(start, zg[i].astype(F32), total).astype(BF)

    z_out[...] = chunk_of(place[2] * 2 + place[3])
    block_body(place, chunk_of, tab, w_in, mod, w_qkv, h_out, *scratch)


BLOCK_SCRATCH = [
    pltpu.VMEM((S, C), BF),
    pltpu.VMEM((S, D), F32),
    pltpu.VMEM((S, D), BF),
    pltpu.VMEM((D, HL * 3 * HD), BF),
    pltpu.VMEM((3, S, HD), BF),
    pltpu.SemaphoreType.DMA((HL,)),
]
BLOCK_PARAMS = pltpu.CompilerParams(vmem_limit_bytes=32 * MIB)


def out_kernel(mine, peer, w_mine, w_peer, first, *others):
    for j in range(6):
        cut = slice(j * 512, j * 512 + 512)
        part = jnp.dot(mine[...], w_mine[:, cut], preferred_element_type=F32)
        part += jnp.dot(peer[...], w_peer[:, cut], preferred_element_type=F32)
        part = part.astype(BF)
        first[:, cut] = part[:ROWS]
        for k in range(3):
            others[k][:, cut] = part[ROWS * (k + 1) : ROWS * (k + 2)]


def drift_kernel(place, size, z, zstart, p0, p1, p2, p3, w_in, mod, w_fin, out):
    e = jnp.dot(unpack(z[...]), w_in[...], preferred_element_type=F32)
    attn = p0[...].astype(F32) + p1[...].astype(F32) + p2[...].astype(F32) + p3[...].astype(F32)
    h = e + mod[2:3, :] * attn
    mean = jnp.sum(h, axis=-1, keepdims=True) * (1.0 / D)
    h = h - mean
    var = jnp.sum(h * h, axis=-1, keepdims=True) * (1.0 / D)
    normed = (h * lax.rsqrt(var + EPS)).astype(BF)
    drift = size[0] * jnp.dot(normed, w_fin[...], preferred_element_type=F32)
    start = place[0] * NZ + place[1] == 0
    drift = drift + jnp.where(start, zstart[...], jnp.zeros((ROWS, C), F32))
    packed = pack(drift)
    for k in range(out.shape[0]):
        out[k] = packed


def relay_kernel(place, got, out):
    y, z = place[0], place[1]
    for to in range(NY):
        total = jnp.zeros((NC, 16, 128), F32)
        for s in range(NZ):
            keep = y * NZ + s < to * NZ + z
            total = total + jnp.where(keep, got[s], jnp.zeros((NC, 16, 128), F32))
        for x in range(NX):
            out[to, x] = total


def final_kernel(place, slide, got, out):
    target = jnp.minimum(place[0] * NZ + place[1] + slide[0], NY * NZ - 1)
    total = got[0]
    for s in range(1, NY * NZ - 1):
        total = total + jnp.where(s < target, got[s], jnp.zeros((16, 128), F32))
    out[0] = unpack(total)


def call(body, out_shape, in_specs, scratch=(), params=None):
    several = isinstance(out_shape, (list, tuple))
    return pl.pallas_call(
        body,
        out_shape=out_shape,
        in_specs=in_specs,
        out_specs=[VM] * len(out_shape) if several else VM,
        scratch_shapes=list(scratch),
        compiler_params=params or pltpu.CompilerParams(vmem_limit_bytes=24 * MIB),
    )


def shape(dims, dtype):
    return jax.ShapeDtypeStruct(dims, dtype)


def swap_cores(x):
    return lax.ppermute(x, "c", [(0, 1), (1, 0)])


def local(
    guesses, step_ids, step_sizes, slide, offsets, mod_table, w_in, w_qkv, qk_gain, w_out, w_fin
):
    place = jnp.stack([lax.axis_index(a) for a in ("y", "z", "x", "c")]).astype(jnp.int32)
    state = guesses[0]
    w_peer = swap_cores(w_out)
    z = pack(state.astype(BF))
    zg = lax.all_to_all(
        jnp.broadcast_to(z[None], (8, 16, 128)), ("x", "c"), 0, 0, tiled=True
    )
    tab = tables(offsets, qk_gain)
    mod = lax.dynamic_index_in_dim(mod_table, step_ids[0], 0, keepdims=False)

    def to_drift(h, z, copies):
        peer = swap_cores(h[S // 2 :])
        parts = call(
            out_kernel, [shape((ROWS, D), BF)] * 4, [VM] * 4
        )(h[: S // 2], peer, w_out, w_peer)
        got = [parts[0]]
        for k in (2, 1, 3):
            got.append(lax.ppermute(parts[k], "x", [(i, (i + k) % NX) for i in range(NX)]))
        return call(
            drift_kernel, shape((copies, 16, 128), F32), [SM, SM] + [VM] * 9
        )(place, step_sizes, z, state, *got, w_in, mod, w_fin)

    h = call(
        first_kernel,
        shape((S, HL * HD), BF),
        [SM, VM, VM, VM, VM, ANY],
        BLOCK_SCRATCH,
        BLOCK_PARAMS,
    )(place, zg, tab, w_in, mod, w_qkv)
    drift = to_drift(h, z, NZ * NC)
    got = lax.all_to_all(drift, ("z", "c"), 0, 0, tiled=True)
    parts = call(relay_kernel, shape((NY, NX, NC, 16, 128), F32), [SM, VM])(
        place, got.reshape(NZ, NC, 16, 128)
    )
    parts = lax.all_to_all(
        parts.reshape(NY * NX, NC, 16, 128), ("y", "x"), 0, 0, tiled=True
    ).reshape(NY, NX, NC, 16, 128)
    h, z = call(
        second_kernel,
        [shape((S, HL * HD), BF), shape((16, 128), BF)],
        [SM, VM, VM, VM, VM, VM, ANY],
        BLOCK_SCRATCH,
        BLOCK_PARAMS,
    )(place, zg, parts, tab, w_in, mod, w_qkv)
    drift = to_drift(h, z, NY * NZ)
    got = lax.all_to_all(drift, ("y", "z"), 0, 0, tiled=True)
    return call(final_kernel, shape((1, ROWS, C), F32), [SM, SM, VM])(place, slide, got)


def solution(mesh):
    grid = Mesh(mesh.devices.reshape(NY, NZ, NX, NC), ("y", "z", "x", "c"))
    step, head = ("y", "z"), ("x", "c")
    in_specs = (
        P(step, head, None),
        P(step),
        P(step),
        P(),
        P(),
        P(),
        P(),
        P(None, head),
        P(),
        P(head, None),
        P(),
    )
    out_specs = P(step, head, None)
    return jax.shard_map(local, mesh=grid, in_specs=in_specs, out_specs=out_specs, check_vma=False)
```

time: 372 us -> 134 us (0.36)
  blocking collectives: 153 us -> 31.7 us
  waiting for transfers between devices: 140 us -> 27.6 us
  Pallas kernels: 0 us -> 31.9 us
  matrix products: 28.2 us -> 0 us
  other arithmetic: 25.5 us -> 3.19 us
  starting transfers between devices: 0.31 us -> 21.1 us
  between operations: 15.7 us -> 2.39 us
  local copies, waits for them, and re-layouts: 6.27 us -> 15.7 us
    all_gather x3 -> x0, blocking collectives: 153 us -> none  [the longest x2 103 us: carried_in(): gathered = lax.all_gather(part, axis)]
    all_gather x2 -> x0, waiting for transfers between devices: 70.1 us -> none  [local_drift(): lax.all_gather(features, 'head', axis=0, tiled=True)]
    reduce_scatter x2 -> x0, waiting for transfers between devices: 69.8 us -> none  [local_drift(): lax.psum_scatter(jnp.dot(heads_out, w_out, preferred_element_type=jnp.flo...]
    pallas_call x0 -> x8, Pallas kernels: none -> 31.9 us  [the longest x1 10.4 us: local(): call(second_kernel, [shape((S, HL * HD), BF), shape((16, 128), BF)], [SM,...]
    all_to_all x0 -> x2, blocking collectives: none -> 31.7 us  [the longest x1 16 us: local(): lax.all_to_all(parts.reshape(NY * NX, NC, 16, 128), ('y', 'x'), 0, 0, til...]
    dot_general x12 -> x0, matrix products: 27.3 us -> none  [the longest x2 12.8 us: local_drift(): jnp.dot(lax.all_gather(features, 'head', axis=0, tiled=True), w_qkv, pref...]
    ppermute x0 -> x9, waiting for transfers between devices: none -> 15.4 us  [the longest x6 13.2 us: to_drift(): lax.ppermute(parts[k], 'x', [(i, (i + k) % NX) for i in range(NX)])]
    all_to_all x0 -> x2, waiting for transfers between devices: none -> 12.2 us  [the longest x1 12.2 us: local(): got = lax.all_to_all(drift, ('y', 'z'), 0, 0, tiled=True)]
  transfers between devices with their start and end apart: 4 -> 11, of which waited for: 4 -> 8; matrix products, arithmetic and copies ran while one was open for 1% -> 6% of each run, Pallas kernels for 0% -> 8%
where the time goes in v1:
time: 134 us
  Pallas kernels  31.9 us (24%)
  blocking collectives  31.7 us (24%)
  waiting for transfers between devices  27.6 us (21%)
  starting transfers between devices  21.1 us (16%)
  local copies, waits for them, and re-layouts  15.7 us (12%)
  other arithmetic  3.19 us (2%)
  between operations  2.39 us (2%)
    all_to_all x1, blocking collectives, local(): lax.all_to_all(parts.reshape(NY * NX, NC, 16, 128), ('y', 'x'), 0, 0, til...  16 us
    all_to_all x1, blocking collectives, local(): got = lax.all_to_all(drift, ('z', 'c'), 0, 0, tiled=True)  15.7 us
    ppermute x6, waiting for transfers between devices, to_drift(): lax.ppermute(parts[k], 'x', [(i, (i + k) % NX) for i in range(NX)])  13.2 us
    unnamed x50, local copies, waits for them, and re-layouts  12.6 us
    all_to_all x1, waiting for transfers between devices, local(): got = lax.all_to_all(drift, ('y', 'z'), 0, 0, tiled=True)  12.2 us
    ppermute x6, starting transfers between devices, to_drift(): lax.ppermute(parts[k], 'x', [(i, (i + k) % NX) for i in range(NX)])  10.9 us
    pallas_call x1, Pallas kernels, local(): call(second_kernel, [shape((S, HL * HD), BF), shape((16, 128), BF)], [SM,...  10.4 us
    pallas_call x1, Pallas kernels, local(): call(first_kernel, shape((S, HL * HD), BF), [SM, VM, VM, VM, VM, ANY], BL...  10.4 us
  transfers between devices with their start and end apart: 11, of which 8 were waited for; matrix products, arithmetic and copies ran while one was open for 6% of the time, Pallas kernels for 8%

profile of v1, /device:TPU:32, one launch (start us, length us, event | category | flops | bytes accessed | tf_op | source)
XLA Modules:
  0.0 133.6 jit_solution(11824767230638590920)
XLA Ops:
  0.0 0.0 collective-permute-start.1
  0.0 0.9 bitcast_convert_fusion
  0.9 0.1 pad_maximum_fusion.2.z
  1.0 0.6 broadcast_in_dim.27
  1.6 4.3 %all-to-all-start = ((bf16[8,16,128]{2,1,0:T(8,128)(2,1)}), bf16[8,16,128]{2,1,0:T(8,128)(2,1)S(1)}, u32[]{:S(2)}, u32[]{:S(2)}) async-start(bf16[8,16,128]{2,1,0:T(8,128)(2,1)} %broadcast_in_dim.27), calls=%async_computation | async-start | bytes 65536 | tf_op jit(solution)/shard_map/all_to_all | solution.py:216
  6.0 0.8 fusion.5
  6.7 0.1 broadcast_multiply_fusion.3
  6.8 0.3 fusion.1
  7.2 0.2 cos.21
  7.4 0.0 copy-start.5
  7.4 0.9 copy.14
  8.3 0.2 sin.21
  8.6 0.2 copy.15
  8.8 0.1 slice.56
  8.9 0.1 slice.57
  9.0 0.2 mul.132
  9.2 0.1 slice.60
  9.3 0.1 slice.61
  9.4 0.2 mul.137
  10.2 1.0 multiply_multiply_fusion.1
  11.3 0.1 pad_add_fusion.place
  11.4 0.0 copy-start.8
  11.4 0.0 all-to-all-done.zg
  11.4 0.0 copy-start.1
  11.4 3.0 %copy-done.1 = bf16[3072,1152]{1,0:T(8,128)(2,1)S(1)} copy-done((bf16[3072,1152]{1,0:T(8,128)(2,1)S(1)}, bf16[3072,1152]{1,0:T(8,128)(2,1)}, u32[]{:S(2)}) %copy-start.1) | copy-done | bytes 7077912
  14.5 10.4 %shard_map.109 = bf16[256,384]{1,0:T(8,128)(2,1)S(1)} custom-call(s32[4]{0:T(128)S(1)} %pad_add_fusion.place, bf16[8,16,128]{2,1,0:T(8,128)(2,1)S(1)} %all-to-all-done.zg, f32[4,8,32,128]{3,2,1,0:T(8,128)S(1)} %pad_maximum_fusion.tab, bf16[64,3072]{1,0:T(8,128)(2,1)S(1)} %copy-done.5, f32[3,3072]{1,0:T(4,128)S(1)} %bitcast.26, bf16[3072,1152]{1,0:T(8,128)(2,1)S(1)} %copy-done.1), custom_call_target="tpu_custom_call" | custom-call | tf_op jit(solution)/shard_map/pallas_call | solution.py:234
  24.9 0.6 collective-permute-start
  25.5 0.9 collective-permute-done.peer
  26.4 0.0 collective-permute-done.1.w_peer
  26.5 3.5 %shard_map.110 = (bf16[32,3072]{1,0:T(8,128)(2,1)S(1)}, bf16[32,3072]{1,0:T(8,128)(2,1)}, bf16[32,3072]{1,0:T(8,128)(2,1)}, bf16[32,3072]{1,0:T(8,128)(2,1)}) custom-call(bf16[128,384]{1,0:T(8,128)(2,1)S(1)} %get-tuple-element.30.mine, bf16[128,384]{1,0:T(8,128)(2,1)S(1)} %collective-permute-done.peer, bf16[384,3072]{1,0:T(8,128)(2,1)S(1)} %copy-done.3, ...), custom_call_target="tpu_custom_call" | custom-call | tf_op jit(solution)/shard_map/pallas_call | solution.py:224
  30.0 0.7 copy-done.14
  30.6 3.4 %collective-permute-start.2 = (bf16[32,3072]{1,0:T(8,128)(2,1)}, bf16[32,3072]{1,0:T(8,128)(2,1)}, u32[]{:S(2)}, u32[]{:S(2)}) collective-permute-start(bf16[32,3072]{1,0:T(8,128)(2,1)} %get-tuple-element.16), channel_id=1, source_target_pairs={{0,4},{2,6},{4,0},{6,2},{1,5},{3,7},{5,1},{7,3},{8,12},{10,14},{12... | collective-permute-start | bytes 589832 | tf_op jit(solution)/shard_map/ppermute | solution.py:229
  34.0 0.6 collective-permute-start.3
  34.6 2.7 %collective-permute-start.4 = (bf16[32,3072]{1,0:T(8,128)(2,1)}, bf16[32,3072]{1,0:T(8,128)(2,1)}, u32[]{:S(2)}, u32[]{:S(2)}) collective-permute-start(bf16[32,3072]{1,0:T(8,128)(2,1)} %get-tuple-element.18), channel_id=1, source_target_pairs={{0,6},{2,0},{4,2},{6,4},{1,7},{3,1},{5,3},{7,5},{8,14},{10,8},{12,... | collective-permute-start | bytes 589832 | tf_op jit(solution)/shard_map/ppermute | solution.py:229
  37.2 1.4 %copy.17.w_fin = bf16[3072,64]{1,0:T(8,128)(2,1)S(1)} copy(bf16[3072,64]{0,1:T(8,128)(2,1)} %param.21) | data formatting | bytes 786432 | tf_op args[10]
  39.3 0.8 collective-permute-done.2.p1
  40.2 3.7 %collective-permute-done.3.p2 = bf16[32,3072]{1,0:T(8,128)(2,1)} collective-permute-done((bf16[32,3072]{1,0:T(8,128)(2,1)}, bf16[32,3072]{1,0:T(8,128)(2,1)}, u32[]{:S(2)}, u32[]{:S(2)}) %collective-permute-start.3) | collective-permute-done | bytes 196640 | tf_op jit(solution)/shard_map/ppermute | solution.py:229
  43.8 0.2 collective-permute-done.4.p3
  44.0 0.8 copy-done.9
  44.8 0.9 copy-done.15
  45.8 0.7 copy-done.18
  46.4 0.7 copy-done.20
  47.1 1.9 %shard_map.111 = f32[16,16,128]{2,1,0:T(8,128)S(1)} custom-call(s32[4]{0:T(128)S(1)} %copy-done.20, f32[1]{0:T(128)S(6)} %copy.23.size, bf16[16,128]{1,0:T(8,128)(2,1)S(1)} %copy-done.18, f32[32,64]{1,0:T(8,128)S(1)} %bitcast.33, bf16[32,3072]{1,0:T(8,128)(2,1)S(1)} %copy-done.15, bf16[32,3072]{1,0:T(8,128)(2,1)} %collective-permute-done.2.p1, ...), custom_call_target="tpu_custom_call" | custom-call | tf_op jit(solution)/shard_map/pallas_call | solution.py:230
  49.0 15.7 %all_to_all.20 = f32[16,16,128]{2,1,0:T(8,128)S(1)} all-to-all(f32[16,16,128]{2,1,0:T(8,128)S(1)} %shard_map.111), channel_id=1, replica_groups=mesh['y'=4,'z'=8,'x'=4,'c'=2] {'z','c'}, dimensions={0} | all-to-all | bytes 262144 | tf_op jit(solution)/shard_map/all_to_all | solution.py:242
  64.7 0.6 shard_map.112
  65.3 16.0 %all_to_all.21 = f32[16,2,16,128]{3,2,1,0:T(8,128)S(1)} all-to-all(f32[16,2,16,128]{3,2,1,0:T(8,128)S(1)} %bitcast.31), channel_id=1, replica_groups=mesh['y'=4,'z'=8,'x'=4,'c'=2] {'y','x'}, dimensions={0} | all-to-all | bytes 524288 | tf_op jit(solution)/shard_map/all_to_all | solution.py:246
  81.4 0.0 copy-start.2
  81.4 3.0 %copy-done.2 = bf16[3072,1152]{1,0:T(8,128)(2,1)S(1)} copy-done((bf16[3072,1152]{1,0:T(8,128)(2,1)S(1)}, bf16[3072,1152]{1,0:T(8,128)(2,1)}, u32[]{:S(2)}) %copy-start.2) | copy-done | bytes 7077912
  84.4 10.4 %shard_map.113 = (bf16[256,384]{1,0:T(8,128)(2,1)S(1)}, bf16[16,128]{1,0:T(8,128)(2,1)S(1)}) custom-call(s32[4]{0:T(128)S(1)} %copy-done.21, bf16[8,16,128]{2,1,0:T(8,128)(2,1)S(1)} %copy-done.13, f32[4,4,2,16,128]{4,3,2,1,0:T(8,128)S(1)} %bitcast.30, f32[4,8,32,128]{3,2,1,0:T(8,128)S(1)} %copy-done.7, bf16[64,3072]{1,0:T(8,128)(2,1)S(1)} %copy-done.5, ...), custom_call_target="tpu_custom_call" | custom-call | tf_op jit(solution)/shard_map/pallas_call | solution.py:249
  94.8 0.1 collective-permute-start.5
  94.9 1.3 collective-permute-done.5.peer
  96.2 2.6 %shard_map.114 = (bf16[32,3072]{1,0:T(8,128)(2,1)S(1)}, bf16[32,3072]{1,0:T(8,128)(2,1)S(1)}, bf16[32,3072]{1,0:T(8,128)(2,1)S(1)}, bf16[32,3072]{1,0:T(8,128)(2,1)S(1)}) custom-call(bf16[128,384]{1,0:T(8,128)(2,1)S(1)} %get-tuple-element.28.mine, bf16[128,384]{1,0:T(8,128)(2,1)S(1)} %collective-permute-done.5.peer, bf16[384,3072]{1,0:T(8,128)(2,1)S(1)} %copy-done.4, ...), custom_call_target="tpu_custom_call" | custom-call | tf_op jit(solution)/shard_map/pallas_call | solution.py:224
  98.9 1.0 collective-permute-start.6
  99.9 0.5 collective-permute-start.7
  100.4 2.8 %collective-permute-start.8 = (bf16[32,3072]{1,0:T(8,128)(2,1)S(1)}, bf16[32,3072]{1,0:T(8,128)(2,1)S(1)}, u32[]{:S(2)}, u32[]{:S(2)}) collective-permute-start(bf16[32,3072]{1,0:T(8,128)(2,1)S(1)} %get-tuple-element.24), channel_id=1, source_target_pairs={{0,6},{2,0},{4,2},{6,4},{1,7},{3,1},{5,3},{7,5},{8,14},{10,8},{12,... | collective-permute-start | bytes 589832 | tf_op jit(solution)/shard_map/ppermute | solution.py:229
  103.2 5.1 %collective-permute-done.6.p1 = bf16[32,3072]{1,0:T(8,128)(2,1)S(1)} collective-permute-done((bf16[32,3072]{1,0:T(8,128)(2,1)S(1)}, bf16[32,3072]{1,0:T(8,128)(2,1)S(1)}, u32[]{:S(2)}, u32[]{:S(2)}) %collective-permute-start.6) | collective-permute-done | bytes 196640 | tf_op jit(solution)/shard_map/ppermute | solution.py:229
  108.3 3.4 %collective-permute-done.7.p2 = bf16[32,3072]{1,0:T(8,128)(2,1)S(1)} collective-permute-done((bf16[32,3072]{1,0:T(8,128)(2,1)S(1)}, bf16[32,3072]{1,0:T(8,128)(2,1)S(1)}, u32[]{:S(2)}, u32[]{:S(2)}) %collective-permute-start.7) | collective-permute-done | bytes 196640 | tf_op jit(solution)/shard_map/ppermute | solution.py:229
  111.6 0.0 collective-permute-done.8.p3
  111.6 1.3 shard_map.115
  113.0 0.7 copy-done.11
  113.6 5.2 %all-to-all-start.3 = ((f32[32,16,128]{2,1,0:T(8,128)}), f32[32,16,128]{2,1,0:T(8,128)S(1)}, u32[]{:S(2)}, u32[]{:S(2)}) async-start(f32[32,16,128]{2,1,0:T(8,128)} %copy-done.11), calls=%async_computation.3 | async-start | bytes 524288 | tf_op jit(solution)/shard_map/all_to_all | solution.py:257
  119.5 12.2 %all-to-all-done.3.got = f32[32,16,128]{2,1,0:T(8,128)S(1)} async-done(((f32[32,16,128]{2,1,0:T(8,128)}), f32[32,16,128]{2,1,0:T(8,128)S(1)}, u32[]{:S(2)}, u32[]{:S(2)}) %all-to-all-start.3) | async-done | bytes 262176 | tf_op jit(solution)/shard_map/all_to_all | solution.py:257
  131.7 0.7 copy-done.22
  132.4 1.3 shard_map.116
  (48 shorter events, 0.3 us)
Async XLA Ops:
  0.0 11.2 %copy-start = (f32[64,3,3072]{2,0,1:T(8,128)S(1)}, f32[64,3,3072]{2,0,1:T(8,128)}, u32[]{:S(2)}) copy-start(f32[64,3,3072]{2,0,1:T(8,128)} %param.16) | copy-start | bytes 7077892
  0.0 8.8 %copy-start.23 = (f32[2,128]{1,0:T(2,128)S(1)}, f32[2,128]{1,0:T(2,128)}, u32[]{:S(2)}) copy-start(f32[2,128]{1,0:T(2,128)} %param.19) | copy-start | bytes 3076
  0.0 26.4 %collective-permute-start.1 = (bf16[384,3072]{1,0:T(8,128)(2,1)}, bf16[384,3072]{1,0:T(8,128)(2,1)}, u32[]{:S(2)}, u32[]{:S(2)}) collective-permute-start(bf16[384,3072]{1,0:T(8,128)(2,1)} %w_mine.3), channel_id=1, source_target_pairs={{0,1},{1,0},{2,3},{3,2},{4,5},{5,4},{6,7},{7,6},{8,9},{9,8},{10,11... | collective-permute-start | bytes 7077896 | tf_op jit(solution)/shard_map/ppermute | solution.py:206
  1.0 6.2 %copy-start.17 = (bf16[16,128]{1,0:T(8,128)(2,1)}, bf16[16,128]{1,0:T(8,128)(2,1)S(1)}, u32[]{:S(2)}) copy-start(bf16[16,128]{1,0:T(8,128)(2,1)S(1)} %pad_maximum_fusion.2.z) | copy-start | bytes 12292
  1.6 9.8 %all-to-all-start = ((bf16[8,16,128]{2,1,0:T(8,128)(2,1)}), bf16[8,16,128]{2,1,0:T(8,128)(2,1)S(1)}, u32[]{:S(2)}, u32[]{:S(2)}) async-start(bf16[8,16,128]{2,1,0:T(8,128)(2,1)} %broadcast_in_dim.27), calls=%async_computation | async-start | bytes 65536 | tf_op jit(solution)/shard_map/all_to_all | solution.py:216
  7.4 4.0 %copy-start.5 = (bf16[64,3072]{1,0:T(8,128)(2,1)S(1)}, bf16[64,3072]{1,0:T(8,128)(2,1)}, u32[]{:S(2)}) copy-start(bf16[64,3072]{1,0:T(8,128)(2,1)} %w_in.7) | copy-start | bytes 1179652
  11.2 13.6 %copy-start.6 = (f32[4,8,32,128]{3,2,1,0:T(8,128)}, f32[4,8,32,128]{3,2,1,0:T(8,128)S(1)}, u32[]{:S(2)}) copy-start(f32[4,8,32,128]{3,2,1,0:T(8,128)S(1)} %pad_maximum_fusion.tab) | copy-start | bytes 1572868
  11.4 13.5 %copy-start.19 = (s32[4]{0:T(128)}, s32[4]{0:T(128)S(1)}, u32[]{:S(2)}) copy-start(s32[4]{0:T(128)S(1)} %pad_add_fusion.place) | copy-start | bytes 52
  11.4 13.5 %copy-start.8 = (f32[1,3,3072]{2,1,0:T(4,128)}, f32[1,3,3072]{2,1,0:T(4,128)S(1)}, u32[]{:S(2)}) copy-start(f32[1,3,3072]{2,1,0:T(4,128)S(1)} %copy.21) | copy-start | bytes 110596
  11.4 13.5 %copy-start.12 = (bf16[8,16,128]{2,1,0:T(8,128)(2,1)}, bf16[8,16,128]{2,1,0:T(8,128)(2,1)S(1)}, u32[]{:S(2)}) copy-start(bf16[8,16,128]{2,1,0:T(8,128)(2,1)S(1)} %all-to-all-done.zg) | copy-start | bytes 98308
  11.4 3.0 %copy-start.1 = (bf16[3072,1152]{1,0:T(8,128)(2,1)S(1)}, bf16[3072,1152]{1,0:T(8,128)(2,1)}, u32[]{:S(2)}) copy-start(bf16[3072,1152]{1,0:T(8,128)(2,1)} %w_qkv.3) | copy-start | bytes 21233668
  14.5 12.0 %copy-start.3 = (bf16[384,3072]{1,0:T(8,128)(2,1)S(1)}, bf16[384,3072]{1,0:T(8,128)(2,1)}, u32[]{:S(2)}) copy-start(bf16[384,3072]{1,0:T(8,128)(2,1)} %w_mine.3) | copy-start | bytes 7077892
  24.9 1.5 %collective-permute-start = (bf16[128,384]{1,0:T(8,128)(2,1)S(1)}, bf16[128,384]{1,0:T(8,128)(2,1)S(1)}, u32[]{:S(2)}, u32[]{:S(2)}) collective-permute-start(bf16[128,384]{1,0:T(8,128)(2,1)S(1)} %get-tuple-element.29), channel_id=1, source_target_pairs={{0,1},{1,0},{2,3},{3,2},{4,5},{5,4},{6,7},{7,6},{8,9},{9,8},{10,11... | collective-permute-start | bytes 294920 | tf_op jit(solution)/shard_map/ppermute | solution.py:206
  26.5 17.6 %copy-start.16 = (f32[1,32,64]{2,1,0:T(8,128)S(1)}, f32[1,32,64]{2,1,0:T(8,128)}, u32[]{:S(2)}) copy-start(f32[1,32,64]{2,1,0:T(8,128)} %param.11) | copy-start | bytes 24580
  30.0 0.7 copy-start.14
  30.6 9.5 %collective-permute-start.2 = (bf16[32,3072]{1,0:T(8,128)(2,1)}, bf16[32,3072]{1,0:T(8,128)(2,1)}, u32[]{:S(2)}, u32[]{:S(2)}) collective-permute-start(bf16[32,3072]{1,0:T(8,128)(2,1)} %get-tuple-element.16), channel_id=1, source_target_pairs={{0,4},{2,6},{4,0},{6,2},{1,5},{3,7},{5,1},{7,3},{8,12},{10,14},{12... | collective-permute-start | bytes 589832 | tf_op jit(solution)/shard_map/ppermute | solution.py:229
  34.0 9.8 %collective-permute-start.3 = (bf16[32,3072]{1,0:T(8,128)(2,1)}, bf16[32,3072]{1,0:T(8,128)(2,1)}, u32[]{:S(2)}, u32[]{:S(2)}) collective-permute-start(bf16[32,3072]{1,0:T(8,128)(2,1)} %get-tuple-element.17), channel_id=1, source_target_pairs={{0,2},{2,4},{4,6},{6,0},{1,3},{3,5},{5,7},{7,1},{8,10},{10,12},{12... | collective-permute-start | bytes 589832 | tf_op jit(solution)/shard_map/ppermute | solution.py:229
  34.6 9.4 %collective-permute-start.4 = (bf16[32,3072]{1,0:T(8,128)(2,1)}, bf16[32,3072]{1,0:T(8,128)(2,1)}, u32[]{:S(2)}, u32[]{:S(2)}) collective-permute-start(bf16[32,3072]{1,0:T(8,128)(2,1)} %get-tuple-element.18), channel_id=1, source_target_pairs={{0,6},{2,0},{4,2},{6,4},{1,7},{3,1},{5,3},{7,5},{8,14},{10,8},{12,... | collective-permute-start | bytes 589832 | tf_op jit(solution)/shard_map/ppermute | solution.py:229
  38.6 42.7 %copy-start.7 = (f32[4,8,32,128]{3,2,1,0:T(8,128)S(1)}, f32[4,8,32,128]{3,2,1,0:T(8,128)}, u32[]{:S(2)}) copy-start(f32[4,8,32,128]{3,2,1,0:T(8,128)} %copy-done.6) | copy-start | bytes 1572868
  44.0 0.8 copy-start.9
  44.8 0.9 copy-start.15
  45.7 0.7 copy-start.18
  46.4 0.7 copy-start.20
  47.1 34.2 %copy-start.10 = (f32[1,3,3072]{2,1,0:T(4,128)S(1)}, f32[1,3,3072]{2,1,0:T(4,128)}, u32[]{:S(2)}) copy-start(f32[1,3,3072]{2,1,0:T(4,128)} %copy-done.8) | copy-start | bytes 110596
  47.1 34.2 %copy-start.13 = (bf16[8,16,128]{2,1,0:T(8,128)(2,1)S(1)}, bf16[8,16,128]{2,1,0:T(8,128)(2,1)}, u32[]{:S(2)}) copy-start(bf16[8,16,128]{2,1,0:T(8,128)(2,1)} %copy-done.12) | copy-start | bytes 98308
  47.1 34.2 %copy-start.21 = (s32[4]{0:T(128)S(1)}, s32[4]{0:T(128)}, u32[]{:S(2)}) copy-start(s32[4]{0:T(128)} %copy-done.19) | copy-start | bytes 52
  81.4 3.0 %copy-start.2 = (bf16[3072,1152]{1,0:T(8,128)(2,1)S(1)}, bf16[3072,1152]{1,0:T(8,128)(2,1)}, u32[]{:S(2)}) copy-start(bf16[3072,1152]{1,0:T(8,128)(2,1)} %w_qkv.3) | copy-start | bytes 21233668
  84.4 11.8 %copy-start.4 = (bf16[384,3072]{1,0:T(8,128)(2,1)S(1)}, bf16[384,3072]{1,0:T(8,128)(2,1)}, u32[]{:S(2)}) copy-start(bf16[384,3072]{1,0:T(8,128)(2,1)} %w_mine.3) | copy-start | bytes 7077892
  94.8 1.4 %collective-permute-start.5 = (bf16[128,384]{1,0:T(8,128)(2,1)S(1)}, bf16[128,384]{1,0:T(8,128)(2,1)S(1)}, u32[]{:S(2)}, u32[]{:S(2)}) collective-permute-start(bf16[128,384]{1,0:T(8,128)(2,1)S(1)} %get-tuple-element.27), channel_id=1, source_target_pairs={{0,1},{1,0},{2,3},{3,2},{4,5},{5,4},{6,7},{7,6},{8,9},{9,8},{10,11... | collective-permute-start | bytes 294920 | tf_op jit(solution)/shard_map/ppermute | solution.py:206
  98.9 9.4 %collective-permute-start.6 = (bf16[32,3072]{1,0:T(8,128)(2,1)S(1)}, bf16[32,3072]{1,0:T(8,128)(2,1)S(1)}, u32[]{:S(2)}, u32[]{:S(2)}) collective-permute-start(bf16[32,3072]{1,0:T(8,128)(2,1)S(1)} %get-tuple-element.22), channel_id=1, source_target_pairs={{0,4},{2,6},{4,0},{6,2},{1,5},{3,7},{5,1},{7,3},{8,12},{10,14},{12... | collective-permute-start | bytes 589832 | tf_op jit(solution)/shard_map/ppermute | solution.py:229
  99.9 11.7 %collective-permute-start.7 = (bf16[32,3072]{1,0:T(8,128)(2,1)S(1)}, bf16[32,3072]{1,0:T(8,128)(2,1)S(1)}, u32[]{:S(2)}, u32[]{:S(2)}) collective-permute-start(bf16[32,3072]{1,0:T(8,128)(2,1)S(1)} %get-tuple-element.23), channel_id=1, source_target_pairs={{0,2},{2,4},{4,6},{6,0},{1,3},{3,5},{5,7},{7,1},{8,10},{10,12},{12... | collective-permute-start | bytes 589832 | tf_op jit(solution)/shard_map/ppermute | solution.py:229
  100.4 11.3 %collective-permute-start.8 = (bf16[32,3072]{1,0:T(8,128)(2,1)S(1)}, bf16[32,3072]{1,0:T(8,128)(2,1)S(1)}, u32[]{:S(2)}, u32[]{:S(2)}) collective-permute-start(bf16[32,3072]{1,0:T(8,128)(2,1)S(1)} %get-tuple-element.24), channel_id=1, source_target_pairs={{0,6},{2,0},{4,2},{6,4},{1,7},{3,1},{5,3},{7,5},{8,14},{10,8},{12,... | collective-permute-start | bytes 589832 | tf_op jit(solution)/shard_map/ppermute | solution.py:229
  112.9 0.7 copy-start.11
  113.6 18.0 %all-to-all-start.3 = ((f32[32,16,128]{2,1,0:T(8,128)}), f32[32,16,128]{2,1,0:T(8,128)S(1)}, u32[]{:S(2)}, u32[]{:S(2)}) async-start(f32[32,16,128]{2,1,0:T(8,128)} %copy-done.11), calls=%async_computation.3 | async-start | bytes 524288 | tf_op jit(solution)/shard_map/all_to_all | solution.py:257
  131.7 0.7 copy-start.22

commit v2 on v1

v2 whole, which is shorter than its diff:
```python
import math

import jax
import jax.numpy as jnp
import numpy as np
from jax import lax
from jax.experimental import pallas as pl
from jax.experimental.pallas import tpu as pltpu
from jax.sharding import Mesh
from jax.sharding import PartitionSpec as P

NY, NZ, NX, NC = 4, 8, 4, 2
D = 3072
HD = 128
HL = 3
C = 64
S = 256
ROWS = 32
GRID_W = 16
ROT_DIM = 56
EPS = 1e-06
BF = jnp.bfloat16
F32 = jnp.float32
MIB = 1024 * 1024

VM = pl.BlockSpec(memory_space=pltpu.VMEM)
SM = pl.BlockSpec(memory_space=pltpu.SMEM)
ANY = pl.BlockSpec(memory_space=pl.ANY)


def pack(x):
    return jnp.concatenate([x[:16], x[16:]], axis=1)


def unpack(x):
    return jnp.concatenate([x[:, :C], x[:, C:]], axis=0)


FREQ = 10000.0 ** (-np.arange(ROT_DIM // 2) * 2.0 / ROT_DIM)
LANE_FREQ = np.zeros((2, HD), np.float32)
LANE_FREQ[0, HD - 4 * (ROT_DIM // 2) : HD - 2 * (ROT_DIM // 2)] = np.repeat(FREQ, 2)
LANE_FREQ[1, HD - 2 * (ROT_DIM // 2) :] = np.repeat(FREQ, 2)
QKV = 3 * HD
CUTS = ((0, 512), (512, 1024), (1024, 1152))


def swap_lanes(x):
    lane = lax.broadcasted_iota(jnp.int32, x.shape, len(x.shape) - 1)
    axis = len(x.shape) - 1
    return jnp.where(lane % 2 == 0, pltpu.roll(x, HD - 1, axis), pltpu.roll(x, 1, axis))


def halves(x):
    high = x.astype(BF)
    return high, (x - high.astype(F32)).astype(BF)


def prepare_kernel(offsets, freq, gain, w_in, mod, tab, wc, rows):
    index = lax.broadcasted_iota(jnp.int32, (S, 1), 0)
    row = (index // GRID_W + offsets[:, 0:1]).astype(F32)
    col = (index % GRID_W + offsets[:, 1:2]).astype(F32)
    angle = row * freq[0:1, :] + col * freq[1:2, :]
    sign = jnp.where(lax.broadcasted_iota(jnp.int32, (1, HD), 1) % 2 == 0, -1.0, 1.0)
    cosine = jnp.cos(angle)
    sine = jnp.sin(angle) * sign
    for k in range(2):
        g = gain[k : k + 1, :]
        turned = swap_lanes(jnp.broadcast_to(g, (8, HD)))[0:1]
        tab[2 * k] = (cosine * g).reshape(8, ROWS, HD)
        tab[2 * k + 1] = (sine * turned).reshape(8, ROWS, HD)
    w = w_in[...].astype(F32)
    w = w - jnp.sum(w, axis=-1, keepdims=True) * (1.0 / D)
    high, low = halves(w)
    wc[:C, :] = high
    wc[C:, :] = low
    rows[0:1, :] = 1.0 + mod[1:2, :]
    rows[1:2, :] = mod[0:1, :]
    rows[2:3, :] = mod[2:3, :]
    rows[3:, :] = jnp.zeros((5, D), F32)


def block_body(
    chunk_of, tab, wc, rows, w_qkv, mine, send, zs, es, fs, wv, qkv, qs, tabv, wcv, rowv, sems
):
    my_x, my_c = lax.axis_index("x"), lax.axis_index("c")
    order = [((my_x + r % 4) % 4) * 2 + (my_c + r // 4) % 2 for r in range(8)]
    wc_copy = pltpu.make_async_copy(wc, wcv, sems.at[3])
    wc_copy.start()
    row_copy = pltpu.make_async_copy(rows, rowv, sems.at[4])
    row_copy.start()
    copies = []
    for i, (low, high) in enumerate(CUTS):
        copy = pltpu.make_async_copy(
            w_qkv.at[:, pl.ds(low, high - low)], wv.at[:, pl.ds(low, high - low)], sems.at[i]
        )
        copy.start()
        copies.append(copy)
        if i == 0:
            tab_copies = [
                pltpu.make_async_copy(
                    tab.at[:, order[r]], tabv.at[:, pl.ds(32 * r, 32)], sems.at[5 + r]
                )
                for r in range(8)
            ]
            for copy in tab_copies:
                copy.start()
    for r in range(8):
        piece = chunk_of(order[r])
        zs[32 * r : 32 * r + 16, :] = piece[:, :C]
        zs[32 * r + 16 : 32 * r + 32, :] = piece[:, C:]
    z = zs[...]
    twice = jnp.concatenate([z, z], axis=1)
    total = jnp.zeros((S, 128), F32)
    wc_copy.wait()
    for j in range(6):
        cut = slice(j * 512, j * 512 + 512)
        e = jnp.dot(twice, wcv[:, cut], preferred_element_type=F32)
        es[:, cut] = e
        e = e * e
        total += (e[:, :128] + e[:, 128:256]) + (e[:, 256:384] + e[:, 384:])
    scale = lax.rsqrt(jnp.sum(total, axis=-1, keepdims=True) * (1.0 / D) + EPS)
    row_copy.wait()
    for j in range(6):
        cut = slice(j * 512, j * 512 + 512)
        fs[:, cut] = (es[:, cut] * scale * rowv[0:1, cut] + rowv[1:2, cut]).astype(BF)
    for copy in tab_copies:
        copy.wait()
    mean = jnp.full((2 * HD, HD), 1.0 / HD, BF)

    def turned(x, k):
        high, low = halves(x * x)
        square = jnp.dot(jnp.concatenate([high, low], axis=1), mean, preferred_element_type=F32)
        x = x * tabv[2 * k] + swap_lanes(x) * tabv[2 * k + 1]
        return (x * lax.rsqrt(square + EPS)).astype(BF)

    def attend(head):
        base = head * QKV
        for k in range(2):
            qs[head, k] = turned(qkv[:, base + k * HD : base + k * HD + HD], k)
        qs[head, 2] = qkv[:, base + 2 * HD : base + QKV].astype(BF)
        scores = lax.dot_general(
            qs[head, 0], qs[head, 1], (((1,), (1,)), ((), ())), preferred_element_type=F32
        )
        top = jnp.max(scores, axis=-1, keepdims=True)
        p = jnp.exp((scores - top) * (1.0 / math.sqrt(HD)))
        p = p * (1.0 / jnp.sum(p, axis=-1, keepdims=True))
        out = jnp.dot(p.astype(BF), qs[head, 2], preferred_element_type=F32).astype(BF)
        mine[:, head * HD : head * HD + HD] = out[: S // 2]
        send[:, head * HD : head * HD + HD] = out[S // 2 :]

    for i, (low, high) in enumerate(CUTS):
        copies[i].wait()
        qkv[:, low:high] = jnp.dot(fs[...], wv[:, low:high], preferred_element_type=F32)
        if i > 0:
            attend(i - 1)
    attend(2)


def first_kernel(zg, *rest):
    block_body(lambda i: zg[i], *rest)


def second_kernel(zg, parts, tab, wc, rows, w_qkv, mine, send, z_out, *scratch):
    start = lax.axis_index("y") * NZ + lax.axis_index("z") == 0

    def chunk_of(i):
        x, c = i // 2, i % 2
        total = parts[0, x, c] + parts[1, x, c] + parts[2, x, c] + parts[3, x, c]
        return jnp.where(start, zg[i].astype(F32), total).astype(BF)

    z_out[...] = chunk_of(lax.axis_index("x") * 2 + lax.axis_index("c"))
    block_body(chunk_of, tab, wc, rows, w_qkv, mine, send, *scratch)


BLOCK_SCRATCH = [
    pltpu.VMEM((S, C), BF),
    pltpu.VMEM((S, D), F32),
    pltpu.VMEM((S, D), BF),
    pltpu.VMEM((D, HL * QKV), BF),
    pltpu.VMEM((S, HL * QKV), F32),
    pltpu.VMEM((HL, 3, S, HD), BF),
    pltpu.VMEM((4, S, HD), F32),
    pltpu.VMEM((2 * C, D), BF),
    pltpu.VMEM((8, D), F32),
    pltpu.SemaphoreType.DMA((13,)),
]
LIMIT = 56 * MIB
PIECES = 6


def out_kernel(mine, peer, w_mine, w_peer, first, *rest):
    others, (wa, wb, sems) = rest[:3], rest[3:]
    wide = D // PIECES
    copies = []
    for j in range(PIECES):
        cut = pl.ds(j * wide, wide)
        pair = [
            pltpu.make_async_copy(w_mine.at[:, cut], wa.at[:, cut], sems.at[0, j]),
            pltpu.make_async_copy(w_peer.at[:, cut], wb.at[:, cut], sems.at[1, j]),
        ]
        for copy in pair:
            copy.start()
        copies.append(pair)
    for j in range(PIECES):
        cut = slice(j * wide, j * wide + wide)
        for copy in copies[j]:
            copy.wait()
        part = jnp.dot(mine[...], wa[:, cut], preferred_element_type=F32)
        part += jnp.dot(peer[...], wb[:, cut], preferred_element_type=F32)
        part = part.astype(BF)
        first[:, cut] = part[:ROWS]
        for k in range(3):
            others[k][:, cut] = part[ROWS * (k + 1) : ROWS * (k + 2)]


OUT_SCRATCH = [
    pltpu.VMEM((HL * HD, D), BF),
    pltpu.VMEM((HL * HD, D), BF),
    pltpu.SemaphoreType.DMA((2, PIECES)),
]


def drift_kernel(size, z, zstart, p0, p1, p2, p3, w_in, gate, w_fin, out):
    e = jnp.dot(unpack(z[...]), w_in[...], preferred_element_type=F32)
    attn = p0[...].astype(F32) + p1[...].astype(F32) + p2[...].astype(F32) + p3[...].astype(F32)
    h = e + gate[2:3, :] * attn
    mean = jnp.sum(h, axis=-1, keepdims=True) * (1.0 / D)
    h = h - mean
    var = jnp.sum(h * h, axis=-1, keepdims=True) * (1.0 / D)
    normed = (h * lax.rsqrt(var + EPS)).astype(BF)
    drift = size[0] * lax.dot_general(
        normed, w_fin[...], (((1,), (1,)), ((), ())), preferred_element_type=F32
    )
    start = lax.axis_index("y") * NZ + lax.axis_index("z") == 0
    drift = drift + jnp.where(start, zstart[...], jnp.zeros((ROWS, C), F32))
    packed = pack(drift)
    for k in range(out.shape[0]):
        out[k] = packed


def relay_kernel(got, out):
    y, z = lax.axis_index("y"), lax.axis_index("z")
    for to in range(NY):
        total = jnp.zeros((NC, 16, 128), F32)
        for s in range(NZ):
            keep = y * NZ + s < to * NZ + z
            total = total + jnp.where(keep, got[s], jnp.zeros((NC, 16, 128), F32))
        for x in range(NX):
            out[to, x] = total


def final_kernel(slide, got, out):
    here = lax.axis_index("y") * NZ + lax.axis_index("z")
    target = jnp.minimum(here + slide[0], NY * NZ - 1)
    total = got[0]
    for s in range(1, NY * NZ - 1):
        total = total + jnp.where(s < target, got[s], jnp.zeros((16, 128), F32))
    out[0] = unpack(total)


def call(body, out_shape, in_specs, scratch=()):
    several = isinstance(out_shape, (list, tuple))
    return pl.pallas_call(
        body,
        out_shape=out_shape,
        in_specs=in_specs,
        out_specs=[VM] * len(out_shape) if several else VM,
        scratch_shapes=list(scratch),
        compiler_params=pltpu.CompilerParams(vmem_limit_bytes=LIMIT),
    )


def shape(dims, dtype):
    return jax.ShapeDtypeStruct(dims, dtype)


def swap_cores(x):
    return lax.ppermute(x, "c", [(0, 1), (1, 0)])


def local(
    guesses, step_ids, step_sizes, slide, offsets, mod_table, w_in, w_qkv, qk_gain, w_out, w_fin
):
    state = guesses[0]
    w_peer = swap_cores(w_out)
    z = pack(state.astype(BF))
    zg = lax.all_to_all(jnp.broadcast_to(z[None], (8, 16, 128)), ("x", "c"), 0, 0, tiled=True)
    mod = lax.dynamic_index_in_dim(mod_table, step_ids[0], 0, keepdims=False)
    w_fin_rows = w_fin.T
    tab, wc, rows = call(
        prepare_kernel,
        [shape((4, 8, ROWS, HD), F32), shape((2 * C, D), BF), shape((8, D), F32)],
        [VM] * 5,
    )(offsets, jnp.asarray(LANE_FREQ), qk_gain, w_in, mod)
    half = shape((S // 2, HL * HD), BF)

    def to_drift(mine, send, z, copies):
        peer = swap_cores(send)
        parts = call(out_kernel, [shape((ROWS, D), BF)] * 4, [VM, VM, ANY, ANY], OUT_SCRATCH)(
            mine, peer, w_out, w_peer
        )
        got = [parts[0]]
        for k in (2, 1, 3):
            got.append(lax.ppermute(parts[k], "x", [(i, (i + k) % NX) for i in range(NX)]))
        return call(drift_kernel, shape((copies, 16, 128), F32), [SM] + [VM] * 9)(
            step_sizes, z, state, *got, w_in, rows, w_fin_rows
        )

    mine, send = call(first_kernel, [half, half], [VM] + [ANY] * 4, BLOCK_SCRATCH)(
        zg, tab, wc, rows, w_qkv
    )
    drift = to_drift(mine, send, z, NZ * NC)
    got = lax.all_to_all(drift, ("z", "c"), 0, 0, tiled=True)
    parts = call(relay_kernel, shape((NY, NX, NC, 16, 128), F32), [VM])(
        got.reshape(NZ, NC, 16, 128)
    )
    parts = lax.all_to_all(
        parts.reshape(NY * NX, NC, 16, 128), ("y", "x"), 0, 0, tiled=True
    ).reshape(NY, NX, NC, 16, 128)
    mine, send, z = call(
        second_kernel, [half, half, shape((16, 128), BF)], [VM] * 2 + [ANY] * 4, BLOCK_SCRATCH
    )(zg, parts, tab, wc, rows, w_qkv)
    drift = to_drift(mine, send, z, NY * NZ)
    got = lax.all_to_all(drift, ("y", "z"), 0, 0, tiled=True)
    return call(final_kernel, shape((1, ROWS, C), F32), [SM, VM])(slide, got)


def solution(mesh):
    grid = Mesh(mesh.devices.reshape(NY, NZ, NX, NC), ("y", "z", "x", "c"))
    step, head = ("y", "z"), ("x", "c")
    in_specs = (
        P(step, head, None),
        P(step),
        P(step),
        P(),
        P(),
        P(),
        P(),
        P(None, head),
        P(),
        P(head, None),
        P(),
    )
    out_specs = P(step, head, None)
    return jax.shard_map(local, mesh=grid, in_specs=in_specs, out_specs=out_specs, check_vma=False)
```

time: 134 us -> 132 us (0.985)
  local copies, waits for them, and re-layouts: 15.7 us -> 6.77 us
  Pallas kernels: 31.9 us -> 38.8 us
  other arithmetic: 3.19 us -> 0.95 us
  waiting for transfers between devices: 27.6 us -> 29.6 us
    pallas_call x8 -> x9, Pallas kernels: 31.9 us -> 38.8 us  [the longest x2 9.84 us: to_drift(): call(out_kernel, [shape((ROWS, D), BF)] * 4, [VM, VM, ANY, ANY], OUT_SCRA...]
    unnamed x50 -> x26, local copies, waits for them, and re-layouts: 12.6 us -> 6.11 us
    ppermute x6, waiting for transfers between devices: 13.2 us -> 14.8 us  [to_drift(): lax.ppermute(parts[k], 'x', [(i, (i + k) % NX) for i in range(NX)])]
  transfers between devices with their start and end apart: 11 -> 11, of which waited for: 8 -> 8; matrix products, arithmetic and copies ran while one was open for 6% -> 3% of each run, Pallas kernels for 8% -> 8%
where the time goes in v2:
time: 132 us
  Pallas kernels  38.8 us (29%)
  blocking collectives  32.3 us (24%)
  waiting for transfers between devices  29.6 us (22%)
  starting transfers between devices  21.2 us (16%)
  local copies, waits for them, and re-layouts  6.77 us (5%)
  between operations  2.06 us (2%)
    all_to_all x1, blocking collectives, local(): lax.all_to_all(parts.reshape(NY * NX, NC, 16, 128), ('y', 'x'), 0, 0, til...  16.3 us
    all_to_all x1, blocking collectives, local(): got = lax.all_to_all(drift, ('z', 'c'), 0, 0, tiled=True)  16.1 us
    ppermute x6, waiting for transfers between devices, to_drift(): lax.ppermute(parts[k], 'x', [(i, (i + k) % NX) for i in range(NX)])  14.8 us
    all_to_all x1, waiting for transfers between devices, local(): got = lax.all_to_all(drift, ('y', 'z'), 0, 0, tiled=True)  12.2 us
    ppermute x6, starting transfers between devices, to_drift(): lax.ppermute(parts[k], 'x', [(i, (i + k) % NX) for i in range(NX)])  10.9 us
    pallas_call x2, Pallas kernels, to_drift(): call(out_kernel, [shape((ROWS, D), BF)] * 4, [VM, VM, ANY, ANY], OUT_SCRA...  9.84 us
    pallas_call x1, Pallas kernels, local(): call(second_kernel, [half, half, shape((16, 128), BF)], [VM] * 2 + [ANY]...  8.54 us
    pallas_call x1, Pallas kernels, local(): call(first_kernel, [half, half], [VM] + [ANY] * 4, BLOCK_SCRATCH)  8.26 us
  transfers between devices with their start and end apart: 11, of which 8 were waited for; matrix products, arithmetic and copies ran while one was open for 3% of the time, Pallas kernels for 8%

profile of v2, /device:TPU:32, one launch (start us, length us, event | category | flops | bytes accessed | tf_op | source)
XLA Modules:
  0.0 131.7 jit_solution(17062528360798622514)
XLA Ops:
  0.0 0.0 copy-start
  0.0 0.0 collective-permute-start.1
  0.0 0.9 bitcast_convert_fusion
  0.9 0.1 pad_maximum_fusion.z
  1.0 0.0 copy-start.11
  1.0 0.6 broadcast_in_dim.2
  1.6 4.3 %all-to-all-start = ((bf16[8,16,128]{2,1,0:T(8,128)(2,1)}), bf16[8,16,128]{2,1,0:T(8,128)(2,1)S(1)}, u32[]{:S(2)}, u32[]{:S(2)}) async-start(bf16[8,16,128]{2,1,0:T(8,128)(2,1)} %broadcast_in_dim.2), calls=%async_computation | async-start | bytes 65536 | tf_op jit(solution)/shard_map/all_to_all | solution.py:287
  6.6 0.0 copy-done
  6.6 0.6 copy.17
  7.2 1.5 %copy.14.offsets = s32[256,2]{1,0:T(8,128)} copy(s32[256,2]{0,1:T(2,128)} %param.16) | data formatting | bytes 4096 | tf_op args[4]
  8.7 2.9 %shard_map.118 = (f32[4,8,32,128]{3,2,1,0:T(8,128)}, bf16[128,3072]{1,0:T(8,128)(2,1)}, f32[8,3072]{1,0:T(8,128)}) custom-call(s32[256,2]{1,0:T(8,128)} %copy.14.offsets, f32[2,128]{1,0:T(2,128)} %constant.8.clone.freq, f32[2,128]{1,0:T(2,128)} %gain.1, bf16[64,3072]{1,0:T(8,128)(2,1)} %w_in.5, f32[3,3072]{1,0:T(4,128)} %bitcast.18), custom_call_target="tpu_custom_call" | custom-call | tf_op jit(solution)/shard_map/pallas_call | solution.py:290
  11.6 0.0 all-to-all-done.zg
  11.6 0.0 copy-start.2
  11.6 0.6 copy-done.2
  12.2 8.3 %shard_map.119 = (bf16[128,384]{1,0:T(8,128)(2,1)}, bf16[128,384]{1,0:T(8,128)(2,1)}) custom-call(bf16[8,16,128]{2,1,0:T(8,128)(2,1)} %copy-done.2, f32[4,8,32,128]{3,2,1,0:T(8,128)} %get-tuple-element.21.rest_0_.tab, bf16[128,3072]{1,0:T(8,128)(2,1)} %get-tuple-element.22.rest_1_.wc, f32[8,3072]{1,0:T(8,128)} %get-tuple-element.23.rest_2_.gate.rows, ...), custom_call_target="tpu_custom_call" | custom-call | tf_op jit(solution)/shard_map/pallas_call | solution.py:309
  20.5 0.0 copy-done.11
  20.5 0.6 collective-permute-start
  21.1 1.2 collective-permute-done.peer
  22.3 0.0 copy-start.9
  22.3 0.0 collective-permute-done.1.w_peer
  22.3 0.6 copy-done.9
  22.9 4.9 %shard_map.120 = (bf16[32,3072]{1,0:T(8,128)(2,1)}, bf16[32,3072]{1,0:T(8,128)(2,1)}, bf16[32,3072]{1,0:T(8,128)(2,1)}, bf16[32,3072]{1,0:T(8,128)(2,1)}) custom-call(bf16[128,384]{1,0:T(8,128)(2,1)} %get-tuple-element.24.mine, bf16[128,384]{1,0:T(8,128)(2,1)} %copy-done.9, bf16[384,3072]{1,0:T(8,128)(2,1)} %w_mine.3, ...), custom_call_target="tpu_custom_call" | custom-call | tf_op jit(solution)/shard_map/pallas_call | solution.py:299
  27.8 3.5 %collective-permute-start.2 = (bf16[32,3072]{1,0:T(8,128)(2,1)}, bf16[32,3072]{1,0:T(8,128)(2,1)S(1)}, u32[]{:S(2)}, u32[]{:S(2)}) collective-permute-start(bf16[32,3072]{1,0:T(8,128)(2,1)} %get-tuple-element.27), channel_id=1, source_target_pairs={{0,4},{2,6},{4,0},{6,2},{1,5},{3,7},{5,1},{7,3},{8,12},{10,14},{12... | collective-permute-start | bytes 589832 | tf_op jit(solution)/shard_map/ppermute | solution.py:304
  31.3 0.6 collective-permute-start.3
  31.8 2.7 %collective-permute-start.4 = (bf16[32,3072]{1,0:T(8,128)(2,1)}, bf16[32,3072]{1,0:T(8,128)(2,1)S(1)}, u32[]{:S(2)}, u32[]{:S(2)}) collective-permute-start(bf16[32,3072]{1,0:T(8,128)(2,1)} %get-tuple-element.29), channel_id=1, source_target_pairs={{0,6},{2,0},{4,2},{6,4},{1,7},{3,1},{5,3},{7,5},{8,14},{10,8},{12,... | collective-permute-start | bytes 589832 | tf_op jit(solution)/shard_map/ppermute | solution.py:304
  35.2 2.2 %collective-permute-done.2.p1 = bf16[32,3072]{1,0:T(8,128)(2,1)S(1)} collective-permute-done((bf16[32,3072]{1,0:T(8,128)(2,1)}, bf16[32,3072]{1,0:T(8,128)(2,1)S(1)}, u32[]{:S(2)}, u32[]{:S(2)}) %collective-permute-start.2) | collective-permute-done | bytes 196640 | tf_op jit(solution)/shard_map/ppermute | solution.py:304
  37.3 0.0 copy-start.6
  37.3 3.7 %collective-permute-done.3.p2 = bf16[32,3072]{1,0:T(8,128)(2,1)S(1)} collective-permute-done((bf16[32,3072]{1,0:T(8,128)(2,1)}, bf16[32,3072]{1,0:T(8,128)(2,1)S(1)}, u32[]{:S(2)}, u32[]{:S(2)}) %collective-permute-start.3) | collective-permute-done | bytes 196640 | tf_op jit(solution)/shard_map/ppermute | solution.py:304
  41.0 0.0 copy-start.7
  41.0 0.2 collective-permute-done.4.p3
  41.2 0.0 copy-start.8
  41.2 0.0 copy-done.6
  41.2 0.5 copy-done.7
  41.7 0.2 copy-done.8
  41.9 2.9 %shard_map.121 = f32[16,16,128]{2,1,0:T(8,128)} custom-call(f32[1]{0:T(128)S(6)} %copy.19.size, bf16[16,128]{1,0:T(8,128)(2,1)} %copy-done.11, f32[32,64]{1,0:T(8,128)} %bitcast.19, bf16[32,3072]{1,0:T(8,128)(2,1)} %get-tuple-element.26.p0, bf16[32,3072]{1,0:T(8,128)(2,1)} %copy-done.6, bf16[32,3072]{1,0:T(8,128)(2,1)} %copy-done.7, ...), custom_call_target="tpu_custom_call" | custom-call | tf_op jit(solution)/shard_map/pallas_call | solution.py:305
  44.8 16.1 %all_to_all.20 = f32[16,16,128]{2,1,0:T(8,128)} all-to-all(f32[16,16,128]{2,1,0:T(8,128)} %shard_map.121), channel_id=1, replica_groups=mesh['y'=4,'z'=8,'x'=4,'c'=2] {'z','c'}, dimensions={0} | all-to-all | bytes 262144 | tf_op jit(solution)/shard_map/all_to_all | solution.py:313
  60.9 1.7 %shard_map.122 = f32[4,4,2,16,128]{4,3,2,1,0:T(8,128)} custom-call(f32[8,2,16,128]{3,2,1,0:T(8,128)} %bitcast.17), custom_call_target="tpu_custom_call" | custom-call | tf_op jit(solution)/shard_map/pallas_call | solution.py:314
  62.5 16.3 %all_to_all.21 = f32[16,2,16,128]{3,2,1,0:T(8,128)} all-to-all(f32[16,2,16,128]{3,2,1,0:T(8,128)} %bitcast.16), channel_id=1, replica_groups=mesh['y'=4,'z'=8,'x'=4,'c'=2] {'y','x'}, dimensions={0} | all-to-all | bytes 524288 | tf_op jit(solution)/shard_map/all_to_all | solution.py:317
  78.8 8.5 %shard_map.123 = (bf16[128,384]{1,0:T(8,128)(2,1)}, bf16[128,384]{1,0:T(8,128)(2,1)}, bf16[16,128]{1,0:T(8,128)(2,1)}) custom-call(bf16[8,16,128]{2,1,0:T(8,128)(2,1)} %copy-done.2, f32[4,4,2,16,128]{4,3,2,1,0:T(8,128)} %bitcast.15, f32[4,8,32,128]{3,2,1,0:T(8,128)} %get-tuple-element.21.rest_0_.tab, bf16[128,3072]{1,0:T(8,128)(2,1)} %get-tuple-element.22.rest_1_.wc, ...), custom_call_target="tpu_custom_call" | custom-call | tf_op jit(solution)/shard_map/pallas_call | solution.py:320
  87.3 0.1 collective-permute-start.5
  87.4 1.5 %collective-permute-done.5.peer = bf16[128,384]{1,0:T(8,128)(2,1)S(1)} collective-permute-done((bf16[128,384]{1,0:T(8,128)(2,1)}, bf16[128,384]{1,0:T(8,128)(2,1)S(1)}, u32[]{:S(2)}, u32[]{:S(2)}) %collective-permute-start.5) | collective-permute-done | bytes 98336 | tf_op jit(solution)/shard_map/ppermute | solution.py:278
  88.9 0.0 copy-start.10
  88.9 0.6 copy-done.10
  89.6 4.9 %shard_map.124 = (bf16[32,3072]{1,0:T(8,128)(2,1)}, bf16[32,3072]{1,0:T(8,128)(2,1)}, bf16[32,3072]{1,0:T(8,128)(2,1)}, bf16[32,3072]{1,0:T(8,128)(2,1)}) custom-call(bf16[128,384]{1,0:T(8,128)(2,1)} %get-tuple-element.31.mine, bf16[128,384]{1,0:T(8,128)(2,1)} %copy-done.10, bf16[384,3072]{1,0:T(8,128)(2,1)} %w_mine.3, ...), custom_call_target="tpu_custom_call" | custom-call | tf_op jit(solution)/shard_map/pallas_call | solution.py:299
  94.5 1.0 collective-permute-start.6
  95.5 0.5 collective-permute-start.7
  96.0 2.7 %collective-permute-start.8 = (bf16[32,3072]{1,0:T(8,128)(2,1)}, bf16[32,3072]{1,0:T(8,128)(2,1)S(1)}, u32[]{:S(2)}, u32[]{:S(2)}) collective-permute-start(bf16[32,3072]{1,0:T(8,128)(2,1)} %get-tuple-element.36), channel_id=1, source_target_pairs={{0,6},{2,0},{4,2},{6,4},{1,7},{3,1},{5,3},{7,5},{8,14},{10,8},{12,... | collective-permute-start | bytes 589832 | tf_op jit(solution)/shard_map/ppermute | solution.py:304
  98.8 5.3 %collective-permute-done.6.p1 = bf16[32,3072]{1,0:T(8,128)(2,1)S(1)} collective-permute-done((bf16[32,3072]{1,0:T(8,128)(2,1)}, bf16[32,3072]{1,0:T(8,128)(2,1)S(1)}, u32[]{:S(2)}, u32[]{:S(2)}) %collective-permute-start.6) | collective-permute-done | bytes 196640 | tf_op jit(solution)/shard_map/ppermute | solution.py:304
  104.1 0.0 copy-start.3
  104.1 3.4 %collective-permute-done.7.p2 = bf16[32,3072]{1,0:T(8,128)(2,1)S(1)} collective-permute-done((bf16[32,3072]{1,0:T(8,128)(2,1)}, bf16[32,3072]{1,0:T(8,128)(2,1)S(1)}, u32[]{:S(2)}, u32[]{:S(2)}) %collective-permute-start.7) | collective-permute-done | bytes 196640 | tf_op jit(solution)/shard_map/ppermute | solution.py:304
  107.5 0.0 copy-start.4
  107.5 0.0 collective-permute-done.8.p3
  107.5 0.0 copy-start.5
  107.5 0.0 copy-done.3
  107.5 0.7 copy-done.4
  108.2 0.1 copy-done.5
  108.3 3.0 %shard_map.125 = f32[32,16,128]{2,1,0:T(8,128)} custom-call(f32[1]{0:T(128)S(6)} %copy.19.size, bf16[16,128]{1,0:T(8,128)(2,1)} %get-tuple-element.30.z, f32[32,64]{1,0:T(8,128)} %bitcast.20, bf16[32,3072]{1,0:T(8,128)(2,1)} %get-tuple-element.33.p0, bf16[32,3072]{1,0:T(8,128)(2,1)} %copy-done.3, bf16[32,3072]{1,0:T(8,128)(2,1)} %copy-done.4, ...), custom_call_target="tpu_custom_call" | custom-call | tf_op jit(solution)/shard_map/pallas_call | solution.py:305
  111.3 5.2 %all-to-all-start.3 = ((f32[32,16,128]{2,1,0:T(8,128)}), f32[32,16,128]{2,1,0:T(8,128)S(1)}, u32[]{:S(2)}, u32[]{:S(2)}) async-start(f32[32,16,128]{2,1,0:T(8,128)} %shard_map.125), calls=%async_computation.3 | async-start | bytes 524288 | tf_op jit(solution)/shard_map/all_to_all | solution.py:324
  117.1 12.2 %all-to-all-done.3.got = f32[32,16,128]{2,1,0:T(8,128)S(1)} async-done(((f32[32,16,128]{2,1,0:T(8,128)}), f32[32,16,128]{2,1,0:T(8,128)S(1)}, u32[]{:S(2)}, u32[]{:S(2)}) %all-to-all-start.3) | async-done | bytes 262176 | tf_op jit(solution)/shard_map/all_to_all | solution.py:324
  129.3 0.0 copy-start.1
  129.3 0.7 copy-done.1
  130.0 1.7 %shard_map.126 = f32[1,32,64]{2,1,0:T(8,128)} custom-call(s32[1]{0:T(128)S(6)} %copy.20.slide, f32[32,16,128]{2,1,0:T(8,128)} %copy-done.1), custom_call_target="tpu_custom_call" | custom-call | tf_op jit(solution)/shard_map/pallas_call | solution.py:325
  (2 shorter events, 0.0 us)
Async XLA Ops:
  0.0 6.6 %copy-start = (f32[64,3,3072]{2,0,1:T(8,128)S(1)}, f32[64,3,3072]{2,0,1:T(8,128)}, u32[]{:S(2)}) copy-start(f32[64,3,3072]{2,0,1:T(8,128)} %param.17) | copy-start | bytes 7077892
  0.0 22.3 %collective-permute-start.1 = (bf16[384,3072]{1,0:T(8,128)(2,1)}, bf16[384,3072]{1,0:T(8,128)(2,1)}, u32[]{:S(2)}, u32[]{:S(2)}) collective-permute-start(bf16[384,3072]{1,0:T(8,128)(2,1)} %w_mine.3), channel_id=1, source_target_pairs={{0,1},{1,0},{2,3},{3,2},{4,5},{5,4},{6,7},{7,6},{8,9},{9,8},{10,11... | collective-permute-start | bytes 7077896 | tf_op jit(solution)/shard_map/ppermute | solution.py:278
  1.0 19.5 %copy-start.11 = (bf16[16,128]{1,0:T(8,128)(2,1)}, bf16[16,128]{1,0:T(8,128)(2,1)S(1)}, u32[]{:S(2)}) copy-start(bf16[16,128]{1,0:T(8,128)(2,1)S(1)} %pad_maximum_fusion.z) | copy-start | bytes 12292
  1.6 10.0 %all-to-all-start = ((bf16[8,16,128]{2,1,0:T(8,128)(2,1)}), bf16[8,16,128]{2,1,0:T(8,128)(2,1)S(1)}, u32[]{:S(2)}, u32[]{:S(2)}) async-start(bf16[8,16,128]{2,1,0:T(8,128)(2,1)} %broadcast_in_dim.2), calls=%async_computation | async-start | bytes 65536 | tf_op jit(solution)/shard_map/all_to_all | solution.py:287
  11.6 0.6 copy-start.2
  20.5 1.8 %collective-permute-start = (bf16[128,384]{1,0:T(8,128)(2,1)}, bf16[128,384]{1,0:T(8,128)(2,1)S(1)}, u32[]{:S(2)}, u32[]{:S(2)}) collective-permute-start(bf16[128,384]{1,0:T(8,128)(2,1)} %get-tuple-element.25), channel_id=1, source_target_pairs={{0,1},{1,0},{2,3},{3,2},{4,5},{5,4},{6,7},{7,6},{8,9},{9,8},{10,11... | collective-permute-start | bytes 294920 | tf_op jit(solution)/shard_map/ppermute | solution.py:278
  22.3 0.6 copy-start.9
  27.8 9.5 %collective-permute-start.2 = (bf16[32,3072]{1,0:T(8,128)(2,1)}, bf16[32,3072]{1,0:T(8,128)(2,1)S(1)}, u32[]{:S(2)}, u32[]{:S(2)}) collective-permute-start(bf16[32,3072]{1,0:T(8,128)(2,1)} %get-tuple-element.27), channel_id=1, source_target_pairs={{0,4},{2,6},{4,0},{6,2},{1,5},{3,7},{5,1},{7,3},{8,12},{10,14},{12... | collective-permute-start | bytes 589832 | tf_op jit(solution)/shard_map/ppermute | solution.py:304
  31.3 9.7 %collective-permute-start.3 = (bf16[32,3072]{1,0:T(8,128)(2,1)}, bf16[32,3072]{1,0:T(8,128)(2,1)S(1)}, u32[]{:S(2)}, u32[]{:S(2)}) collective-permute-start(bf16[32,3072]{1,0:T(8,128)(2,1)} %get-tuple-element.28), channel_id=1, source_target_pairs={{0,2},{2,4},{4,6},{6,0},{1,3},{3,5},{5,7},{7,1},{8,10},{10,12},{12... | collective-permute-start | bytes 589832 | tf_op jit(solution)/shard_map/ppermute | solution.py:304
  31.8 9.4 %collective-permute-start.4 = (bf16[32,3072]{1,0:T(8,128)(2,1)}, bf16[32,3072]{1,0:T(8,128)(2,1)S(1)}, u32[]{:S(2)}, u32[]{:S(2)}) collective-permute-start(bf16[32,3072]{1,0:T(8,128)(2,1)} %get-tuple-element.29), channel_id=1, source_target_pairs={{0,6},{2,0},{4,2},{6,4},{1,7},{3,1},{5,3},{7,5},{8,14},{10,8},{12,... | collective-permute-start | bytes 589832 | tf_op jit(solution)/shard_map/ppermute | solution.py:304
  37.3 3.9 %copy-start.6 = (bf16[32,3072]{1,0:T(8,128)(2,1)}, bf16[32,3072]{1,0:T(8,128)(2,1)S(1)}, u32[]{:S(2)}) copy-start(bf16[32,3072]{1,0:T(8,128)(2,1)S(1)} %collective-permute-done.2.p1) | copy-start | bytes 589828
  41.0 0.7 copy-start.7
  41.2 0.7 copy-start.8
  87.3 1.6 %collective-permute-start.5 = (bf16[128,384]{1,0:T(8,128)(2,1)}, bf16[128,384]{1,0:T(8,128)(2,1)S(1)}, u32[]{:S(2)}, u32[]{:S(2)}) collective-permute-start(bf16[128,384]{1,0:T(8,128)(2,1)} %get-tuple-element.32), channel_id=1, source_target_pairs={{0,1},{1,0},{2,3},{3,2},{4,5},{5,4},{6,7},{7,6},{8,9},{9,8},{10,11... | collective-permute-start | bytes 294920 | tf_op jit(solution)/shard_map/ppermute | solution.py:278
  88.9 0.6 copy-start.10
  94.5 9.6 %collective-permute-start.6 = (bf16[32,3072]{1,0:T(8,128)(2,1)}, bf16[32,3072]{1,0:T(8,128)(2,1)S(1)}, u32[]{:S(2)}, u32[]{:S(2)}) collective-permute-start(bf16[32,3072]{1,0:T(8,128)(2,1)} %get-tuple-element.34), channel_id=1, source_target_pairs={{0,4},{2,6},{4,0},{6,2},{1,5},{3,7},{5,1},{7,3},{8,12},{10,14},{12... | collective-permute-start | bytes 589832 | tf_op jit(solution)/shard_map/ppermute | solution.py:304
  95.5 12.0 %collective-permute-start.7 = (bf16[32,3072]{1,0:T(8,128)(2,1)}, bf16[32,3072]{1,0:T(8,128)(2,1)S(1)}, u32[]{:S(2)}, u32[]{:S(2)}) collective-permute-start(bf16[32,3072]{1,0:T(8,128)(2,1)} %get-tuple-element.35), channel_id=1, source_target_pairs={{0,2},{2,4},{4,6},{6,0},{1,3},{3,5},{5,7},{7,1},{8,10},{10,12},{12... | collective-permute-start | bytes 589832 | tf_op jit(solution)/shard_map/ppermute | solution.py:304
  96.0 11.5 %collective-permute-start.8 = (bf16[32,3072]{1,0:T(8,128)(2,1)}, bf16[32,3072]{1,0:T(8,128)(2,1)S(1)}, u32[]{:S(2)}, u32[]{:S(2)}) collective-permute-start(bf16[32,3072]{1,0:T(8,128)(2,1)} %get-tuple-element.36), channel_id=1, source_target_pairs={{0,6},{2,0},{4,2},{6,4},{1,7},{3,1},{5,3},{7,5},{8,14},{10,8},{12,... | collective-permute-start | bytes 589832 | tf_op jit(solution)/shard_map/ppermute | solution.py:304
  104.1 3.4 %copy-start.3 = (bf16[32,3072]{1,0:T(8,128)(2,1)}, bf16[32,3072]{1,0:T(8,128)(2,1)S(1)}, u32[]{:S(2)}) copy-start(bf16[32,3072]{1,0:T(8,128)(2,1)S(1)} %collective-permute-done.6.p1) | copy-start | bytes 589828
  107.5 0.7 copy-start.4
  107.5 0.8 copy-start.5
  111.3 18.1 %all-to-all-start.3 = ((f32[32,16,128]{2,1,0:T(8,128)}), f32[32,16,128]{2,1,0:T(8,128)S(1)}, u32[]{:S(2)}, u32[]{:S(2)}) async-start(f32[32,16,128]{2,1,0:T(8,128)} %shard_map.125), calls=%async_computation.3 | async-start | bytes 524288 | tf_op jit(solution)/shard_map/all_to_all | solution.py:324
  129.3 0.7 copy-start.1

commit v3 on v2

v3 whole, which is shorter than its diff:
```python
import math

import jax
import jax.numpy as jnp
import numpy as np
from jax import lax
from jax.experimental import pallas as pl
from jax.experimental.pallas import tpu as pltpu
from jax.sharding import Mesh
from jax.sharding import PartitionSpec as P

NY, NZ, NX, NC = 4, 8, 4, 2
D = 3072
HD = 128
HL = 3
C = 64
S = 256
ROWS = 32
GRID_W = 16
ROT_DIM = 56
EPS = 1e-06
BF = jnp.bfloat16
F32 = jnp.float32
MIB = 1024 * 1024

VM = pl.BlockSpec(memory_space=pltpu.VMEM)
HB = pl.BlockSpec(memory_space=pltpu.HBM)
SM = pl.BlockSpec(memory_space=pltpu.SMEM)


def pack(x):
    return jnp.concatenate([x[:16], x[16:]], axis=1)


def unpack(x):
    return jnp.concatenate([x[:, :C], x[:, C:]], axis=0)


FREQ = [float(np.float32(10000.0 ** (-j * 2.0 / ROT_DIM))) for j in range(ROT_DIM // 2)]
QKV = 3 * HD


def swap_lanes(x):
    lane = lax.broadcasted_iota(jnp.int32, x.shape, len(x.shape) - 1)
    axis = len(x.shape) - 1
    return jnp.where(lane % 2 == 0, pltpu.roll(x, HD - 1, axis), pltpu.roll(x, 1, axis))


def halves(x):
    high = x.astype(BF)
    return high, (x - high.astype(F32)).astype(BF)


def prepare_kernel(offsets, gain, w_in, mod, tab, wc, rows):
    lane = lax.broadcasted_iota(jnp.int32, (1, HD), 1)
    pair = lane // 2
    by_row = jnp.zeros((1, HD), F32)
    by_col = jnp.zeros((1, HD), F32)
    count = ROT_DIM // 2
    for j in range(count):
        by_row = jnp.where(pair == HD // 2 - 2 * count + j, FREQ[j], by_row)
        by_col = jnp.where(pair == HD // 2 - count + j, FREQ[j], by_col)
    index = lax.broadcasted_iota(jnp.int32, (1, S), 1)
    row = (index // GRID_W + offsets[0:1, :]).astype(F32)
    col = (index % GRID_W + offsets[1:2, :]).astype(F32)
    both = jnp.concatenate([row, col, jnp.zeros((6, S), F32)], axis=0).T
    angle = both[:, 0:1] * by_row + both[:, 1:2] * by_col
    cosine = jnp.cos(angle)
    sine = jnp.sin(angle) * jnp.where(lane % 2 == 0, -1.0, 1.0)
    for k in range(2):
        g = gain[k : k + 1, :]
        turned = swap_lanes(jnp.broadcast_to(g, (8, HD)))[0:1]
        tab[2 * k] = (cosine * g).reshape(8, ROWS, HD)
        tab[2 * k + 1] = (sine * turned).reshape(8, ROWS, HD)
    w = w_in[...].astype(F32)
    w = w - jnp.sum(w, axis=-1, keepdims=True) * (1.0 / D)
    high, low = halves(w)
    wc[:C, :] = high
    wc[C:, :] = low
    rows[0:1, :] = 1.0 + mod[1:2, :]
    rows[1:2, :] = mod[0:1, :]
    rows[2:3, :] = mod[2:3, :]
    rows[3:, :] = jnp.zeros((5, D), F32)


def block_body(chunk_of, wait, cuts, tab, wc, rows, w_qkv, mine, send, zs, es, fs, qkv, qs):
    my_x, my_c = lax.axis_index("x"), lax.axis_index("c")
    order = [((my_x + r % 4) % 4) * 2 + (my_c + r // 4) % 2 for r in range(8)]
    for r in range(8):
        piece = chunk_of(order[r])
        zs[32 * r : 32 * r + 16, :] = piece[:, :C]
        zs[32 * r + 16 : 32 * r + 32, :] = piece[:, C:]
    z = zs[...]
    twice = jnp.concatenate([z, z], axis=1)
    total = jnp.zeros((S, 128), F32)
    wait("wc")
    for j in range(6):
        cut = slice(j * 512, j * 512 + 512)
        e = jnp.dot(twice, wc[:, cut], preferred_element_type=F32)
        es[:, cut] = e
        e = e * e
        total += (e[:, :128] + e[:, 128:256]) + (e[:, 256:384] + e[:, 384:])
    scale = lax.rsqrt(jnp.sum(total, axis=-1, keepdims=True) * (1.0 / D) + EPS)
    wait("rows")
    for j in range(6):
        cut = slice(j * 512, j * 512 + 512)
        fs[:, cut] = (es[:, cut] * scale * rows[0:1, cut] + rows[1:2, cut]).astype(BF)
    for i, (low, high) in enumerate(cuts):
        wait(i)
        qkv[:, low:high] = jnp.dot(fs[...], w_qkv[:, low:high], preferred_element_type=F32)
    wait("tab")
    mean = jnp.full((2 * HD, HD), 1.0 / HD, BF)

    def table(k):
        return jnp.concatenate([tab[k, order[r]] for r in range(8)], axis=0)

    def turned(x, k):
        high, low = halves(x * x)
        square = jnp.dot(jnp.concatenate([high, low], axis=1), mean, preferred_element_type=F32)
        x = x * table(2 * k) + swap_lanes(x) * table(2 * k + 1)
        return (x * lax.rsqrt(square + EPS)).astype(BF)

    for head in range(HL):
        base = head * QKV
        for k in range(2):
            qs[head, k] = turned(qkv[:, base + k * HD : base + k * HD + HD], k)
        qs[head, 2] = qkv[:, base + 2 * HD : base + QKV].astype(BF)
        scores = lax.dot_general(
            qs[head, 0], qs[head, 1], (((1,), (1,)), ((), ())), preferred_element_type=F32
        )
        top = jnp.max(scores, axis=-1, keepdims=True)
        p = jnp.exp((scores - top) * (1.0 / math.sqrt(HD)))
        p = p * (1.0 / jnp.sum(p, axis=-1, keepdims=True))
        out = jnp.dot(p.astype(BF), qs[head, 2], preferred_element_type=F32).astype(BF)
        mine[:, head * HD : head * HD + HD] = out[: S // 2]
        send[:, head * HD : head * HD + HD] = out[S // 2 :]


WHOLE = ((0, HL * QKV),)


def no_wait(key):
    return None


def first_kernel(zg, *rest):
    block_body(lambda i: zg[i], no_wait, WHOLE, *rest)


def second_kernel(zg, parts, tab, wc, rows, w_qkv, mine, send, z_out, *scratch):
    start = lax.axis_index("y") * NZ + lax.axis_index("z") == 0

    def chunk_of(i):
        x, c = i // 2, i % 2
        total = (parts[0, x, c] + parts[1, x, c]) + (parts[2, x, c] + parts[3, x, c])
        return jnp.where(start, zg[i].astype(F32), total).astype(BF)

    z_out[...] = chunk_of(lax.axis_index("x") * 2 + lax.axis_index("c"))
    block_body(chunk_of, no_wait, WHOLE, tab, wc, rows, w_qkv, mine, send, *scratch)


BLOCK_SCRATCH = [
    pltpu.VMEM((S, C), BF),
    pltpu.VMEM((S, D), F32),
    pltpu.VMEM((S, D), BF),
    pltpu.VMEM((S, HL * QKV), F32),
    pltpu.VMEM((HL, 3, S, HD), BF),
]


def projected(mine, peer, w_mine, w_peer, cut):
    middle = jnp.concatenate([mine[:, 2 * HD :], peer[:, :HD]], axis=1)
    w_middle = jnp.concatenate([w_mine[2 * HD :, cut], w_peer[:HD, cut]], axis=0)
    part = jnp.dot(mine[:, : 2 * HD], w_mine[: 2 * HD, cut], preferred_element_type=F32)
    part += jnp.dot(middle, w_middle, preferred_element_type=F32)
    part += jnp.dot(peer[:, HD:], w_peer[HD:, cut], preferred_element_type=F32)
    return part.astype(BF)


def out_kernel(mine, peer, w_mine, w_peer, *outs):
    for j in range(6):
        cut = slice(j * 512, j * 512 + 512)
        part = projected(mine, peer, w_mine, w_peer, cut)
        for k in range(NX):
            outs[k][:, cut] = part[ROWS * k : ROWS * (k + 1)]


def drift_kernel(size, z, zstart, p0, p1, p2, p3, w_in, gate, w_fin, out):
    e = jnp.dot(unpack(z[...]), w_in[...], preferred_element_type=F32)
    attn = p0[...].astype(F32) + p1[...].astype(F32) + p2[...].astype(F32) + p3[...].astype(F32)
    h = e + gate[2:3, :] * attn
    mean = jnp.sum(h, axis=-1, keepdims=True) * (1.0 / D)
    h = h - mean
    var = jnp.sum(h * h, axis=-1, keepdims=True) * (1.0 / D)
    normed = (h * lax.rsqrt(var + EPS)).astype(BF)
    drift = size[0] * lax.dot_general(
        normed, w_fin[...], (((1,), (1,)), ((), ())), preferred_element_type=F32
    )
    start = lax.axis_index("y") * NZ + lax.axis_index("z") == 0
    drift = drift + jnp.where(start, zstart[...], jnp.zeros((ROWS, C), F32))
    packed = pack(drift)
    for k in range(out.shape[0]):
        out[k] = packed


def relay_kernel(got, out):
    y, z = lax.axis_index("y"), lax.axis_index("z")
    for to in range(NY):
        total = jnp.zeros((NC, 16, 128), F32)
        for s in range(NZ):
            keep = y * NZ + s < to * NZ + z
            total = total + jnp.where(keep, got[s], jnp.zeros((NC, 16, 128), F32))
        for x in range(NX):
            out[to, x] = total


def final_kernel(slide, got, out):
    here = lax.axis_index("y") * NZ + lax.axis_index("z")
    target = jnp.minimum(here + slide[0], NY * NZ - 1)
    total = got[0]
    for s in range(1, NY * NZ - 1):
        total = total + jnp.where(s < target, got[s], jnp.zeros((16, 128), F32))
    out[0] = unpack(total)


def call(body, out_shape, in_specs, scratch=(), limit=8):
    several = isinstance(out_shape, (list, tuple))
    return pl.pallas_call(
        body,
        out_shape=out_shape,
        in_specs=in_specs,
        out_specs=[VM] * len(out_shape) if several else VM,
        scratch_shapes=list(scratch),
        compiler_params=pltpu.CompilerParams(vmem_limit_bytes=limit * MIB),
    )


def shape(dims, dtype):
    return jax.ShapeDtypeStruct(dims, dtype)


def swap_cores(x):
    return lax.ppermute(x, "c", [(0, 1), (1, 0)])


def local(
    guesses, step_ids, step_sizes, slide, offsets, mod_table, w_in, w_qkv, qk_gain, w_out, w_fin
):
    state = guesses[0]
    w_peer = swap_cores(w_out)
    z = pack(state.astype(BF))
    zg = lax.all_to_all(jnp.broadcast_to(z[None], (8, 16, 128)), ("x", "c"), 0, 0, tiled=True)
    w_fin_rows = w_fin.T
    mod = lax.dynamic_index_in_dim(mod_table, step_ids[0], 0, keepdims=False)
    tab, wc, rows = call(
        prepare_kernel,
        [shape((4, 8, ROWS, HD), F32), shape((2 * C, D), BF), shape((8, D), F32)],
        [VM] * 4,
        limit=12,
    )(offsets.T, qk_gain, w_in, mod)
    half = shape((S // 2, HL * HD), BF)
    row = shape((ROWS, D), BF)

    def to_right(x, k):
        return lax.ppermute(x, "x", [(i, (i + k) % NX) for i in range(NX)])

    def to_drift(mine, send, z, w_peer, copies):
        operands = (mine, swap_cores(send), w_out, w_peer)
        parts = call(out_kernel, [row] * NX, [VM] * 4, limit=16)(*operands)
        got = [to_right(parts[k], k) for k in (2, 1, 3)]
        return call(drift_kernel, shape((copies, 16, 128), F32), [SM] + [VM] * 9)(
            step_sizes, z, state, parts[0], *got, w_in, rows, w_fin_rows
        )

    mine, send = call(
        first_kernel, [half, half], [VM] * 5, BLOCK_SCRATCH, limit=16
    )(zg, tab, wc, rows, w_qkv)
    drift = to_drift(mine, send, z, w_peer, NZ * NC)
    got = lax.all_to_all(drift, ("z", "c"), 0, 0, tiled=True)
    parts = call(relay_kernel, shape((NY, NX, NC, 16, 128), F32), [VM])(
        got.reshape(NZ, NC, 16, 128)
    )
    parts = lax.all_to_all(
        parts.reshape(NY * NX, NC, 16, 128), ("y", "x"), 0, 0, tiled=True
    ).reshape(NY, NX, NC, 16, 128)
    mine, send, z = call(
        second_kernel,
        [half, half, shape((16, 128), BF)],
        [VM] * 6,
        BLOCK_SCRATCH,
        limit=16,
    )(zg, parts, tab, wc, rows, w_qkv)
    drift = to_drift(mine, send, z, w_peer, NY * NZ)
    got = lax.all_to_all(drift, ("y", "z"), 0, 0, tiled=True)
    return call(final_kernel, shape((1, ROWS, C), F32), [SM, VM])(slide, got)


def solution(mesh):
    grid = Mesh(mesh.devices.reshape(NY, NZ, NX, NC), ("y", "z", "x", "c"))
    step, head = ("y", "z"), ("x", "c")
    in_specs = (
        P(step, head, None),
        P(step),
        P(step),
        P(),
        P(),
        P(),
        P(),
        P(None, head),
        P(),
        P(head, None),
        P(),
    )
    out_specs = P(step, head, None)
    return jax.shard_map(local, mesh=grid, in_specs=in_specs, out_specs=out_specs, check_vma=False)
```

time: 132 us -> 112 us (0.85)
  Pallas kernels: 38.8 us -> 18.6 us
    pallas_call x4, Pallas kernels: 26.6 us -> 14.8 us  [the longest x2 5.1 us: to_drift(): parts = call(out_kernel, [row] * NX, [VM] * 4, limit=16)(*operands)]
    pallas_call x2, Pallas kernels: 5.95 us -> 2.18 us  [to_drift(): call(drift_kernel, shape((copies, 16, 128), F32), [SM] + [VM] * 9)]
    pallas_call x1, Pallas kernels: 2.91 us -> 0.92 us  [local(): call(prepare_kernel, [shape((4, 8, ROWS, HD), F32), shape((2 * C, D), BF)...]
    pallas_call x1, Pallas kernels: 1.66 us -> 0.05 us  [local(): call(relay_kernel, shape((NY, NX, NC, 16, 128), F32), [VM])]
    unnamed x26 -> x27, local copies, waits for them, and re-layouts: 6.11 us -> 7.25 us
  transfers between devices with their start and end apart: 11 -> 11, of which waited for: 8 -> 8; matrix products, arithmetic and copies ran while one was open for 3% -> 1% of each run, Pallas kernels for 8% -> 5%
where the time goes in v3:
time: 112 us; the launch traced here: 111 us
  blocking collectives  31.7 us (28%)
  waiting for transfers between devices  29.8 us (27%)
  starting transfers between devices  20.2 us (18%)
  Pallas kernels  18.6 us (17%)
  local copies, waits for them, and re-layouts  7.89 us (7%)
  between operations  2.13 us (2%)
    all_to_all x1, blocking collectives, local(): lax.all_to_all(parts.reshape(NY * NX, NC, 16, 128), ('y', 'x'), 0, 0, til...  15.9 us
    all_to_all x1, blocking collectives, local(): got = lax.all_to_all(drift, ('z', 'c'), 0, 0, tiled=True)  15.7 us
    ppermute x6, waiting for transfers between devices, to_right(): return lax.ppermute(x, 'x', [(i, (i + k) % NX) for i in range(NX)])  14.4 us
    all_to_all x1, waiting for transfers between devices, local(): got = lax.all_to_all(drift, ('y', 'z'), 0, 0, tiled=True)  12.2 us
    ppermute x6, starting transfers between devices, to_right(): return lax.ppermute(x, 'x', [(i, (i + k) % NX) for i in range(NX)])  10.5 us
    unnamed x27, local copies, waits for them, and re-layouts  7.25 us
    all_to_all x1, starting transfers between devices, local(): got = lax.all_to_all(drift, ('y', 'z'), 0, 0, tiled=True)  5.19 us
    pallas_call x2, Pallas kernels, to_drift(): parts = call(out_kernel, [row] * NX, [VM] * 4, limit=16)(*operands)  5.1 us
  transfers between devices with their start and end apart: 11, of which 8 were waited for; matrix products, arithmetic and copies ran while one was open for 1% of the time, Pallas kernels for 5%

profile of v3, /device:TPU:32, one launch (start us, length us, event | category | flops | bytes accessed | tf_op | source)
XLA Modules:
  0.0 111.2 jit_solution(12360176242130654303)
XLA Ops:
  0.0 0.0 copy-start
  0.0 0.0 collective-permute-start.1
  0.0 0.9 bitcast_convert_fusion
  0.9 0.1 pad_maximum_fusion.z
  1.0 0.6 broadcast_in_dim.2
  1.6 4.3 %all-to-all-start = ((bf16[8,16,128]{2,1,0:T(8,128)(2,1)}), bf16[8,16,128]{2,1,0:T(8,128)(2,1)S(1)}, u32[]{:S(2)}, u32[]{:S(2)}) async-start(bf16[8,16,128]{2,1,0:T(8,128)(2,1)} %broadcast_in_dim.2), calls=%async_computation | async-start | bytes 65536 | tf_op jit(solution)/shard_map/all_to_all | solution.py:252
  6.6 0.0 copy-done
  6.6 0.0 copy-start.4
  6.6 1.0 copy-done.4
  7.6 0.0 copy-start.11
  7.6 0.7 copy-done.11
  8.3 0.0 copy-start.12
  8.3 0.7 copy-done.12
  9.0 0.9 shard_map.109
  9.9 0.0 copy-start.6
  9.9 0.8 copy-done.6
  10.7 0.6 all-to-all-done.zg
  11.3 0.0 copy-start.1
  11.4 3.0 %copy-done.1 = bf16[3072,1152]{1,0:T(8,128)(2,1)S(1)} copy-done((bf16[3072,1152]{1,0:T(8,128)(2,1)S(1)}, bf16[3072,1152]{1,0:T(8,128)(2,1)}, u32[]{:S(2)}) %copy-start.1) | copy-done | bytes 7077912
  14.4 0.0 copy-start.7
  14.4 1.0 copy-done.7
  15.4 0.0 copy-start.3
  15.4 0.0 copy-start.5
  15.4 0.0 copy-start.9
  15.4 0.0 copy-start.10
  15.4 4.8 %shard_map.110 = (bf16[128,384]{1,0:T(8,128)(2,1)S(1)}, bf16[128,384]{1,0:T(8,128)(2,1)S(1)}) custom-call(bf16[8,16,128]{2,1,0:T(8,128)(2,1)S(1)} %all-to-all-done.zg, f32[4,8,32,128]{3,2,1,0:T(8,128)S(1)} %copy-done.7, bf16[128,3072]{1,0:T(8,128)(2,1)S(1)} %get-tuple-element.22.rest_1_.wc, f32[8,3072]{1,0:T(8,128)S(1)} %get-tuple-element.23.rest_2_.gate.rows, ...), custom_call_target="tpu_custom_call" | custom-call | tf_op jit(solution)/shard_map/pallas_call | solution.py:275
  20.2 0.1 collective-permute-start
  20.3 1.3 %collective-permute-done.peer = bf16[128,384]{1,0:T(8,128)(2,1)S(1)} collective-permute-done((bf16[128,384]{1,0:T(8,128)(2,1)S(1)}, bf16[128,384]{1,0:T(8,128)(2,1)S(1)}, u32[]{:S(2)}, u32[]{:S(2)}) %collective-permute-start) | collective-permute-done | bytes 98336 | tf_op jit(solution)/shard_map/ppermute | solution.py:243
  21.6 0.0 collective-permute-done.1.w_peer
  21.6 0.0 copy-done.3
  21.6 0.0 copy-start.2
  21.6 2.6 %shard_map.111 = (bf16[32,3072]{1,0:T(8,128)(2,1)S(1)}, bf16[32,3072]{1,0:T(8,128)(2,1)S(1)}, bf16[32,3072]{1,0:T(8,128)(2,1)S(1)}, bf16[32,3072]{1,0:T(8,128)(2,1)S(1)}) custom-call(bf16[128,384]{1,0:T(8,128)(2,1)S(1)} %get-tuple-element.24.mine, bf16[128,384]{1,0:T(8,128)(2,1)S(1)} %collective-permute-done.peer, bf16[384,3072]{1,0:T(8,128)(2,1)S(1)} %copy-done.3, ...), custom_call_target="tpu_custom_call" | custom-call | tf_op jit(solution)/shard_map/pallas_call | solution.py:269
  24.2 0.0 copy-start.8
  24.3 3.0 %collective-permute-start.2 = (bf16[32,3072]{1,0:T(8,128)(2,1)S(1)}, bf16[32,3072]{1,0:T(8,128)(2,1)S(1)}, u32[]{:S(2)}, u32[]{:S(2)}) collective-permute-start(bf16[32,3072]{1,0:T(8,128)(2,1)S(1)} %get-tuple-element.27), channel_id=1, source_target_pairs={{0,4},{2,6},{4,0},{6,2},{1,5},{3,7},{5,1},{7,3},{8,12},{10,14},{12... | collective-permute-start | bytes 589832 | tf_op jit(solution)/shard_map/ppermute | solution.py:265
  27.3 0.6 collective-permute-start.3
  27.8 2.7 %collective-permute-start.4 = (bf16[32,3072]{1,0:T(8,128)(2,1)S(1)}, bf16[32,3072]{1,0:T(8,128)(2,1)S(1)}, u32[]{:S(2)}, u32[]{:S(2)}) collective-permute-start(bf16[32,3072]{1,0:T(8,128)(2,1)S(1)} %get-tuple-element.29), channel_id=1, source_target_pairs={{0,6},{2,0},{4,2},{6,4},{1,7},{3,1},{5,3},{7,5},{8,14},{10,8},{12,... | collective-permute-start | bytes 589832 | tf_op jit(solution)/shard_map/ppermute | solution.py:265
  31.2 2.4 %collective-permute-done.2.p1 = bf16[32,3072]{1,0:T(8,128)(2,1)S(1)} collective-permute-done((bf16[32,3072]{1,0:T(8,128)(2,1)S(1)}, bf16[32,3072]{1,0:T(8,128)(2,1)S(1)}, u32[]{:S(2)}, u32[]{:S(2)}) %collective-permute-start.2) | collective-permute-done | bytes 196640 | tf_op jit(solution)/shard_map/ppermute | solution.py:265
  33.6 3.4 %collective-permute-done.3.p2 = bf16[32,3072]{1,0:T(8,128)(2,1)S(1)} collective-permute-done((bf16[32,3072]{1,0:T(8,128)(2,1)S(1)}, bf16[32,3072]{1,0:T(8,128)(2,1)S(1)}, u32[]{:S(2)}, u32[]{:S(2)}) %collective-permute-start.3) | collective-permute-done | bytes 196640 | tf_op jit(solution)/shard_map/ppermute | solution.py:265
  37.0 0.0 collective-permute-done.4.p3
  37.0 0.0 copy-done.5
  37.0 0.0 copy-done.9
  37.0 0.0 copy-done.10
  37.0 0.7 shard_map.112
  37.8 15.7 %all_to_all.20 = f32[16,16,128]{2,1,0:T(8,128)S(1)} all-to-all(f32[16,16,128]{2,1,0:T(8,128)S(1)} %shard_map.112), channel_id=1, replica_groups=mesh['y'=4,'z'=8,'x'=4,'c'=2] {'z','c'}, dimensions={0} | all-to-all | bytes 262144 | tf_op jit(solution)/shard_map/all_to_all | solution.py:279
  53.5 0.1 shard_map.113
  53.6 15.9 %all_to_all.21 = f32[16,2,16,128]{3,2,1,0:T(8,128)S(1)} all-to-all(f32[16,2,16,128]{3,2,1,0:T(8,128)S(1)} %bitcast.17), channel_id=1, replica_groups=mesh['y'=4,'z'=8,'x'=4,'c'=2] {'y','x'}, dimensions={0} | all-to-all | bytes 524288 | tf_op jit(solution)/shard_map/all_to_all | solution.py:283
  69.5 0.0 copy-done.2
  69.5 0.0 copy-done.8
  69.5 4.9 %shard_map.114 = (bf16[128,384]{1,0:T(8,128)(2,1)S(1)}, bf16[128,384]{1,0:T(8,128)(2,1)S(1)}, bf16[16,128]{1,0:T(8,128)(2,1)S(1)}) custom-call(bf16[8,16,128]{2,1,0:T(8,128)(2,1)S(1)} %all-to-all-done.zg, f32[4,4,2,16,128]{4,3,2,1,0:T(8,128)S(1)} %bitcast.16, f32[4,8,32,128]{3,2,1,0:T(8,128)S(1)} %copy-done.8, ...), custom_call_target="tpu_custom_call" | custom-call | tf_op jit(solution)/shard_map/pallas_call | solution.py:286
  74.4 0.1 collective-permute-start.5
  74.5 1.3 %collective-permute-done.5.peer = bf16[128,384]{1,0:T(8,128)(2,1)S(1)} collective-permute-done((bf16[128,384]{1,0:T(8,128)(2,1)S(1)}, bf16[128,384]{1,0:T(8,128)(2,1)S(1)}, u32[]{:S(2)}, u32[]{:S(2)}) %collective-permute-start.5) | collective-permute-done | bytes 98336 | tf_op jit(solution)/shard_map/ppermute | solution.py:243
  75.8 2.5 %shard_map.115 = (bf16[32,3072]{1,0:T(8,128)(2,1)S(1)}, bf16[32,3072]{1,0:T(8,128)(2,1)S(1)}, bf16[32,3072]{1,0:T(8,128)(2,1)S(1)}, bf16[32,3072]{1,0:T(8,128)(2,1)S(1)}) custom-call(bf16[128,384]{1,0:T(8,128)(2,1)S(1)} %get-tuple-element.31.mine, bf16[128,384]{1,0:T(8,128)(2,1)S(1)} %collective-permute-done.5.peer, bf16[384,3072]{1,0:T(8,128)(2,1)S(1)} %copy-done.3, ...), custom_call_target="tpu_custom_call" | custom-call | tf_op jit(solution)/shard_map/pallas_call | solution.py:269
  78.2 1.0 collective-permute-start.6
  79.3 0.5 collective-permute-start.7
  79.7 2.8 %collective-permute-start.8 = (bf16[32,3072]{1,0:T(8,128)(2,1)S(1)}, bf16[32,3072]{1,0:T(8,128)(2,1)S(1)}, u32[]{:S(2)}, u32[]{:S(2)}) collective-permute-start(bf16[32,3072]{1,0:T(8,128)(2,1)S(1)} %get-tuple-element.36), channel_id=1, source_target_pairs={{0,6},{2,0},{4,2},{6,4},{1,7},{3,1},{5,3},{7,5},{8,14},{10,8},{12,... | collective-permute-start | bytes 589832 | tf_op jit(solution)/shard_map/ppermute | solution.py:265
  82.5 5.1 %collective-permute-done.6.p1 = bf16[32,3072]{1,0:T(8,128)(2,1)S(1)} collective-permute-done((bf16[32,3072]{1,0:T(8,128)(2,1)S(1)}, bf16[32,3072]{1,0:T(8,128)(2,1)S(1)}, u32[]{:S(2)}, u32[]{:S(2)}) %collective-permute-start.6) | collective-permute-done | bytes 196640 | tf_op jit(solution)/shard_map/ppermute | solution.py:265
  87.6 3.4 %collective-permute-done.7.p2 = bf16[32,3072]{1,0:T(8,128)(2,1)S(1)} collective-permute-done((bf16[32,3072]{1,0:T(8,128)(2,1)S(1)}, bf16[32,3072]{1,0:T(8,128)(2,1)S(1)}, u32[]{:S(2)}, u32[]{:S(2)}) %collective-permute-start.7) | collective-permute-done | bytes 196640 | tf_op jit(solution)/shard_map/ppermute | solution.py:265
  91.0 0.0 collective-permute-done.8.p3
  91.0 1.5 %shard_map.116 = f32[32,16,128]{2,1,0:T(8,128)} custom-call(f32[1]{0:T(128)S(6)} %copy.16.size, bf16[16,128]{1,0:T(8,128)(2,1)S(1)} %get-tuple-element.30.z, f32[32,64]{1,0:T(8,128)S(1)} %bitcast.21, bf16[32,3072]{1,0:T(8,128)(2,1)S(1)} %get-tuple-element.33.p0, bf16[32,3072]{1,0:T(8,128)(2,1)S(1)} %collective-permute-done.6.p1, ...), custom_call_target="tpu_custom_call" | custom-call | tf_op jit(solution)/shard_map/pallas_call | solution.py:271
  92.5 5.2 %all-to-all-start.3 = ((f32[32,16,128]{2,1,0:T(8,128)}), f32[32,16,128]{2,1,0:T(8,128)S(1)}, u32[]{:S(2)}, u32[]{:S(2)}) async-start(f32[32,16,128]{2,1,0:T(8,128)} %shard_map.116), calls=%async_computation.3 | async-start | bytes 524288 | tf_op jit(solution)/shard_map/all_to_all | solution.py:294
  98.3 12.2 %all-to-all-done.3.got = f32[32,16,128]{2,1,0:T(8,128)S(1)} async-done(((f32[32,16,128]{2,1,0:T(8,128)}), f32[32,16,128]{2,1,0:T(8,128)S(1)}, u32[]{:S(2)}, u32[]{:S(2)}) %all-to-all-start.3) | async-done | bytes 262176 | tf_op jit(solution)/shard_map/all_to_all | solution.py:294
  110.5 0.7 shard_map.117
  (3 shorter events, 0.1 us)
Async XLA Ops:
  0.0 6.6 %copy-start = (f32[64,3,3072]{2,0,1:T(8,128)S(1)}, f32[64,3,3072]{2,0,1:T(8,128)}, u32[]{:S(2)}) copy-start(f32[64,3,3072]{2,0,1:T(8,128)} %param.16) | copy-start | bytes 7077892
  0.0 21.6 %collective-permute-start.1 = (bf16[384,3072]{1,0:T(8,128)(2,1)}, bf16[384,3072]{1,0:T(8,128)(2,1)}, u32[]{:S(2)}, u32[]{:S(2)}) collective-permute-start(bf16[384,3072]{1,0:T(8,128)(2,1)} %w_mine.3), channel_id=1, source_target_pairs={{0,1},{1,0},{2,3},{3,2},{4,5},{5,4},{6,7},{7,6},{8,9},{9,8},{10,11... | collective-permute-start | bytes 7077896 | tf_op jit(solution)/shard_map/ppermute | solution.py:243
  1.6 9.8 %all-to-all-start = ((bf16[8,16,128]{2,1,0:T(8,128)(2,1)}), bf16[8,16,128]{2,1,0:T(8,128)(2,1)S(1)}, u32[]{:S(2)}, u32[]{:S(2)}) async-start(bf16[8,16,128]{2,1,0:T(8,128)(2,1)} %broadcast_in_dim.2), calls=%async_computation | async-start | bytes 65536 | tf_op jit(solution)/shard_map/all_to_all | solution.py:252
  6.6 1.0 copy-start.4
  7.6 0.7 copy-start.11
  8.3 0.7 copy-start.12
  9.9 0.8 copy-start.6
  11.3 3.0 %copy-start.1 = (bf16[3072,1152]{1,0:T(8,128)(2,1)S(1)}, bf16[3072,1152]{1,0:T(8,128)(2,1)}, u32[]{:S(2)}) copy-start(bf16[3072,1152]{1,0:T(8,128)(2,1)} %w_qkv.1) | copy-start | bytes 21233668
  14.4 1.0 copy-start.7
  15.4 6.2 %copy-start.3 = (bf16[384,3072]{1,0:T(8,128)(2,1)S(1)}, bf16[384,3072]{1,0:T(8,128)(2,1)}, u32[]{:S(2)}) copy-start(bf16[384,3072]{1,0:T(8,128)(2,1)} %w_mine.3) | copy-start | bytes 7077892
  15.4 21.6 %copy-start.5 = (bf16[64,3072]{1,0:T(8,128)(2,1)S(1)}, bf16[64,3072]{1,0:T(8,128)(2,1)}, u32[]{:S(2)}) copy-start(bf16[64,3072]{1,0:T(8,128)(2,1)} %w_in.5) | copy-start | bytes 1179652
  15.4 21.6 %copy-start.9 = (bf16[3072,64]{0,1:T(8,128)(2,1)S(1)}, bf16[3072,64]{0,1:T(8,128)(2,1)}, u32[]{:S(2)}) copy-start(bf16[3072,64]{0,1:T(8,128)(2,1)} %param.21) | copy-start | bytes 1179652
  15.4 21.6 %copy-start.10 = (f32[1,32,64]{2,1,0:T(8,128)S(1)}, f32[1,32,64]{2,1,0:T(8,128)}, u32[]{:S(2)}) copy-start(f32[1,32,64]{2,1,0:T(8,128)} %param.11) | copy-start | bytes 24580
  20.2 1.4 %collective-permute-start = (bf16[128,384]{1,0:T(8,128)(2,1)S(1)}, bf16[128,384]{1,0:T(8,128)(2,1)S(1)}, u32[]{:S(2)}, u32[]{:S(2)}) collective-permute-start(bf16[128,384]{1,0:T(8,128)(2,1)S(1)} %get-tuple-element.25), channel_id=1, source_target_pairs={{0,1},{1,0},{2,3},{3,2},{4,5},{5,4},{6,7},{7,6},{8,9},{9,8},{10,11... | collective-permute-start | bytes 294920 | tf_op jit(solution)/shard_map/ppermute | solution.py:243
  21.6 47.9 %copy-start.2 = (bf16[3072,1152]{1,0:T(8,128)(2,1)S(1)}, bf16[3072,1152]{1,0:T(8,128)(2,1)}, u32[]{:S(2)}) copy-start(bf16[3072,1152]{1,0:T(8,128)(2,1)} %w_qkv.1) | copy-start | bytes 21233668
  24.2 45.3 %copy-start.8 = (f32[4,8,32,128]{3,2,1,0:T(8,128)S(1)}, f32[4,8,32,128]{3,2,1,0:T(8,128)}, u32[]{:S(2)}) copy-start(f32[4,8,32,128]{3,2,1,0:T(8,128)} %copy-done.6) | copy-start | bytes 1572868
  24.3 9.3 %collective-permute-start.2 = (bf16[32,3072]{1,0:T(8,128)(2,1)S(1)}, bf16[32,3072]{1,0:T(8,128)(2,1)S(1)}, u32[]{:S(2)}, u32[]{:S(2)}) collective-permute-start(bf16[32,3072]{1,0:T(8,128)(2,1)S(1)} %get-tuple-element.27), channel_id=1, source_target_pairs={{0,4},{2,6},{4,0},{6,2},{1,5},{3,7},{5,1},{7,3},{8,12},{10,14},{12... | collective-permute-start | bytes 589832 | tf_op jit(solution)/shard_map/ppermute | solution.py:265
  27.3 9.7 %collective-permute-start.3 = (bf16[32,3072]{1,0:T(8,128)(2,1)S(1)}, bf16[32,3072]{1,0:T(8,128)(2,1)S(1)}, u32[]{:S(2)}, u32[]{:S(2)}) collective-permute-start(bf16[32,3072]{1,0:T(8,128)(2,1)S(1)} %get-tuple-element.28), channel_id=1, source_target_pairs={{0,2},{2,4},{4,6},{6,0},{1,3},{3,5},{5,7},{7,1},{8,10},{10,12},{12... | collective-permute-start | bytes 589832 | tf_op jit(solution)/shard_map/ppermute | solution.py:265
  27.8 9.2 %collective-permute-start.4 = (bf16[32,3072]{1,0:T(8,128)(2,1)S(1)}, bf16[32,3072]{1,0:T(8,128)(2,1)S(1)}, u32[]{:S(2)}, u32[]{:S(2)}) collective-permute-start(bf16[32,3072]{1,0:T(8,128)(2,1)S(1)} %get-tuple-element.29), channel_id=1, source_target_pairs={{0,6},{2,0},{4,2},{6,4},{1,7},{3,1},{5,3},{7,5},{8,14},{10,8},{12,... | collective-permute-start | bytes 589832 | tf_op jit(solution)/shard_map/ppermute | solution.py:265
  74.4 1.4 %collective-permute-start.5 = (bf16[128,384]{1,0:T(8,128)(2,1)S(1)}, bf16[128,384]{1,0:T(8,128)(2,1)S(1)}, u32[]{:S(2)}, u32[]{:S(2)}) collective-permute-start(bf16[128,384]{1,0:T(8,128)(2,1)S(1)} %get-tuple-element.32), channel_id=1, source_target_pairs={{0,1},{1,0},{2,3},{3,2},{4,5},{5,4},{6,7},{7,6},{8,9},{9,8},{10,11... | collective-permute-start | bytes 294920 | tf_op jit(solution)/shard_map/ppermute | solution.py:243
  78.2 9.4 %collective-permute-start.6 = (bf16[32,3072]{1,0:T(8,128)(2,1)S(1)}, bf16[32,3072]{1,0:T(8,128)(2,1)S(1)}, u32[]{:S(2)}, u32[]{:S(2)}) collective-permute-start(bf16[32,3072]{1,0:T(8,128)(2,1)S(1)} %get-tuple-element.34), channel_id=1, source_target_pairs={{0,4},{2,6},{4,0},{6,2},{1,5},{3,7},{5,1},{7,3},{8,12},{10,14},{12... | collective-permute-start | bytes 589832 | tf_op jit(solution)/shard_map/ppermute | solution.py:265
  79.3 11.7 %collective-permute-start.7 = (bf16[32,3072]{1,0:T(8,128)(2,1)S(1)}, bf16[32,3072]{1,0:T(8,128)(2,1)S(1)}, u32[]{:S(2)}, u32[]{:S(2)}) collective-permute-start(bf16[32,3072]{1,0:T(8,128)(2,1)S(1)} %get-tuple-element.35), channel_id=1, source_target_pairs={{0,2},{2,4},{4,6},{6,0},{1,3},{3,5},{5,7},{7,1},{8,10},{10,12},{12... | collective-permute-start | bytes 589832 | tf_op jit(solution)/shard_map/ppermute | solution.py:265
  79.7 11.3 %collective-permute-start.8 = (bf16[32,3072]{1,0:T(8,128)(2,1)S(1)}, bf16[32,3072]{1,0:T(8,128)(2,1)S(1)}, u32[]{:S(2)}, u32[]{:S(2)}) collective-permute-start(bf16[32,3072]{1,0:T(8,128)(2,1)S(1)} %get-tuple-element.36), channel_id=1, source_target_pairs={{0,6},{2,0},{4,2},{6,4},{1,7},{3,1},{5,3},{7,5},{8,14},{10,8},{12,... | collective-permute-start | bytes 589832 | tf_op jit(solution)/shard_map/ppermute | solution.py:265
  92.5 18.0 %all-to-all-start.3 = ((f32[32,16,128]{2,1,0:T(8,128)}), f32[32,16,128]{2,1,0:T(8,128)S(1)}, u32[]{:S(2)}, u32[]{:S(2)}) async-start(f32[32,16,128]{2,1,0:T(8,128)} %shard_map.116), calls=%async_computation.3 | async-start | bytes 524288 | tf_op jit(solution)/shard_map/all_to_all | solution.py:294

commit v4 on v3

--- a/solution.py
+++ b/solution.py
@@ -51,7 +51,25 @@
     return high, (x - high.astype(F32)).astype(BF)
 
 
-def prepare_kernel(offsets, gain, w_in, mod, tab, wc, rows):
+def prepare_kernel(
+    step, after, offsets, gain, w_in, mod_table, w_fin, w_qkv, w_out,
+    tab, wc, rows, w_in_out, w_fin_out, w_qkv_out, w_out_out,
+    offv, gainv, modv, sems,
+):
+    at = jnp.clip(step[0], 0, mod_table.shape[1] - 1)
+    block = pl.ds(pl.multiple_of(at // 8 * 8, 8), 8)
+    pairs = [
+        (offsets, offv),
+        (gain, gainv),
+        (w_in, w_in_out),
+        (mod_table.at[:, block, :], modv),
+        (w_qkv, w_qkv_out),
+        (w_out, w_out_out),
+        (w_fin, w_fin_out),
+    ]
+    copies = [pltpu.make_async_copy(a, b, sems.at[i]) for i, (a, b) in enumerate(pairs)]
+    for copy in copies:
+        copy.start()
     lane = lax.broadcasted_iota(jnp.int32, (1, HD), 1)
     pair = lane // 2
     by_row = jnp.zeros((1, HD), F32)
@@ -60,40 +78,58 @@
     for j in range(count):
         by_row = jnp.where(pair == HD // 2 - 2 * count + j, FREQ[j], by_row)
         by_col = jnp.where(pair == HD // 2 - count + j, FREQ[j], by_col)
+    copies[0].wait()
     index = lax.broadcasted_iota(jnp.int32, (1, S), 1)
-    row = (index // GRID_W + offsets[0:1, :]).astype(F32)
-    col = (index % GRID_W + offsets[1:2, :]).astype(F32)
+    row = (index // GRID_W + offv[0:1, :]).astype(F32)
+    col = (index % GRID_W + offv[1:2, :]).astype(F32)
     both = jnp.concatenate([row, col, jnp.zeros((6, S), F32)], axis=0).T
     angle = both[:, 0:1] * by_row + both[:, 1:2] * by_col
     cosine = jnp.cos(angle)
     sine = jnp.sin(angle) * jnp.where(lane % 2 == 0, -1.0, 1.0)
+    copies[1].wait()
     for k in range(2):
-        g = gain[k : k + 1, :]
+        g = gainv[k : k + 1, :]
         turned = swap_lanes(jnp.broadcast_to(g, (8, HD)))[0:1]
         tab[2 * k] = (cosine * g).reshape(8, ROWS, HD)
         tab[2 * k + 1] = (sine * turned).reshape(8, ROWS, HD)
-    w = w_in[...].astype(F32)
+    copies[2].wait()
+    w = w_in_out[...].astype(F32)
     w = w - jnp.sum(w, axis=-1, keepdims=True) * (1.0 / D)
     high, low = halves(w)
     wc[:C, :] = high
     wc[C:, :] = low
-    rows[0:1, :] = 1.0 + mod[1:2, :]
-    rows[1:2, :] = mod[0:1, :]
-    rows[2:3, :] = mod[2:3, :]
+    copies[3].wait()
+    chosen = lax.broadcasted_iota(jnp.int32, (8, D), 0) == at % 8
+
+    def pick(k):
+        return jnp.sum(jnp.where(chosen, modv[k], 0.0), axis=0, keepdims=True)
+
+    rows[0:1, :] = 1.0 + pick(1)
+    rows[1:2, :] = pick(0)
+    rows[2:3, :] = pick(2)
     rows[3:, :] = jnp.zeros((5, D), F32)
-
-
-def block_body(chunk_of, wait, cuts, tab, wc, rows, w_qkv, mine, send, zs, es, fs, qkv, qs):
+    for copy in copies[4:]:
+        copy.wait()
+
+
+PREPARE_SCRATCH = [
+    pltpu.VMEM((2, S), jnp.int32),
+    pltpu.VMEM((2, HD), F32),
+    pltpu.VMEM((3, 8, D), F32),
+    pltpu.SemaphoreType.DMA((7,)),
+]
+
+
+def block_body(chunk_of, tab, wc, rows, w_qkv, mine, send, zs, es, fs, qkv, qs):
     my_x, my_c = lax.axis_index("x"), lax.axis_index("c")
     order = [((my_x + r % 4) % 4) * 2 + (my_c + r // 4) % 2 for r in range(8)]
     for r in range(8):
-        piece = chunk_of(order[r])
+        piece = chunk_of(r, order[r])
         zs[32 * r : 32 * r + 16, :] = piece[:, :C]
         zs[32 * r + 16 : 32 * r + 32, :] = piece[:, C:]
     z = zs[...]
     twice = jnp.concatenate([z, z], axis=1)
     total = jnp.zeros((S, 128), F32)
-    wait("wc")
     for j in range(6):
         cut = slice(j * 512, j * 512 + 512)
         e = jnp.dot(twice, wc[:, cut], preferred_element_type=F32)
@@ -101,14 +137,10 @@
         e = e * e
         total += (e[:, :128] + e[:, 128:256]) + (e[:, 256:384] + e[:, 384:])
     scale = lax.rsqrt(jnp.sum(total, axis=-1, keepdims=True) * (1.0 / D) + EPS)
-    wait("rows")
     for j in range(6):
         cut = slice(j * 512, j * 512 + 512)
         fs[:, cut] = (es[:, cut] * scale * rows[0:1, cut] + rows[1:2, cut]).astype(BF)
-    for i, (low, high) in enumerate(cuts):
-        wait(i)
-        qkv[:, low:high] = jnp.dot(fs[...], w_qkv[:, low:high], preferred_element_type=F32)
-    wait("tab")
+    qkv[...] = jnp.dot(fs[...], w_qkv[...], preferred_element_type=F32)
     mean = jnp.full((2 * HD, HD), 1.0 / HD, BF)
 
     def table(k):
@@ -136,27 +168,24 @@
         send[:, head * HD : head * HD + HD] = out[S // 2 :]
 
 
-WHOLE = ((0, HL * QKV),)
-
-
-def no_wait(key):
-    return None
-
-
-def first_kernel(zg, *rest):
-    block_body(lambda i: zg[i], no_wait, WHOLE, *rest)
-
-
-def second_kernel(zg, parts, tab, wc, rows, w_qkv, mine, send, z_out, *scratch):
+def first_kernel(z0, z1, z2, z3, *rest):
+    z = (z0, z1, z2, z3)
+    block_body(lambda r, i: z[r % 4][r // 4], *rest)
+
+
+def second_kernel(
+    z0, z1, z2, z3, parts, tab, wc, rows, w_qkv, mine, send, z_out, *scratch
+):
+    z = (z0, z1, z2, z3)
     start = lax.axis_index("y") * NZ + lax.axis_index("z") == 0
 
-    def chunk_of(i):
+    def chunk_of(r, i):
         x, c = i // 2, i % 2
         total = (parts[0, x, c] + parts[1, x, c]) + (parts[2, x, c] + parts[3, x, c])
-        return jnp.where(start, zg[i].astype(F32), total).astype(BF)
-
-    z_out[...] = chunk_of(lax.axis_index("x") * 2 + lax.axis_index("c"))
-    block_body(chunk_of, no_wait, WHOLE, tab, wc, rows, w_qkv, mine, send, *scratch)
+        return jnp.where(start, z[r % 4][r // 4].astype(F32), total).astype(BF)
+
+    z_out[...] = chunk_of(0, lax.axis_index("x") * 2 + lax.axis_index("c"))
+    block_body(chunk_of, tab, wc, rows, w_qkv, mine, send, *scratch)
 
 
 BLOCK_SCRATCH = [
@@ -239,6 +268,18 @@
     return jax.ShapeDtypeStruct(dims, dtype)
 
 
+def kept(dims, dtype):
+    return pltpu.VMEM(dims, dtype)
+
+
+def far(x):
+    return pltpu.with_memory_space_constraint(x, pltpu.HBM)
+
+
+def to_right(x, k):
+    return lax.ppermute(x, "x", [(i, (i + k) % NX) for i in range(NX)])
+
+
 def swap_cores(x):
     return lax.ppermute(x, "c", [(0, 1), (1, 0)])
 
@@ -247,22 +288,28 @@
     guesses, step_ids, step_sizes, slide, offsets, mod_table, w_in, w_qkv, qk_gain, w_out, w_fin
 ):
     state = guesses[0]
-    w_peer = swap_cores(w_out)
     z = pack(state.astype(BF))
-    zg = lax.all_to_all(jnp.broadcast_to(z[None], (8, 16, 128)), ("x", "c"), 0, 0, tiled=True)
-    w_fin_rows = w_fin.T
-    mod = lax.dynamic_index_in_dim(mod_table, step_ids[0], 0, keepdims=False)
-    tab, wc, rows = call(
+    own = jnp.stack([z, swap_cores(z)])
+    w_peer = swap_cores(lax.optimization_barrier((w_out, own))[0])
+    zg = [own] + [to_right(own, NX - k) for k in range(1, NX)]
+    operands = (offsets.T, qk_gain, w_in, mod_table.transpose(1, 0, 2), w_fin.T, w_qkv, w_out)
+    tab, wc, rows, w_in, w_fin_rows, w_qkv, w_out = call(
         prepare_kernel,
-        [shape((4, 8, ROWS, HD), F32), shape((2 * C, D), BF), shape((8, D), F32)],
-        [VM] * 4,
+        [
+            kept((4, 8, ROWS, HD), F32),
+            kept((2 * C, D), BF),
+            kept((8, D), F32),
+            kept((C, D), BF),
+            kept((C, D), BF),
+            kept(w_qkv.shape, BF),
+            kept(w_out.shape, BF),
+        ],
+        [SM, VM] + [HB] * 7,
+        PREPARE_SCRATCH,
         limit=12,
-    )(offsets.T, qk_gain, w_in, mod)
+    )(step_ids, own, *[far(x) for x in operands])
     half = shape((S // 2, HL * HD), BF)
     row = shape((ROWS, D), BF)
-
-    def to_right(x, k):
-        return lax.ppermute(x, "x", [(i, (i + k) % NX) for i in range(NX)])
 
     def to_drift(mine, send, z, w_peer, copies):
         operands = (mine, swap_cores(send), w_out, w_peer)
@@ -272,9 +319,9 @@
             step_sizes, z, state, parts[0], *got, w_in, rows, w_fin_rows
         )
 
-    mine, send = call(
-        first_kernel, [half, half], [VM] * 5, BLOCK_SCRATCH, limit=16
-    )(zg, tab, wc, rows, w_qkv)
+    mine, send = call(first_kernel, [half, half], [VM] * 8, BLOCK_SCRATCH, limit=16)(
+        *zg, tab, wc, rows, w_qkv
+    )
     drift = to_drift(mine, send, z, w_peer, NZ * NC)
     got = lax.all_to_all(drift, ("z", "c"), 0, 0, tiled=True)
     parts = call(relay_kernel, shape((NY, NX, NC, 16, 128), F32), [VM])(
@@ -286,10 +333,10 @@
     mine, send, z = call(
         second_kernel,
         [half, half, shape((16, 128), BF)],
-        [VM] * 6,
+        [VM] * 9,
         BLOCK_SCRATCH,
         limit=16,
-    )(zg, parts, tab, wc, rows, w_qkv)
+    )(*zg, parts, tab, wc, rows, w_qkv)
     drift = to_drift(mine, send, z, w_peer, NY * NZ)
     got = lax.all_to_all(drift, ("y", "z"), 0, 0, tiled=True)
     return call(final_kernel, shape((1, ROWS, C), F32), [SM, VM])(slide, got)

time: 112 us -> 104 us (0.929)
  local copies, waits for them, and re-layouts: 7.89 us -> 0.01 us
  waiting for transfers between devices: 29.8 us -> 31.3 us
    unnamed x27 -> x2, local copies, waits for them, and re-layouts: 7.25 us -> 0.01 us
    all_to_all x1 -> x0, starting transfers between devices: 4.32 us -> none  [local(): lax.all_to_all(jnp.broadcast_to(z[None], (8, 16, 128)), ('x', 'c'), 0, 0,...]
    pallas_call x2, Pallas kernels: 5.1 us -> 1.65 us  [to_drift(): parts = call(out_kernel, [row] * NX, [VM] * 4, limit=16)(*operands)]
    ppermute x6 -> x9, starting transfers between devices: 10.5 us -> 13.9 us  [to_right(): return lax.ppermute(x, 'x', [(i, (i + k) % NX) for i in range(NX)])]
    pallas_call x3, Pallas kernels: 10.6 us -> 13.8 us  [the longest x1 4.91 us: local(): call(second_kernel, [half, half, shape((16, 128), BF)], [VM] * 9, BLOCK_S...]
    ppermute x6 -> x9, waiting for transfers between devices: 14.4 us -> 15.4 us  [to_right(): return lax.ppermute(x, 'x', [(i, (i + k) % NX) for i in range(NX)])]
    ppermute x3 -> x4, waiting for transfers between devices: 2.58 us -> 3.65 us  [swap_cores(): return lax.ppermute(x, 'c', [(0, 1), (1, 0)])]
  transfers between devices with their start and end apart: 11 -> 14, of which waited for: 8 -> 8; matrix products, arithmetic and copies ran while one was open for 1% -> 0% of each run, Pallas kernels for 5% -> 9%
where the time goes in v4:
time: 104 us
  blocking collectives  31.5 us (30%)
  waiting for transfers between devices  31.3 us (30%)
  starting transfers between devices  19.4 us (19%)
  Pallas kernels  18.4 us (18%)
  between operations  2.08 us (2%)
    all_to_all x1, blocking collectives, local(): lax.all_to_all(parts.reshape(NY * NX, NC, 16, 128), ('y', 'x'), 0, 0, til...  15.7 us
    all_to_all x1, blocking collectives, local(): got = lax.all_to_all(drift, ('z', 'c'), 0, 0, tiled=True)  15.7 us
    ppermute x9, waiting for transfers between devices, to_right(): return lax.ppermute(x, 'x', [(i, (i + k) % NX) for i in range(NX)])  15.4 us
    ppermute x9, starting transfers between devices, to_right(): return lax.ppermute(x, 'x', [(i, (i + k) % NX) for i in range(NX)])  13.9 us
    all_to_all x1, waiting for transfers between devices, local(): got = lax.all_to_all(drift, ('y', 'z'), 0, 0, tiled=True)  12.2 us
    all_to_all x1, starting transfers between devices, local(): got = lax.all_to_all(drift, ('y', 'z'), 0, 0, tiled=True)  5.19 us
    pallas_call x1, Pallas kernels, local(): call(second_kernel, [half, half, shape((16, 128), BF)], [VM] * 9, BLOCK_S...  4.91 us
    pallas_call x1, Pallas kernels, local(): call(first_kernel, [half, half], [VM] * 8, BLOCK_SCRATCH, limit=16)  4.9 us
  transfers between devices with their start and end apart: 14, of which 8 were waited for; matrix products, arithmetic and copies ran while one was open for 0% of the time, Pallas kernels for 9%

profile of v4, /device:TPU:32, one launch (start us, length us, event | category | flops | bytes accessed | tf_op | source)
XLA Modules:
  0.0 103.6 jit_solution(13767040989146853862)
XLA Ops:
  0.0 0.7 bitcast_convert_fusion
  0.7 0.1 pad_maximum_fusion.1.z
  0.8 0.0 collective-permute-start
  0.8 0.1 fusion.1
  0.9 1.1 %collective-permute-done = bf16[16,128]{1,0:T(8,128)(2,1)S(1)} collective-permute-done((bf16[16,128]{1,0:T(8,128)(2,1)S(1)}, bf16[16,128]{1,0:T(8,128)(2,1)S(1)}, u32[]{:S(2)}, u32[]{:S(2)}) %collective-permute-start) | collective-permute-done | bytes 4128 | tf_op jit(solution)/shard_map/ppermute | solution.py:284
  2.0 0.2 collective-permute-start.5
  2.2 2.8 %collective-permute-start.1 = (bf16[2,16,128]{2,1,0:T(8,128)(2,1)S(1)}, bf16[2,16,128]{2,1,0:T(8,128)(2,1)S(1)}, u32[]{:S(2)}, u32[]{:S(2)}) collective-permute-start(bf16[2,16,128]{2,1,0:T(8,128)(2,1)S(1)} %pad_maximum_fusion.after.z0), channel_id=1, source_target_pairs={{0,6},{2,0},{4,2},{6,4},{1,7},{3,1},{5,3},{7,5},{8,14},{10,8},{12,... | collective-permute-start | bytes 24584 | tf_op jit(solution)/shard_map/ppermute | solution.py:280
  4.9 0.8 collective-permute-start.2
  5.7 0.9 collective-permute-start.3
  7.3 4.0 %shard_map.109 = (f32[4,8,32,128]{3,2,1,0:T(8,128)S(1)}, bf16[128,3072]{1,0:T(8,128)(2,1)S(1)}, f32[8,3072]{1,0:T(8,128)S(1)}, bf16[64,3072]{1,0:T(8,128)(2,1)S(...) custom-call(s32[1]{0:T(128)S(6)} %copy.12.step, ...), custom_call_target="tpu_custom_call" | custom-call | tf_op jit(solution)/shard_map/pallas_call | solution.py:296
  11.3 0.0 collective-permute-done.1.z1
  11.3 0.0 collective-permute-done.2.z2
  11.3 0.0 collective-permute-done.3.z3
  11.3 4.9 %shard_map.110 = (bf16[128,384]{1,0:T(8,128)(2,1)S(1)}, bf16[128,384]{1,0:T(8,128)(2,1)S(1)}) custom-call(bf16[2,16,128]{2,1,0:T(8,128)(2,1)S(1)} %pad_maximum_fusion.after.z0, bf16[2,16,128]{2,1,0:T(8,128)(2,1)S(1)} %collective-permute-done.1.z1, bf16[2,16,128]{2,1,0:T(8,128)(2,1)S(1)} %collective-permute-done.2.z2, ...), custom_call_target="tpu_custom_call" | custom-call | tf_op jit(solution)/shard_map/pallas_call | solution.py:322
  16.2 0.1 collective-permute-start.4
  16.3 1.3 %collective-permute-done.4.peer = bf16[128,384]{1,0:T(8,128)(2,1)S(1)} collective-permute-done((bf16[128,384]{1,0:T(8,128)(2,1)S(1)}, bf16[128,384]{1,0:T(8,128)(2,1)S(1)}, u32[]{:S(2)}, u32[]{:S(2)}) %collective-permute-start.4) | collective-permute-done | bytes 98336 | tf_op jit(solution)/shard_map/ppermute | solution.py:284
  17.6 0.0 collective-permute-done.5.w_peer
  17.6 0.0 copy-start
  17.6 0.8 shard_map.111
  18.4 1.9 %collective-permute-start.6 = (bf16[32,3072]{1,0:T(8,128)(2,1)S(1)}, bf16[32,3072]{1,0:T(8,128)(2,1)S(1)}, u32[]{:S(2)}, u32[]{:S(2)}) collective-permute-start(bf16[32,3072]{1,0:T(8,128)(2,1)S(1)} %get-tuple-element.35), channel_id=1, source_target_pairs={{0,4},{2,6},{4,0},{6,2},{1,5},{3,7},{5,1},{7,3},{8,12},{10,14},{12... | collective-permute-start | bytes 589832 | tf_op jit(solution)/shard_map/ppermute | solution.py:280
  20.4 1.4 %collective-permute-start.7 = (bf16[32,3072]{1,0:T(8,128)(2,1)S(1)}, bf16[32,3072]{1,0:T(8,128)(2,1)S(1)}, u32[]{:S(2)}, u32[]{:S(2)}) collective-permute-start(bf16[32,3072]{1,0:T(8,128)(2,1)S(1)} %get-tuple-element.36), channel_id=1, source_target_pairs={{0,2},{2,4},{4,6},{6,0},{1,3},{3,5},{5,7},{7,1},{8,10},{10,12},{12... | collective-permute-start | bytes 589832 | tf_op jit(solution)/shard_map/ppermute | solution.py:280
  21.7 1.9 %collective-permute-start.8 = (bf16[32,3072]{1,0:T(8,128)(2,1)S(1)}, bf16[32,3072]{1,0:T(8,128)(2,1)S(1)}, u32[]{:S(2)}, u32[]{:S(2)}) collective-permute-start(bf16[32,3072]{1,0:T(8,128)(2,1)S(1)} %get-tuple-element.37), channel_id=1, source_target_pairs={{0,6},{2,0},{4,2},{6,4},{1,7},{3,1},{5,3},{7,5},{8,14},{10,8},{12,... | collective-permute-start | bytes 589832 | tf_op jit(solution)/shard_map/ppermute | solution.py:280
  24.3 3.6 %collective-permute-done.6.p1 = bf16[32,3072]{1,0:T(8,128)(2,1)S(1)} collective-permute-done((bf16[32,3072]{1,0:T(8,128)(2,1)S(1)}, bf16[32,3072]{1,0:T(8,128)(2,1)S(1)}, u32[]{:S(2)}, u32[]{:S(2)}) %collective-permute-start.6) | collective-permute-done | bytes 196640 | tf_op jit(solution)/shard_map/ppermute | solution.py:280
  27.8 3.4 %collective-permute-done.7.p2 = bf16[32,3072]{1,0:T(8,128)(2,1)S(1)} collective-permute-done((bf16[32,3072]{1,0:T(8,128)(2,1)S(1)}, bf16[32,3072]{1,0:T(8,128)(2,1)S(1)}, u32[]{:S(2)}, u32[]{:S(2)}) %collective-permute-start.7) | collective-permute-done | bytes 196640 | tf_op jit(solution)/shard_map/ppermute | solution.py:280
  31.2 0.0 collective-permute-done.8.p3
  31.2 0.0 copy-done
  31.2 0.7 shard_map.112
  32.0 15.7 %all_to_all.15 = f32[16,16,128]{2,1,0:T(8,128)S(1)} all-to-all(f32[16,16,128]{2,1,0:T(8,128)S(1)} %shard_map.112), channel_id=1, replica_groups=mesh['y'=4,'z'=8,'x'=4,'c'=2] {'z','c'}, dimensions={0} | all-to-all | bytes 262144 | tf_op jit(solution)/shard_map/all_to_all | solution.py:326
  47.7 0.1 shard_map.113
  47.8 15.7 %all_to_all.16 = f32[16,2,16,128]{3,2,1,0:T(8,128)S(1)} all-to-all(f32[16,2,16,128]{3,2,1,0:T(8,128)S(1)} %bitcast.12), channel_id=1, replica_groups=mesh['y'=4,'z'=8,'x'=4,'c'=2] {'y','x'}, dimensions={0} | all-to-all | bytes 524288 | tf_op jit(solution)/shard_map/all_to_all | solution.py:330
  63.5 4.9 %shard_map.114 = (bf16[128,384]{1,0:T(8,128)(2,1)S(1)}, bf16[128,384]{1,0:T(8,128)(2,1)S(1)}, bf16[16,128]{1,0:T(8,128)(2,1)S(1)}) custom-call(bf16[2,16,128]{2,1,0:T(8,128)(2,1)S(1)} %pad_maximum_fusion.after.z0, bf16[2,16,128]{2,1,0:T(8,128)(2,1)S(1)} %collective-permute-done.1.z1, bf16[2,16,128]{2,1,0:T(8,128)(2,1)S(1)} %collective-permute-done.2.z2, ...), custom_call_target="tpu_custom_call" | custom-call | tf_op jit(solution)/shard_map/pallas_call | solution.py:333
  68.4 0.1 collective-permute-start.9
  68.5 1.3 %collective-permute-done.9.peer = bf16[128,384]{1,0:T(8,128)(2,1)S(1)} collective-permute-done((bf16[128,384]{1,0:T(8,128)(2,1)S(1)}, bf16[128,384]{1,0:T(8,128)(2,1)S(1)}, u32[]{:S(2)}, u32[]{:S(2)}) %collective-permute-start.9) | collective-permute-done | bytes 98336 | tf_op jit(solution)/shard_map/ppermute | solution.py:284
  69.8 0.8 shard_map.115
  70.6 1.0 collective-permute-start.10
  71.7 0.5 collective-permute-start.11
  72.1 2.8 %collective-permute-start.12 = (bf16[32,3072]{1,0:T(8,128)(2,1)S(1)}, bf16[32,3072]{1,0:T(8,128)(2,1)S(1)}, u32[]{:S(2)}, u32[]{:S(2)}) collective-permute-start(bf16[32,3072]{1,0:T(8,128)(2,1)S(1)} %get-tuple-element.46), channel_id=1, source_target_pairs={{0,6},{2,0},{4,2},{6,4},{1,7},{3,1},{5,3},{7,5},{8,14},{10,8},{12,... | collective-permute-start | bytes 589832 | tf_op jit(solution)/shard_map/ppermute | solution.py:280
  74.9 5.1 %collective-permute-done.10.p1 = bf16[32,3072]{1,0:T(8,128)(2,1)S(1)} collective-permute-done((bf16[32,3072]{1,0:T(8,128)(2,1)S(1)}, bf16[32,3072]{1,0:T(8,128)(2,1)S(1)}, u32[]{:S(2)}, u32[]{:S(2)}) %collective-permute-start.10) | collective-permute-done | bytes 196640 | tf_op jit(solution)/shard_map/ppermute | solution.py:280
  80.0 3.4 %collective-permute-done.11.p2 = bf16[32,3072]{1,0:T(8,128)(2,1)S(1)} collective-permute-done((bf16[32,3072]{1,0:T(8,128)(2,1)S(1)}, bf16[32,3072]{1,0:T(8,128)(2,1)S(1)}, u32[]{:S(2)}, u32[]{:S(2)}) %collective-permute-start.11) | collective-permute-done | bytes 196640 | tf_op jit(solution)/shard_map/ppermute | solution.py:280
  83.4 0.0 collective-permute-done.12.p3
  83.4 1.4 %shard_map.116 = f32[32,16,128]{2,1,0:T(8,128)} custom-call(f32[1]{0:T(128)S(6)} %copy.13.size, bf16[16,128]{1,0:T(8,128)(2,1)S(1)} %get-tuple-element.40.z, f32[32,64]{1,0:T(8,128)S(1)} %bitcast.15, bf16[32,3072]{1,0:T(8,128)(2,1)S(1)} %get-tuple-element.43.p0, bf16[32,3072]{1,0:T(8,128)(2,1)S(1)} %collective-permute-done.10.p1, ...), custom_call_target="tpu_custom_call" | custom-call | tf_op jit(solution)/shard_map/pallas_call | solution.py:318
  84.8 5.2 %all-to-all-start.2 = ((f32[32,16,128]{2,1,0:T(8,128)}), f32[32,16,128]{2,1,0:T(8,128)S(1)}, u32[]{:S(2)}, u32[]{:S(2)}) async-start(f32[32,16,128]{2,1,0:T(8,128)} %shard_map.116), calls=%async_computation.2 | async-start | bytes 524288 | tf_op jit(solution)/shard_map/all_to_all | solution.py:341
  90.7 12.2 %all-to-all-done.2.got = f32[32,16,128]{2,1,0:T(8,128)S(1)} async-done(((f32[32,16,128]{2,1,0:T(8,128)}), f32[32,16,128]{2,1,0:T(8,128)S(1)}, u32[]{:S(2)}, u32[]{:S(2)}) %all-to-all-start.2) | async-done | bytes 262176 | tf_op jit(solution)/shard_map/all_to_all | solution.py:341
  102.9 0.7 shard_map.117
  (2 shorter events, 0.0 us)
Async XLA Ops:
  0.8 1.2 %collective-permute-start = (bf16[16,128]{1,0:T(8,128)(2,1)S(1)}, bf16[16,128]{1,0:T(8,128)(2,1)S(1)}, u32[]{:S(2)}, u32[]{:S(2)}) collective-permute-start(bf16[16,128]{1,0:T(8,128)(2,1)S(1)} %pad_maximum_fusion.1.z), channel_id=1, source_target_pairs={{0,1},{1,0},{2,3},{3,2},{4,5},{5,4},{6,7},{7,6},{8,9},{9,8},{10,11... | collective-permute-start | bytes 12296 | tf_op jit(solution)/shard_map/ppermute | solution.py:284
  2.0 15.6 %collective-permute-start.5 = (bf16[384,3072]{1,0:T(8,128)(2,1)}, bf16[384,3072]{1,0:T(8,128)(2,1)S(1)}, u32[]{:S(2)}, u32[]{:S(2)}) collective-permute-start(bf16[384,3072]{1,0:T(8,128)(2,1)} %w_out.1), channel_id=1, source_target_pairs={{0,1},{1,0},{2,3},{3,2},{4,5},{5,4},{6,7},{7,6},{8,9},{9,8},{10,11... | collective-permute-start | bytes 7077896 | tf_op jit(solution)/shard_map/ppermute | solution.py:284
  2.2 9.1 %collective-permute-start.1 = (bf16[2,16,128]{2,1,0:T(8,128)(2,1)S(1)}, bf16[2,16,128]{2,1,0:T(8,128)(2,1)S(1)}, u32[]{:S(2)}, u32[]{:S(2)}) collective-permute-start(bf16[2,16,128]{2,1,0:T(8,128)(2,1)S(1)} %pad_maximum_fusion.after.z0), channel_id=1, source_target_pairs={{0,6},{2,0},{4,2},{6,4},{1,7},{3,1},{5,3},{7,5},{8,14},{10,8},{12,... | collective-permute-start | bytes 24584 | tf_op jit(solution)/shard_map/ppermute | solution.py:280
  4.9 6.4 %collective-permute-start.2 = (bf16[2,16,128]{2,1,0:T(8,128)(2,1)S(1)}, bf16[2,16,128]{2,1,0:T(8,128)(2,1)S(1)}, u32[]{:S(2)}, u32[]{:S(2)}) collective-permute-start(bf16[2,16,128]{2,1,0:T(8,128)(2,1)S(1)} %pad_maximum_fusion.after.z0), channel_id=1, source_target_pairs={{0,4},{2,6},{4,0},{6,2},{1,5},{3,7},{5,1},{7,3},{8,12},{10,14},{12... | collective-permute-start | bytes 24584 | tf_op jit(solution)/shard_map/ppermute | solution.py:280
  5.7 5.6 %collective-permute-start.3 = (bf16[2,16,128]{2,1,0:T(8,128)(2,1)S(1)}, bf16[2,16,128]{2,1,0:T(8,128)(2,1)S(1)}, u32[]{:S(2)}, u32[]{:S(2)}) collective-permute-start(bf16[2,16,128]{2,1,0:T(8,128)(2,1)S(1)} %pad_maximum_fusion.after.z0), channel_id=1, source_target_pairs={{0,2},{2,4},{4,6},{6,0},{1,3},{3,5},{5,7},{7,1},{8,10},{10,12},{12... | collective-permute-start | bytes 24584 | tf_op jit(solution)/shard_map/ppermute | solution.py:280
  16.2 1.4 %collective-permute-start.4 = (bf16[128,384]{1,0:T(8,128)(2,1)S(1)}, bf16[128,384]{1,0:T(8,128)(2,1)S(1)}, u32[]{:S(2)}, u32[]{:S(2)}) collective-permute-start(bf16[128,384]{1,0:T(8,128)(2,1)S(1)} %get-tuple-element.31), channel_id=1, source_target_pairs={{0,1},{1,0},{2,3},{3,2},{4,5},{5,4},{6,7},{7,6},{8,9},{9,8},{10,11... | collective-permute-start | bytes 294920 | tf_op jit(solution)/shard_map/ppermute | solution.py:284
  17.6 13.6 %copy-start = (f32[1,32,64]{2,1,0:T(8,128)S(1)}, f32[1,32,64]{2,1,0:T(8,128)}, u32[]{:S(2)}) copy-start(f32[1,32,64]{2,1,0:T(8,128)} %param.11) | copy-start | bytes 24580
  18.4 9.4 %collective-permute-start.6 = (bf16[32,3072]{1,0:T(8,128)(2,1)S(1)}, bf16[32,3072]{1,0:T(8,128)(2,1)S(1)}, u32[]{:S(2)}, u32[]{:S(2)}) collective-permute-start(bf16[32,3072]{1,0:T(8,128)(2,1)S(1)} %get-tuple-element.35), channel_id=1, source_target_pairs={{0,4},{2,6},{4,0},{6,2},{1,5},{3,7},{5,1},{7,3},{8,12},{10,14},{12... | collective-permute-start | bytes 589832 | tf_op jit(solution)/shard_map/ppermute | solution.py:280
  20.4 10.8 %collective-permute-start.7 = (bf16[32,3072]{1,0:T(8,128)(2,1)S(1)}, bf16[32,3072]{1,0:T(8,128)(2,1)S(1)}, u32[]{:S(2)}, u32[]{:S(2)}) collective-permute-start(bf16[32,3072]{1,0:T(8,128)(2,1)S(1)} %get-tuple-element.36), channel_id=1, source_target_pairs={{0,2},{2,4},{4,6},{6,0},{1,3},{3,5},{5,7},{7,1},{8,10},{10,12},{12... | collective-permute-start | bytes 589832 | tf_op jit(solution)/shard_map/ppermute | solution.py:280
  21.7 9.5 %collective-permute-start.8 = (bf16[32,3072]{1,0:T(8,128)(2,1)S(1)}, bf16[32,3072]{1,0:T(8,128)(2,1)S(1)}, u32[]{:S(2)}, u32[]{:S(2)}) collective-permute-start(bf16[32,3072]{1,0:T(8,128)(2,1)S(1)} %get-tuple-element.37), channel_id=1, source_target_pairs={{0,6},{2,0},{4,2},{6,4},{1,7},{3,1},{5,3},{7,5},{8,14},{10,8},{12,... | collective-permute-start | bytes 589832 | tf_op jit(solution)/shard_map/ppermute | solution.py:280
  68.4 1.4 %collective-permute-start.9 = (bf16[128,384]{1,0:T(8,128)(2,1)S(1)}, bf16[128,384]{1,0:T(8,128)(2,1)S(1)}, u32[]{:S(2)}, u32[]{:S(2)}) collective-permute-start(bf16[128,384]{1,0:T(8,128)(2,1)S(1)} %get-tuple-element.42), channel_id=1, source_target_pairs={{0,1},{1,0},{2,3},{3,2},{4,5},{5,4},{6,7},{7,6},{8,9},{9,8},{10,11... | collective-permute-start | bytes 294920 | tf_op jit(solution)/shard_map/ppermute | solution.py:284
  70.6 9.4 %collective-permute-start.10 = (bf16[32,3072]{1,0:T(8,128)(2,1)S(1)}, bf16[32,3072]{1,0:T(8,128)(2,1)S(1)}, u32[]{:S(2)}, u32[]{:S(2)}) collective-permute-start(bf16[32,3072]{1,0:T(8,128)(2,1)S(1)} %get-tuple-element.44), channel_id=1, source_target_pairs={{0,4},{2,6},{4,0},{6,2},{1,5},{3,7},{5,1},{7,3},{8,12},{10,14},{12... | collective-permute-start | bytes 589832 | tf_op jit(solution)/shard_map/ppermute | solution.py:280
  71.7 11.7 %collective-permute-start.11 = (bf16[32,3072]{1,0:T(8,128)(2,1)S(1)}, bf16[32,3072]{1,0:T(8,128)(2,1)S(1)}, u32[]{:S(2)}, u32[]{:S(2)}) collective-permute-start(bf16[32,3072]{1,0:T(8,128)(2,1)S(1)} %get-tuple-element.45), channel_id=1, source_target_pairs={{0,2},{2,4},{4,6},{6,0},{1,3},{3,5},{5,7},{7,1},{8,10},{10,12},{12... | collective-permute-start | bytes 589832 | tf_op jit(solution)/shard_map/ppermute | solution.py:280
  72.1 11.2 %collective-permute-start.12 = (bf16[32,3072]{1,0:T(8,128)(2,1)S(1)}, bf16[32,3072]{1,0:T(8,128)(2,1)S(1)}, u32[]{:S(2)}, u32[]{:S(2)}) collective-permute-start(bf16[32,3072]{1,0:T(8,128)(2,1)S(1)} %get-tuple-element.46), channel_id=1, source_target_pairs={{0,6},{2,0},{4,2},{6,4},{1,7},{3,1},{5,3},{7,5},{8,14},{10,8},{12,... | collective-permute-start | bytes 589832 | tf_op jit(solution)/shard_map/ppermute | solution.py:280
  84.8 18.1 %all-to-all-start.2 = ((f32[32,16,128]{2,1,0:T(8,128)}), f32[32,16,128]{2,1,0:T(8,128)S(1)}, u32[]{:S(2)}, u32[]{:S(2)}) async-start(f32[32,16,128]{2,1,0:T(8,128)} %shard_map.116), calls=%async_computation.2 | async-start | bytes 524288 | tf_op jit(solution)/shard_map/all_to_all | solution.py:341

commit v5 on v4

--- a/solution.py
+++ b/solution.py
@@ -177,11 +177,12 @@
     z0, z1, z2, z3, parts, tab, wc, rows, w_qkv, mine, send, z_out, *scratch
 ):
     z = (z0, z1, z2, z3)
-    start = lax.axis_index("y") * NZ + lax.axis_index("z") == 0
+    start = position() == 0
 
     def chunk_of(r, i):
         x, c = i // 2, i % 2
-        total = (parts[0, x, c] + parts[1, x, c]) + (parts[2, x, c] + parts[3, x, c])
+        part = [parts[k, x, c].astype(F32) for k in range(NY)]
+        total = (part[0] + part[1]) + (part[2] + part[3])
         return jnp.where(start, z[r % 4][r // 4].astype(F32), total).astype(BF)
 
     z_out[...] = chunk_of(0, lax.axis_index("x") * 2 + lax.axis_index("c"))
@@ -214,7 +215,7 @@
             outs[k][:, cut] = part[ROWS * k : ROWS * (k + 1)]
 
 
-def drift_kernel(size, z, zstart, p0, p1, p2, p3, w_in, gate, w_fin, out):
+def drift(size, z, p0, p1, p2, p3, w_in, gate, w_fin):
     e = jnp.dot(unpack(z[...]), w_in[...], preferred_element_type=F32)
     attn = p0[...].astype(F32) + p1[...].astype(F32) + p2[...].astype(F32) + p3[...].astype(F32)
     h = e + gate[2:3, :] * attn
@@ -222,14 +223,33 @@
     h = h - mean
     var = jnp.sum(h * h, axis=-1, keepdims=True) * (1.0 / D)
     normed = (h * lax.rsqrt(var + EPS)).astype(BF)
-    drift = size[0] * lax.dot_general(
+    return size[0] * lax.dot_general(
         normed, w_fin[...], (((1,), (1,)), ((), ())), preferred_element_type=F32
     )
-    start = lax.axis_index("y") * NZ + lax.axis_index("z") == 0
-    drift = drift + jnp.where(start, zstart[...], jnp.zeros((ROWS, C), F32))
-    packed = pack(drift)
+
+
+def position():
+    return lax.axis_index("y") * NZ + lax.axis_index("z")
+
+
+def first_drift_kernel(zstart, *rest):
+    out, start = rest[-2:]
+    value = drift(*rest[:-2])
+    value = value + jnp.where(position() == 0, zstart[...], jnp.zeros((ROWS, C), F32))
+    packed = pack(value)
+    start[...] = packed
     for k in range(out.shape[0]):
-        out[k] = packed
+        out[k] = packed.astype(BF)
+
+
+def second_drift_kernel(start, first, *rest):
+    out = rest[-1]
+    low = first[...] - first[...].astype(BF).astype(F32)
+    here = position()
+    value = jnp.where(here == 0, start[...], pack(drift(*rest[:-1])))
+    value = jnp.where(here == NY * NZ - 1, low, value).astype(BF)
+    for k in range(out.shape[0]):
+        out[k] = value
 
 
 def relay_kernel(got, out):
@@ -238,17 +258,17 @@
         total = jnp.zeros((NC, 16, 128), F32)
         for s in range(NZ):
             keep = y * NZ + s < to * NZ + z
-            total = total + jnp.where(keep, got[s], jnp.zeros((NC, 16, 128), F32))
+            total = total + jnp.where(keep, got[s].astype(F32), jnp.zeros((NC, 16, 128), F32))
         for x in range(NX):
-            out[to, x] = total
+            out[to, x] = total.astype(out.dtype)
 
 
 def final_kernel(slide, got, out):
-    here = lax.axis_index("y") * NZ + lax.axis_index("z")
-    target = jnp.minimum(here + slide[0], NY * NZ - 1)
-    total = got[0]
-    for s in range(1, NY * NZ - 1):
-        total = total + jnp.where(s < target, got[s], jnp.zeros((16, 128), F32))
+    last = NY * NZ - 1
+    target = jnp.minimum(position() + slide[0], last)
+    total = got[0].astype(F32) + got[last].astype(F32)
+    for s in range(1, last):
+        total = total + jnp.where(s < target, got[s].astype(F32), jnp.zeros((16, 128), F32))
     out[0] = unpack(total)
 
 
@@ -311,20 +331,22 @@
     half = shape((S // 2, HL * HD), BF)
     row = shape((ROWS, D), BF)
 
-    def to_drift(mine, send, z, w_peer, copies):
+    def exchanged(mine, send):
         operands = (mine, swap_cores(send), w_out, w_peer)
         parts = call(out_kernel, [row] * NX, [VM] * 4, limit=16)(*operands)
-        got = [to_right(parts[k], k) for k in (2, 1, 3)]
-        return call(drift_kernel, shape((copies, 16, 128), F32), [SM] + [VM] * 9)(
-            step_sizes, z, state, parts[0], *got, w_in, rows, w_fin_rows
-        )
+        return [parts[0]] + [to_right(parts[k], k) for k in (2, 1, 3)]
 
     mine, send = call(first_kernel, [half, half], [VM] * 8, BLOCK_SCRATCH, limit=16)(
         *zg, tab, wc, rows, w_qkv
     )
-    drift = to_drift(mine, send, z, w_peer, NZ * NC)
-    got = lax.all_to_all(drift, ("z", "c"), 0, 0, tiled=True)
-    parts = call(relay_kernel, shape((NY, NX, NC, 16, 128), F32), [VM])(
+    outs, start = call(
+        first_drift_kernel,
+        [shape((NZ * NC, 16, 128), BF), shape((16, 128), F32)],
+        [VM, SM] + [VM] * 8,
+    )(state, step_sizes, z, *exchanged(mine, send), w_in, rows, w_fin_rows)
+    first = lax.ppermute(start, ("y", "z"), [(0, NY * NZ - 1)])
+    got = lax.all_to_all(outs, ("z", "c"), 0, 0, tiled=True)
+    parts = call(relay_kernel, shape((NY, NX, NC, 16, 128), BF), [VM])(
         got.reshape(NZ, NC, 16, 128)
     )
     parts = lax.all_to_all(
@@ -337,8 +359,12 @@
         BLOCK_SCRATCH,
         limit=16,
     )(*zg, parts, tab, wc, rows, w_qkv)
-    drift = to_drift(mine, send, z, w_peer, NY * NZ)
-    got = lax.all_to_all(drift, ("y", "z"), 0, 0, tiled=True)
+    outs = call(
+        second_drift_kernel,
+        shape((NY * NZ, 16, 128), BF),
+        [VM, VM, SM] + [VM] * 8,
+    )(start, first, step_sizes, z, *exchanged(mine, send), w_in, rows, w_fin_rows)
+    got = lax.all_to_all(outs, ("y", "z"), 0, 0, tiled=True)
     return call(final_kernel, shape((1, ROWS, C), F32), [SM, VM])(slide, got)
 
 

time: 104 us -> 98.9 us (0.951)
  waiting for transfers between devices: 31.3 us -> 27.8 us
  blocking collectives: 31.5 us -> 29.2 us
    all_to_all x1, waiting for transfers between devices: 12.2 us -> 9.63 us  [local(): got = lax.all_to_all(outs, ('y', 'z'), 0, 0, tiled=True)]
    all_to_all x1, blocking collectives: 15.7 us -> 14.2 us  [local(): lax.all_to_all(parts.reshape(NY * NX, NC, 16, 128), ('y', 'x'), 0, 0, til...]
  transfers between devices with their start and end apart: 14 -> 15, of which waited for: 8 -> 8; matrix products, arithmetic and copies ran while one was open for 0% -> 0% of each run, Pallas kernels for 9% -> 9%
where the time goes in v5:
time: 98.9 us; the launch traced here: 98.4 us
  blocking collectives  29.2 us (30%)
  waiting for transfers between devices  27.8 us (28%)
  starting transfers between devices  20.1 us (20%)
  Pallas kernels  18.3 us (19%)
  between operations  2.08 us (2%)
    all_to_all x1, blocking collectives, local(): got = lax.all_to_all(outs, ('z', 'c'), 0, 0, tiled=True)  14.9 us
    ppermute x9, waiting for transfers between devices, to_right(): return lax.ppermute(x, 'x', [(i, (i + k) % NX) for i in range(NX)])  14.5 us
    all_to_all x1, blocking collectives, local(): lax.all_to_all(parts.reshape(NY * NX, NC, 16, 128), ('y', 'x'), 0, 0, til...  14.2 us
    ppermute x9, starting transfers between devices, to_right(): return lax.ppermute(x, 'x', [(i, (i + k) % NX) for i in range(NX)])  14.1 us
    all_to_all x1, waiting for transfers between devices, local(): got = lax.all_to_all(outs, ('y', 'z'), 0, 0, tiled=True)  9.63 us
    all_to_all x1, starting transfers between devices, local(): got = lax.all_to_all(outs, ('y', 'z'), 0, 0, tiled=True)  4.95 us
    pallas_call x1, Pallas kernels, local(): call(first_kernel, [half, half], [VM] * 8, BLOCK_SCRATCH, limit=16)  4.9 us
    pallas_call x1, Pallas kernels, local(): call(second_kernel, [half, half, shape((16, 128), BF)], [VM] * 9, BLOCK_S...  4.9 us
  transfers between devices with their start and end apart: 15, of which 8 were waited for; matrix products, arithmetic and copies ran while one was open for 0% of the time, Pallas kernels for 9%

profile of v5, /device:TPU:32, one launch (start us, length us, event | category | flops | bytes accessed | tf_op | source)
XLA Modules:
  0.0 98.4 jit_solution(5488284014739975846)
XLA Ops:
  0.0 0.7 bitcast_convert_fusion
  0.7 0.1 pad_maximum_fusion.1.rest_1_
  0.8 0.0 collective-permute-start
  0.8 0.1 fusion.1
  0.9 1.1 %collective-permute-done = bf16[16,128]{1,0:T(8,128)(2,1)S(1)} collective-permute-done((bf16[16,128]{1,0:T(8,128)(2,1)S(1)}, bf16[16,128]{1,0:T(8,128)(2,1)S(1)}, u32[]{:S(2)}, u32[]{:S(2)}) %collective-permute-start) | collective-permute-done | bytes 4128 | tf_op jit(solution)/shard_map/ppermute | solution.py:304
  2.0 0.2 collective-permute-start.5
  2.2 2.8 %collective-permute-start.1 = (bf16[2,16,128]{2,1,0:T(8,128)(2,1)S(1)}, bf16[2,16,128]{2,1,0:T(8,128)(2,1)S(1)}, u32[]{:S(2)}, u32[]{:S(2)}) collective-permute-start(bf16[2,16,128]{2,1,0:T(8,128)(2,1)S(1)} %pad_maximum_fusion.after.z0), channel_id=1, source_target_pairs={{0,6},{2,0},{4,2},{6,4},{1,7},{3,1},{5,3},{7,5},{8,14},{10,8},{12,... | collective-permute-start | bytes 24584 | tf_op jit(solution)/shard_map/ppermute | solution.py:300
  4.9 0.8 collective-permute-start.2
  5.7 0.9 collective-permute-start.3
  7.3 4.0 %shard_map.109 = (f32[4,8,32,128]{3,2,1,0:T(8,128)S(1)}, bf16[128,3072]{1,0:T(8,128)(2,1)S(1)}, f32[8,3072]{1,0:T(8,128)S(1)}, bf16[64,3072]{1,0:T(8,128)(2,1)S(...) custom-call(s32[1]{0:T(128)S(6)} %copy.12.step, ...), custom_call_target="tpu_custom_call" | custom-call | tf_op jit(solution)/shard_map/pallas_call | solution.py:316
  11.3 0.0 collective-permute-done.1.z1
  11.3 0.0 collective-permute-done.2.z2
  11.3 0.0 collective-permute-done.3.z3
  11.3 4.9 %shard_map.110 = (bf16[128,384]{1,0:T(8,128)(2,1)S(1)}, bf16[128,384]{1,0:T(8,128)(2,1)S(1)}) custom-call(bf16[2,16,128]{2,1,0:T(8,128)(2,1)S(1)} %pad_maximum_fusion.after.z0, bf16[2,16,128]{2,1,0:T(8,128)(2,1)S(1)} %collective-permute-done.1.z1, bf16[2,16,128]{2,1,0:T(8,128)(2,1)S(1)} %collective-permute-done.2.z2, ...), custom_call_target="tpu_custom_call" | custom-call | tf_op jit(solution)/shard_map/pallas_call | solution.py:339
  16.2 0.1 collective-permute-start.4
  16.3 1.3 %collective-permute-done.4.peer = bf16[128,384]{1,0:T(8,128)(2,1)S(1)} collective-permute-done((bf16[128,384]{1,0:T(8,128)(2,1)S(1)}, bf16[128,384]{1,0:T(8,128)(2,1)S(1)}, u32[]{:S(2)}, u32[]{:S(2)}) %collective-permute-start.4) | collective-permute-done | bytes 98336 | tf_op jit(solution)/shard_map/ppermute | solution.py:304
  17.6 0.0 collective-permute-done.5.w_peer
  17.6 0.0 copy-start
  17.6 0.8 shard_map.111
  18.4 1.9 %collective-permute-start.6 = (bf16[32,3072]{1,0:T(8,128)(2,1)S(1)}, bf16[32,3072]{1,0:T(8,128)(2,1)S(1)}, u32[]{:S(2)}, u32[]{:S(2)}) collective-permute-start(bf16[32,3072]{1,0:T(8,128)(2,1)S(1)} %get-tuple-element.37), channel_id=1, source_target_pairs={{0,4},{2,6},{4,0},{6,2},{1,5},{3,7},{5,1},{7,3},{8,12},{10,14},{12... | collective-permute-start | bytes 589832 | tf_op jit(solution)/shard_map/ppermute | solution.py:300
  20.4 1.4 %collective-permute-start.7 = (bf16[32,3072]{1,0:T(8,128)(2,1)S(1)}, bf16[32,3072]{1,0:T(8,128)(2,1)S(1)}, u32[]{:S(2)}, u32[]{:S(2)}) collective-permute-start(bf16[32,3072]{1,0:T(8,128)(2,1)S(1)} %get-tuple-element.38), channel_id=1, source_target_pairs={{0,2},{2,4},{4,6},{6,0},{1,3},{3,5},{5,7},{7,1},{8,10},{10,12},{12... | collective-permute-start | bytes 589832 | tf_op jit(solution)/shard_map/ppermute | solution.py:300
  21.7 1.9 %collective-permute-start.8 = (bf16[32,3072]{1,0:T(8,128)(2,1)S(1)}, bf16[32,3072]{1,0:T(8,128)(2,1)S(1)}, u32[]{:S(2)}, u32[]{:S(2)}) collective-permute-start(bf16[32,3072]{1,0:T(8,128)(2,1)S(1)} %get-tuple-element.39), channel_id=1, source_target_pairs={{0,6},{2,0},{4,2},{6,4},{1,7},{3,1},{5,3},{7,5},{8,14},{10,8},{12,... | collective-permute-start | bytes 589832 | tf_op jit(solution)/shard_map/ppermute | solution.py:300
  24.3 3.6 %collective-permute-done.6.rest_3_ = bf16[32,3072]{1,0:T(8,128)(2,1)S(1)} collective-permute-done((bf16[32,3072]{1,0:T(8,128)(2,1)S(1)}, bf16[32,3072]{1,0:T(8,128)(2,1)S(1)}, u32[]{:S(2)}, u32[]{:S(2)}) %collective-permute-start.6) | collective-permute-done | bytes 196640 | tf_op jit(solution)/shard_map/ppermute | solution.py:300
  27.8 3.4 %collective-permute-done.7.rest_4_ = bf16[32,3072]{1,0:T(8,128)(2,1)S(1)} collective-permute-done((bf16[32,3072]{1,0:T(8,128)(2,1)S(1)}, bf16[32,3072]{1,0:T(8,128)(2,1)S(1)}, u32[]{:S(2)}, u32[]{:S(2)}) %collective-permute-start.7) | collective-permute-done | bytes 196640 | tf_op jit(solution)/shard_map/ppermute | solution.py:300
  31.2 0.0 collective-permute-done.8.rest_5_
  31.2 0.0 copy-done
  31.2 0.7 shard_map.112
  31.9 14.9 %all_to_all.15 = bf16[16,16,128]{2,1,0:T(8,128)(2,1)S(1)} all-to-all(bf16[16,16,128]{2,1,0:T(8,128)(2,1)S(1)} %get-tuple-element.43), channel_id=1, replica_groups=mesh['y'=4,'z'=8,'x'=4,'c'=2] {'z','c'}, dimensions={0} | all-to-all | bytes 131072 | tf_op jit(solution)/shard_map/all_to_all | solution.py:348
  46.9 0.1 shard_map.113
  46.9 14.2 %all_to_all.16 = bf16[16,2,16,128]{3,2,1,0:T(8,128)(2,1)S(1)} all-to-all(bf16[16,2,16,128]{3,2,1,0:T(8,128)(2,1)S(1)} %bitcast.12), channel_id=1, replica_groups=mesh['y'=4,'z'=8,'x'=4,'c'=2] {'y','x'}, dimensions={0} | all-to-all | bytes 262144 | tf_op jit(solution)/shard_map/all_to_all | solution.py:352
  61.2 4.9 %shard_map.114 = (bf16[128,384]{1,0:T(8,128)(2,1)S(1)}, bf16[128,384]{1,0:T(8,128)(2,1)S(1)}, bf16[16,128]{1,0:T(8,128)(2,1)S(1)}) custom-call(bf16[2,16,128]{2,1,0:T(8,128)(2,1)S(1)} %pad_maximum_fusion.after.z0, bf16[2,16,128]{2,1,0:T(8,128)(2,1)S(1)} %collective-permute-done.1.z1, bf16[2,16,128]{2,1,0:T(8,128)(2,1)S(1)} %collective-permute-done.2.z2, ...), custom_call_target="tpu_custom_call" | custom-call | tf_op jit(solution)/shard_map/pallas_call | solution.py:355
  66.1 0.1 collective-permute-start.10
  66.2 1.3 %collective-permute-done.10.peer = bf16[128,384]{1,0:T(8,128)(2,1)S(1)} collective-permute-done((bf16[128,384]{1,0:T(8,128)(2,1)S(1)}, bf16[128,384]{1,0:T(8,128)(2,1)S(1)}, u32[]{:S(2)}, u32[]{:S(2)}) %collective-permute-start.10) | collective-permute-done | bytes 98336 | tf_op jit(solution)/shard_map/ppermute | solution.py:304
  67.5 0.8 shard_map.115
  68.3 1.3 %collective-permute-start.11 = (bf16[32,3072]{1,0:T(8,128)(2,1)S(1)}, bf16[32,3072]{1,0:T(8,128)(2,1)S(1)}, u32[]{:S(2)}, u32[]{:S(2)}) collective-permute-start(bf16[32,3072]{1,0:T(8,128)(2,1)S(1)} %get-tuple-element.48), channel_id=1, source_target_pairs={{0,4},{2,6},{4,0},{6,2},{1,5},{3,7},{5,1},{7,3},{8,12},{10,14},{12... | collective-permute-start | bytes 589832 | tf_op jit(solution)/shard_map/ppermute | solution.py:300
  69.6 0.6 collective-permute-start.12
  70.1 2.7 %collective-permute-start.13 = (bf16[32,3072]{1,0:T(8,128)(2,1)S(1)}, bf16[32,3072]{1,0:T(8,128)(2,1)S(1)}, u32[]{:S(2)}, u32[]{:S(2)}) collective-permute-start(bf16[32,3072]{1,0:T(8,128)(2,1)S(1)} %get-tuple-element.50), channel_id=1, source_target_pairs={{0,6},{2,0},{4,2},{6,4},{1,7},{3,1},{5,3},{7,5},{8,14},{10,8},{12,... | collective-permute-start | bytes 589832 | tf_op jit(solution)/shard_map/ppermute | solution.py:300
  72.8 0.6 collective-permute-start.9
  73.5 0.0 collective-permute-done.9.first
  73.5 4.2 %collective-permute-done.11.rest_3_ = bf16[32,3072]{1,0:T(8,128)(2,1)S(1)} collective-permute-done((bf16[32,3072]{1,0:T(8,128)(2,1)S(1)}, bf16[32,3072]{1,0:T(8,128)(2,1)S(1)}, u32[]{:S(2)}, u32[]{:S(2)}) %collective-permute-start.11) | collective-permute-done | bytes 196640 | tf_op jit(solution)/shard_map/ppermute | solution.py:300
  77.6 3.4 %collective-permute-done.12.rest_4_ = bf16[32,3072]{1,0:T(8,128)(2,1)S(1)} collective-permute-done((bf16[32,3072]{1,0:T(8,128)(2,1)S(1)}, bf16[32,3072]{1,0:T(8,128)(2,1)S(1)}, u32[]{:S(2)}, u32[]{:S(2)}) %collective-permute-start.12) | collective-permute-done | bytes 196640 | tf_op jit(solution)/shard_map/ppermute | solution.py:300
  81.0 0.0 collective-permute-done.13.rest_5_
  81.0 1.4 %shard_map.116 = bf16[32,16,128]{2,1,0:T(8,128)(2,1)} custom-call(f32[16,128]{1,0:T(8,128)S(1)} %get-tuple-element.42.start, f32[16,128]{1,0:T(8,128)S(1)} %collective-permute-done.9.first, f32[1]{0:T(128)S(6)} %copy.13.rest_0_, bf16[16,128]{1,0:T(8,128)(2,1)S(1)} %get-tuple-element.44.rest_1_, bf16[32,3072]{1,0:T(8,128)(2,1)S(1)} %get-tuple-element.47.rest_2_, ...), custom_call_target="tpu_custom_call" | custom-call | tf_op jit(solution)/shard_map/pallas_call | solution.py:362
  82.4 4.9 %all-to-all-start.2 = ((bf16[32,16,128]{2,1,0:T(8,128)(2,1)}), bf16[32,16,128]{2,1,0:T(8,128)(2,1)S(1)}, u32[]{:S(2)}, u32[]{:S(2)}) async-start(bf16[32,16,128]{2,1,0:T(8,128)(2,1)} %shard_map.116), calls=%async_computation.2 | async-start | bytes 262144 | tf_op jit(solution)/shard_map/all_to_all | solution.py:367
  88.0 9.6 %all-to-all-done.2.got = bf16[32,16,128]{2,1,0:T(8,128)(2,1)S(1)} async-done(((bf16[32,16,128]{2,1,0:T(8,128)(2,1)}), bf16[32,16,128]{2,1,0:T(8,128)(2,1)S(1)}, u32[]{:S(2)}, u32[]{:S(2)}) %all-to-all-start.2) | async-done | bytes 131104 | tf_op jit(solution)/shard_map/all_to_all | solution.py:367
  97.7 0.7 shard_map.117
  (2 shorter events, 0.0 us)
Async XLA Ops:
  0.8 1.2 %collective-permute-start = (bf16[16,128]{1,0:T(8,128)(2,1)S(1)}, bf16[16,128]{1,0:T(8,128)(2,1)S(1)}, u32[]{:S(2)}, u32[]{:S(2)}) collective-permute-start(bf16[16,128]{1,0:T(8,128)(2,1)S(1)} %pad_maximum_fusion.1.rest_1_), channel_id=1, source_target_pairs={{0,1},{1,0},{2,3},{3,2},{4,5},{5,4},{6,7},{7,6},{8,9},{9,8},{10,11... | collective-permute-start | bytes 12296 | tf_op jit(solution)/shard_map/ppermute | solution.py:304
  2.0 15.6 %collective-permute-start.5 = (bf16[384,3072]{1,0:T(8,128)(2,1)}, bf16[384,3072]{1,0:T(8,128)(2,1)S(1)}, u32[]{:S(2)}, u32[]{:S(2)}) collective-permute-start(bf16[384,3072]{1,0:T(8,128)(2,1)} %w_out.1), channel_id=1, source_target_pairs={{0,1},{1,0},{2,3},{3,2},{4,5},{5,4},{6,7},{7,6},{8,9},{9,8},{10,11... | collective-permute-start | bytes 7077896 | tf_op jit(solution)/shard_map/ppermute | solution.py:304
  2.2 9.1 %collective-permute-start.1 = (bf16[2,16,128]{2,1,0:T(8,128)(2,1)S(1)}, bf16[2,16,128]{2,1,0:T(8,128)(2,1)S(1)}, u32[]{:S(2)}, u32[]{:S(2)}) collective-permute-start(bf16[2,16,128]{2,1,0:T(8,128)(2,1)S(1)} %pad_maximum_fusion.after.z0), channel_id=1, source_target_pairs={{0,6},{2,0},{4,2},{6,4},{1,7},{3,1},{5,3},{7,5},{8,14},{10,8},{12,... | collective-permute-start | bytes 24584 | tf_op jit(solution)/shard_map/ppermute | solution.py:300
  4.9 6.4 %collective-permute-start.2 = (bf16[2,16,128]{2,1,0:T(8,128)(2,1)S(1)}, bf16[2,16,128]{2,1,0:T(8,128)(2,1)S(1)}, u32[]{:S(2)}, u32[]{:S(2)}) collective-permute-start(bf16[2,16,128]{2,1,0:T(8,128)(2,1)S(1)} %pad_maximum_fusion.after.z0), channel_id=1, source_target_pairs={{0,4},{2,6},{4,0},{6,2},{1,5},{3,7},{5,1},{7,3},{8,12},{10,14},{12... | collective-permute-start | bytes 24584 | tf_op jit(solution)/shard_map/ppermute | solution.py:300
  5.7 5.6 %collective-permute-start.3 = (bf16[2,16,128]{2,1,0:T(8,128)(2,1)S(1)}, bf16[2,16,128]{2,1,0:T(8,128)(2,1)S(1)}, u32[]{:S(2)}, u32[]{:S(2)}) collective-permute-start(bf16[2,16,128]{2,1,0:T(8,128)(2,1)S(1)} %pad_maximum_fusion.after.z0), channel_id=1, source_target_pairs={{0,2},{2,4},{4,6},{6,0},{1,3},{3,5},{5,7},{7,1},{8,10},{10,12},{12... | collective-permute-start | bytes 24584 | tf_op jit(solution)/shard_map/ppermute | solution.py:300
  16.2 1.4 %collective-permute-start.4 = (bf16[128,384]{1,0:T(8,128)(2,1)S(1)}, bf16[128,384]{1,0:T(8,128)(2,1)S(1)}, u32[]{:S(2)}, u32[]{:S(2)}) collective-permute-start(bf16[128,384]{1,0:T(8,128)(2,1)S(1)} %get-tuple-element.33), channel_id=1, source_target_pairs={{0,1},{1,0},{2,3},{3,2},{4,5},{5,4},{6,7},{7,6},{8,9},{9,8},{10,11... | collective-permute-start | bytes 294920 | tf_op jit(solution)/shard_map/ppermute | solution.py:304
  17.6 13.6 %copy-start = (f32[1,32,64]{2,1,0:T(8,128)S(1)}, f32[1,32,64]{2,1,0:T(8,128)}, u32[]{:S(2)}) copy-start(f32[1,32,64]{2,1,0:T(8,128)} %param.11) | copy-start | bytes 24580
  18.4 9.4 %collective-permute-start.6 = (bf16[32,3072]{1,0:T(8,128)(2,1)S(1)}, bf16[32,3072]{1,0:T(8,128)(2,1)S(1)}, u32[]{:S(2)}, u32[]{:S(2)}) collective-permute-start(bf16[32,3072]{1,0:T(8,128)(2,1)S(1)} %get-tuple-element.37), channel_id=1, source_target_pairs={{0,4},{2,6},{4,0},{6,2},{1,5},{3,7},{5,1},{7,3},{8,12},{10,14},{12... | collective-permute-start | bytes 589832 | tf_op jit(solution)/shard_map/ppermute | solution.py:300
  20.4 10.8 %collective-permute-start.7 = (bf16[32,3072]{1,0:T(8,128)(2,1)S(1)}, bf16[32,3072]{1,0:T(8,128)(2,1)S(1)}, u32[]{:S(2)}, u32[]{:S(2)}) collective-permute-start(bf16[32,3072]{1,0:T(8,128)(2,1)S(1)} %get-tuple-element.38), channel_id=1, source_target_pairs={{0,2},{2,4},{4,6},{6,0},{1,3},{3,5},{5,7},{7,1},{8,10},{10,12},{12... | collective-permute-start | bytes 589832 | tf_op jit(solution)/shard_map/ppermute | solution.py:300
  21.7 9.5 %collective-permute-start.8 = (bf16[32,3072]{1,0:T(8,128)(2,1)S(1)}, bf16[32,3072]{1,0:T(8,128)(2,1)S(1)}, u32[]{:S(2)}, u32[]{:S(2)}) collective-permute-start(bf16[32,3072]{1,0:T(8,128)(2,1)S(1)} %get-tuple-element.39), channel_id=1, source_target_pairs={{0,6},{2,0},{4,2},{6,4},{1,7},{3,1},{5,3},{7,5},{8,14},{10,8},{12,... | collective-permute-start | bytes 589832 | tf_op jit(solution)/shard_map/ppermute | solution.py:300
  66.1 1.4 %collective-permute-start.10 = (bf16[128,384]{1,0:T(8,128)(2,1)S(1)}, bf16[128,384]{1,0:T(8,128)(2,1)S(1)}, u32[]{:S(2)}, u32[]{:S(2)}) collective-permute-start(bf16[128,384]{1,0:T(8,128)(2,1)S(1)} %get-tuple-element.46), channel_id=1, source_target_pairs={{0,1},{1,0},{2,3},{3,2},{4,5},{5,4},{6,7},{7,6},{8,9},{9,8},{10,11... | collective-permute-start | bytes 294920 | tf_op jit(solution)/shard_map/ppermute | solution.py:304
  68.3 9.4 %collective-permute-start.11 = (bf16[32,3072]{1,0:T(8,128)(2,1)S(1)}, bf16[32,3072]{1,0:T(8,128)(2,1)S(1)}, u32[]{:S(2)}, u32[]{:S(2)}) collective-permute-start(bf16[32,3072]{1,0:T(8,128)(2,1)S(1)} %get-tuple-element.48), channel_id=1, source_target_pairs={{0,4},{2,6},{4,0},{6,2},{1,5},{3,7},{5,1},{7,3},{8,12},{10,14},{12... | collective-permute-start | bytes 589832 | tf_op jit(solution)/shard_map/ppermute | solution.py:300
  69.6 11.5 %collective-permute-start.12 = (bf16[32,3072]{1,0:T(8,128)(2,1)S(1)}, bf16[32,3072]{1,0:T(8,128)(2,1)S(1)}, u32[]{:S(2)}, u32[]{:S(2)}) collective-permute-start(bf16[32,3072]{1,0:T(8,128)(2,1)S(1)} %get-tuple-element.49), channel_id=1, source_target_pairs={{0,2},{2,4},{4,6},{6,0},{1,3},{3,5},{5,7},{7,1},{8,10},{10,12},{12... | collective-permute-start | bytes 589832 | tf_op jit(solution)/shard_map/ppermute | solution.py:300
  70.1 10.9 %collective-permute-start.13 = (bf16[32,3072]{1,0:T(8,128)(2,1)S(1)}, bf16[32,3072]{1,0:T(8,128)(2,1)S(1)}, u32[]{:S(2)}, u32[]{:S(2)}) collective-permute-start(bf16[32,3072]{1,0:T(8,128)(2,1)S(1)} %get-tuple-element.50), channel_id=1, source_target_pairs={{0,6},{2,0},{4,2},{6,4},{1,7},{3,1},{5,3},{7,5},{8,14},{10,8},{12,... | collective-permute-start | bytes 589832 | tf_op jit(solution)/shard_map/ppermute | solution.py:300
  72.8 0.7 collective-permute-start.9
  82.4 15.2 %all-to-all-start.2 = ((bf16[32,16,128]{2,1,0:T(8,128)(2,1)}), bf16[32,16,128]{2,1,0:T(8,128)(2,1)S(1)}, u32[]{:S(2)}, u32[]{:S(2)}) async-start(bf16[32,16,128]{2,1,0:T(8,128)(2,1)} %shard_map.116), calls=%async_computation.2 | async-start | bytes 262144 | tf_op jit(solution)/shard_map/all_to_all | solution.py:367

commit v6 on v4

--- a/solution.py
+++ b/solution.py
@@ -52,8 +52,8 @@
 
 
 def prepare_kernel(
-    step, after, offsets, gain, w_in, mod_table, w_fin, w_qkv, w_out,
-    tab, wc, rows, w_in_out, w_fin_out, w_qkv_out, w_out_out,
+    step, after, offsets, gain, w_in, mod_table, w_fin, w_qkv, w_out, state,
+    tab, wc, rows, w_in_out, w_fin_out, w_qkv_out, w_out_out, state_out,
     offv, gainv, modv, sems,
 ):
     at = jnp.clip(step[0], 0, mod_table.shape[1] - 1)
@@ -66,6 +66,7 @@
         (w_qkv, w_qkv_out),
         (w_out, w_out_out),
         (w_fin, w_fin_out),
+        (state, state_out),
     ]
     copies = [pltpu.make_async_copy(a, b, sems.at[i]) for i, (a, b) in enumerate(pairs)]
     for copy in copies:
@@ -116,7 +117,7 @@
     pltpu.VMEM((2, S), jnp.int32),
     pltpu.VMEM((2, HD), F32),
     pltpu.VMEM((3, 8, D), F32),
-    pltpu.SemaphoreType.DMA((7,)),
+    pltpu.SemaphoreType.DMA((8,)),
 ]
 
 
@@ -173,19 +174,8 @@
     block_body(lambda r, i: z[r % 4][r // 4], *rest)
 
 
-def second_kernel(
-    z0, z1, z2, z3, parts, tab, wc, rows, w_qkv, mine, send, z_out, *scratch
-):
-    z = (z0, z1, z2, z3)
-    start = lax.axis_index("y") * NZ + lax.axis_index("z") == 0
-
-    def chunk_of(r, i):
-        x, c = i // 2, i % 2
-        total = (parts[0, x, c] + parts[1, x, c]) + (parts[2, x, c] + parts[3, x, c])
-        return jnp.where(start, z[r % 4][r // 4].astype(F32), total).astype(BF)
-
-    z_out[...] = chunk_of(0, lax.axis_index("x") * 2 + lax.axis_index("c"))
-    block_body(chunk_of, tab, wc, rows, w_qkv, mine, send, *scratch)
+def second_kernel(zg, *rest):
+    block_body(lambda r, i: zg[i], *rest)
 
 
 BLOCK_SCRATCH = [
@@ -214,7 +204,16 @@
             outs[k][:, cut] = part[ROWS * k : ROWS * (k + 1)]
 
 
-def drift_kernel(size, z, zstart, p0, p1, p2, p3, w_in, gate, w_fin, out):
+def position():
+    return lax.axis_index("y") * NZ + lax.axis_index("z")
+
+
+LAST = NY * NZ - 1
+
+
+def drift_kernel(
+    size, slide, high, zstart, z, p0, p1, p2, p3, w_in, gate, w_fin, out, target=None
+):
     e = jnp.dot(unpack(z[...]), w_in[...], preferred_element_type=F32)
     attn = p0[...].astype(F32) + p1[...].astype(F32) + p2[...].astype(F32) + p3[...].astype(F32)
     h = e + gate[2:3, :] * attn
@@ -225,31 +224,33 @@
     drift = size[0] * lax.dot_general(
         normed, w_fin[...], (((1,), (1,)), ((), ())), preferred_element_type=F32
     )
-    start = lax.axis_index("y") * NZ + lax.axis_index("z") == 0
-    drift = drift + jnp.where(start, zstart[...], jnp.zeros((ROWS, C), F32))
-    packed = pack(drift)
+    here = position()
+    low = zstart[...] - zstart[...].astype(BF).astype(F32)
+    value = pack(drift + jnp.where(here == 0, low, 0.0)).astype(BF)
+    value = jnp.where(here == LAST, high[...].astype(F32), value.astype(F32)).astype(BF)
     for k in range(out.shape[0]):
-        out[k] = packed
-
-
-def relay_kernel(got, out):
-    y, z = lax.axis_index("y"), lax.axis_index("z")
-    for to in range(NY):
-        total = jnp.zeros((NC, 16, 128), F32)
-        for s in range(NZ):
-            keep = y * NZ + s < to * NZ + z
-            total = total + jnp.where(keep, got[s], jnp.zeros((NC, 16, 128), F32))
-        for x in range(NX):
-            out[to, x] = total
-
-
-def final_kernel(slide, got, out):
-    here = lax.axis_index("y") * NZ + lax.axis_index("z")
-    target = jnp.minimum(here + slide[0], NY * NZ - 1)
-    total = got[0]
-    for s in range(1, NY * NZ - 1):
-        total = total + jnp.where(s < target, got[s], jnp.zeros((16, 128), F32))
-    out[0] = unpack(total)
+        out[k] = value
+    if target is not None:
+        target[...] = jnp.full((8, 128), jnp.minimum(here + slide[0], LAST), jnp.int32)
+
+
+def summed(got, target):
+    total = got[0].astype(F32) + got[LAST].astype(F32)
+    for s in range(1, LAST):
+        total = total + jnp.where(s < target, got[s].astype(F32), 0.0)
+    return total
+
+
+def state_kernel(z, got, z_out, copies):
+    here = position()
+    value = jnp.where(here == 0, z[...].astype(F32), summed(got, here)).astype(BF)
+    z_out[...] = value
+    for k in range(8):
+        copies[k] = value
+
+
+def final_kernel(target, got, out):
+    out[0] = unpack(summed(got, jnp.concatenate([target[...], target[...]], axis=0)))
 
 
 def call(body, out_shape, in_specs, scratch=(), limit=8):
@@ -293,7 +294,8 @@
     w_peer = swap_cores(lax.optimization_barrier((w_out, own))[0])
     zg = [own] + [to_right(own, NX - k) for k in range(1, NX)]
     operands = (offsets.T, qk_gain, w_in, mod_table.transpose(1, 0, 2), w_fin.T, w_qkv, w_out)
-    tab, wc, rows, w_in, w_fin_rows, w_qkv, w_out = call(
+    operands += (state,)
+    tab, wc, rows, w_in, w_fin_rows, w_qkv, w_out, state = call(
         prepare_kernel,
         [
             kept((4, 8, ROWS, HD), F32),
@@ -303,43 +305,41 @@
             kept((C, D), BF),
             kept(w_qkv.shape, BF),
             kept(w_out.shape, BF),
+            kept((ROWS, C), F32),
         ],
-        [SM, VM] + [HB] * 7,
+        [SM, VM] + [HB] * 8,
         PREPARE_SCRATCH,
         limit=12,
     )(step_ids, own, *[far(x) for x in operands])
     half = shape((S // 2, HL * HD), BF)
     row = shape((ROWS, D), BF)
 
-    def to_drift(mine, send, z, w_peer, copies):
+    high = lax.ppermute(z, ("y", "z"), [(0, LAST)])
+
+    def gathered_drifts(mine, send, z, *extra):
         operands = (mine, swap_cores(send), w_out, w_peer)
         parts = call(out_kernel, [row] * NX, [VM] * 4, limit=16)(*operands)
-        got = [to_right(parts[k], k) for k in (2, 1, 3)]
-        return call(drift_kernel, shape((copies, 16, 128), F32), [SM] + [VM] * 9)(
-            step_sizes, z, state, parts[0], *got, w_in, rows, w_fin_rows
-        )
+        got = [parts[0]] + [to_right(parts[k], k) for k in (2, 1, 3)]
+        outs, *extra = call(
+            drift_kernel,
+            [shape((NY * NZ, 16, 128), BF), *extra],
+            [SM, SM] + [VM] * 10,
+        )(step_sizes, slide, high, state, z, *got, w_in, rows, w_fin_rows)
+        return lax.all_to_all(outs, ("y", "z"), 0, 0, tiled=True), *extra
 
     mine, send = call(first_kernel, [half, half], [VM] * 8, BLOCK_SCRATCH, limit=16)(
         *zg, tab, wc, rows, w_qkv
     )
-    drift = to_drift(mine, send, z, w_peer, NZ * NC)
-    got = lax.all_to_all(drift, ("z", "c"), 0, 0, tiled=True)
-    parts = call(relay_kernel, shape((NY, NX, NC, 16, 128), F32), [VM])(
-        got.reshape(NZ, NC, 16, 128)
-    )
-    parts = lax.all_to_all(
-        parts.reshape(NY * NX, NC, 16, 128), ("y", "x"), 0, 0, tiled=True
-    ).reshape(NY, NX, NC, 16, 128)
-    mine, send, z = call(
-        second_kernel,
-        [half, half, shape((16, 128), BF)],
-        [VM] * 9,
-        BLOCK_SCRATCH,
-        limit=16,
-    )(*zg, parts, tab, wc, rows, w_qkv)
-    drift = to_drift(mine, send, z, w_peer, NY * NZ)
-    got = lax.all_to_all(drift, ("y", "z"), 0, 0, tiled=True)
-    return call(final_kernel, shape((1, ROWS, C), F32), [SM, VM])(slide, got)
+    (got,) = gathered_drifts(mine, send, z)
+    z, copies = call(
+        state_kernel, [shape((16, 128), BF), shape((8, 16, 128), BF)], [VM] * 2
+    )(z, got)
+    zg = lax.all_to_all(copies, ("x", "c"), 0, 0, tiled=True)
+    mine, send = call(second_kernel, [half, half], [VM] * 5, BLOCK_SCRATCH, limit=16)(
+        zg, tab, wc, rows, w_qkv
+    )
+    got, target = gathered_drifts(mine, send, z, shape((8, 128), jnp.int32))
+    return call(final_kernel, shape((1, ROWS, C), F32), [VM] * 2)(target, got)
 
 
 def solution(mesh):

time: 104 us -> 97.6 us (0.938)
  waiting for transfers between devices: 31.3 us -> 17.7 us
  blocking collectives: 31.5 us -> 43.9 us
  starting transfers between devices: 19.4 us -> 15 us
    all_to_all x2 -> x3, blocking collectives: 31.5 us -> 43.9 us  [the longest x2 35.1 us: gathered_drifts(): return (lax.all_to_all(outs, ('y', 'z'), 0, 0, tiled=True), *extra)]
    all_to_all x1 -> x0, waiting for transfers between devices: 12.2 us -> none  [local(): got = lax.all_to_all(drift, ('y', 'z'), 0, 0, tiled=True)]
    all_to_all x1 -> x0, starting transfers between devices: 5.19 us -> none  [local(): got = lax.all_to_all(drift, ('y', 'z'), 0, 0, tiled=True)]
    ppermute x9, waiting for transfers between devices: 15.4 us -> 14 us  [to_right(): return lax.ppermute(x, 'x', [(i, (i + k) % NX) for i in range(NX)])]
  transfers between devices with their start and end apart: 14 -> 14, of which waited for: 8 -> 7; matrix products, arithmetic and copies ran while one was open for 0% -> 0% of each run, Pallas kernels for 9% -> 9%
where the time goes in v6:
time: 97.6 us; the launch traced here: 97 us
  blocking collectives  43.9 us (45%)
  waiting for transfers between devices  17.7 us (18%)
  Pallas kernels  17.4 us (18%)
  starting transfers between devices  15 us (15%)
  between operations  2.08 us (2%)
    all_to_all x2, blocking collectives, gathered_drifts(): return (lax.all_to_all(outs, ('y', 'z'), 0, 0, tiled=True), *extra)  35.1 us
    ppermute x9, starting transfers between devices, to_right(): return lax.ppermute(x, 'x', [(i, (i + k) % NX) for i in range(NX)])  14 us
    ppermute x9, waiting for transfers between devices, to_right(): return lax.ppermute(x, 'x', [(i, (i + k) % NX) for i in range(NX)])  14 us
    all_to_all x1, blocking collectives, local(): zg = lax.all_to_all(copies, ('x', 'c'), 0, 0, tiled=True)  8.87 us
    pallas_call x1, Pallas kernels, local(): call(second_kernel, [half, half], [VM] * 5, BLOCK_SCRATCH, limit=16)  4.78 us
    pallas_call x1, Pallas kernels, local(): call(first_kernel, [half, half], [VM] * 8, BLOCK_SCRATCH, limit=16)  4.78 us
    pallas_call x1, Pallas kernels, local(): call(prepare_kernel, [kept((4, 8, ROWS, HD), F32), kept((2 * C, D), BF),...  4.03 us
    ppermute x4, waiting for transfers between devices, swap_cores(): return lax.ppermute(x, 'c', [(0, 1), (1, 0)])  3.73 us
  transfers between devices with their start and end apart: 14, of which 7 were waited for; matrix products, arithmetic and copies ran while one was open for 0% of the time, Pallas kernels for 9%

profile of v6, /device:TPU:32, one launch (start us, length us, event | category | flops | bytes accessed | tf_op | source)
XLA Modules:
  0.0 97.0 jit_solution(10872923177339357433)
XLA Ops:
  0.0 0.7 bitcast_convert_fusion
  0.7 0.1 pad_maximum_fusion.1.z
  0.8 0.0 collective-permute-start.1
  0.8 1.2 %collective-permute-done.1 = bf16[16,128]{1,0:T(8,128)(2,1)S(1)} collective-permute-done((bf16[16,128]{1,0:T(8,128)(2,1)S(1)}, bf16[16,128]{1,0:T(8,128)(2,1)S(1)}, u32[]{:S(2)}, u32[]{:S(2)}) %collective-permute-start.1) | collective-permute-done | bytes 4128 | tf_op jit(solution)/shard_map/ppermute | solution.py:285
  2.0 0.2 collective-permute-start.6
  2.2 2.8 %collective-permute-start.2 = (bf16[2,16,128]{2,1,0:T(8,128)(2,1)S(1)}, bf16[2,16,128]{2,1,0:T(8,128)(2,1)S(1)}, u32[]{:S(2)}, u32[]{:S(2)}) collective-permute-start(bf16[2,16,128]{2,1,0:T(8,128)(2,1)S(1)} %pad_maximum_fusion.after.z0), channel_id=1, source_target_pairs={{0,6},{2,0},{4,2},{6,4},{1,7},{3,1},{5,3},{7,5},{8,14},{10,8},{12,... | collective-permute-start | bytes 24584 | tf_op jit(solution)/shard_map/ppermute | solution.py:281
  4.9 0.8 collective-permute-start.3
  5.7 0.9 collective-permute-start.4
  7.3 4.0 %shard_map.109 = (f32[4,8,32,128]{3,2,1,0:T(8,128)S(1)}, bf16[128,3072]{1,0:T(8,128)(2,1)S(1)}, f32[8,3072]{1,0:T(8,128)S(1)}, bf16[64,3072]{1,0:T(8,128)(2,1)S(...) custom-call(s32[1]{0:T(128)S(6)} %copy.12.step, ...), custom_call_target="tpu_custom_call" | custom-call | tf_op jit(solution)/shard_map/pallas_call | solution.py:298
  11.3 0.0 collective-permute-done.2.z1
  11.3 0.0 collective-permute-done.3.z2
  11.3 0.0 collective-permute-done.4.z3
  11.3 4.8 %shard_map.110 = (bf16[128,384]{1,0:T(8,128)(2,1)S(1)}, bf16[128,384]{1,0:T(8,128)(2,1)S(1)}) custom-call(bf16[2,16,128]{2,1,0:T(8,128)(2,1)S(1)} %pad_maximum_fusion.after.z0, bf16[2,16,128]{2,1,0:T(8,128)(2,1)S(1)} %collective-permute-done.2.z1, bf16[2,16,128]{2,1,0:T(8,128)(2,1)S(1)} %collective-permute-done.3.z2, ...), custom_call_target="tpu_custom_call" | custom-call | tf_op jit(solution)/shard_map/pallas_call | solution.py:330
  16.1 0.1 collective-permute-start.5
  16.2 1.3 %collective-permute-done.5.peer = bf16[128,384]{1,0:T(8,128)(2,1)S(1)} collective-permute-done((bf16[128,384]{1,0:T(8,128)(2,1)S(1)}, bf16[128,384]{1,0:T(8,128)(2,1)S(1)}, u32[]{:S(2)}, u32[]{:S(2)}) %collective-permute-start.5) | collective-permute-done | bytes 98336 | tf_op jit(solution)/shard_map/ppermute | solution.py:285
  17.5 0.0 collective-permute-done.6.w_peer
  17.5 0.8 shard_map.111
  18.3 1.9 %collective-permute-start.7 = (bf16[32,3072]{1,0:T(8,128)(2,1)S(1)}, bf16[32,3072]{1,0:T(8,128)(2,1)S(1)}, u32[]{:S(2)}, u32[]{:S(2)}) collective-permute-start(bf16[32,3072]{1,0:T(8,128)(2,1)S(1)} %get-tuple-element.40), channel_id=1, source_target_pairs={{0,4},{2,6},{4,0},{6,2},{1,5},{3,7},{5,1},{7,3},{8,12},{10,14},{12... | collective-permute-start | bytes 589832 | tf_op jit(solution)/shard_map/ppermute | solution.py:281
  20.2 1.4 %collective-permute-start.8 = (bf16[32,3072]{1,0:T(8,128)(2,1)S(1)}, bf16[32,3072]{1,0:T(8,128)(2,1)S(1)}, u32[]{:S(2)}, u32[]{:S(2)}) collective-permute-start(bf16[32,3072]{1,0:T(8,128)(2,1)S(1)} %get-tuple-element.41), channel_id=1, source_target_pairs={{0,2},{2,4},{4,6},{6,0},{1,3},{3,5},{5,7},{7,1},{8,10},{10,12},{12... | collective-permute-start | bytes 589832 | tf_op jit(solution)/shard_map/ppermute | solution.py:281
  21.6 1.9 %collective-permute-start.9 = (bf16[32,3072]{1,0:T(8,128)(2,1)S(1)}, bf16[32,3072]{1,0:T(8,128)(2,1)S(1)}, u32[]{:S(2)}, u32[]{:S(2)}) collective-permute-start(bf16[32,3072]{1,0:T(8,128)(2,1)S(1)} %get-tuple-element.42), channel_id=1, source_target_pairs={{0,6},{2,0},{4,2},{6,4},{1,7},{3,1},{5,3},{7,5},{8,14},{10,8},{12,... | collective-permute-start | bytes 589832 | tf_op jit(solution)/shard_map/ppermute | solution.py:281
  23.5 0.6 collective-permute-start
  25.4 0.0 collective-permute-done.high
  25.4 2.2 %collective-permute-done.7.p1 = bf16[32,3072]{1,0:T(8,128)(2,1)S(1)} collective-permute-done((bf16[32,3072]{1,0:T(8,128)(2,1)S(1)}, bf16[32,3072]{1,0:T(8,128)(2,1)S(1)}, u32[]{:S(2)}, u32[]{:S(2)}) %collective-permute-start.7) | collective-permute-done | bytes 196640 | tf_op jit(solution)/shard_map/ppermute | solution.py:281
  27.7 3.4 %collective-permute-done.8.p2 = bf16[32,3072]{1,0:T(8,128)(2,1)S(1)} collective-permute-done((bf16[32,3072]{1,0:T(8,128)(2,1)S(1)}, bf16[32,3072]{1,0:T(8,128)(2,1)S(1)}, u32[]{:S(2)}, u32[]{:S(2)}) %collective-permute-start.8) | collective-permute-done | bytes 196640 | tf_op jit(solution)/shard_map/ppermute | solution.py:281
  31.1 0.0 collective-permute-done.9.p3
  31.1 0.7 shard_map.112
  31.8 21.0 %all_to_all.15.got = bf16[32,16,128]{2,1,0:T(8,128)(2,1)S(1)} all-to-all(bf16[32,16,128]{2,1,0:T(8,128)(2,1)S(1)} %shard_map.112), channel_id=1, replica_groups=mesh['y'=4,'z'=8,'x'=4,'c'=2] {'y','z'}, dimensions={0} | all-to-all | bytes 262144 | tf_op jit(solution)/shard_map/all_to_all | solution.py:328
  52.9 8.9 %all_to_all.16.zg = bf16[8,16,128]{2,1,0:T(8,128)(2,1)S(1)} all-to-all(bf16[8,16,128]{2,1,0:T(8,128)(2,1)S(1)} %get-tuple-element.46), channel_id=1, replica_groups=mesh['y'=4,'z'=8,'x'=4,'c'=2] {'x','c'}, dimensions={0} | all-to-all | bytes 65536 | tf_op jit(solution)/shard_map/all_to_all | solution.py:337
  61.8 4.8 %shard_map.114 = (bf16[128,384]{1,0:T(8,128)(2,1)S(1)}, bf16[128,384]{1,0:T(8,128)(2,1)S(1)}) custom-call(bf16[8,16,128]{2,1,0:T(8,128)(2,1)S(1)} %all_to_all.16.zg, f32[4,8,32,128]{3,2,1,0:T(8,128)S(1)} %get-tuple-element.31.rest_0_, bf16[128,3072]{1,0:T(8,128)(2,1)S(1)} %get-tuple-element.32.rest_1_, f32[8,3072]{1,0:T(8,128)S(1)} %get-tuple-element.33.rest_2_.gate, ...), custom_call_target="tpu_custom_call" | custom-call | tf_op jit(solution)/shard_map/pallas_call | solution.py:338
  66.6 0.1 collective-permute-start.10
  66.7 1.3 %collective-permute-done.10.peer = bf16[128,384]{1,0:T(8,128)(2,1)S(1)} collective-permute-done((bf16[128,384]{1,0:T(8,128)(2,1)S(1)}, bf16[128,384]{1,0:T(8,128)(2,1)S(1)}, u32[]{:S(2)}, u32[]{:S(2)}) %collective-permute-start.10) | collective-permute-done | bytes 98336 | tf_op jit(solution)/shard_map/ppermute | solution.py:285
  68.0 0.8 shard_map.115
  68.8 1.2 %collective-permute-start.11 = (bf16[32,3072]{1,0:T(8,128)(2,1)S(1)}, bf16[32,3072]{1,0:T(8,128)(2,1)S(1)}, u32[]{:S(2)}, u32[]{:S(2)}) collective-permute-start(bf16[32,3072]{1,0:T(8,128)(2,1)S(1)} %get-tuple-element.50), channel_id=1, source_target_pairs={{0,4},{2,6},{4,0},{6,2},{1,5},{3,7},{5,1},{7,3},{8,12},{10,14},{12... | collective-permute-start | bytes 589832 | tf_op jit(solution)/shard_map/ppermute | solution.py:281
  69.9 0.9 collective-permute-start.12
  70.9 2.3 %collective-permute-start.13 = (bf16[32,3072]{1,0:T(8,128)(2,1)S(1)}, bf16[32,3072]{1,0:T(8,128)(2,1)S(1)}, u32[]{:S(2)}, u32[]{:S(2)}) collective-permute-start(bf16[32,3072]{1,0:T(8,128)(2,1)S(1)} %get-tuple-element.52), channel_id=1, source_target_pairs={{0,6},{2,0},{4,2},{6,4},{1,7},{3,1},{5,3},{7,5},{8,14},{10,8},{12,... | collective-permute-start | bytes 589832 | tf_op jit(solution)/shard_map/ppermute | solution.py:281
  73.2 5.0 %collective-permute-done.11.p1 = bf16[32,3072]{1,0:T(8,128)(2,1)S(1)} collective-permute-done((bf16[32,3072]{1,0:T(8,128)(2,1)S(1)}, bf16[32,3072]{1,0:T(8,128)(2,1)S(1)}, u32[]{:S(2)}, u32[]{:S(2)}) %collective-permute-start.11) | collective-permute-done | bytes 196640 | tf_op jit(solution)/shard_map/ppermute | solution.py:281
  78.2 3.4 %collective-permute-done.12.p2 = bf16[32,3072]{1,0:T(8,128)(2,1)S(1)} collective-permute-done((bf16[32,3072]{1,0:T(8,128)(2,1)S(1)}, bf16[32,3072]{1,0:T(8,128)(2,1)S(1)}, u32[]{:S(2)}, u32[]{:S(2)}) %collective-permute-start.12) | collective-permute-done | bytes 196640 | tf_op jit(solution)/shard_map/ppermute | solution.py:281
  81.5 0.0 collective-permute-done.13.p3
  81.5 0.7 shard_map.116
  82.3 14.0 %all_to_all.17.got = bf16[32,16,128]{2,1,0:T(8,128)(2,1)S(1)} all-to-all(bf16[32,16,128]{2,1,0:T(8,128)(2,1)S(1)} %get-tuple-element.54), channel_id=1, replica_groups=mesh['y'=4,'z'=8,'x'=4,'c'=2] {'y','z'}, dimensions={0} | all-to-all | bytes 262144 | tf_op jit(solution)/shard_map/all_to_all | solution.py:328
  96.3 0.7 shard_map.117
  (3 shorter events, 0.1 us)
Async XLA Ops:
  0.8 1.2 %collective-permute-start.1 = (bf16[16,128]{1,0:T(8,128)(2,1)S(1)}, bf16[16,128]{1,0:T(8,128)(2,1)S(1)}, u32[]{:S(2)}, u32[]{:S(2)}) collective-permute-start(bf16[16,128]{1,0:T(8,128)(2,1)S(1)} %pad_maximum_fusion.1.z), channel_id=1, source_target_pairs={{0,1},{1,0},{2,3},{3,2},{4,5},{5,4},{6,7},{7,6},{8,9},{9,8},{10,11... | collective-permute-start | bytes 12296 | tf_op jit(solution)/shard_map/ppermute | solution.py:285
  2.0 15.5 %collective-permute-start.6 = (bf16[384,3072]{1,0:T(8,128)(2,1)}, bf16[384,3072]{1,0:T(8,128)(2,1)S(1)}, u32[]{:S(2)}, u32[]{:S(2)}) collective-permute-start(bf16[384,3072]{1,0:T(8,128)(2,1)} %w_out.1), channel_id=1, source_target_pairs={{0,1},{1,0},{2,3},{3,2},{4,5},{5,4},{6,7},{7,6},{8,9},{9,8},{10,11... | collective-permute-start | bytes 7077896 | tf_op jit(solution)/shard_map/ppermute | solution.py:285
  2.2 9.1 %collective-permute-start.2 = (bf16[2,16,128]{2,1,0:T(8,128)(2,1)S(1)}, bf16[2,16,128]{2,1,0:T(8,128)(2,1)S(1)}, u32[]{:S(2)}, u32[]{:S(2)}) collective-permute-start(bf16[2,16,128]{2,1,0:T(8,128)(2,1)S(1)} %pad_maximum_fusion.after.z0), channel_id=1, source_target_pairs={{0,6},{2,0},{4,2},{6,4},{1,7},{3,1},{5,3},{7,5},{8,14},{10,8},{12,... | collective-permute-start | bytes 24584 | tf_op jit(solution)/shard_map/ppermute | solution.py:281
  4.9 6.4 %collective-permute-start.3 = (bf16[2,16,128]{2,1,0:T(8,128)(2,1)S(1)}, bf16[2,16,128]{2,1,0:T(8,128)(2,1)S(1)}, u32[]{:S(2)}, u32[]{:S(2)}) collective-permute-start(bf16[2,16,128]{2,1,0:T(8,128)(2,1)S(1)} %pad_maximum_fusion.after.z0), channel_id=1, source_target_pairs={{0,4},{2,6},{4,0},{6,2},{1,5},{3,7},{5,1},{7,3},{8,12},{10,14},{12... | collective-permute-start | bytes 24584 | tf_op jit(solution)/shard_map/ppermute | solution.py:281
  5.7 5.6 %collective-permute-start.4 = (bf16[2,16,128]{2,1,0:T(8,128)(2,1)S(1)}, bf16[2,16,128]{2,1,0:T(8,128)(2,1)S(1)}, u32[]{:S(2)}, u32[]{:S(2)}) collective-permute-start(bf16[2,16,128]{2,1,0:T(8,128)(2,1)S(1)} %pad_maximum_fusion.after.z0), channel_id=1, source_target_pairs={{0,2},{2,4},{4,6},{6,0},{1,3},{3,5},{5,7},{7,1},{8,10},{10,12},{12... | collective-permute-start | bytes 24584 | tf_op jit(solution)/shard_map/ppermute | solution.py:281
  16.1 1.4 %collective-permute-start.5 = (bf16[128,384]{1,0:T(8,128)(2,1)S(1)}, bf16[128,384]{1,0:T(8,128)(2,1)S(1)}, u32[]{:S(2)}, u32[]{:S(2)}) collective-permute-start(bf16[128,384]{1,0:T(8,128)(2,1)S(1)} %get-tuple-element.36), channel_id=1, source_target_pairs={{0,1},{1,0},{2,3},{3,2},{4,5},{5,4},{6,7},{7,6},{8,9},{9,8},{10,11... | collective-permute-start | bytes 294920 | tf_op jit(solution)/shard_map/ppermute | solution.py:285
  18.3 9.4 %collective-permute-start.7 = (bf16[32,3072]{1,0:T(8,128)(2,1)S(1)}, bf16[32,3072]{1,0:T(8,128)(2,1)S(1)}, u32[]{:S(2)}, u32[]{:S(2)}) collective-permute-start(bf16[32,3072]{1,0:T(8,128)(2,1)S(1)} %get-tuple-element.40), channel_id=1, source_target_pairs={{0,4},{2,6},{4,0},{6,2},{1,5},{3,7},{5,1},{7,3},{8,12},{10,14},{12... | collective-permute-start | bytes 589832 | tf_op jit(solution)/shard_map/ppermute | solution.py:281
  20.2 10.8 %collective-permute-start.8 = (bf16[32,3072]{1,0:T(8,128)(2,1)S(1)}, bf16[32,3072]{1,0:T(8,128)(2,1)S(1)}, u32[]{:S(2)}, u32[]{:S(2)}) collective-permute-start(bf16[32,3072]{1,0:T(8,128)(2,1)S(1)} %get-tuple-element.41), channel_id=1, source_target_pairs={{0,2},{2,4},{4,6},{6,0},{1,3},{3,5},{5,7},{7,1},{8,10},{10,12},{12... | collective-permute-start | bytes 589832 | tf_op jit(solution)/shard_map/ppermute | solution.py:281
  21.6 9.5 %collective-permute-start.9 = (bf16[32,3072]{1,0:T(8,128)(2,1)S(1)}, bf16[32,3072]{1,0:T(8,128)(2,1)S(1)}, u32[]{:S(2)}, u32[]{:S(2)}) collective-permute-start(bf16[32,3072]{1,0:T(8,128)(2,1)S(1)} %get-tuple-element.42), channel_id=1, source_target_pairs={{0,6},{2,0},{4,2},{6,4},{1,7},{3,1},{5,3},{7,5},{8,14},{10,8},{12,... | collective-permute-start | bytes 589832 | tf_op jit(solution)/shard_map/ppermute | solution.py:281
  23.5 2.0 %collective-permute-start = (bf16[16,128]{1,0:T(8,128)(2,1)S(1)}, bf16[16,128]{1,0:T(8,128)(2,1)S(1)}, u32[]{:S(2)}, u32[]{:S(2)}) collective-permute-start(bf16[16,128]{1,0:T(8,128)(2,1)S(1)} %pad_maximum_fusion.1.z), channel_id=1, source_target_pairs={{0,248},{1,249},{2,250},{3,251},{4,252},{5,253},{6,254},{7,255}} | collective-permute-start | bytes 12296 | tf_op jit(solution)/shard_map/ppermute | solution.py:317
  66.6 1.4 %collective-permute-start.10 = (bf16[128,384]{1,0:T(8,128)(2,1)S(1)}, bf16[128,384]{1,0:T(8,128)(2,1)S(1)}, u32[]{:S(2)}, u32[]{:S(2)}) collective-permute-start(bf16[128,384]{1,0:T(8,128)(2,1)S(1)} %get-tuple-element.48), channel_id=1, source_target_pairs={{0,1},{1,0},{2,3},{3,2},{4,5},{5,4},{6,7},{7,6},{8,9},{9,8},{10,11... | collective-permute-start | bytes 294920 | tf_op jit(solution)/shard_map/ppermute | solution.py:285
  68.8 9.4 %collective-permute-start.11 = (bf16[32,3072]{1,0:T(8,128)(2,1)S(1)}, bf16[32,3072]{1,0:T(8,128)(2,1)S(1)}, u32[]{:S(2)}, u32[]{:S(2)}) collective-permute-start(bf16[32,3072]{1,0:T(8,128)(2,1)S(1)} %get-tuple-element.50), channel_id=1, source_target_pairs={{0,4},{2,6},{4,0},{6,2},{1,5},{3,7},{5,1},{7,3},{8,12},{10,14},{12... | collective-permute-start | bytes 589832 | tf_op jit(solution)/shard_map/ppermute | solution.py:281
  69.9 11.6 %collective-permute-start.12 = (bf16[32,3072]{1,0:T(8,128)(2,1)S(1)}, bf16[32,3072]{1,0:T(8,128)(2,1)S(1)}, u32[]{:S(2)}, u32[]{:S(2)}) collective-permute-start(bf16[32,3072]{1,0:T(8,128)(2,1)S(1)} %get-tuple-element.51), channel_id=1, source_target_pairs={{0,2},{2,4},{4,6},{6,0},{1,3},{3,5},{5,7},{7,1},{8,10},{10,12},{12... | collective-permute-start | bytes 589832 | tf_op jit(solution)/shard_map/ppermute | solution.py:281
  70.9 10.6 %collective-permute-start.13 = (bf16[32,3072]{1,0:T(8,128)(2,1)S(1)}, bf16[32,3072]{1,0:T(8,128)(2,1)S(1)}, u32[]{:S(2)}, u32[]{:S(2)}) collective-permute-start(bf16[32,3072]{1,0:T(8,128)(2,1)S(1)} %get-tuple-element.52), channel_id=1, source_target_pairs={{0,6},{2,0},{4,2},{6,4},{1,7},{3,1},{5,3},{7,5},{8,14},{10,8},{12,... | collective-permute-start | bytes 589832 | tf_op jit(solution)/shard_map/ppermute | solution.py:281

commit v7 on v6

--- a/solution.py
+++ b/solution.py
@@ -52,8 +52,8 @@
 
 
 def prepare_kernel(
-    step, after, offsets, gain, w_in, mod_table, w_fin, w_qkv, w_out, state,
-    tab, wc, rows, w_in_out, w_fin_out, w_qkv_out, w_out_out, state_out,
+    step, after, offsets, gain, w_in, mod_table, w_qkv,
+    tab, wc, rows, w_in_out, w_qkv_out,
     offv, gainv, modv, sems,
 ):
     at = jnp.clip(step[0], 0, mod_table.shape[1] - 1)
@@ -64,9 +64,6 @@
         (w_in, w_in_out),
         (mod_table.at[:, block, :], modv),
         (w_qkv, w_qkv_out),
-        (w_out, w_out_out),
-        (w_fin, w_fin_out),
-        (state, state_out),
     ]
     copies = [pltpu.make_async_copy(a, b, sems.at[i]) for i, (a, b) in enumerate(pairs)]
     for copy in copies:
@@ -117,8 +114,20 @@
     pltpu.VMEM((2, S), jnp.int32),
     pltpu.VMEM((2, HD), F32),
     pltpu.VMEM((3, 8, D), F32),
-    pltpu.SemaphoreType.DMA((8,)),
+    pltpu.SemaphoreType.DMA((5,)),
 ]
+
+
+def late_kernel(after, *refs):
+    count = len(refs) // 2
+    sems = refs[-1]
+    copies = [
+        pltpu.make_async_copy(refs[i], refs[count + i], sems.at[i]) for i in range(count)
+    ]
+    for copy in copies:
+        copy.start()
+    for copy in copies:
+        copy.wait()
 
 
 def block_body(chunk_of, tab, wc, rows, w_qkv, mine, send, zs, es, fs, qkv, qs):
@@ -158,13 +167,22 @@
         for k in range(2):
             qs[head, k] = turned(qkv[:, base + k * HD : base + k * HD + HD], k)
         qs[head, 2] = qkv[:, base + 2 * HD : base + QKV].astype(BF)
-        scores = lax.dot_general(
+    scores = [
+        lax.dot_general(
             qs[head, 0], qs[head, 1], (((1,), (1,)), ((), ())), preferred_element_type=F32
         )
-        top = jnp.max(scores, axis=-1, keepdims=True)
-        p = jnp.exp((scores - top) * (1.0 / math.sqrt(HD)))
-        p = p * (1.0 / jnp.sum(p, axis=-1, keepdims=True))
-        out = jnp.dot(p.astype(BF), qs[head, 2], preferred_element_type=F32).astype(BF)
+        for head in range(HL)
+    ]
+    tops = [jnp.max(score, axis=-1, keepdims=True) for score in scores]
+    factor = math.log2(math.e) / math.sqrt(HD)
+    probs = [jnp.exp2((score - top) * factor) for score, top in zip(scores, tops)]
+    totals = [jnp.sum(p, axis=-1, keepdims=True) for p in probs]
+    outs = [
+        jnp.dot(p.astype(BF), qs[head, 2], preferred_element_type=F32)
+        for head, p in enumerate(probs)
+    ]
+    for head in range(HL):
+        out = (outs[head] * (1.0 / totals[head])).astype(BF)
         mine[:, head * HD : head * HD + HD] = out[: S // 2]
         send[:, head * HD : head * HD + HD] = out[S // 2 :]
 
@@ -293,21 +311,17 @@
     own = jnp.stack([z, swap_cores(z)])
     w_peer = swap_cores(lax.optimization_barrier((w_out, own))[0])
     zg = [own] + [to_right(own, NX - k) for k in range(1, NX)]
-    operands = (offsets.T, qk_gain, w_in, mod_table.transpose(1, 0, 2), w_fin.T, w_qkv, w_out)
-    operands += (state,)
-    tab, wc, rows, w_in, w_fin_rows, w_qkv, w_out, state = call(
+    operands = (offsets.T, qk_gain, w_in, mod_table.transpose(1, 0, 2), w_qkv)
+    tab, wc, rows, w_in, w_qkv = call(
         prepare_kernel,
         [
             kept((4, 8, ROWS, HD), F32),
             kept((2 * C, D), BF),
             kept((8, D), F32),
             kept((C, D), BF),
-            kept((C, D), BF),
             kept(w_qkv.shape, BF),
-            kept(w_out.shape, BF),
-            kept((ROWS, C), F32),
         ],
-        [SM, VM] + [HB] * 8,
+        [SM, VM] + [HB] * 5,
         PREPARE_SCRATCH,
         limit=12,
     )(step_ids, own, *[far(x) for x in operands])
@@ -315,6 +329,17 @@
     row = shape((ROWS, D), BF)
 
     high = lax.ppermute(z, ("y", "z"), [(0, LAST)])
+
+    mine, send = call(first_kernel, [half, half], [VM] * 8, BLOCK_SCRATCH, limit=16)(
+        *zg, tab, wc, rows, w_qkv
+    )
+    operands = (w_out, w_fin.T, state)
+    w_out, w_fin_rows, state = call(
+        late_kernel,
+        [kept(x.shape, x.dtype) for x in operands],
+        [VM] + [HB] * 3,
+        [pltpu.SemaphoreType.DMA((3,))],
+    )(send, *[far(x) for x in operands])
 
     def gathered_drifts(mine, send, z, *extra):
         operands = (mine, swap_cores(send), w_out, w_peer)
@@ -327,9 +352,6 @@
         )(step_sizes, slide, high, state, z, *got, w_in, rows, w_fin_rows)
         return lax.all_to_all(outs, ("y", "z"), 0, 0, tiled=True), *extra
 
-    mine, send = call(first_kernel, [half, half], [VM] * 8, BLOCK_SCRATCH, limit=16)(
-        *zg, tab, wc, rows, w_qkv
-    )
     (got,) = gathered_drifts(mine, send, z)
     z, copies = call(
         state_kernel, [shape((16, 128), BF), shape((8, 16, 128), BF)], [VM] * 2

time: 97.6 us -> 95.4 us (0.977)
  Pallas kernels: 17.4 us -> 16.2 us
    pallas_call x0 -> x1, Pallas kernels: none -> 1.74 us  [local(): call(late_kernel, [kept(x.shape, x.dtype) for x in operands], [VM] + [HB]...]
    ppermute x4, waiting for transfers between devices: 3.73 us -> 2.45 us  [swap_cores(): return lax.ppermute(x, 'c', [(0, 1), (1, 0)])]
    pallas_call x1, Pallas kernels: 4.78 us -> 3.65 us  [local(): call(second_kernel, [half, half], [VM] * 5, BLOCK_SCRATCH, limit=16)]
    pallas_call x1, Pallas kernels: 4.78 us -> 3.65 us  [local(): call(first_kernel, [half, half], [VM] * 8, BLOCK_SCRATCH, limit=16)]
  transfers between devices with their start and end apart: 14 -> 14, of which waited for: 7 -> 6; matrix products, arithmetic and copies ran while one was open for 0% -> 0% of each run, Pallas kernels for 9% -> 9%
where the time goes in v7:
time: 95.4 us; the launch traced here: 94.9 us
  blocking collectives  44 us (46%)
  waiting for transfers between devices  16.8 us (18%)
  Pallas kernels  16.2 us (17%)
  starting transfers between devices  15 us (16%)
  between operations  2.1 us (2%)
    all_to_all x2, blocking collectives, gathered_drifts(): return (lax.all_to_all(outs, ('y', 'z'), 0, 0, tiled=True), *extra)  35.1 us
    ppermute x9, waiting for transfers between devices, to_right(): return lax.ppermute(x, 'x', [(i, (i + k) % NX) for i in range(NX)])  14.3 us
    ppermute x9, starting transfers between devices, to_right(): return lax.ppermute(x, 'x', [(i, (i + k) % NX) for i in range(NX)])  14 us
    all_to_all x1, blocking collectives, local(): zg = lax.all_to_all(copies, ('x', 'c'), 0, 0, tiled=True)  8.84 us
    pallas_call x1, Pallas kernels, local(): call(first_kernel, [half, half], [VM] * 8, BLOCK_SCRATCH, limit=16)  3.65 us
    pallas_call x1, Pallas kernels, local(): call(second_kernel, [half, half], [VM] * 5, BLOCK_SCRATCH, limit=16)  3.65 us
    pallas_call x1, Pallas kernels, local(): call(prepare_kernel, [kept((4, 8, ROWS, HD), F32), kept((2 * C, D), BF),...  3.32 us
    ppermute x4, waiting for transfers between devices, swap_cores(): return lax.ppermute(x, 'c', [(0, 1), (1, 0)])  2.45 us
  transfers between devices with their start and end apart: 14, of which 6 were waited for; matrix products, arithmetic and copies ran while one was open for 0% of the time, Pallas kernels for 9%

profile of v7, /device:TPU:32, one launch (start us, length us, event | category | flops | bytes accessed | tf_op | source)
XLA Modules:
  0.0 94.9 jit_solution(11176620949724804731)
XLA Ops:
  0.0 0.7 bitcast_convert_fusion
  0.7 0.1 pad_maximum_fusion.1.z
  0.8 0.0 collective-permute-start.1
  0.8 1.2 %collective-permute-done.1 = bf16[16,128]{1,0:T(8,128)(2,1)S(1)} collective-permute-done((bf16[16,128]{1,0:T(8,128)(2,1)S(1)}, bf16[16,128]{1,0:T(8,128)(2,1)S(1)}, u32[]{:S(2)}, u32[]{:S(2)}) %collective-permute-start.1) | collective-permute-done | bytes 4128 | tf_op jit(solution)/shard_map/ppermute | solution.py:303
  2.0 0.2 collective-permute-start.6
  2.2 2.8 %collective-permute-start.2 = (bf16[2,16,128]{2,1,0:T(8,128)(2,1)S(1)}, bf16[2,16,128]{2,1,0:T(8,128)(2,1)S(1)}, u32[]{:S(2)}, u32[]{:S(2)}) collective-permute-start(bf16[2,16,128]{2,1,0:T(8,128)(2,1)S(1)} %pad_maximum_fusion.after.z0), channel_id=1, source_target_pairs={{0,6},{2,0},{4,2},{6,4},{1,7},{3,1},{5,3},{7,5},{8,14},{10,8},{12,... | collective-permute-start | bytes 24584 | tf_op jit(solution)/shard_map/ppermute | solution.py:299
  4.9 0.8 collective-permute-start.3
  5.7 0.9 collective-permute-start.4
  7.3 3.3 %shard_map.109 = (f32[4,8,32,128]{3,2,1,0:T(8,128)S(1)}, bf16[128,3072]{1,0:T(8,128)(2,1)S(1)}, f32[8,3072]{1,0:T(8,128)S(1)}, bf16[64,3072]{1,0:T(8,128)(2,1)S(1)}, bf16[3072,1152]{1,0:T(8,128)(2,1)S(1)}) custom-call(s32[1]{0:T(128)S(6)} %copy.12.step, bf16[2,16,128]{2,1,0:T(8,128)(2,1)S(1)} %pad_maximum_fusion.after.z0, s32[2,256]{1,0:T(2,128)} %bitcast.12, ...), custom_call_target="tpu_custom_call" | custom-call | tf_op jit(solution)/shard_map/pallas_call | solution.py:315
  10.6 0.0 collective-permute-done.2.z1
  10.6 0.0 collective-permute-done.3.z2
  10.6 0.0 collective-permute-done.4.z3
  10.6 3.6 %shard_map.110 = (bf16[128,384]{1,0:T(8,128)(2,1)S(1)}, bf16[128,384]{1,0:T(8,128)(2,1)S(1)}) custom-call(bf16[2,16,128]{2,1,0:T(8,128)(2,1)S(1)} %pad_maximum_fusion.after.z0, bf16[2,16,128]{2,1,0:T(8,128)(2,1)S(1)} %collective-permute-done.2.z1, bf16[2,16,128]{2,1,0:T(8,128)(2,1)S(1)} %collective-permute-done.3.z2, ...), custom_call_target="tpu_custom_call" | custom-call | tf_op jit(solution)/shard_map/pallas_call | solution.py:333
  14.3 0.1 collective-permute-start.5
  14.4 1.7 %shard_map.111 = (bf16[384,3072]{1,0:T(8,128)(2,1)S(1)}, bf16[64,3072]{1,0:T(8,128)(2,1)S(1)}, f32[32,64]{1,0:T(8,128)S(1)}) custom-call(bf16[128,384]{1,0:T(8,128)(2,1)S(1)} %get-tuple-element.34.after, bf16[384,3072]{1,0:T(8,128)(2,1)} %refs_0_.1, bf16[64,3072]{1,0:T(8,128)(2,1)} %bitcast.9, f32[32,64]{1,0:T(8,128)} %bitcast.10), custom_call_target="tpu_custom_call" | custom-call | tf_op jit(solution)/shard_map/pallas_call | solution.py:337
  16.1 0.0 collective-permute-done.5.peer
  16.1 0.0 collective-permute-done.6.w_peer
  16.1 0.8 shard_map.112
  16.9 1.9 %collective-permute-start.7 = (bf16[32,3072]{1,0:T(8,128)(2,1)S(1)}, bf16[32,3072]{1,0:T(8,128)(2,1)S(1)}, u32[]{:S(2)}, u32[]{:S(2)}) collective-permute-start(bf16[32,3072]{1,0:T(8,128)(2,1)S(1)} %get-tuple-element.40), channel_id=1, source_target_pairs={{0,4},{2,6},{4,0},{6,2},{1,5},{3,7},{5,1},{7,3},{8,12},{10,14},{12... | collective-permute-start | bytes 589832 | tf_op jit(solution)/shard_map/ppermute | solution.py:299
  18.9 1.4 %collective-permute-start.8 = (bf16[32,3072]{1,0:T(8,128)(2,1)S(1)}, bf16[32,3072]{1,0:T(8,128)(2,1)S(1)}, u32[]{:S(2)}, u32[]{:S(2)}) collective-permute-start(bf16[32,3072]{1,0:T(8,128)(2,1)S(1)} %get-tuple-element.41), channel_id=1, source_target_pairs={{0,2},{2,4},{4,6},{6,0},{1,3},{3,5},{5,7},{7,1},{8,10},{10,12},{12... | collective-permute-start | bytes 589832 | tf_op jit(solution)/shard_map/ppermute | solution.py:299
  20.2 1.9 %collective-permute-start.9 = (bf16[32,3072]{1,0:T(8,128)(2,1)S(1)}, bf16[32,3072]{1,0:T(8,128)(2,1)S(1)}, u32[]{:S(2)}, u32[]{:S(2)}) collective-permute-start(bf16[32,3072]{1,0:T(8,128)(2,1)S(1)} %get-tuple-element.42), channel_id=1, source_target_pairs={{0,6},{2,0},{4,2},{6,4},{1,7},{3,1},{5,3},{7,5},{8,14},{10,8},{12,... | collective-permute-start | bytes 589832 | tf_op jit(solution)/shard_map/ppermute | solution.py:299
  22.1 0.6 collective-permute-start
  24.1 0.0 collective-permute-done.high
  24.1 2.2 %collective-permute-done.7.p1 = bf16[32,3072]{1,0:T(8,128)(2,1)S(1)} collective-permute-done((bf16[32,3072]{1,0:T(8,128)(2,1)S(1)}, bf16[32,3072]{1,0:T(8,128)(2,1)S(1)}, u32[]{:S(2)}, u32[]{:S(2)}) %collective-permute-start.7) | collective-permute-done | bytes 196640 | tf_op jit(solution)/shard_map/ppermute | solution.py:299
  26.3 3.8 %collective-permute-done.8.p2 = bf16[32,3072]{1,0:T(8,128)(2,1)S(1)} collective-permute-done((bf16[32,3072]{1,0:T(8,128)(2,1)S(1)}, bf16[32,3072]{1,0:T(8,128)(2,1)S(1)}, u32[]{:S(2)}, u32[]{:S(2)}) %collective-permute-start.8) | collective-permute-done | bytes 196640 | tf_op jit(solution)/shard_map/ppermute | solution.py:299
  30.0 0.0 collective-permute-done.9.p3
  30.0 0.7 shard_map.113
  30.8 21.1 %all_to_all.15.got = bf16[32,16,128]{2,1,0:T(8,128)(2,1)S(1)} all-to-all(bf16[32,16,128]{2,1,0:T(8,128)(2,1)S(1)} %shard_map.113), channel_id=1, replica_groups=mesh['y'=4,'z'=8,'x'=4,'c'=2] {'y','z'}, dimensions={0} | all-to-all | bytes 262144 | tf_op jit(solution)/shard_map/all_to_all | solution.py:353
  51.9 8.8 %all_to_all.16.zg = bf16[8,16,128]{2,1,0:T(8,128)(2,1)S(1)} all-to-all(bf16[8,16,128]{2,1,0:T(8,128)(2,1)S(1)} %get-tuple-element.46), channel_id=1, replica_groups=mesh['y'=4,'z'=8,'x'=4,'c'=2] {'x','c'}, dimensions={0} | all-to-all | bytes 65536 | tf_op jit(solution)/shard_map/all_to_all | solution.py:359
  60.7 3.6 %shard_map.115 = (bf16[128,384]{1,0:T(8,128)(2,1)S(1)}, bf16[128,384]{1,0:T(8,128)(2,1)S(1)}) custom-call(bf16[8,16,128]{2,1,0:T(8,128)(2,1)S(1)} %all_to_all.16.zg, f32[4,8,32,128]{3,2,1,0:T(8,128)S(1)} %get-tuple-element.30.rest_0_, bf16[128,3072]{1,0:T(8,128)(2,1)S(1)} %get-tuple-element.31.rest_1_, f32[8,3072]{1,0:T(8,128)S(1)} %get-tuple-element.32.rest_2_.gate, ...), custom_call_target="tpu_custom_call" | custom-call | tf_op jit(solution)/shard_map/pallas_call | solution.py:360
  64.4 0.1 collective-permute-start.10
  64.5 1.3 %collective-permute-done.10.peer = bf16[128,384]{1,0:T(8,128)(2,1)S(1)} collective-permute-done((bf16[128,384]{1,0:T(8,128)(2,1)S(1)}, bf16[128,384]{1,0:T(8,128)(2,1)S(1)}, u32[]{:S(2)}, u32[]{:S(2)}) %collective-permute-start.10) | collective-permute-done | bytes 98336 | tf_op jit(solution)/shard_map/ppermute | solution.py:303
  65.8 0.8 shard_map.116
  66.6 1.2 %collective-permute-start.11 = (bf16[32,3072]{1,0:T(8,128)(2,1)S(1)}, bf16[32,3072]{1,0:T(8,128)(2,1)S(1)}, u32[]{:S(2)}, u32[]{:S(2)}) collective-permute-start(bf16[32,3072]{1,0:T(8,128)(2,1)S(1)} %get-tuple-element.50), channel_id=1, source_target_pairs={{0,4},{2,6},{4,0},{6,2},{1,5},{3,7},{5,1},{7,3},{8,12},{10,14},{12... | collective-permute-start | bytes 589832 | tf_op jit(solution)/shard_map/ppermute | solution.py:299
  67.8 0.9 collective-permute-start.12
  68.7 2.3 %collective-permute-start.13 = (bf16[32,3072]{1,0:T(8,128)(2,1)S(1)}, bf16[32,3072]{1,0:T(8,128)(2,1)S(1)}, u32[]{:S(2)}, u32[]{:S(2)}) collective-permute-start(bf16[32,3072]{1,0:T(8,128)(2,1)S(1)} %get-tuple-element.52), channel_id=1, source_target_pairs={{0,6},{2,0},{4,2},{6,4},{1,7},{3,1},{5,3},{7,5},{8,14},{10,8},{12,... | collective-permute-start | bytes 589832 | tf_op jit(solution)/shard_map/ppermute | solution.py:299
  71.0 5.0 %collective-permute-done.11.p1 = bf16[32,3072]{1,0:T(8,128)(2,1)S(1)} collective-permute-done((bf16[32,3072]{1,0:T(8,128)(2,1)S(1)}, bf16[32,3072]{1,0:T(8,128)(2,1)S(1)}, u32[]{:S(2)}, u32[]{:S(2)}) %collective-permute-start.11) | collective-permute-done | bytes 196640 | tf_op jit(solution)/shard_map/ppermute | solution.py:299
  76.0 3.4 %collective-permute-done.12.p2 = bf16[32,3072]{1,0:T(8,128)(2,1)S(1)} collective-permute-done((bf16[32,3072]{1,0:T(8,128)(2,1)S(1)}, bf16[32,3072]{1,0:T(8,128)(2,1)S(1)}, u32[]{:S(2)}, u32[]{:S(2)}) %collective-permute-start.12) | collective-permute-done | bytes 196640 | tf_op jit(solution)/shard_map/ppermute | solution.py:299
  79.3 0.0 collective-permute-done.13.p3
  79.3 0.7 shard_map.117
  80.1 14.0 %all_to_all.17.got = bf16[32,16,128]{2,1,0:T(8,128)(2,1)S(1)} all-to-all(bf16[32,16,128]{2,1,0:T(8,128)(2,1)S(1)} %get-tuple-element.54), channel_id=1, replica_groups=mesh['y'=4,'z'=8,'x'=4,'c'=2] {'y','z'}, dimensions={0} | all-to-all | bytes 262144 | tf_op jit(solution)/shard_map/all_to_all | solution.py:353
  94.1 0.7 shard_map.118
  (3 shorter events, 0.1 us)
Async XLA Ops:
  0.8 1.2 %collective-permute-start.1 = (bf16[16,128]{1,0:T(8,128)(2,1)S(1)}, bf16[16,128]{1,0:T(8,128)(2,1)S(1)}, u32[]{:S(2)}, u32[]{:S(2)}) collective-permute-start(bf16[16,128]{1,0:T(8,128)(2,1)S(1)} %pad_maximum_fusion.1.z), channel_id=1, source_target_pairs={{0,1},{1,0},{2,3},{3,2},{4,5},{5,4},{6,7},{7,6},{8,9},{9,8},{10,11... | collective-permute-start | bytes 12296 | tf_op jit(solution)/shard_map/ppermute | solution.py:303
  2.0 14.1 %collective-permute-start.6 = (bf16[384,3072]{1,0:T(8,128)(2,1)}, bf16[384,3072]{1,0:T(8,128)(2,1)S(1)}, u32[]{:S(2)}, u32[]{:S(2)}) collective-permute-start(bf16[384,3072]{1,0:T(8,128)(2,1)} %refs_0_.1), channel_id=1, source_target_pairs={{0,1},{1,0},{2,3},{3,2},{4,5},{5,4},{6,7},{7,6},{8,9},{9,8},{10,11... | collective-permute-start | bytes 7077896 | tf_op jit(solution)/shard_map/ppermute | solution.py:303
  2.2 8.4 %collective-permute-start.2 = (bf16[2,16,128]{2,1,0:T(8,128)(2,1)S(1)}, bf16[2,16,128]{2,1,0:T(8,128)(2,1)S(1)}, u32[]{:S(2)}, u32[]{:S(2)}) collective-permute-start(bf16[2,16,128]{2,1,0:T(8,128)(2,1)S(1)} %pad_maximum_fusion.after.z0), channel_id=1, source_target_pairs={{0,6},{2,0},{4,2},{6,4},{1,7},{3,1},{5,3},{7,5},{8,14},{10,8},{12,... | collective-permute-start | bytes 24584 | tf_op jit(solution)/shard_map/ppermute | solution.py:299
  4.9 5.7 %collective-permute-start.3 = (bf16[2,16,128]{2,1,0:T(8,128)(2,1)S(1)}, bf16[2,16,128]{2,1,0:T(8,128)(2,1)S(1)}, u32[]{:S(2)}, u32[]{:S(2)}) collective-permute-start(bf16[2,16,128]{2,1,0:T(8,128)(2,1)S(1)} %pad_maximum_fusion.after.z0), channel_id=1, source_target_pairs={{0,4},{2,6},{4,0},{6,2},{1,5},{3,7},{5,1},{7,3},{8,12},{10,14},{12... | collective-permute-start | bytes 24584 | tf_op jit(solution)/shard_map/ppermute | solution.py:299
  5.7 4.9 %collective-permute-start.4 = (bf16[2,16,128]{2,1,0:T(8,128)(2,1)S(1)}, bf16[2,16,128]{2,1,0:T(8,128)(2,1)S(1)}, u32[]{:S(2)}, u32[]{:S(2)}) collective-permute-start(bf16[2,16,128]{2,1,0:T(8,128)(2,1)S(1)} %pad_maximum_fusion.after.z0), channel_id=1, source_target_pairs={{0,2},{2,4},{4,6},{6,0},{1,3},{3,5},{5,7},{7,1},{8,10},{10,12},{12... | collective-permute-start | bytes 24584 | tf_op jit(solution)/shard_map/ppermute | solution.py:299
  14.3 1.8 %collective-permute-start.5 = (bf16[128,384]{1,0:T(8,128)(2,1)S(1)}, bf16[128,384]{1,0:T(8,128)(2,1)S(1)}, u32[]{:S(2)}, u32[]{:S(2)}) collective-permute-start(bf16[128,384]{1,0:T(8,128)(2,1)S(1)} %get-tuple-element.34.after), channel_id=1, source_target_pairs={{0,1},{1,0},{2,3},{3,2},{4,5},{5,4},{6,7},{7,6},{8,9},{9,8},{10,11... | collective-permute-start | bytes 294920 | tf_op jit(solution)/shard_map/ppermute | solution.py:303
  16.9 9.3 %collective-permute-start.7 = (bf16[32,3072]{1,0:T(8,128)(2,1)S(1)}, bf16[32,3072]{1,0:T(8,128)(2,1)S(1)}, u32[]{:S(2)}, u32[]{:S(2)}) collective-permute-start(bf16[32,3072]{1,0:T(8,128)(2,1)S(1)} %get-tuple-element.40), channel_id=1, source_target_pairs={{0,4},{2,6},{4,0},{6,2},{1,5},{3,7},{5,1},{7,3},{8,12},{10,14},{12... | collective-permute-start | bytes 589832 | tf_op jit(solution)/shard_map/ppermute | solution.py:299
  18.9 11.2 %collective-permute-start.8 = (bf16[32,3072]{1,0:T(8,128)(2,1)S(1)}, bf16[32,3072]{1,0:T(8,128)(2,1)S(1)}, u32[]{:S(2)}, u32[]{:S(2)}) collective-permute-start(bf16[32,3072]{1,0:T(8,128)(2,1)S(1)} %get-tuple-element.41), channel_id=1, source_target_pairs={{0,2},{2,4},{4,6},{6,0},{1,3},{3,5},{5,7},{7,1},{8,10},{10,12},{12... | collective-permute-start | bytes 589832 | tf_op jit(solution)/shard_map/ppermute | solution.py:299
  20.2 9.8 %collective-permute-start.9 = (bf16[32,3072]{1,0:T(8,128)(2,1)S(1)}, bf16[32,3072]{1,0:T(8,128)(2,1)S(1)}, u32[]{:S(2)}, u32[]{:S(2)}) collective-permute-start(bf16[32,3072]{1,0:T(8,128)(2,1)S(1)} %get-tuple-element.42), channel_id=1, source_target_pairs={{0,6},{2,0},{4,2},{6,4},{1,7},{3,1},{5,3},{7,5},{8,14},{10,8},{12,... | collective-permute-start | bytes 589832 | tf_op jit(solution)/shard_map/ppermute | solution.py:299
  22.1 2.0 %collective-permute-start = (bf16[16,128]{1,0:T(8,128)(2,1)S(1)}, bf16[16,128]{1,0:T(8,128)(2,1)S(1)}, u32[]{:S(2)}, u32[]{:S(2)}) collective-permute-start(bf16[16,128]{1,0:T(8,128)(2,1)S(1)} %pad_maximum_fusion.1.z), channel_id=1, source_target_pairs={{0,248},{1,249},{2,250},{3,251},{4,252},{5,253},{6,254},{7,255}} | collective-permute-start | bytes 12296 | tf_op jit(solution)/shard_map/ppermute | solution.py:331
  64.4 1.4 %collective-permute-start.10 = (bf16[128,384]{1,0:T(8,128)(2,1)S(1)}, bf16[128,384]{1,0:T(8,128)(2,1)S(1)}, u32[]{:S(2)}, u32[]{:S(2)}) collective-permute-start(bf16[128,384]{1,0:T(8,128)(2,1)S(1)} %get-tuple-element.48), channel_id=1, source_target_pairs={{0,1},{1,0},{2,3},{3,2},{4,5},{5,4},{6,7},{7,6},{8,9},{9,8},{10,11... | collective-permute-start | bytes 294920 | tf_op jit(solution)/shard_map/ppermute | solution.py:303
  66.6 9.4 %collective-permute-start.11 = (bf16[32,3072]{1,0:T(8,128)(2,1)S(1)}, bf16[32,3072]{1,0:T(8,128)(2,1)S(1)}, u32[]{:S(2)}, u32[]{:S(2)}) collective-permute-start(bf16[32,3072]{1,0:T(8,128)(2,1)S(1)} %get-tuple-element.50), channel_id=1, source_target_pairs={{0,4},{2,6},{4,0},{6,2},{1,5},{3,7},{5,1},{7,3},{8,12},{10,14},{12... | collective-permute-start | bytes 589832 | tf_op jit(solution)/shard_map/ppermute | solution.py:299
  67.8 11.6 %collective-permute-start.12 = (bf16[32,3072]{1,0:T(8,128)(2,1)S(1)}, bf16[32,3072]{1,0:T(8,128)(2,1)S(1)}, u32[]{:S(2)}, u32[]{:S(2)}) collective-permute-start(bf16[32,3072]{1,0:T(8,128)(2,1)S(1)} %get-tuple-element.51), channel_id=1, source_target_pairs={{0,2},{2,4},{4,6},{6,0},{1,3},{3,5},{5,7},{7,1},{8,10},{10,12},{12... | collective-permute-start | bytes 589832 | tf_op jit(solution)/shard_map/ppermute | solution.py:299
  68.7 10.6 %collective-permute-start.13 = (bf16[32,3072]{1,0:T(8,128)(2,1)S(1)}, bf16[32,3072]{1,0:T(8,128)(2,1)S(1)}, u32[]{:S(2)}, u32[]{:S(2)}) collective-permute-start(bf16[32,3072]{1,0:T(8,128)(2,1)S(1)} %get-tuple-element.52), channel_id=1, source_target_pairs={{0,6},{2,0},{4,2},{6,4},{1,7},{3,1},{5,3},{7,5},{8,14},{10,8},{12,... | collective-permute-start | bytes 589832 | tf_op jit(solution)/shard_map/ppermute | solution.py:299

commit v8 on v7

--- a/solution.py
+++ b/solution.py
@@ -118,18 +118,6 @@
 ]
 
 
-def late_kernel(after, *refs):
-    count = len(refs) // 2
-    sems = refs[-1]
-    copies = [
-        pltpu.make_async_copy(refs[i], refs[count + i], sems.at[i]) for i in range(count)
-    ]
-    for copy in copies:
-        copy.start()
-    for copy in copies:
-        copy.wait()
-
-
 def block_body(chunk_of, tab, wc, rows, w_qkv, mine, send, zs, es, fs, qkv, qs):
     my_x, my_c = lax.axis_index("x"), lax.axis_index("c")
     order = [((my_x + r % 4) % 4) * 2 + (my_c + r // 4) % 2 for r in range(8)]
@@ -333,13 +321,7 @@
     mine, send = call(first_kernel, [half, half], [VM] * 8, BLOCK_SCRATCH, limit=16)(
         *zg, tab, wc, rows, w_qkv
     )
-    operands = (w_out, w_fin.T, state)
-    w_out, w_fin_rows, state = call(
-        late_kernel,
-        [kept(x.shape, x.dtype) for x in operands],
-        [VM] + [HB] * 3,
-        [pltpu.SemaphoreType.DMA((3,))],
-    )(send, *[far(x) for x in operands])
+    w_fin_rows = w_fin.T
 
     def gathered_drifts(mine, send, z, *extra):
         operands = (mine, swap_cores(send), w_out, w_peer)
@@ -350,7 +332,8 @@
             [shape((NY * NZ, 16, 128), BF), *extra],
             [SM, SM] + [VM] * 10,
         )(step_sizes, slide, high, state, z, *got, w_in, rows, w_fin_rows)
-        return lax.all_to_all(outs, ("y", "z"), 0, 0, tiled=True), *extra
+        got = lax.all_to_all(outs, ("y", "z"), 0, 0, tiled=True)
+        return got, *extra
 
     (got,) = gathered_drifts(mine, send, z)
     z, copies = call(

time: 95.4 us -> 94.6 us (level)
  Pallas kernels: 16.2 us -> 14.5 us
    pallas_call x1 -> x0, Pallas kernels: 1.74 us -> none  [local(): call(late_kernel, [kept(x.shape, x.dtype) for x in operands], [VM] + [HB]...]
    ppermute x4, waiting for transfers between devices: 2.45 us -> 3.73 us  [swap_cores(): return lax.ppermute(x, 'c', [(0, 1), (1, 0)])]
  transfers between devices with their start and end apart: 14 -> 14, of which waited for: 6 -> 7; matrix products, arithmetic and copies ran while one was open for 0% -> 0% of each run, Pallas kernels for 9% -> 7%
where the time goes in v8:
time: 94.6 us; the launch traced here: 94.1 us
  blocking collectives  43.9 us (46%)
  waiting for transfers between devices  17.7 us (19%)
  starting transfers between devices  15 us (16%)
  Pallas kernels  14.5 us (15%)
  between operations  2.1 us (2%)
    all_to_all x2, blocking collectives, gathered_drifts(): got = lax.all_to_all(outs, ('y', 'z'), 0, 0, tiled=True)  35.1 us
    ppermute x9, waiting for transfers between devices, to_right(): return lax.ppermute(x, 'x', [(i, (i + k) % NX) for i in range(NX)])  14 us
    ppermute x9, starting transfers between devices, to_right(): return lax.ppermute(x, 'x', [(i, (i + k) % NX) for i in range(NX)])  14 us
    all_to_all x1, blocking collectives, local(): zg = lax.all_to_all(copies, ('x', 'c'), 0, 0, tiled=True)  8.86 us
    ppermute x4, waiting for transfers between devices, swap_cores(): return lax.ppermute(x, 'c', [(0, 1), (1, 0)])  3.73 us
    pallas_call x1, Pallas kernels, local(): call(second_kernel, [half, half], [VM] * 5, BLOCK_SCRATCH, limit=16)  3.66 us
    pallas_call x1, Pallas kernels, local(): call(first_kernel, [half, half], [VM] * 8, BLOCK_SCRATCH, limit=16)  3.65 us
    pallas_call x1, Pallas kernels, local(): call(prepare_kernel, [kept((4, 8, ROWS, HD), F32), kept((2 * C, D), BF),...  3.32 us
  transfers between devices with their start and end apart: 14, of which 7 were waited for; matrix products, arithmetic and copies ran while one was open for 0% of the time, Pallas kernels for 7%

profile of v8, /device:TPU:32, one launch (start us, length us, event | category | flops | bytes accessed | tf_op | source)
XLA Modules:
  0.0 94.1 jit_solution(8438137603263585695)
XLA Ops:
  0.0 0.7 bitcast_convert_fusion
  0.7 0.1 pad_maximum_fusion.1.z
  0.8 0.0 collective-permute-start.1
  0.8 1.2 %collective-permute-done.1 = bf16[16,128]{1,0:T(8,128)(2,1)S(1)} collective-permute-done((bf16[16,128]{1,0:T(8,128)(2,1)S(1)}, bf16[16,128]{1,0:T(8,128)(2,1)S(1)}, u32[]{:S(2)}, u32[]{:S(2)}) %collective-permute-start.1) | collective-permute-done | bytes 4128 | tf_op jit(solution)/shard_map/ppermute | solution.py:291
  2.0 0.2 collective-permute-start.6
  2.2 2.8 %collective-permute-start.2 = (bf16[2,16,128]{2,1,0:T(8,128)(2,1)S(1)}, bf16[2,16,128]{2,1,0:T(8,128)(2,1)S(1)}, u32[]{:S(2)}, u32[]{:S(2)}) collective-permute-start(bf16[2,16,128]{2,1,0:T(8,128)(2,1)S(1)} %pad_maximum_fusion.after.z0), channel_id=1, source_target_pairs={{0,6},{2,0},{4,2},{6,4},{1,7},{3,1},{5,3},{7,5},{8,14},{10,8},{12,... | collective-permute-start | bytes 24584 | tf_op jit(solution)/shard_map/ppermute | solution.py:287
  4.9 0.8 collective-permute-start.3
  5.7 0.9 collective-permute-start.4
  7.3 3.3 %shard_map.109 = (f32[4,8,32,128]{3,2,1,0:T(8,128)S(1)}, bf16[128,3072]{1,0:T(8,128)(2,1)S(1)}, f32[8,3072]{1,0:T(8,128)S(1)}, bf16[64,3072]{1,0:T(8,128)(2,1)S(1)}, bf16[3072,1152]{1,0:T(8,128)(2,1)S(1)}) custom-call(s32[1]{0:T(128)S(6)} %copy.12.step, bf16[2,16,128]{2,1,0:T(8,128)(2,1)S(1)} %pad_maximum_fusion.after.z0, s32[2,256]{1,0:T(2,128)} %bitcast.14, ...), custom_call_target="tpu_custom_call" | custom-call | tf_op jit(solution)/shard_map/pallas_call | solution.py:303
  10.6 0.0 collective-permute-done.2.z1
  10.6 0.0 collective-permute-done.3.z2
  10.6 0.0 collective-permute-done.4.z3
  10.6 0.0 copy-start
  10.6 3.6 %shard_map.110 = (bf16[128,384]{1,0:T(8,128)(2,1)S(1)}, bf16[128,384]{1,0:T(8,128)(2,1)S(1)}) custom-call(bf16[2,16,128]{2,1,0:T(8,128)(2,1)S(1)} %pad_maximum_fusion.after.z0, bf16[2,16,128]{2,1,0:T(8,128)(2,1)S(1)} %collective-permute-done.2.z1, bf16[2,16,128]{2,1,0:T(8,128)(2,1)S(1)} %collective-permute-done.3.z2, ...), custom_call_target="tpu_custom_call" | custom-call | tf_op jit(solution)/shard_map/pallas_call | solution.py:321
  14.3 0.1 collective-permute-start.5
  14.4 1.3 %collective-permute-done.5.peer = bf16[128,384]{1,0:T(8,128)(2,1)S(1)} collective-permute-done((bf16[128,384]{1,0:T(8,128)(2,1)S(1)}, bf16[128,384]{1,0:T(8,128)(2,1)S(1)}, u32[]{:S(2)}, u32[]{:S(2)}) %collective-permute-start.5) | collective-permute-done | bytes 98336 | tf_op jit(solution)/shard_map/ppermute | solution.py:291
  15.7 0.0 collective-permute-done.6.w_peer
  15.7 0.0 copy-done
  15.7 0.0 copy-start.1
  15.7 0.0 copy-start.2
  15.7 0.8 shard_map.111
  16.5 1.9 %collective-permute-start.7 = (bf16[32,3072]{1,0:T(8,128)(2,1)S(1)}, bf16[32,3072]{1,0:T(8,128)(2,1)S(1)}, u32[]{:S(2)}, u32[]{:S(2)}) collective-permute-start(bf16[32,3072]{1,0:T(8,128)(2,1)S(1)} %get-tuple-element.35), channel_id=1, source_target_pairs={{0,4},{2,6},{4,0},{6,2},{1,5},{3,7},{5,1},{7,3},{8,12},{10,14},{12... | collective-permute-start | bytes 589832 | tf_op jit(solution)/shard_map/ppermute | solution.py:287
  18.4 1.3 %collective-permute-start.8 = (bf16[32,3072]{1,0:T(8,128)(2,1)S(1)}, bf16[32,3072]{1,0:T(8,128)(2,1)S(1)}, u32[]{:S(2)}, u32[]{:S(2)}) collective-permute-start(bf16[32,3072]{1,0:T(8,128)(2,1)S(1)} %get-tuple-element.36), channel_id=1, source_target_pairs={{0,2},{2,4},{4,6},{6,0},{1,3},{3,5},{5,7},{7,1},{8,10},{10,12},{12... | collective-permute-start | bytes 589832 | tf_op jit(solution)/shard_map/ppermute | solution.py:287
  19.8 1.9 %collective-permute-start.9 = (bf16[32,3072]{1,0:T(8,128)(2,1)S(1)}, bf16[32,3072]{1,0:T(8,128)(2,1)S(1)}, u32[]{:S(2)}, u32[]{:S(2)}) collective-permute-start(bf16[32,3072]{1,0:T(8,128)(2,1)S(1)} %get-tuple-element.37), channel_id=1, source_target_pairs={{0,6},{2,0},{4,2},{6,4},{1,7},{3,1},{5,3},{7,5},{8,14},{10,8},{12,... | collective-permute-start | bytes 589832 | tf_op jit(solution)/shard_map/ppermute | solution.py:287
  21.7 0.6 collective-permute-start
  23.6 0.0 collective-permute-done.high
  23.6 2.3 %collective-permute-done.7.p1 = bf16[32,3072]{1,0:T(8,128)(2,1)S(1)} collective-permute-done((bf16[32,3072]{1,0:T(8,128)(2,1)S(1)}, bf16[32,3072]{1,0:T(8,128)(2,1)S(1)}, u32[]{:S(2)}, u32[]{:S(2)}) %collective-permute-start.7) | collective-permute-done | bytes 196640 | tf_op jit(solution)/shard_map/ppermute | solution.py:287
  25.9 3.4 %collective-permute-done.8.p2 = bf16[32,3072]{1,0:T(8,128)(2,1)S(1)} collective-permute-done((bf16[32,3072]{1,0:T(8,128)(2,1)S(1)}, bf16[32,3072]{1,0:T(8,128)(2,1)S(1)}, u32[]{:S(2)}, u32[]{:S(2)}) %collective-permute-start.8) | collective-permute-done | bytes 196640 | tf_op jit(solution)/shard_map/ppermute | solution.py:287
  29.3 0.0 collective-permute-done.9.p3
  29.3 0.0 copy-done.1
  29.3 0.0 copy-done.2
  29.3 0.7 shard_map.112
  30.0 21.1 %all_to_all.15.got = bf16[32,16,128]{2,1,0:T(8,128)(2,1)S(1)} all-to-all(bf16[32,16,128]{2,1,0:T(8,128)(2,1)S(1)} %shard_map.112), channel_id=1, replica_groups=mesh['y'=4,'z'=8,'x'=4,'c'=2] {'y','z'}, dimensions={0} | all-to-all | bytes 262144 | tf_op jit(solution)/shard_map/all_to_all | solution.py:335
  51.1 8.9 %all_to_all.16.zg = bf16[8,16,128]{2,1,0:T(8,128)(2,1)S(1)} all-to-all(bf16[8,16,128]{2,1,0:T(8,128)(2,1)S(1)} %get-tuple-element.40), channel_id=1, replica_groups=mesh['y'=4,'z'=8,'x'=4,'c'=2] {'x','c'}, dimensions={0} | all-to-all | bytes 65536 | tf_op jit(solution)/shard_map/all_to_all | solution.py:342
  60.0 3.7 %shard_map.114 = (bf16[128,384]{1,0:T(8,128)(2,1)S(1)}, bf16[128,384]{1,0:T(8,128)(2,1)S(1)}) custom-call(bf16[8,16,128]{2,1,0:T(8,128)(2,1)S(1)} %all_to_all.16.zg, f32[4,8,32,128]{3,2,1,0:T(8,128)S(1)} %get-tuple-element.27.rest_0_, bf16[128,3072]{1,0:T(8,128)(2,1)S(1)} %get-tuple-element.28.rest_1_, f32[8,3072]{1,0:T(8,128)S(1)} %get-tuple-element.29.rest_2_.gate, ...), custom_call_target="tpu_custom_call" | custom-call | tf_op jit(solution)/shard_map/pallas_call | solution.py:343
  63.6 0.1 collective-permute-start.10
  63.7 1.3 %collective-permute-done.10.peer = bf16[128,384]{1,0:T(8,128)(2,1)S(1)} collective-permute-done((bf16[128,384]{1,0:T(8,128)(2,1)S(1)}, bf16[128,384]{1,0:T(8,128)(2,1)S(1)}, u32[]{:S(2)}, u32[]{:S(2)}) %collective-permute-start.10) | collective-permute-done | bytes 98336 | tf_op jit(solution)/shard_map/ppermute | solution.py:291
  65.0 0.8 shard_map.115
  65.8 1.2 %collective-permute-start.11 = (bf16[32,3072]{1,0:T(8,128)(2,1)S(1)}, bf16[32,3072]{1,0:T(8,128)(2,1)S(1)}, u32[]{:S(2)}, u32[]{:S(2)}) collective-permute-start(bf16[32,3072]{1,0:T(8,128)(2,1)S(1)} %get-tuple-element.44), channel_id=1, source_target_pairs={{0,4},{2,6},{4,0},{6,2},{1,5},{3,7},{5,1},{7,3},{8,12},{10,14},{12... | collective-permute-start | bytes 589832 | tf_op jit(solution)/shard_map/ppermute | solution.py:287
  67.0 0.9 %collective-permute-start.12 = (bf16[32,3072]{1,0:T(8,128)(2,1)S(1)}, bf16[32,3072]{1,0:T(8,128)(2,1)S(1)}, u32[]{:S(2)}, u32[]{:S(2)}) collective-permute-start(bf16[32,3072]{1,0:T(8,128)(2,1)S(1)} %get-tuple-element.45), channel_id=1, source_target_pairs={{0,2},{2,4},{4,6},{6,0},{1,3},{3,5},{5,7},{7,1},{8,10},{10,12},{12... | collective-permute-start | bytes 589832 | tf_op jit(solution)/shard_map/ppermute | solution.py:287
  67.9 2.3 %collective-permute-start.13 = (bf16[32,3072]{1,0:T(8,128)(2,1)S(1)}, bf16[32,3072]{1,0:T(8,128)(2,1)S(1)}, u32[]{:S(2)}, u32[]{:S(2)}) collective-permute-start(bf16[32,3072]{1,0:T(8,128)(2,1)S(1)} %get-tuple-element.46), channel_id=1, source_target_pairs={{0,6},{2,0},{4,2},{6,4},{1,7},{3,1},{5,3},{7,5},{8,14},{10,8},{12,... | collective-permute-start | bytes 589832 | tf_op jit(solution)/shard_map/ppermute | solution.py:287
  70.2 5.0 %collective-permute-done.11.p1 = bf16[32,3072]{1,0:T(8,128)(2,1)S(1)} collective-permute-done((bf16[32,3072]{1,0:T(8,128)(2,1)S(1)}, bf16[32,3072]{1,0:T(8,128)(2,1)S(1)}, u32[]{:S(2)}, u32[]{:S(2)}) %collective-permute-start.11) | collective-permute-done | bytes 196640 | tf_op jit(solution)/shard_map/ppermute | solution.py:287
  75.2 3.4 %collective-permute-done.12.p2 = bf16[32,3072]{1,0:T(8,128)(2,1)S(1)} collective-permute-done((bf16[32,3072]{1,0:T(8,128)(2,1)S(1)}, bf16[32,3072]{1,0:T(8,128)(2,1)S(1)}, u32[]{:S(2)}, u32[]{:S(2)}) %collective-permute-start.12) | collective-permute-done | bytes 196640 | tf_op jit(solution)/shard_map/ppermute | solution.py:287
  78.6 0.0 collective-permute-done.13.p3
  78.6 0.7 shard_map.116
  79.3 14.0 %all_to_all.17.got = bf16[32,16,128]{2,1,0:T(8,128)(2,1)S(1)} all-to-all(bf16[32,16,128]{2,1,0:T(8,128)(2,1)S(1)} %get-tuple-element.48), channel_id=1, replica_groups=mesh['y'=4,'z'=8,'x'=4,'c'=2] {'y','z'}, dimensions={0} | all-to-all | bytes 262144 | tf_op jit(solution)/shard_map/all_to_all | solution.py:335
  93.4 0.7 shard_map.117
  (3 shorter events, 0.1 us)
Async XLA Ops:
  0.8 1.2 %collective-permute-start.1 = (bf16[16,128]{1,0:T(8,128)(2,1)S(1)}, bf16[16,128]{1,0:T(8,128)(2,1)S(1)}, u32[]{:S(2)}, u32[]{:S(2)}) collective-permute-start(bf16[16,128]{1,0:T(8,128)(2,1)S(1)} %pad_maximum_fusion.1.z), channel_id=1, source_target_pairs={{0,1},{1,0},{2,3},{3,2},{4,5},{5,4},{6,7},{7,6},{8,9},{9,8},{10,11... | collective-permute-start | bytes 12296 | tf_op jit(solution)/shard_map/ppermute | solution.py:291
  2.0 13.7 %collective-permute-start.6 = (bf16[384,3072]{1,0:T(8,128)(2,1)}, bf16[384,3072]{1,0:T(8,128)(2,1)S(1)}, u32[]{:S(2)}, u32[]{:S(2)}) collective-permute-start(bf16[384,3072]{1,0:T(8,128)(2,1)} %w_mine.3), channel_id=1, source_target_pairs={{0,1},{1,0},{2,3},{3,2},{4,5},{5,4},{6,7},{7,6},{8,9},{9,8},{10,11... | collective-permute-start | bytes 7077896 | tf_op jit(solution)/shard_map/ppermute | solution.py:291
  2.2 8.4 %collective-permute-start.2 = (bf16[2,16,128]{2,1,0:T(8,128)(2,1)S(1)}, bf16[2,16,128]{2,1,0:T(8,128)(2,1)S(1)}, u32[]{:S(2)}, u32[]{:S(2)}) collective-permute-start(bf16[2,16,128]{2,1,0:T(8,128)(2,1)S(1)} %pad_maximum_fusion.after.z0), channel_id=1, source_target_pairs={{0,6},{2,0},{4,2},{6,4},{1,7},{3,1},{5,3},{7,5},{8,14},{10,8},{12,... | collective-permute-start | bytes 24584 | tf_op jit(solution)/shard_map/ppermute | solution.py:287
  4.9 5.7 %collective-permute-start.3 = (bf16[2,16,128]{2,1,0:T(8,128)(2,1)S(1)}, bf16[2,16,128]{2,1,0:T(8,128)(2,1)S(1)}, u32[]{:S(2)}, u32[]{:S(2)}) collective-permute-start(bf16[2,16,128]{2,1,0:T(8,128)(2,1)S(1)} %pad_maximum_fusion.after.z0), channel_id=1, source_target_pairs={{0,4},{2,6},{4,0},{6,2},{1,5},{3,7},{5,1},{7,3},{8,12},{10,14},{12... | collective-permute-start | bytes 24584 | tf_op jit(solution)/shard_map/ppermute | solution.py:287
  5.7 4.9 %collective-permute-start.4 = (bf16[2,16,128]{2,1,0:T(8,128)(2,1)S(1)}, bf16[2,16,128]{2,1,0:T(8,128)(2,1)S(1)}, u32[]{:S(2)}, u32[]{:S(2)}) collective-permute-start(bf16[2,16,128]{2,1,0:T(8,128)(2,1)S(1)} %pad_maximum_fusion.after.z0), channel_id=1, source_target_pairs={{0,2},{2,4},{4,6},{6,0},{1,3},{3,5},{5,7},{7,1},{8,10},{10,12},{12... | collective-permute-start | bytes 24584 | tf_op jit(solution)/shard_map/ppermute | solution.py:287
  10.6 5.1 %copy-start = (bf16[384,3072]{1,0:T(8,128)(2,1)S(1)}, bf16[384,3072]{1,0:T(8,128)(2,1)}, u32[]{:S(2)}) copy-start(bf16[384,3072]{1,0:T(8,128)(2,1)} %w_mine.3) | copy-start | bytes 7077892
  14.3 1.4 %collective-permute-start.5 = (bf16[128,384]{1,0:T(8,128)(2,1)S(1)}, bf16[128,384]{1,0:T(8,128)(2,1)S(1)}, u32[]{:S(2)}, u32[]{:S(2)}) collective-permute-start(bf16[128,384]{1,0:T(8,128)(2,1)S(1)} %get-tuple-element.32), channel_id=1, source_target_pairs={{0,1},{1,0},{2,3},{3,2},{4,5},{5,4},{6,7},{7,6},{8,9},{9,8},{10,11... | collective-permute-start | bytes 294920 | tf_op jit(solution)/shard_map/ppermute | solution.py:291
  15.7 13.6 %copy-start.1 = (bf16[3072,64]{0,1:T(8,128)(2,1)S(1)}, bf16[3072,64]{0,1:T(8,128)(2,1)}, u32[]{:S(2)}) copy-start(bf16[3072,64]{0,1:T(8,128)(2,1)} %param.21) | copy-start | bytes 1179652
  15.7 13.6 %copy-start.2 = (f32[1,32,64]{2,1,0:T(8,128)S(1)}, f32[1,32,64]{2,1,0:T(8,128)}, u32[]{:S(2)}) copy-start(f32[1,32,64]{2,1,0:T(8,128)} %param.11) | copy-start | bytes 24580
  16.5 9.4 %collective-permute-start.7 = (bf16[32,3072]{1,0:T(8,128)(2,1)S(1)}, bf16[32,3072]{1,0:T(8,128)(2,1)S(1)}, u32[]{:S(2)}, u32[]{:S(2)}) collective-permute-start(bf16[32,3072]{1,0:T(8,128)(2,1)S(1)} %get-tuple-element.35), channel_id=1, source_target_pairs={{0,4},{2,6},{4,0},{6,2},{1,5},{3,7},{5,1},{7,3},{8,12},{10,14},{12... | collective-permute-start | bytes 589832 | tf_op jit(solution)/shard_map/ppermute | solution.py:287
  18.4 10.8 %collective-permute-start.8 = (bf16[32,3072]{1,0:T(8,128)(2,1)S(1)}, bf16[32,3072]{1,0:T(8,128)(2,1)S(1)}, u32[]{:S(2)}, u32[]{:S(2)}) collective-permute-start(bf16[32,3072]{1,0:T(8,128)(2,1)S(1)} %get-tuple-element.36), channel_id=1, source_target_pairs={{0,2},{2,4},{4,6},{6,0},{1,3},{3,5},{5,7},{7,1},{8,10},{10,12},{12... | collective-permute-start | bytes 589832 | tf_op jit(solution)/shard_map/ppermute | solution.py:287
  19.8 9.5 %collective-permute-start.9 = (bf16[32,3072]{1,0:T(8,128)(2,1)S(1)}, bf16[32,3072]{1,0:T(8,128)(2,1)S(1)}, u32[]{:S(2)}, u32[]{:S(2)}) collective-permute-start(bf16[32,3072]{1,0:T(8,128)(2,1)S(1)} %get-tuple-element.37), channel_id=1, source_target_pairs={{0,6},{2,0},{4,2},{6,4},{1,7},{3,1},{5,3},{7,5},{8,14},{10,8},{12,... | collective-permute-start | bytes 589832 | tf_op jit(solution)/shard_map/ppermute | solution.py:287
  21.7 2.0 %collective-permute-start = (bf16[16,128]{1,0:T(8,128)(2,1)S(1)}, bf16[16,128]{1,0:T(8,128)(2,1)S(1)}, u32[]{:S(2)}, u32[]{:S(2)}) collective-permute-start(bf16[16,128]{1,0:T(8,128)(2,1)S(1)} %pad_maximum_fusion.1.z), channel_id=1, source_target_pairs={{0,248},{1,249},{2,250},{3,251},{4,252},{5,253},{6,254},{7,255}} | collective-permute-start | bytes 12296 | tf_op jit(solution)/shard_map/ppermute | solution.py:319
  63.6 1.4 %collective-permute-start.10 = (bf16[128,384]{1,0:T(8,128)(2,1)S(1)}, bf16[128,384]{1,0:T(8,128)(2,1)S(1)}, u32[]{:S(2)}, u32[]{:S(2)}) collective-permute-start(bf16[128,384]{1,0:T(8,128)(2,1)S(1)} %get-tuple-element.42), channel_id=1, source_target_pairs={{0,1},{1,0},{2,3},{3,2},{4,5},{5,4},{6,7},{7,6},{8,9},{9,8},{10,11... | collective-permute-start | bytes 294920 | tf_op jit(solution)/shard_map/ppermute | solution.py:291
  65.8 9.4 %collective-permute-start.11 = (bf16[32,3072]{1,0:T(8,128)(2,1)S(1)}, bf16[32,3072]{1,0:T(8,128)(2,1)S(1)}, u32[]{:S(2)}, u32[]{:S(2)}) collective-permute-start(bf16[32,3072]{1,0:T(8,128)(2,1)S(1)} %get-tuple-element.44), channel_id=1, source_target_pairs={{0,4},{2,6},{4,0},{6,2},{1,5},{3,7},{5,1},{7,3},{8,12},{10,14},{12... | collective-permute-start | bytes 589832 | tf_op jit(solution)/shard_map/ppermute | solution.py:287
  67.0 11.6 %collective-permute-start.12 = (bf16[32,3072]{1,0:T(8,128)(2,1)S(1)}, bf16[32,3072]{1,0:T(8,128)(2,1)S(1)}, u32[]{:S(2)}, u32[]{:S(2)}) collective-permute-start(bf16[32,3072]{1,0:T(8,128)(2,1)S(1)} %get-tuple-element.45), channel_id=1, source_target_pairs={{0,2},{2,4},{4,6},{6,0},{1,3},{3,5},{5,7},{7,1},{8,10},{10,12},{12... | collective-permute-start | bytes 589832 | tf_op jit(solution)/shard_map/ppermute | solution.py:287
  67.9 10.7 %collective-permute-start.13 = (bf16[32,3072]{1,0:T(8,128)(2,1)S(1)}, bf16[32,3072]{1,0:T(8,128)(2,1)S(1)}, u32[]{:S(2)}, u32[]{:S(2)}) collective-permute-start(bf16[32,3072]{1,0:T(8,128)(2,1)S(1)} %get-tuple-element.46), channel_id=1, source_target_pairs={{0,6},{2,0},{4,2},{6,4},{1,7},{3,1},{5,3},{7,5},{8,14},{10,8},{12,... | collective-permute-start | bytes 589832 | tf_op jit(solution)/shard_map/ppermute | solution.py:287

commit v9 on v8

--- a/solution.py
+++ b/solution.py
@@ -193,21 +193,20 @@
 ]
 
 
-def projected(mine, peer, w_mine, w_peer, cut):
-    middle = jnp.concatenate([mine[:, 2 * HD :], peer[:, :HD]], axis=1)
-    w_middle = jnp.concatenate([w_mine[2 * HD :, cut], w_peer[:HD, cut]], axis=0)
-    part = jnp.dot(mine[:, : 2 * HD], w_mine[: 2 * HD, cut], preferred_element_type=F32)
-    part += jnp.dot(middle, w_middle, preferred_element_type=F32)
-    part += jnp.dot(peer[:, HD:], w_peer[HD:, cut], preferred_element_type=F32)
-    return part.astype(BF)
-
-
-def out_kernel(mine, peer, w_mine, w_peer, *outs):
+def own_kernel(after, mine, w_mine, z, w_in, out, embed):
+    embed[...] = jnp.dot(unpack(z[...]), w_in[...], preferred_element_type=F32)
     for j in range(6):
         cut = slice(j * 512, j * 512 + 512)
-        part = projected(mine, peer, w_mine, w_peer, cut)
+        out[:, cut] = jnp.dot(mine[...], w_mine[:, cut], preferred_element_type=F32)
+
+
+def sum_kernel(part, peer, w_peer, *outs):
+    for j in range(6):
+        cut = slice(j * 512, j * 512 + 512)
+        total = part[:, cut] + jnp.dot(peer[...], w_peer[:, cut], preferred_element_type=F32)
+        total = total.astype(BF)
         for k in range(NX):
-            outs[k][:, cut] = part[ROWS * k : ROWS * (k + 1)]
+            outs[k][:, cut] = total[ROWS * k : ROWS * (k + 1)]
 
 
 def position():
@@ -218,11 +217,10 @@
 
 
 def drift_kernel(
-    size, slide, high, zstart, z, p0, p1, p2, p3, w_in, gate, w_fin, out, target=None
+    size, slide, high, zstart, embed, p0, p1, p2, p3, gate, w_fin, out, target=None
 ):
-    e = jnp.dot(unpack(z[...]), w_in[...], preferred_element_type=F32)
     attn = p0[...].astype(F32) + p1[...].astype(F32) + p2[...].astype(F32) + p3[...].astype(F32)
-    h = e + gate[2:3, :] * attn
+    h = embed[...] + gate[2:3, :] * attn
     mean = jnp.sum(h, axis=-1, keepdims=True) * (1.0 / D)
     h = h - mean
     var = jnp.sum(h * h, axis=-1, keepdims=True) * (1.0 / D)
@@ -324,14 +322,17 @@
     w_fin_rows = w_fin.T
 
     def gathered_drifts(mine, send, z, *extra):
-        operands = (mine, swap_cores(send), w_out, w_peer)
-        parts = call(out_kernel, [row] * NX, [VM] * 4, limit=16)(*operands)
+        peer = swap_cores(send)
+        part, embed = call(
+            own_kernel, [shape((S // 2, D), F32), shape((ROWS, D), F32)], [VM] * 5, limit=16
+        )(send, mine, w_out, z, w_in)
+        parts = call(sum_kernel, [row] * NX, [VM] * 3, limit=16)(part, peer, w_peer)
         got = [parts[0]] + [to_right(parts[k], k) for k in (2, 1, 3)]
         outs, *extra = call(
             drift_kernel,
             [shape((NY * NZ, 16, 128), BF), *extra],
-            [SM, SM] + [VM] * 10,
-        )(step_sizes, slide, high, state, z, *got, w_in, rows, w_fin_rows)
+            [SM, SM] + [VM] * 9,
+        )(step_sizes, slide, high, state, embed, *got, rows, w_fin_rows)
         got = lax.all_to_all(outs, ("y", "z"), 0, 0, tiled=True)
         return got, *extra
 

time: 94.6 us -> 94 us (level)
  waiting for transfers between devices: 17.7 us -> 16.3 us
    ppermute x4, waiting for transfers between devices: 3.73 us -> 2.27 us  [swap_cores(): return lax.ppermute(x, 'c', [(0, 1), (1, 0)])]
    pallas_call x2 -> x4, Pallas kernels: 1.58 us -> 2.57 us  [the longest x2 1.41 us: gathered_drifts(): call(own_kernel, [shape((S // 2, D), F32), shape((ROWS, D), F32)], [VM] *...]
  transfers between devices with their start and end apart: 14 -> 14, of which waited for: 7 -> 7; matrix products, arithmetic and copies ran while one was open for 0% -> 0% of each run, Pallas kernels for 7% -> 9%
where the time goes in v9:
time: 94 us; the launch traced here: 93.5 us
  blocking collectives  43.9 us (47%)
  waiting for transfers between devices  16.3 us (17%)
  Pallas kernels  15.2 us (16%)
  starting transfers between devices  15 us (16%)
  between operations  2.13 us (2%)
    all_to_all x2, blocking collectives, gathered_drifts(): got = lax.all_to_all(outs, ('y', 'z'), 0, 0, tiled=True)  35.1 us
    ppermute x9, starting transfers between devices, to_right(): return lax.ppermute(x, 'x', [(i, (i + k) % NX) for i in range(NX)])  14 us
    ppermute x9, waiting for transfers between devices, to_right(): return lax.ppermute(x, 'x', [(i, (i + k) % NX) for i in range(NX)])  14 us
    all_to_all x1, blocking collectives, local(): zg = lax.all_to_all(copies, ('x', 'c'), 0, 0, tiled=True)  8.87 us
    pallas_call x1, Pallas kernels, local(): call(second_kernel, [half, half], [VM] * 5, BLOCK_SCRATCH, limit=16)  3.66 us
    pallas_call x1, Pallas kernels, local(): call(first_kernel, [half, half], [VM] * 8, BLOCK_SCRATCH, limit=16)  3.64 us
    pallas_call x1, Pallas kernels, local(): call(prepare_kernel, [kept((4, 8, ROWS, HD), F32), kept((2 * C, D), BF),...  3.32 us
    ppermute x4, waiting for transfers between devices, swap_cores(): return lax.ppermute(x, 'c', [(0, 1), (1, 0)])  2.27 us
  transfers between devices with their start and end apart: 14, of which 7 were waited for; matrix products, arithmetic and copies ran while one was open for 0% of the time, Pallas kernels for 9%

profile of v9, /device:TPU:32, one launch (start us, length us, event | category | flops | bytes accessed | tf_op | source)
XLA Modules:
  0.0 93.5 jit_solution(5956488573675372347)
XLA Ops:
  0.0 0.7 bitcast_convert_fusion
  0.7 0.1 pad_maximum_fusion.1.z
  0.8 0.0 collective-permute-start.1
  0.8 1.2 %collective-permute-done.1 = bf16[16,128]{1,0:T(8,128)(2,1)S(1)} collective-permute-done((bf16[16,128]{1,0:T(8,128)(2,1)S(1)}, bf16[16,128]{1,0:T(8,128)(2,1)S(1)}, u32[]{:S(2)}, u32[]{:S(2)}) %collective-permute-start.1) | collective-permute-done | bytes 4128 | tf_op jit(solution)/shard_map/ppermute | solution.py:289
  2.0 0.2 collective-permute-start.6
  2.2 2.8 %collective-permute-start.2 = (bf16[2,16,128]{2,1,0:T(8,128)(2,1)S(1)}, bf16[2,16,128]{2,1,0:T(8,128)(2,1)S(1)}, u32[]{:S(2)}, u32[]{:S(2)}) collective-permute-start(bf16[2,16,128]{2,1,0:T(8,128)(2,1)S(1)} %pad_maximum_fusion.after.z0), channel_id=1, source_target_pairs={{0,6},{2,0},{4,2},{6,4},{1,7},{3,1},{5,3},{7,5},{8,14},{10,8},{12,... | collective-permute-start | bytes 24584 | tf_op jit(solution)/shard_map/ppermute | solution.py:285
  4.9 0.8 collective-permute-start.3
  5.7 0.9 collective-permute-start.4
  7.3 3.3 %shard_map.109 = (f32[4,8,32,128]{3,2,1,0:T(8,128)S(1)}, bf16[128,3072]{1,0:T(8,128)(2,1)S(1)}, f32[8,3072]{1,0:T(8,128)S(1)}, bf16[64,3072]{1,0:T(8,128)(2,1)S(1)}, bf16[3072,1152]{1,0:T(8,128)(2,1)S(1)}) custom-call(s32[1]{0:T(128)S(6)} %copy.12.step, bf16[2,16,128]{2,1,0:T(8,128)(2,1)S(1)} %pad_maximum_fusion.after.z0, s32[2,256]{1,0:T(2,128)} %bitcast.14, ...), custom_call_target="tpu_custom_call" | custom-call | tf_op jit(solution)/shard_map/pallas_call | solution.py:301
  10.6 0.0 collective-permute-done.2.z1
  10.6 0.0 collective-permute-done.3.z2
  10.6 0.0 collective-permute-done.4.z3
  10.6 0.0 copy-start
  10.6 3.6 %shard_map.110 = (bf16[128,384]{1,0:T(8,128)(2,1)S(1)}, bf16[128,384]{1,0:T(8,128)(2,1)S(1)}) custom-call(bf16[2,16,128]{2,1,0:T(8,128)(2,1)S(1)} %pad_maximum_fusion.after.z0, bf16[2,16,128]{2,1,0:T(8,128)(2,1)S(1)} %collective-permute-done.2.z1, bf16[2,16,128]{2,1,0:T(8,128)(2,1)S(1)} %collective-permute-done.3.z2, ...), custom_call_target="tpu_custom_call" | custom-call | tf_op jit(solution)/shard_map/pallas_call | solution.py:319
  14.3 0.1 collective-permute-start.5
  14.4 0.0 copy-done
  14.4 0.7 shard_map.111
  15.1 0.0 copy-start.1
  15.1 0.0 copy-start.2
  15.1 0.5 collective-permute-done.5.peer
  15.7 0.0 collective-permute-done.6.w_peer
  15.7 0.6 shard_map.112
  16.3 1.9 %collective-permute-start.7 = (bf16[32,3072]{1,0:T(8,128)(2,1)S(1)}, bf16[32,3072]{1,0:T(8,128)(2,1)S(1)}, u32[]{:S(2)}, u32[]{:S(2)}) collective-permute-start(bf16[32,3072]{1,0:T(8,128)(2,1)S(1)} %get-tuple-element.42), channel_id=1, source_target_pairs={{0,4},{2,6},{4,0},{6,2},{1,5},{3,7},{5,1},{7,3},{8,12},{10,14},{12... | collective-permute-start | bytes 589832 | tf_op jit(solution)/shard_map/ppermute | solution.py:285
  18.2 1.4 %collective-permute-start.8 = (bf16[32,3072]{1,0:T(8,128)(2,1)S(1)}, bf16[32,3072]{1,0:T(8,128)(2,1)S(1)}, u32[]{:S(2)}, u32[]{:S(2)}) collective-permute-start(bf16[32,3072]{1,0:T(8,128)(2,1)S(1)} %get-tuple-element.43), channel_id=1, source_target_pairs={{0,2},{2,4},{4,6},{6,0},{1,3},{3,5},{5,7},{7,1},{8,10},{10,12},{12... | collective-permute-start | bytes 589832 | tf_op jit(solution)/shard_map/ppermute | solution.py:285
  19.6 1.9 %collective-permute-start.9 = (bf16[32,3072]{1,0:T(8,128)(2,1)S(1)}, bf16[32,3072]{1,0:T(8,128)(2,1)S(1)}, u32[]{:S(2)}, u32[]{:S(2)}) collective-permute-start(bf16[32,3072]{1,0:T(8,128)(2,1)S(1)} %get-tuple-element.44), channel_id=1, source_target_pairs={{0,6},{2,0},{4,2},{6,4},{1,7},{3,1},{5,3},{7,5},{8,14},{10,8},{12,... | collective-permute-start | bytes 589832 | tf_op jit(solution)/shard_map/ppermute | solution.py:285
  21.4 0.6 collective-permute-start
  23.4 0.0 collective-permute-done.high
  23.4 2.2 %collective-permute-done.7.p1 = bf16[32,3072]{1,0:T(8,128)(2,1)S(1)} collective-permute-done((bf16[32,3072]{1,0:T(8,128)(2,1)S(1)}, bf16[32,3072]{1,0:T(8,128)(2,1)S(1)}, u32[]{:S(2)}, u32[]{:S(2)}) %collective-permute-start.7) | collective-permute-done | bytes 196640 | tf_op jit(solution)/shard_map/ppermute | solution.py:285
  25.6 3.4 %collective-permute-done.8.p2 = bf16[32,3072]{1,0:T(8,128)(2,1)S(1)} collective-permute-done((bf16[32,3072]{1,0:T(8,128)(2,1)S(1)}, bf16[32,3072]{1,0:T(8,128)(2,1)S(1)}, u32[]{:S(2)}, u32[]{:S(2)}) %collective-permute-start.8) | collective-permute-done | bytes 196640 | tf_op jit(solution)/shard_map/ppermute | solution.py:285
  29.0 0.0 collective-permute-done.9.p3
  29.0 0.0 copy-done.1
  29.0 0.0 copy-done.2
  29.0 0.6 shard_map.113
  29.7 21.0 %all_to_all.15.got = bf16[32,16,128]{2,1,0:T(8,128)(2,1)S(1)} all-to-all(bf16[32,16,128]{2,1,0:T(8,128)(2,1)S(1)} %shard_map.113), channel_id=1, replica_groups=mesh['y'=4,'z'=8,'x'=4,'c'=2] {'y','z'}, dimensions={0} | all-to-all | bytes 262144 | tf_op jit(solution)/shard_map/all_to_all | solution.py:336
  50.8 8.9 %all_to_all.16.zg = bf16[8,16,128]{2,1,0:T(8,128)(2,1)S(1)} all-to-all(bf16[8,16,128]{2,1,0:T(8,128)(2,1)S(1)} %get-tuple-element.45), channel_id=1, replica_groups=mesh['y'=4,'z'=8,'x'=4,'c'=2] {'x','c'}, dimensions={0} | all-to-all | bytes 65536 | tf_op jit(solution)/shard_map/all_to_all | solution.py:343
  59.6 3.7 %shard_map.115 = (bf16[128,384]{1,0:T(8,128)(2,1)S(1)}, bf16[128,384]{1,0:T(8,128)(2,1)S(1)}) custom-call(bf16[8,16,128]{2,1,0:T(8,128)(2,1)S(1)} %all_to_all.16.zg, f32[4,8,32,128]{3,2,1,0:T(8,128)S(1)} %get-tuple-element.31.rest_0_, bf16[128,3072]{1,0:T(8,128)(2,1)S(1)} %get-tuple-element.32.rest_1_, f32[8,3072]{1,0:T(8,128)S(1)} %get-tuple-element.33.rest_2_.gate, ...), custom_call_target="tpu_custom_call" | custom-call | tf_op jit(solution)/shard_map/pallas_call | solution.py:344
  63.3 0.1 collective-permute-start.10
  63.4 0.7 shard_map.116
  64.1 0.6 collective-permute-done.10.peer
  64.7 0.6 shard_map.117
  65.3 1.2 %collective-permute-start.11 = (bf16[32,3072]{1,0:T(8,128)(2,1)S(1)}, bf16[32,3072]{1,0:T(8,128)(2,1)S(1)}, u32[]{:S(2)}, u32[]{:S(2)}) collective-permute-start(bf16[32,3072]{1,0:T(8,128)(2,1)S(1)} %get-tuple-element.52), channel_id=1, source_target_pairs={{0,4},{2,6},{4,0},{6,2},{1,5},{3,7},{5,1},{7,3},{8,12},{10,14},{12... | collective-permute-start | bytes 589832 | tf_op jit(solution)/shard_map/ppermute | solution.py:285
  66.5 0.9 %collective-permute-start.12 = (bf16[32,3072]{1,0:T(8,128)(2,1)S(1)}, bf16[32,3072]{1,0:T(8,128)(2,1)S(1)}, u32[]{:S(2)}, u32[]{:S(2)}) collective-permute-start(bf16[32,3072]{1,0:T(8,128)(2,1)S(1)} %get-tuple-element.53), channel_id=1, source_target_pairs={{0,2},{2,4},{4,6},{6,0},{1,3},{3,5},{5,7},{7,1},{8,10},{10,12},{12... | collective-permute-start | bytes 589832 | tf_op jit(solution)/shard_map/ppermute | solution.py:285
  67.4 2.3 %collective-permute-start.13 = (bf16[32,3072]{1,0:T(8,128)(2,1)S(1)}, bf16[32,3072]{1,0:T(8,128)(2,1)S(1)}, u32[]{:S(2)}, u32[]{:S(2)}) collective-permute-start(bf16[32,3072]{1,0:T(8,128)(2,1)S(1)} %get-tuple-element.54), channel_id=1, source_target_pairs={{0,6},{2,0},{4,2},{6,4},{1,7},{3,1},{5,3},{7,5},{8,14},{10,8},{12,... | collective-permute-start | bytes 589832 | tf_op jit(solution)/shard_map/ppermute | solution.py:285
  69.7 5.0 %collective-permute-done.11.p1 = bf16[32,3072]{1,0:T(8,128)(2,1)S(1)} collective-permute-done((bf16[32,3072]{1,0:T(8,128)(2,1)S(1)}, bf16[32,3072]{1,0:T(8,128)(2,1)S(1)}, u32[]{:S(2)}, u32[]{:S(2)}) %collective-permute-start.11) | collective-permute-done | bytes 196640 | tf_op jit(solution)/shard_map/ppermute | solution.py:285
  74.7 3.4 %collective-permute-done.12.p2 = bf16[32,3072]{1,0:T(8,128)(2,1)S(1)} collective-permute-done((bf16[32,3072]{1,0:T(8,128)(2,1)S(1)}, bf16[32,3072]{1,0:T(8,128)(2,1)S(1)}, u32[]{:S(2)}, u32[]{:S(2)}) %collective-permute-start.12) | collective-permute-done | bytes 196640 | tf_op jit(solution)/shard_map/ppermute | solution.py:285
  78.1 0.0 collective-permute-done.13.p3
  78.1 0.6 shard_map.118
  78.7 14.0 %all_to_all.17.got = bf16[32,16,128]{2,1,0:T(8,128)(2,1)S(1)} all-to-all(bf16[32,16,128]{2,1,0:T(8,128)(2,1)S(1)} %get-tuple-element.56), channel_id=1, replica_groups=mesh['y'=4,'z'=8,'x'=4,'c'=2] {'y','z'}, dimensions={0} | all-to-all | bytes 262144 | tf_op jit(solution)/shard_map/all_to_all | solution.py:336
  92.7 0.7 shard_map.119
  (3 shorter events, 0.1 us)
Async XLA Ops:
  0.8 1.2 %collective-permute-start.1 = (bf16[16,128]{1,0:T(8,128)(2,1)S(1)}, bf16[16,128]{1,0:T(8,128)(2,1)S(1)}, u32[]{:S(2)}, u32[]{:S(2)}) collective-permute-start(bf16[16,128]{1,0:T(8,128)(2,1)S(1)} %pad_maximum_fusion.1.z), channel_id=1, source_target_pairs={{0,1},{1,0},{2,3},{3,2},{4,5},{5,4},{6,7},{7,6},{8,9},{9,8},{10,11... | collective-permute-start | bytes 12296 | tf_op jit(solution)/shard_map/ppermute | solution.py:289
  2.0 13.7 %collective-permute-start.6 = (bf16[384,3072]{1,0:T(8,128)(2,1)}, bf16[384,3072]{1,0:T(8,128)(2,1)S(1)}, u32[]{:S(2)}, u32[]{:S(2)}) collective-permute-start(bf16[384,3072]{1,0:T(8,128)(2,1)} %w_mine.3), channel_id=1, source_target_pairs={{0,1},{1,0},{2,3},{3,2},{4,5},{5,4},{6,7},{7,6},{8,9},{9,8},{10,11... | collective-permute-start | bytes 7077896 | tf_op jit(solution)/shard_map/ppermute | solution.py:289
  2.2 8.4 %collective-permute-start.2 = (bf16[2,16,128]{2,1,0:T(8,128)(2,1)S(1)}, bf16[2,16,128]{2,1,0:T(8,128)(2,1)S(1)}, u32[]{:S(2)}, u32[]{:S(2)}) collective-permute-start(bf16[2,16,128]{2,1,0:T(8,128)(2,1)S(1)} %pad_maximum_fusion.after.z0), channel_id=1, source_target_pairs={{0,6},{2,0},{4,2},{6,4},{1,7},{3,1},{5,3},{7,5},{8,14},{10,8},{12,... | collective-permute-start | bytes 24584 | tf_op jit(solution)/shard_map/ppermute | solution.py:285
  4.9 5.7 %collective-permute-start.3 = (bf16[2,16,128]{2,1,0:T(8,128)(2,1)S(1)}, bf16[2,16,128]{2,1,0:T(8,128)(2,1)S(1)}, u32[]{:S(2)}, u32[]{:S(2)}) collective-permute-start(bf16[2,16,128]{2,1,0:T(8,128)(2,1)S(1)} %pad_maximum_fusion.after.z0), channel_id=1, source_target_pairs={{0,4},{2,6},{4,0},{6,2},{1,5},{3,7},{5,1},{7,3},{8,12},{10,14},{12... | collective-permute-start | bytes 24584 | tf_op jit(solution)/shard_map/ppermute | solution.py:285
  5.7 4.9 %collective-permute-start.4 = (bf16[2,16,128]{2,1,0:T(8,128)(2,1)S(1)}, bf16[2,16,128]{2,1,0:T(8,128)(2,1)S(1)}, u32[]{:S(2)}, u32[]{:S(2)}) collective-permute-start(bf16[2,16,128]{2,1,0:T(8,128)(2,1)S(1)} %pad_maximum_fusion.after.z0), channel_id=1, source_target_pairs={{0,2},{2,4},{4,6},{6,0},{1,3},{3,5},{5,7},{7,1},{8,10},{10,12},{12... | collective-permute-start | bytes 24584 | tf_op jit(solution)/shard_map/ppermute | solution.py:285
  10.6 3.8 %copy-start = (bf16[384,3072]{1,0:T(8,128)(2,1)S(1)}, bf16[384,3072]{1,0:T(8,128)(2,1)}, u32[]{:S(2)}) copy-start(bf16[384,3072]{1,0:T(8,128)(2,1)} %w_mine.3) | copy-start | bytes 7077892
  14.3 1.4 %collective-permute-start.5 = (bf16[128,384]{1,0:T(8,128)(2,1)S(1)}, bf16[128,384]{1,0:T(8,128)(2,1)S(1)}, u32[]{:S(2)}, u32[]{:S(2)}) collective-permute-start(bf16[128,384]{1,0:T(8,128)(2,1)S(1)} %get-tuple-element.35.after), channel_id=1, source_target_pairs={{0,1},{1,0},{2,3},{3,2},{4,5},{5,4},{6,7},{7,6},{8,9},{9,8},{10,11... | collective-permute-start | bytes 294920 | tf_op jit(solution)/shard_map/ppermute | solution.py:289
  15.1 13.9 %copy-start.1 = (bf16[3072,64]{0,1:T(8,128)(2,1)S(1)}, bf16[3072,64]{0,1:T(8,128)(2,1)}, u32[]{:S(2)}) copy-start(bf16[3072,64]{0,1:T(8,128)(2,1)} %param.21) | copy-start | bytes 1179652
  15.1 13.9 %copy-start.2 = (f32[1,32,64]{2,1,0:T(8,128)S(1)}, f32[1,32,64]{2,1,0:T(8,128)}, u32[]{:S(2)}) copy-start(f32[1,32,64]{2,1,0:T(8,128)} %param.11) | copy-start | bytes 24580
  16.3 9.4 %collective-permute-start.7 = (bf16[32,3072]{1,0:T(8,128)(2,1)S(1)}, bf16[32,3072]{1,0:T(8,128)(2,1)S(1)}, u32[]{:S(2)}, u32[]{:S(2)}) collective-permute-start(bf16[32,3072]{1,0:T(8,128)(2,1)S(1)} %get-tuple-element.42), channel_id=1, source_target_pairs={{0,4},{2,6},{4,0},{6,2},{1,5},{3,7},{5,1},{7,3},{8,12},{10,14},{12... | collective-permute-start | bytes 589832 | tf_op jit(solution)/shard_map/ppermute | solution.py:285
  18.2 10.8 %collective-permute-start.8 = (bf16[32,3072]{1,0:T(8,128)(2,1)S(1)}, bf16[32,3072]{1,0:T(8,128)(2,1)S(1)}, u32[]{:S(2)}, u32[]{:S(2)}) collective-permute-start(bf16[32,3072]{1,0:T(8,128)(2,1)S(1)} %get-tuple-element.43), channel_id=1, source_target_pairs={{0,2},{2,4},{4,6},{6,0},{1,3},{3,5},{5,7},{7,1},{8,10},{10,12},{12... | collective-permute-start | bytes 589832 | tf_op jit(solution)/shard_map/ppermute | solution.py:285
  19.6 9.5 %collective-permute-start.9 = (bf16[32,3072]{1,0:T(8,128)(2,1)S(1)}, bf16[32,3072]{1,0:T(8,128)(2,1)S(1)}, u32[]{:S(2)}, u32[]{:S(2)}) collective-permute-start(bf16[32,3072]{1,0:T(8,128)(2,1)S(1)} %get-tuple-element.44), channel_id=1, source_target_pairs={{0,6},{2,0},{4,2},{6,4},{1,7},{3,1},{5,3},{7,5},{8,14},{10,8},{12,... | collective-permute-start | bytes 589832 | tf_op jit(solution)/shard_map/ppermute | solution.py:285
  21.4 2.0 %collective-permute-start = (bf16[16,128]{1,0:T(8,128)(2,1)S(1)}, bf16[16,128]{1,0:T(8,128)(2,1)S(1)}, u32[]{:S(2)}, u32[]{:S(2)}) collective-permute-start(bf16[16,128]{1,0:T(8,128)(2,1)S(1)} %pad_maximum_fusion.1.z), channel_id=1, source_target_pairs={{0,248},{1,249},{2,250},{3,251},{4,252},{5,253},{6,254},{7,255}} | collective-permute-start | bytes 12296 | tf_op jit(solution)/shard_map/ppermute | solution.py:317
  63.3 1.4 %collective-permute-start.10 = (bf16[128,384]{1,0:T(8,128)(2,1)S(1)}, bf16[128,384]{1,0:T(8,128)(2,1)S(1)}, u32[]{:S(2)}, u32[]{:S(2)}) collective-permute-start(bf16[128,384]{1,0:T(8,128)(2,1)S(1)} %get-tuple-element.46.after), channel_id=1, source_target_pairs={{0,1},{1,0},{2,3},{3,2},{4,5},{5,4},{6,7},{7,6},{8,9},{9,8},{10,11... | collective-permute-start | bytes 294920 | tf_op jit(solution)/shard_map/ppermute | solution.py:289
  65.3 9.4 %collective-permute-start.11 = (bf16[32,3072]{1,0:T(8,128)(2,1)S(1)}, bf16[32,3072]{1,0:T(8,128)(2,1)S(1)}, u32[]{:S(2)}, u32[]{:S(2)}) collective-permute-start(bf16[32,3072]{1,0:T(8,128)(2,1)S(1)} %get-tuple-element.52), channel_id=1, source_target_pairs={{0,4},{2,6},{4,0},{6,2},{1,5},{3,7},{5,1},{7,3},{8,12},{10,14},{12... | collective-permute-start | bytes 589832 | tf_op jit(solution)/shard_map/ppermute | solution.py:285
  66.5 11.6 %collective-permute-start.12 = (bf16[32,3072]{1,0:T(8,128)(2,1)S(1)}, bf16[32,3072]{1,0:T(8,128)(2,1)S(1)}, u32[]{:S(2)}, u32[]{:S(2)}) collective-permute-start(bf16[32,3072]{1,0:T(8,128)(2,1)S(1)} %get-tuple-element.53), channel_id=1, source_target_pairs={{0,2},{2,4},{4,6},{6,0},{1,3},{3,5},{5,7},{7,1},{8,10},{10,12},{12... | collective-permute-start | bytes 589832 | tf_op jit(solution)/shard_map/ppermute | solution.py:285
  67.4 10.7 %collective-permute-start.13 = (bf16[32,3072]{1,0:T(8,128)(2,1)S(1)}, bf16[32,3072]{1,0:T(8,128)(2,1)S(1)}, u32[]{:S(2)}, u32[]{:S(2)}) collective-permute-start(bf16[32,3072]{1,0:T(8,128)(2,1)S(1)} %get-tuple-element.54), channel_id=1, source_target_pairs={{0,6},{2,0},{4,2},{6,4},{1,7},{3,1},{5,3},{7,5},{8,14},{10,8},{12,... | collective-permute-start | bytes 589832 | tf_op jit(solution)/shard_map/ppermute | solution.py:285

commit v10 on v9

--- a/solution.py
+++ b/solution.py
@@ -49,6 +49,11 @@
 def halves(x):
     high = x.astype(BF)
     return high, (x - high.astype(F32)).astype(BF)
+
+
+def stack_kernel(z, other, own):
+    own[0] = z[...]
+    own[1] = pack(other[0].astype(BF))
 
 
 def prepare_kernel(
@@ -294,7 +299,7 @@
 ):
     state = guesses[0]
     z = pack(state.astype(BF))
-    own = jnp.stack([z, swap_cores(z)])
+    own = call(stack_kernel, shape((2, 16, 128), BF), [VM] * 2)(z, swap_cores(guesses))
     w_peer = swap_cores(lax.optimization_barrier((w_out, own))[0])
     zg = [own] + [to_right(own, NX - k) for k in range(1, NX)]
     operands = (offsets.T, qk_gain, w_in, mod_table.transpose(1, 0, 2), w_qkv)

time: 94 us -> 93.4 us (level)
  transfers between devices with their start and end apart: 14 -> 14, of which waited for: 7 -> 7; matrix products, arithmetic and copies ran while one was open for 0% -> 1% of each run, Pallas kernels for 9% -> 9%
where the time goes in v10:
time: 93.4 us; the launch traced here: 92.9 us
  blocking collectives  43.9 us (47%)
  waiting for transfers between devices  15.7 us (17%)
  Pallas kernels  15.3 us (16%)
  starting transfers between devices  15 us (16%)
  between operations  2.12 us (2%)
    all_to_all x2, blocking collectives, gathered_drifts(): got = lax.all_to_all(outs, ('y', 'z'), 0, 0, tiled=True)  35.1 us
    ppermute x9, starting transfers between devices, to_right(): return lax.ppermute(x, 'x', [(i, (i + k) % NX) for i in range(NX)])  14 us
    ppermute x9, waiting for transfers between devices, to_right(): return lax.ppermute(x, 'x', [(i, (i + k) % NX) for i in range(NX)])  14 us
    all_to_all x1, blocking collectives, local(): zg = lax.all_to_all(copies, ('x', 'c'), 0, 0, tiled=True)  8.87 us
    pallas_call x1, Pallas kernels, local(): call(second_kernel, [half, half], [VM] * 5, BLOCK_SCRATCH, limit=16)  3.66 us
    pallas_call x1, Pallas kernels, local(): call(first_kernel, [half, half], [VM] * 8, BLOCK_SCRATCH, limit=16)  3.65 us
    pallas_call x1, Pallas kernels, local(): call(prepare_kernel, [kept((4, 8, ROWS, HD), F32), kept((2 * C, D), BF),...  3.32 us
  transfers between devices with their start and end apart: 14, of which 7 were waited for; matrix products, arithmetic and copies ran while one was open for 1% of the time, Pallas kernels for 9%

profile of v10, /device:TPU:32, one launch (start us, length us, event | category | flops | bytes accessed | tf_op | source)
XLA Modules:
  0.0 92.9 jit_solution(6648426846154661893)
XLA Ops:
  0.0 0.0 collective-permute-start.1
  0.0 0.7 bitcast_convert_fusion
  0.7 0.1 pad_maximum_fusion.z
  0.8 0.6 collective-permute-done.1.other
  1.4 0.1 shard_map.109.after.z0
  1.5 0.2 collective-permute-start.6
  1.6 2.8 %collective-permute-start.2 = (bf16[2,16,128]{2,1,0:T(8,128)(2,1)S(1)}, bf16[2,16,128]{2,1,0:T(8,128)(2,1)S(1)}, u32[]{:S(2)}, u32[]{:S(2)}) collective-permute-start(bf16[2,16,128]{2,1,0:T(8,128)(2,1)S(1)} %shard_map.109.after.z0), channel_id=1, source_target_pairs={{0,6},{2,0},{4,2},{6,4},{1,7},{3,1},{5,3},{7,5},{8,14},{10,8},{12,... | collective-permute-start | bytes 24584 | tf_op jit(solution)/shard_map/ppermute | solution.py:290
  4.4 0.8 collective-permute-start.3
  5.2 0.9 collective-permute-start.4
  6.7 3.3 %shard_map.110 = (f32[4,8,32,128]{3,2,1,0:T(8,128)S(1)}, bf16[128,3072]{1,0:T(8,128)(2,1)S(1)}, f32[8,3072]{1,0:T(8,128)S(1)}, bf16[64,3072]{1,0:T(8,128)(2,1)S(1)}, bf16[3072,1152]{1,0:T(8,128)(2,1)S(1)}) custom-call(s32[1]{0:T(128)S(6)} %copy.12.step, bf16[2,16,128]{2,1,0:T(8,128)(2,1)S(1)} %shard_map.109.after.z0, s32[2,256]{1,0:T(2,128)} %bitcast.10, ...), custom_call_target="tpu_custom_call" | custom-call | tf_op jit(solution)/shard_map/pallas_call | solution.py:306
  10.1 0.0 collective-permute-done.2.z1
  10.1 0.0 collective-permute-done.3.z2
  10.1 0.0 collective-permute-done.4.z3
  10.1 0.0 copy-start
  10.1 3.6 %shard_map.111 = (bf16[128,384]{1,0:T(8,128)(2,1)S(1)}, bf16[128,384]{1,0:T(8,128)(2,1)S(1)}) custom-call(bf16[2,16,128]{2,1,0:T(8,128)(2,1)S(1)} %shard_map.109.after.z0, bf16[2,16,128]{2,1,0:T(8,128)(2,1)S(1)} %collective-permute-done.2.z1, bf16[2,16,128]{2,1,0:T(8,128)(2,1)S(1)} %collective-permute-done.3.z2, ...), custom_call_target="tpu_custom_call" | custom-call | tf_op jit(solution)/shard_map/pallas_call | solution.py:324
  13.8 0.1 collective-permute-start.5
  13.9 0.0 copy-done
  13.9 0.7 shard_map.112
  14.6 0.0 copy-start.1
  14.6 0.0 copy-start.2
  14.6 0.5 collective-permute-done.5.peer
  15.1 0.0 collective-permute-done.6.w_peer
  15.1 0.6 shard_map.113
  15.7 1.9 %collective-permute-start.7 = (bf16[32,3072]{1,0:T(8,128)(2,1)S(1)}, bf16[32,3072]{1,0:T(8,128)(2,1)S(1)}, u32[]{:S(2)}, u32[]{:S(2)}) collective-permute-start(bf16[32,3072]{1,0:T(8,128)(2,1)S(1)} %get-tuple-element.42), channel_id=1, source_target_pairs={{0,4},{2,6},{4,0},{6,2},{1,5},{3,7},{5,1},{7,3},{8,12},{10,14},{12... | collective-permute-start | bytes 589832 | tf_op jit(solution)/shard_map/ppermute | solution.py:290
  17.7 1.4 %collective-permute-start.8 = (bf16[32,3072]{1,0:T(8,128)(2,1)S(1)}, bf16[32,3072]{1,0:T(8,128)(2,1)S(1)}, u32[]{:S(2)}, u32[]{:S(2)}) collective-permute-start(bf16[32,3072]{1,0:T(8,128)(2,1)S(1)} %get-tuple-element.43), channel_id=1, source_target_pairs={{0,2},{2,4},{4,6},{6,0},{1,3},{3,5},{5,7},{7,1},{8,10},{10,12},{12... | collective-permute-start | bytes 589832 | tf_op jit(solution)/shard_map/ppermute | solution.py:290
  19.0 1.9 %collective-permute-start.9 = (bf16[32,3072]{1,0:T(8,128)(2,1)S(1)}, bf16[32,3072]{1,0:T(8,128)(2,1)S(1)}, u32[]{:S(2)}, u32[]{:S(2)}) collective-permute-start(bf16[32,3072]{1,0:T(8,128)(2,1)S(1)} %get-tuple-element.44), channel_id=1, source_target_pairs={{0,6},{2,0},{4,2},{6,4},{1,7},{3,1},{5,3},{7,5},{8,14},{10,8},{12,... | collective-permute-start | bytes 589832 | tf_op jit(solution)/shard_map/ppermute | solution.py:290
  20.9 0.6 collective-permute-start
  22.9 0.0 collective-permute-done.high
  22.9 2.2 %collective-permute-done.7.p1 = bf16[32,3072]{1,0:T(8,128)(2,1)S(1)} collective-permute-done((bf16[32,3072]{1,0:T(8,128)(2,1)S(1)}, bf16[32,3072]{1,0:T(8,128)(2,1)S(1)}, u32[]{:S(2)}, u32[]{:S(2)}) %collective-permute-start.7) | collective-permute-done | bytes 196640 | tf_op jit(solution)/shard_map/ppermute | solution.py:290
  25.1 3.4 %collective-permute-done.8.p2 = bf16[32,3072]{1,0:T(8,128)(2,1)S(1)} collective-permute-done((bf16[32,3072]{1,0:T(8,128)(2,1)S(1)}, bf16[32,3072]{1,0:T(8,128)(2,1)S(1)}, u32[]{:S(2)}, u32[]{:S(2)}) %collective-permute-start.8) | collective-permute-done | bytes 196640 | tf_op jit(solution)/shard_map/ppermute | solution.py:290
  28.5 0.0 collective-permute-done.9.p3
  28.5 0.0 copy-done.1
  28.5 0.0 copy-done.2
  28.5 0.6 shard_map.114
  29.2 21.0 %all_to_all.15.got = bf16[32,16,128]{2,1,0:T(8,128)(2,1)S(1)} all-to-all(bf16[32,16,128]{2,1,0:T(8,128)(2,1)S(1)} %shard_map.114), channel_id=1, replica_groups=mesh['y'=4,'z'=8,'x'=4,'c'=2] {'y','z'}, dimensions={0} | all-to-all | bytes 262144 | tf_op jit(solution)/shard_map/all_to_all | solution.py:341
  50.3 8.9 %all_to_all.16.zg = bf16[8,16,128]{2,1,0:T(8,128)(2,1)S(1)} all-to-all(bf16[8,16,128]{2,1,0:T(8,128)(2,1)S(1)} %get-tuple-element.45), channel_id=1, replica_groups=mesh['y'=4,'z'=8,'x'=4,'c'=2] {'x','c'}, dimensions={0} | all-to-all | bytes 65536 | tf_op jit(solution)/shard_map/all_to_all | solution.py:348
  59.1 3.7 %shard_map.116 = (bf16[128,384]{1,0:T(8,128)(2,1)S(1)}, bf16[128,384]{1,0:T(8,128)(2,1)S(1)}) custom-call(bf16[8,16,128]{2,1,0:T(8,128)(2,1)S(1)} %all_to_all.16.zg, f32[4,8,32,128]{3,2,1,0:T(8,128)S(1)} %get-tuple-element.31.rest_0_, bf16[128,3072]{1,0:T(8,128)(2,1)S(1)} %get-tuple-element.32.rest_1_, f32[8,3072]{1,0:T(8,128)S(1)} %get-tuple-element.33.rest_2_.gate, ...), custom_call_target="tpu_custom_call" | custom-call | tf_op jit(solution)/shard_map/pallas_call | solution.py:349
  62.8 0.1 collective-permute-start.10
  62.9 0.7 shard_map.117
  63.6 0.6 collective-permute-done.10.peer
  64.2 0.6 shard_map.118
  64.8 1.2 %collective-permute-start.11 = (bf16[32,3072]{1,0:T(8,128)(2,1)S(1)}, bf16[32,3072]{1,0:T(8,128)(2,1)S(1)}, u32[]{:S(2)}, u32[]{:S(2)}) collective-permute-start(bf16[32,3072]{1,0:T(8,128)(2,1)S(1)} %get-tuple-element.52), channel_id=1, source_target_pairs={{0,4},{2,6},{4,0},{6,2},{1,5},{3,7},{5,1},{7,3},{8,12},{10,14},{12... | collective-permute-start | bytes 589832 | tf_op jit(solution)/shard_map/ppermute | solution.py:290
  65.9 0.9 %collective-permute-start.12 = (bf16[32,3072]{1,0:T(8,128)(2,1)S(1)}, bf16[32,3072]{1,0:T(8,128)(2,1)S(1)}, u32[]{:S(2)}, u32[]{:S(2)}) collective-permute-start(bf16[32,3072]{1,0:T(8,128)(2,1)S(1)} %get-tuple-element.53), channel_id=1, source_target_pairs={{0,2},{2,4},{4,6},{6,0},{1,3},{3,5},{5,7},{7,1},{8,10},{10,12},{12... | collective-permute-start | bytes 589832 | tf_op jit(solution)/shard_map/ppermute | solution.py:290
  66.9 2.3 %collective-permute-start.13 = (bf16[32,3072]{1,0:T(8,128)(2,1)S(1)}, bf16[32,3072]{1,0:T(8,128)(2,1)S(1)}, u32[]{:S(2)}, u32[]{:S(2)}) collective-permute-start(bf16[32,3072]{1,0:T(8,128)(2,1)S(1)} %get-tuple-element.54), channel_id=1, source_target_pairs={{0,6},{2,0},{4,2},{6,4},{1,7},{3,1},{5,3},{7,5},{8,14},{10,8},{12,... | collective-permute-start | bytes 589832 | tf_op jit(solution)/shard_map/ppermute | solution.py:290
  69.2 5.0 %collective-permute-done.11.p1 = bf16[32,3072]{1,0:T(8,128)(2,1)S(1)} collective-permute-done((bf16[32,3072]{1,0:T(8,128)(2,1)S(1)}, bf16[32,3072]{1,0:T(8,128)(2,1)S(1)}, u32[]{:S(2)}, u32[]{:S(2)}) %collective-permute-start.11) | collective-permute-done | bytes 196640 | tf_op jit(solution)/shard_map/ppermute | solution.py:290
  74.1 3.4 %collective-permute-done.12.p2 = bf16[32,3072]{1,0:T(8,128)(2,1)S(1)} collective-permute-done((bf16[32,3072]{1,0:T(8,128)(2,1)S(1)}, bf16[32,3072]{1,0:T(8,128)(2,1)S(1)}, u32[]{:S(2)}, u32[]{:S(2)}) %collective-permute-start.12) | collective-permute-done | bytes 196640 | tf_op jit(solution)/shard_map/ppermute | solution.py:290
  77.5 0.0 collective-permute-done.13.p3
  77.5 0.6 shard_map.119
  78.2 14.0 %all_to_all.17.got = bf16[32,16,128]{2,1,0:T(8,128)(2,1)S(1)} all-to-all(bf16[32,16,128]{2,1,0:T(8,128)(2,1)S(1)} %get-tuple-element.56), channel_id=1, replica_groups=mesh['y'=4,'z'=8,'x'=4,'c'=2] {'y','z'}, dimensions={0} | all-to-all | bytes 262144 | tf_op jit(solution)/shard_map/all_to_all | solution.py:341
  92.2 0.7 shard_map.120
  (2 shorter events, 0.0 us)
Async XLA Ops:
  0.0 1.4 %collective-permute-start.1 = (f32[1,32,64]{2,1,0:T(8,128)}, f32[1,32,64]{2,1,0:T(8,128)S(1)}, u32[]{:S(2)}, u32[]{:S(2)}) collective-permute-start(f32[1,32,64]{2,1,0:T(8,128)} %param.11), channel_id=1, source_target_pairs={{0,1},{1,0},{2,3},{3,2},{4,5},{5,4},{6,7},{7,6},{8,9},{9,8},{10,11... | collective-permute-start | bytes 24584 | tf_op jit(solution)/shard_map/ppermute | solution.py:294
  1.5 13.7 %collective-permute-start.6 = (bf16[384,3072]{1,0:T(8,128)(2,1)}, bf16[384,3072]{1,0:T(8,128)(2,1)S(1)}, u32[]{:S(2)}, u32[]{:S(2)}) collective-permute-start(bf16[384,3072]{1,0:T(8,128)(2,1)} %w_mine.3), channel_id=1, source_target_pairs={{0,1},{1,0},{2,3},{3,2},{4,5},{5,4},{6,7},{7,6},{8,9},{9,8},{10,11... | collective-permute-start | bytes 7077896 | tf_op jit(solution)/shard_map/ppermute | solution.py:294
  1.6 8.4 %collective-permute-start.2 = (bf16[2,16,128]{2,1,0:T(8,128)(2,1)S(1)}, bf16[2,16,128]{2,1,0:T(8,128)(2,1)S(1)}, u32[]{:S(2)}, u32[]{:S(2)}) collective-permute-start(bf16[2,16,128]{2,1,0:T(8,128)(2,1)S(1)} %shard_map.109.after.z0), channel_id=1, source_target_pairs={{0,6},{2,0},{4,2},{6,4},{1,7},{3,1},{5,3},{7,5},{8,14},{10,8},{12,... | collective-permute-start | bytes 24584 | tf_op jit(solution)/shard_map/ppermute | solution.py:290
  4.4 5.7 %collective-permute-start.3 = (bf16[2,16,128]{2,1,0:T(8,128)(2,1)S(1)}, bf16[2,16,128]{2,1,0:T(8,128)(2,1)S(1)}, u32[]{:S(2)}, u32[]{:S(2)}) collective-permute-start(bf16[2,16,128]{2,1,0:T(8,128)(2,1)S(1)} %shard_map.109.after.z0), channel_id=1, source_target_pairs={{0,4},{2,6},{4,0},{6,2},{1,5},{3,7},{5,1},{7,3},{8,12},{10,14},{12... | collective-permute-start | bytes 24584 | tf_op jit(solution)/shard_map/ppermute | solution.py:290
  5.2 4.9 %collective-permute-start.4 = (bf16[2,16,128]{2,1,0:T(8,128)(2,1)S(1)}, bf16[2,16,128]{2,1,0:T(8,128)(2,1)S(1)}, u32[]{:S(2)}, u32[]{:S(2)}) collective-permute-start(bf16[2,16,128]{2,1,0:T(8,128)(2,1)S(1)} %shard_map.109.after.z0), channel_id=1, source_target_pairs={{0,2},{2,4},{4,6},{6,0},{1,3},{3,5},{5,7},{7,1},{8,10},{10,12},{12... | collective-permute-start | bytes 24584 | tf_op jit(solution)/shard_map/ppermute | solution.py:290
  10.1 3.8 %copy-start = (bf16[384,3072]{1,0:T(8,128)(2,1)S(1)}, bf16[384,3072]{1,0:T(8,128)(2,1)}, u32[]{:S(2)}) copy-start(bf16[384,3072]{1,0:T(8,128)(2,1)} %w_mine.3) | copy-start | bytes 7077892
  13.8 1.4 %collective-permute-start.5 = (bf16[128,384]{1,0:T(8,128)(2,1)S(1)}, bf16[128,384]{1,0:T(8,128)(2,1)S(1)}, u32[]{:S(2)}, u32[]{:S(2)}) collective-permute-start(bf16[128,384]{1,0:T(8,128)(2,1)S(1)} %get-tuple-element.35.after), channel_id=1, source_target_pairs={{0,1},{1,0},{2,3},{3,2},{4,5},{5,4},{6,7},{7,6},{8,9},{9,8},{10,11... | collective-permute-start | bytes 294920 | tf_op jit(solution)/shard_map/ppermute | solution.py:294
  14.6 13.9 %copy-start.1 = (bf16[3072,64]{0,1:T(8,128)(2,1)S(1)}, bf16[3072,64]{0,1:T(8,128)(2,1)}, u32[]{:S(2)}) copy-start(bf16[3072,64]{0,1:T(8,128)(2,1)} %param.21) | copy-start | bytes 1179652
  14.6 13.9 %copy-start.2 = (f32[1,32,64]{2,1,0:T(8,128)S(1)}, f32[1,32,64]{2,1,0:T(8,128)}, u32[]{:S(2)}) copy-start(f32[1,32,64]{2,1,0:T(8,128)} %param.11) | copy-start | bytes 24580
  15.7 9.4 %collective-permute-start.7 = (bf16[32,3072]{1,0:T(8,128)(2,1)S(1)}, bf16[32,3072]{1,0:T(8,128)(2,1)S(1)}, u32[]{:S(2)}, u32[]{:S(2)}) collective-permute-start(bf16[32,3072]{1,0:T(8,128)(2,1)S(1)} %get-tuple-element.42), channel_id=1, source_target_pairs={{0,4},{2,6},{4,0},{6,2},{1,5},{3,7},{5,1},{7,3},{8,12},{10,14},{12... | collective-permute-start | bytes 589832 | tf_op jit(solution)/shard_map/ppermute | solution.py:290
  17.7 10.9 %collective-permute-start.8 = (bf16[32,3072]{1,0:T(8,128)(2,1)S(1)}, bf16[32,3072]{1,0:T(8,128)(2,1)S(1)}, u32[]{:S(2)}, u32[]{:S(2)}) collective-permute-start(bf16[32,3072]{1,0:T(8,128)(2,1)S(1)} %get-tuple-element.43), channel_id=1, source_target_pairs={{0,2},{2,4},{4,6},{6,0},{1,3},{3,5},{5,7},{7,1},{8,10},{10,12},{12... | collective-permute-start | bytes 589832 | tf_op jit(solution)/shard_map/ppermute | solution.py:290
  19.0 9.5 %collective-permute-start.9 = (bf16[32,3072]{1,0:T(8,128)(2,1)S(1)}, bf16[32,3072]{1,0:T(8,128)(2,1)S(1)}, u32[]{:S(2)}, u32[]{:S(2)}) collective-permute-start(bf16[32,3072]{1,0:T(8,128)(2,1)S(1)} %get-tuple-element.44), channel_id=1, source_target_pairs={{0,6},{2,0},{4,2},{6,4},{1,7},{3,1},{5,3},{7,5},{8,14},{10,8},{12,... | collective-permute-start | bytes 589832 | tf_op jit(solution)/shard_map/ppermute | solution.py:290
  20.9 2.0 %collective-permute-start = (bf16[16,128]{1,0:T(8,128)(2,1)S(1)}, bf16[16,128]{1,0:T(8,128)(2,1)S(1)}, u32[]{:S(2)}, u32[]{:S(2)}) collective-permute-start(bf16[16,128]{1,0:T(8,128)(2,1)S(1)} %pad_maximum_fusion.z), channel_id=1, source_target_pairs={{0,248},{1,249},{2,250},{3,251},{4,252},{5,253},{6,254},{7,255}} | collective-permute-start | bytes 12296 | tf_op jit(solution)/shard_map/ppermute | solution.py:322
  62.8 1.4 %collective-permute-start.10 = (bf16[128,384]{1,0:T(8,128)(2,1)S(1)}, bf16[128,384]{1,0:T(8,128)(2,1)S(1)}, u32[]{:S(2)}, u32[]{:S(2)}) collective-permute-start(bf16[128,384]{1,0:T(8,128)(2,1)S(1)} %get-tuple-element.46.after), channel_id=1, source_target_pairs={{0,1},{1,0},{2,3},{3,2},{4,5},{5,4},{6,7},{7,6},{8,9},{9,8},{10,11... | collective-permute-start | bytes 294920 | tf_op jit(solution)/shard_map/ppermute | solution.py:294
  64.8 9.4 %collective-permute-start.11 = (bf16[32,3072]{1,0:T(8,128)(2,1)S(1)}, bf16[32,3072]{1,0:T(8,128)(2,1)S(1)}, u32[]{:S(2)}, u32[]{:S(2)}) collective-permute-start(bf16[32,3072]{1,0:T(8,128)(2,1)S(1)} %get-tuple-element.52), channel_id=1, source_target_pairs={{0,4},{2,6},{4,0},{6,2},{1,5},{3,7},{5,1},{7,3},{8,12},{10,14},{12... | collective-permute-start | bytes 589832 | tf_op jit(solution)/shard_map/ppermute | solution.py:290
  65.9 11.6 %collective-permute-start.12 = (bf16[32,3072]{1,0:T(8,128)(2,1)S(1)}, bf16[32,3072]{1,0:T(8,128)(2,1)S(1)}, u32[]{:S(2)}, u32[]{:S(2)}) collective-permute-start(bf16[32,3072]{1,0:T(8,128)(2,1)S(1)} %get-tuple-element.53), channel_id=1, source_target_pairs={{0,2},{2,4},{4,6},{6,0},{1,3},{3,5},{5,7},{7,1},{8,10},{10,12},{12... | collective-permute-start | bytes 589832 | tf_op jit(solution)/shard_map/ppermute | solution.py:290
  66.9 10.6 %collective-permute-start.13 = (bf16[32,3072]{1,0:T(8,128)(2,1)S(1)}, bf16[32,3072]{1,0:T(8,128)(2,1)S(1)}, u32[]{:S(2)}, u32[]{:S(2)}) collective-permute-start(bf16[32,3072]{1,0:T(8,128)(2,1)S(1)} %get-tuple-element.54), channel_id=1, source_target_pairs={{0,6},{2,0},{4,2},{6,4},{1,7},{3,1},{5,3},{7,5},{8,14},{10,8},{12,... | collective-permute-start | bytes 589832 | tf_op jit(solution)/shard_map/ppermute | solution.py:290

commit v11 on v10

--- a/solution.py
+++ b/solution.py
@@ -123,7 +123,29 @@
 ]
 
 
-def block_body(chunk_of, tab, wc, rows, w_qkv, mine, send, zs, es, fs, qkv, qs):
+def attend(qs, low, high):
+    scores = [
+        lax.dot_general(
+            qs[head, 0, low:high],
+            qs[head, 1],
+            (((1,), (1,)), ((), ())),
+            preferred_element_type=F32,
+        )
+        for head in range(HL)
+    ]
+    tops = [jnp.max(score, axis=-1, keepdims=True) for score in scores]
+    factor = math.log2(math.e) / math.sqrt(HD)
+    probs = [jnp.exp2((score - top) * factor) for score, top in zip(scores, tops)]
+    totals = [jnp.sum(p, axis=-1, keepdims=True) for p in probs]
+    outs = [
+        jnp.dot(p.astype(BF), qs[head, 2], preferred_element_type=F32)
+        for head, p in enumerate(probs)
+    ]
+    outs = [(out * (1.0 / total)).astype(BF) for out, total in zip(outs, totals)]
+    return jnp.concatenate(outs, axis=1)
+
+
+def block_body(chunk_of, tab, wc, rows, w_qkv, send, qs, zs, es, fs, qkv):
     my_x, my_c = lax.axis_index("x"), lax.axis_index("c")
     order = [((my_x + r % 4) % 4) * 2 + (my_c + r // 4) % 2 for r in range(8)]
     for r in range(8):
@@ -160,24 +182,7 @@
         for k in range(2):
             qs[head, k] = turned(qkv[:, base + k * HD : base + k * HD + HD], k)
         qs[head, 2] = qkv[:, base + 2 * HD : base + QKV].astype(BF)
-    scores = [
-        lax.dot_general(
-            qs[head, 0], qs[head, 1], (((1,), (1,)), ((), ())), preferred_element_type=F32
-        )
-        for head in range(HL)
-    ]
-    tops = [jnp.max(score, axis=-1, keepdims=True) for score in scores]
-    factor = math.log2(math.e) / math.sqrt(HD)
-    probs = [jnp.exp2((score - top) * factor) for score, top in zip(scores, tops)]
-    totals = [jnp.sum(p, axis=-1, keepdims=True) for p in probs]
-    outs = [
-        jnp.dot(p.astype(BF), qs[head, 2], preferred_element_type=F32)
-        for head, p in enumerate(probs)
-    ]
-    for head in range(HL):
-        out = (outs[head] * (1.0 / totals[head])).astype(BF)
-        mine[:, head * HD : head * HD + HD] = out[: S // 2]
-        send[:, head * HD : head * HD + HD] = out[S // 2 :]
+    send[...] = attend(qs, S // 2, S)
 
 
 def first_kernel(z0, z1, z2, z3, *rest):
@@ -194,15 +199,15 @@
     pltpu.VMEM((S, D), F32),
     pltpu.VMEM((S, D), BF),
     pltpu.VMEM((S, HL * QKV), F32),
-    pltpu.VMEM((HL, 3, S, HD), BF),
 ]
 
 
-def own_kernel(after, mine, w_mine, z, w_in, out, embed):
+def own_kernel(after, qs, w_mine, z, w_in, out, embed):
+    mine = attend(qs, 0, S // 2)
     embed[...] = jnp.dot(unpack(z[...]), w_in[...], preferred_element_type=F32)
     for j in range(6):
         cut = slice(j * 512, j * 512 + 512)
-        out[:, cut] = jnp.dot(mine[...], w_mine[:, cut], preferred_element_type=F32)
+        out[:, cut] = jnp.dot(mine, w_mine[:, cut], preferred_element_type=F32)
 
 
 def sum_kernel(part, peer, w_peer, *outs):
@@ -321,16 +326,16 @@
 
     high = lax.ppermute(z, ("y", "z"), [(0, LAST)])
 
-    mine, send = call(first_kernel, [half, half], [VM] * 8, BLOCK_SCRATCH, limit=16)(
+    send, qs = call(first_kernel, [half, shape((HL, 3, S, HD), BF)], [VM] * 8, BLOCK_SCRATCH, limit=16)(
         *zg, tab, wc, rows, w_qkv
     )
     w_fin_rows = w_fin.T
 
-    def gathered_drifts(mine, send, z, *extra):
+    def gathered_drifts(send, qs, z, *extra):
         peer = swap_cores(send)
         part, embed = call(
             own_kernel, [shape((S // 2, D), F32), shape((ROWS, D), F32)], [VM] * 5, limit=16
-        )(send, mine, w_out, z, w_in)
+        )(send, qs, w_out, z, w_in)
         parts = call(sum_kernel, [row] * NX, [VM] * 3, limit=16)(part, peer, w_peer)
         got = [parts[0]] + [to_right(parts[k], k) for k in (2, 1, 3)]
         outs, *extra = call(
@@ -341,15 +346,15 @@
         got = lax.all_to_all(outs, ("y", "z"), 0, 0, tiled=True)
         return got, *extra
 
-    (got,) = gathered_drifts(mine, send, z)
+    (got,) = gathered_drifts(send, qs, z)
     z, copies = call(
         state_kernel, [shape((16, 128), BF), shape((8, 16, 128), BF)], [VM] * 2
     )(z, got)
     zg = lax.all_to_all(copies, ("x", "c"), 0, 0, tiled=True)
-    mine, send = call(second_kernel, [half, half], [VM] * 5, BLOCK_SCRATCH, limit=16)(
+    send, qs = call(second_kernel, [half, shape((HL, 3, S, HD), BF)], [VM] * 5, BLOCK_SCRATCH, limit=16)(
         zg, tab, wc, rows, w_qkv
     )
-    got, target = gathered_drifts(mine, send, z, shape((8, 128), jnp.int32))
+    got, target = gathered_drifts(send, qs, z, shape((8, 128), jnp.int32))
     return call(final_kernel, shape((1, ROWS, C), F32), [VM] * 2)(target, got)
 
 

time: 93.4 us -> 93.6 us (level)
  transfers between devices with their start and end apart: 14 -> 14, of which waited for: 7 -> 7; matrix products, arithmetic and copies ran while one was open for 1% -> 1% of each run, Pallas kernels for 9% -> 10%
where the time goes in v11:
time: 93.6 us; the launch traced here: 93.1 us
  blocking collectives  43.9 us (47%)
  Pallas kernels  15.9 us (17%)
  waiting for transfers between devices  15.3 us (16%)
  starting transfers between devices  15 us (16%)
  between operations  2.12 us (2%)
    all_to_all x2, blocking collectives, gathered_drifts(): got = lax.all_to_all(outs, ('y', 'z'), 0, 0, tiled=True)  35.1 us
    ppermute x9, waiting for transfers between devices, to_right(): return lax.ppermute(x, 'x', [(i, (i + k) % NX) for i in range(NX)])  14.1 us
    ppermute x9, starting transfers between devices, to_right(): return lax.ppermute(x, 'x', [(i, (i + k) % NX) for i in range(NX)])  14 us
    all_to_all x1, blocking collectives, local(): zg = lax.all_to_all(copies, ('x', 'c'), 0, 0, tiled=True)  8.87 us
    pallas_call x1, Pallas kernels, local(): call(second_kernel, [half, shape((HL, 3, S, HD), BF)], [VM] * 5, BLOCK_SC...  3.68 us
    pallas_call x1, Pallas kernels, local(): call(first_kernel, [half, shape((HL, 3, S, HD), BF)], [VM] * 8, BLOCK_SCR...  3.67 us
    pallas_call x1, Pallas kernels, local(): call(prepare_kernel, [kept((4, 8, ROWS, HD), F32), kept((2 * C, D), BF),...  3.32 us
    pallas_call x2, Pallas kernels, gathered_drifts(): call(own_kernel, [shape((S // 2, D), F32), shape((ROWS, D), F32)], [VM] *...  1.92 us
  transfers between devices with their start and end apart: 14, of which 7 were waited for; matrix products, arithmetic and copies ran while one was open for 1% of the time, Pallas kernels for 10%

profile of v11, /device:TPU:32, one launch (start us, length us, event | category | flops | bytes accessed | tf_op | source)
XLA Modules:
  0.0 93.1 jit_solution(3901861167077716947)
XLA Ops:
  0.0 0.0 collective-permute-start.1
  0.0 0.7 bitcast_convert_fusion
  0.7 0.1 pad_maximum_fusion.z
  0.8 0.6 collective-permute-done.1.other
  1.4 0.1 shard_map.109.after.z0
  1.5 0.2 collective-permute-start.6
  1.6 2.8 %collective-permute-start.2 = (bf16[2,16,128]{2,1,0:T(8,128)(2,1)S(1)}, bf16[2,16,128]{2,1,0:T(8,128)(2,1)S(1)}, u32[]{:S(2)}, u32[]{:S(2)}) collective-permute-start(bf16[2,16,128]{2,1,0:T(8,128)(2,1)S(1)} %shard_map.109.after.z0), channel_id=1, source_target_pairs={{0,6},{2,0},{4,2},{6,4},{1,7},{3,1},{5,3},{7,5},{8,14},{10,8},{12,... | collective-permute-start | bytes 24584 | tf_op jit(solution)/shard_map/ppermute | solution.py:295
  4.4 0.8 collective-permute-start.3
  5.2 0.9 collective-permute-start.4
  6.7 3.3 %shard_map.110 = (f32[4,8,32,128]{3,2,1,0:T(8,128)S(1)}, bf16[128,3072]{1,0:T(8,128)(2,1)S(1)}, f32[8,3072]{1,0:T(8,128)S(1)}, bf16[64,3072]{1,0:T(8,128)(2,1)S(1)}, bf16[3072,1152]{1,0:T(8,128)(2,1)S(1)}) custom-call(s32[1]{0:T(128)S(6)} %copy.12.step, bf16[2,16,128]{2,1,0:T(8,128)(2,1)S(1)} %shard_map.109.after.z0, s32[2,256]{1,0:T(2,128)} %bitcast.10, ...), custom_call_target="tpu_custom_call" | custom-call | tf_op jit(solution)/shard_map/pallas_call | solution.py:311
  10.1 0.0 collective-permute-done.2.z1
  10.1 0.0 collective-permute-done.3.z2
  10.1 0.0 collective-permute-done.4.z3
  10.1 0.0 copy-start
  10.1 3.7 %shard_map.111 = (bf16[128,384]{1,0:T(8,128)(2,1)S(1)}, bf16[3,3,256,128]{3,2,1,0:T(8,128)(2,1)S(1)}) custom-call(bf16[2,16,128]{2,1,0:T(8,128)(2,1)S(1)} %shard_map.109.after.z0, bf16[2,16,128]{2,1,0:T(8,128)(2,1)S(1)} %collective-permute-done.2.z1, bf16[2,16,128]{2,1,0:T(8,128)(2,1)S(1)} %collective-permute-done.3.z2, ...), custom_call_target="tpu_custom_call" | custom-call | tf_op jit(solution)/shard_map/pallas_call | solution.py:329
  13.8 0.1 collective-permute-start.5
  13.9 0.0 copy-done
  13.9 1.0 %shard_map.112 = (f32[128,3072]{1,0:T(8,128)S(1)}, f32[32,3072]{1,0:T(8,128)S(1)}) custom-call(bf16[128,384]{1,0:T(8,128)(2,1)S(1)} %get-tuple-element.35.after, bf16[3,3,256,128]{3,2,1,0:T(8,128)(2,1)S(1)} %get-tuple-element.36.qs, bf16[384,3072]{1,0:T(8,128)(2,1)S(1)} %copy-done, bf16[16,128]{1,0:T(8,128)(2,1)S(1)} %pad_maximum_fusion.z, ...), custom_call_target="tpu_custom_call" | custom-call | tf_op jit(solution)/shard_map/pallas_call | solution.py:336
  14.9 0.0 copy-start.1
  14.9 0.0 copy-start.2
  14.9 0.3 collective-permute-done.5.peer
  15.2 0.0 collective-permute-done.6.w_peer
  15.2 0.6 shard_map.113
  15.8 1.9 %collective-permute-start.7 = (bf16[32,3072]{1,0:T(8,128)(2,1)S(1)}, bf16[32,3072]{1,0:T(8,128)(2,1)S(1)}, u32[]{:S(2)}, u32[]{:S(2)}) collective-permute-start(bf16[32,3072]{1,0:T(8,128)(2,1)S(1)} %get-tuple-element.42), channel_id=1, source_target_pairs={{0,4},{2,6},{4,0},{6,2},{1,5},{3,7},{5,1},{7,3},{8,12},{10,14},{12... | collective-permute-start | bytes 589832 | tf_op jit(solution)/shard_map/ppermute | solution.py:295
  17.7 1.3 %collective-permute-start.8 = (bf16[32,3072]{1,0:T(8,128)(2,1)S(1)}, bf16[32,3072]{1,0:T(8,128)(2,1)S(1)}, u32[]{:S(2)}, u32[]{:S(2)}) collective-permute-start(bf16[32,3072]{1,0:T(8,128)(2,1)S(1)} %get-tuple-element.43), channel_id=1, source_target_pairs={{0,2},{2,4},{4,6},{6,0},{1,3},{3,5},{5,7},{7,1},{8,10},{10,12},{12... | collective-permute-start | bytes 589832 | tf_op jit(solution)/shard_map/ppermute | solution.py:295
  19.1 1.9 %collective-permute-start.9 = (bf16[32,3072]{1,0:T(8,128)(2,1)S(1)}, bf16[32,3072]{1,0:T(8,128)(2,1)S(1)}, u32[]{:S(2)}, u32[]{:S(2)}) collective-permute-start(bf16[32,3072]{1,0:T(8,128)(2,1)S(1)} %get-tuple-element.44), channel_id=1, source_target_pairs={{0,6},{2,0},{4,2},{6,4},{1,7},{3,1},{5,3},{7,5},{8,14},{10,8},{12,... | collective-permute-start | bytes 589832 | tf_op jit(solution)/shard_map/ppermute | solution.py:295
  21.0 0.6 collective-permute-start
  22.9 0.0 collective-permute-done.high
  22.9 2.2 %collective-permute-done.7.p1 = bf16[32,3072]{1,0:T(8,128)(2,1)S(1)} collective-permute-done((bf16[32,3072]{1,0:T(8,128)(2,1)S(1)}, bf16[32,3072]{1,0:T(8,128)(2,1)S(1)}, u32[]{:S(2)}, u32[]{:S(2)}) %collective-permute-start.7) | collective-permute-done | bytes 196640 | tf_op jit(solution)/shard_map/ppermute | solution.py:295
  25.2 3.5 %collective-permute-done.8.p2 = bf16[32,3072]{1,0:T(8,128)(2,1)S(1)} collective-permute-done((bf16[32,3072]{1,0:T(8,128)(2,1)S(1)}, bf16[32,3072]{1,0:T(8,128)(2,1)S(1)}, u32[]{:S(2)}, u32[]{:S(2)}) %collective-permute-start.8) | collective-permute-done | bytes 196640 | tf_op jit(solution)/shard_map/ppermute | solution.py:295
  28.6 0.0 collective-permute-done.9.p3
  28.6 0.0 copy-done.1
  28.6 0.0 copy-done.2
  28.6 0.6 shard_map.114
  29.3 21.0 %all_to_all.15.got = bf16[32,16,128]{2,1,0:T(8,128)(2,1)S(1)} all-to-all(bf16[32,16,128]{2,1,0:T(8,128)(2,1)S(1)} %shard_map.114), channel_id=1, replica_groups=mesh['y'=4,'z'=8,'x'=4,'c'=2] {'y','z'}, dimensions={0} | all-to-all | bytes 262144 | tf_op jit(solution)/shard_map/all_to_all | solution.py:346
  50.4 8.9 %all_to_all.16.zg = bf16[8,16,128]{2,1,0:T(8,128)(2,1)S(1)} all-to-all(bf16[8,16,128]{2,1,0:T(8,128)(2,1)S(1)} %get-tuple-element.45), channel_id=1, replica_groups=mesh['y'=4,'z'=8,'x'=4,'c'=2] {'x','c'}, dimensions={0} | all-to-all | bytes 65536 | tf_op jit(solution)/shard_map/all_to_all | solution.py:353
  59.2 3.7 %shard_map.116 = (bf16[128,384]{1,0:T(8,128)(2,1)S(1)}, bf16[3,3,256,128]{3,2,1,0:T(8,128)(2,1)S(1)}) custom-call(bf16[8,16,128]{2,1,0:T(8,128)(2,1)S(1)} %all_to_all.16.zg, f32[4,8,32,128]{3,2,1,0:T(8,128)S(1)} %get-tuple-element.31.rest_0_, bf16[128,3072]{1,0:T(8,128)(2,1)S(1)} %get-tuple-element.32.rest_1_, f32[8,3072]{1,0:T(8,128)S(1)} %get-tuple-element.33.rest_2_.gate, ...), custom_call_target="tpu_custom_call" | custom-call | tf_op jit(solution)/shard_map/pallas_call | solution.py:354
  62.9 0.1 collective-permute-start.10
  63.0 1.0 %shard_map.117 = (f32[128,3072]{1,0:T(8,128)S(1)}, f32[32,3072]{1,0:T(8,128)S(1)}) custom-call(bf16[128,384]{1,0:T(8,128)(2,1)S(1)} %get-tuple-element.46.after, bf16[3,3,256,128]{3,2,1,0:T(8,128)(2,1)S(1)} %get-tuple-element.47.qs, bf16[384,3072]{1,0:T(8,128)(2,1)S(1)} %copy-done, bf16[16,128]{1,0:T(8,128)(2,1)S(1)} %get-tuple-element.48.z, ...), custom_call_target="tpu_custom_call" | custom-call | tf_op jit(solution)/shard_map/pallas_call | solution.py:336
  64.0 0.3 collective-permute-done.10.peer
  64.3 0.6 shard_map.118
  64.9 1.2 %collective-permute-start.11 = (bf16[32,3072]{1,0:T(8,128)(2,1)S(1)}, bf16[32,3072]{1,0:T(8,128)(2,1)S(1)}, u32[]{:S(2)}, u32[]{:S(2)}) collective-permute-start(bf16[32,3072]{1,0:T(8,128)(2,1)S(1)} %get-tuple-element.52), channel_id=1, source_target_pairs={{0,4},{2,6},{4,0},{6,2},{1,5},{3,7},{5,1},{7,3},{8,12},{10,14},{12... | collective-permute-start | bytes 589832 | tf_op jit(solution)/shard_map/ppermute | solution.py:295
  66.1 0.9 %collective-permute-start.12 = (bf16[32,3072]{1,0:T(8,128)(2,1)S(1)}, bf16[32,3072]{1,0:T(8,128)(2,1)S(1)}, u32[]{:S(2)}, u32[]{:S(2)}) collective-permute-start(bf16[32,3072]{1,0:T(8,128)(2,1)S(1)} %get-tuple-element.53), channel_id=1, source_target_pairs={{0,2},{2,4},{4,6},{6,0},{1,3},{3,5},{5,7},{7,1},{8,10},{10,12},{12... | collective-permute-start | bytes 589832 | tf_op jit(solution)/shard_map/ppermute | solution.py:295
  67.0 2.3 %collective-permute-start.13 = (bf16[32,3072]{1,0:T(8,128)(2,1)S(1)}, bf16[32,3072]{1,0:T(8,128)(2,1)S(1)}, u32[]{:S(2)}, u32[]{:S(2)}) collective-permute-start(bf16[32,3072]{1,0:T(8,128)(2,1)S(1)} %get-tuple-element.54), channel_id=1, source_target_pairs={{0,6},{2,0},{4,2},{6,4},{1,7},{3,1},{5,3},{7,5},{8,14},{10,8},{12,... | collective-permute-start | bytes 589832 | tf_op jit(solution)/shard_map/ppermute | solution.py:295
  69.3 5.0 %collective-permute-done.11.p1 = bf16[32,3072]{1,0:T(8,128)(2,1)S(1)} collective-permute-done((bf16[32,3072]{1,0:T(8,128)(2,1)S(1)}, bf16[32,3072]{1,0:T(8,128)(2,1)S(1)}, u32[]{:S(2)}, u32[]{:S(2)}) %collective-permute-start.11) | collective-permute-done | bytes 196640 | tf_op jit(solution)/shard_map/ppermute | solution.py:295
  74.3 3.4 %collective-permute-done.12.p2 = bf16[32,3072]{1,0:T(8,128)(2,1)S(1)} collective-permute-done((bf16[32,3072]{1,0:T(8,128)(2,1)S(1)}, bf16[32,3072]{1,0:T(8,128)(2,1)S(1)}, u32[]{:S(2)}, u32[]{:S(2)}) %collective-permute-start.12) | collective-permute-done | bytes 196640 | tf_op jit(solution)/shard_map/ppermute | solution.py:295
  77.7 0.0 collective-permute-done.13.p3
  77.7 0.6 shard_map.119
  78.4 14.0 %all_to_all.17.got = bf16[32,16,128]{2,1,0:T(8,128)(2,1)S(1)} all-to-all(bf16[32,16,128]{2,1,0:T(8,128)(2,1)S(1)} %get-tuple-element.56), channel_id=1, replica_groups=mesh['y'=4,'z'=8,'x'=4,'c'=2] {'y','z'}, dimensions={0} | all-to-all | bytes 262144 | tf_op jit(solution)/shard_map/all_to_all | solution.py:346
  92.4 0.7 shard_map.120
  (2 shorter events, 0.0 us)
Async XLA Ops:
  0.0 1.4 %collective-permute-start.1 = (f32[1,32,64]{2,1,0:T(8,128)}, f32[1,32,64]{2,1,0:T(8,128)S(1)}, u32[]{:S(2)}, u32[]{:S(2)}) collective-permute-start(f32[1,32,64]{2,1,0:T(8,128)} %param.11), channel_id=1, source_target_pairs={{0,1},{1,0},{2,3},{3,2},{4,5},{5,4},{6,7},{7,6},{8,9},{9,8},{10,11... | collective-permute-start | bytes 24584 | tf_op jit(solution)/shard_map/ppermute | solution.py:299
  1.5 13.7 %collective-permute-start.6 = (bf16[384,3072]{1,0:T(8,128)(2,1)}, bf16[384,3072]{1,0:T(8,128)(2,1)S(1)}, u32[]{:S(2)}, u32[]{:S(2)}) collective-permute-start(bf16[384,3072]{1,0:T(8,128)(2,1)} %w_mine.3), channel_id=1, source_target_pairs={{0,1},{1,0},{2,3},{3,2},{4,5},{5,4},{6,7},{7,6},{8,9},{9,8},{10,11... | collective-permute-start | bytes 7077896 | tf_op jit(solution)/shard_map/ppermute | solution.py:299
  1.6 8.4 %collective-permute-start.2 = (bf16[2,16,128]{2,1,0:T(8,128)(2,1)S(1)}, bf16[2,16,128]{2,1,0:T(8,128)(2,1)S(1)}, u32[]{:S(2)}, u32[]{:S(2)}) collective-permute-start(bf16[2,16,128]{2,1,0:T(8,128)(2,1)S(1)} %shard_map.109.after.z0), channel_id=1, source_target_pairs={{0,6},{2,0},{4,2},{6,4},{1,7},{3,1},{5,3},{7,5},{8,14},{10,8},{12,... | collective-permute-start | bytes 24584 | tf_op jit(solution)/shard_map/ppermute | solution.py:295
  4.4 5.7 %collective-permute-start.3 = (bf16[2,16,128]{2,1,0:T(8,128)(2,1)S(1)}, bf16[2,16,128]{2,1,0:T(8,128)(2,1)S(1)}, u32[]{:S(2)}, u32[]{:S(2)}) collective-permute-start(bf16[2,16,128]{2,1,0:T(8,128)(2,1)S(1)} %shard_map.109.after.z0), channel_id=1, source_target_pairs={{0,4},{2,6},{4,0},{6,2},{1,5},{3,7},{5,1},{7,3},{8,12},{10,14},{12... | collective-permute-start | bytes 24584 | tf_op jit(solution)/shard_map/ppermute | solution.py:295
  5.2 4.9 %collective-permute-start.4 = (bf16[2,16,128]{2,1,0:T(8,128)(2,1)S(1)}, bf16[2,16,128]{2,1,0:T(8,128)(2,1)S(1)}, u32[]{:S(2)}, u32[]{:S(2)}) collective-permute-start(bf16[2,16,128]{2,1,0:T(8,128)(2,1)S(1)} %shard_map.109.after.z0), channel_id=1, source_target_pairs={{0,2},{2,4},{4,6},{6,0},{1,3},{3,5},{5,7},{7,1},{8,10},{10,12},{12... | collective-permute-start | bytes 24584 | tf_op jit(solution)/shard_map/ppermute | solution.py:295
  10.1 3.8 %copy-start = (bf16[384,3072]{1,0:T(8,128)(2,1)S(1)}, bf16[384,3072]{1,0:T(8,128)(2,1)}, u32[]{:S(2)}) copy-start(bf16[384,3072]{1,0:T(8,128)(2,1)} %w_mine.3) | copy-start | bytes 7077892
  13.8 1.4 %collective-permute-start.5 = (bf16[128,384]{1,0:T(8,128)(2,1)S(1)}, bf16[128,384]{1,0:T(8,128)(2,1)S(1)}, u32[]{:S(2)}, u32[]{:S(2)}) collective-permute-start(bf16[128,384]{1,0:T(8,128)(2,1)S(1)} %get-tuple-element.35.after), channel_id=1, source_target_pairs={{0,1},{1,0},{2,3},{3,2},{4,5},{5,4},{6,7},{7,6},{8,9},{9,8},{10,11... | collective-permute-start | bytes 294920 | tf_op jit(solution)/shard_map/ppermute | solution.py:299
  14.9 13.8 %copy-start.1 = (bf16[3072,64]{0,1:T(8,128)(2,1)S(1)}, bf16[3072,64]{0,1:T(8,128)(2,1)}, u32[]{:S(2)}) copy-start(bf16[3072,64]{0,1:T(8,128)(2,1)} %param.21) | copy-start | bytes 1179652
  14.9 13.8 %copy-start.2 = (f32[1,32,64]{2,1,0:T(8,128)S(1)}, f32[1,32,64]{2,1,0:T(8,128)}, u32[]{:S(2)}) copy-start(f32[1,32,64]{2,1,0:T(8,128)} %param.11) | copy-start | bytes 24580
  15.8 9.4 %collective-permute-start.7 = (bf16[32,3072]{1,0:T(8,128)(2,1)S(1)}, bf16[32,3072]{1,0:T(8,128)(2,1)S(1)}, u32[]{:S(2)}, u32[]{:S(2)}) collective-permute-start(bf16[32,3072]{1,0:T(8,128)(2,1)S(1)} %get-tuple-element.42), channel_id=1, source_target_pairs={{0,4},{2,6},{4,0},{6,2},{1,5},{3,7},{5,1},{7,3},{8,12},{10,14},{12... | collective-permute-start | bytes 589832 | tf_op jit(solution)/shard_map/ppermute | solution.py:295
  17.7 10.9 %collective-permute-start.8 = (bf16[32,3072]{1,0:T(8,128)(2,1)S(1)}, bf16[32,3072]{1,0:T(8,128)(2,1)S(1)}, u32[]{:S(2)}, u32[]{:S(2)}) collective-permute-start(bf16[32,3072]{1,0:T(8,128)(2,1)S(1)} %get-tuple-element.43), channel_id=1, source_target_pairs={{0,2},{2,4},{4,6},{6,0},{1,3},{3,5},{5,7},{7,1},{8,10},{10,12},{12... | collective-permute-start | bytes 589832 | tf_op jit(solution)/shard_map/ppermute | solution.py:295
  19.1 9.5 %collective-permute-start.9 = (bf16[32,3072]{1,0:T(8,128)(2,1)S(1)}, bf16[32,3072]{1,0:T(8,128)(2,1)S(1)}, u32[]{:S(2)}, u32[]{:S(2)}) collective-permute-start(bf16[32,3072]{1,0:T(8,128)(2,1)S(1)} %get-tuple-element.44), channel_id=1, source_target_pairs={{0,6},{2,0},{4,2},{6,4},{1,7},{3,1},{5,3},{7,5},{8,14},{10,8},{12,... | collective-permute-start | bytes 589832 | tf_op jit(solution)/shard_map/ppermute | solution.py:295
  21.0 2.0 %collective-permute-start = (bf16[16,128]{1,0:T(8,128)(2,1)S(1)}, bf16[16,128]{1,0:T(8,128)(2,1)S(1)}, u32[]{:S(2)}, u32[]{:S(2)}) collective-permute-start(bf16[16,128]{1,0:T(8,128)(2,1)S(1)} %pad_maximum_fusion.z), channel_id=1, source_target_pairs={{0,248},{1,249},{2,250},{3,251},{4,252},{5,253},{6,254},{7,255}} | collective-permute-start | bytes 12296 | tf_op jit(solution)/shard_map/ppermute | solution.py:327
  62.9 1.4 %collective-permute-start.10 = (bf16[128,384]{1,0:T(8,128)(2,1)S(1)}, bf16[128,384]{1,0:T(8,128)(2,1)S(1)}, u32[]{:S(2)}, u32[]{:S(2)}) collective-permute-start(bf16[128,384]{1,0:T(8,128)(2,1)S(1)} %get-tuple-element.46.after), channel_id=1, source_target_pairs={{0,1},{1,0},{2,3},{3,2},{4,5},{5,4},{6,7},{7,6},{8,9},{9,8},{10,11... | collective-permute-start | bytes 294920 | tf_op jit(solution)/shard_map/ppermute | solution.py:299
  64.9 9.4 %collective-permute-start.11 = (bf16[32,3072]{1,0:T(8,128)(2,1)S(1)}, bf16[32,3072]{1,0:T(8,128)(2,1)S(1)}, u32[]{:S(2)}, u32[]{:S(2)}) collective-permute-start(bf16[32,3072]{1,0:T(8,128)(2,1)S(1)} %get-tuple-element.52), channel_id=1, source_target_pairs={{0,4},{2,6},{4,0},{6,2},{1,5},{3,7},{5,1},{7,3},{8,12},{10,14},{12... | collective-permute-start | bytes 589832 | tf_op jit(solution)/shard_map/ppermute | solution.py:295
  66.1 11.6 %collective-permute-start.12 = (bf16[32,3072]{1,0:T(8,128)(2,1)S(1)}, bf16[32,3072]{1,0:T(8,128)(2,1)S(1)}, u32[]{:S(2)}, u32[]{:S(2)}) collective-permute-start(bf16[32,3072]{1,0:T(8,128)(2,1)S(1)} %get-tuple-element.53), channel_id=1, source_target_pairs={{0,2},{2,4},{4,6},{6,0},{1,3},{3,5},{5,7},{7,1},{8,10},{10,12},{12... | collective-permute-start | bytes 589832 | tf_op jit(solution)/shard_map/ppermute | solution.py:295
  67.0 10.7 %collective-permute-start.13 = (bf16[32,3072]{1,0:T(8,128)(2,1)S(1)}, bf16[32,3072]{1,0:T(8,128)(2,1)S(1)}, u32[]{:S(2)}, u32[]{:S(2)}) collective-permute-start(bf16[32,3072]{1,0:T(8,128)(2,1)S(1)} %get-tuple-element.54), channel_id=1, source_target_pairs={{0,6},{2,0},{4,2},{6,4},{1,7},{3,1},{5,3},{7,5},{8,14},{10,8},{12,... | collective-permute-start | bytes 589832 | tf_op jit(solution)/shard_map/ppermute | solution.py:295

commit v12 on v10

--- a/solution.py
+++ b/solution.py
@@ -206,12 +206,16 @@
 
 
 def sum_kernel(part, peer, w_peer, *outs):
+    even = lax.axis_index("c") == 0
     for j in range(6):
         cut = slice(j * 512, j * 512 + 512)
         total = part[:, cut] + jnp.dot(peer[...], w_peer[:, cut], preferred_element_type=F32)
         total = total.astype(BF)
-        for k in range(NX):
+        for k in (0, 2):
             outs[k][:, cut] = total[ROWS * k : ROWS * (k + 1)]
+        right, left = total[ROWS : 2 * ROWS], total[3 * ROWS :]
+        outs[1][:, cut] = jnp.where(even, right, left)
+        outs[3][:, cut] = jnp.where(even, left, right)
 
 
 def position():
@@ -288,6 +292,11 @@
 
 def to_right(x, k):
     return lax.ppermute(x, "x", [(i, (i + k) % NX) for i in range(NX)])
+
+
+def apart(x, k):
+    pairs = [(i * NC + c, (i + (k if c == 0 else -k)) % NX * NC + c) for i in range(NX) for c in range(NC)]
+    return lax.ppermute(x, ("x", "c"), pairs)
 
 
 def swap_cores(x):
@@ -332,7 +341,7 @@
             own_kernel, [shape((S // 2, D), F32), shape((ROWS, D), F32)], [VM] * 5, limit=16
         )(send, mine, w_out, z, w_in)
         parts = call(sum_kernel, [row] * NX, [VM] * 3, limit=16)(part, peer, w_peer)
-        got = [parts[0]] + [to_right(parts[k], k) for k in (2, 1, 3)]
+        got = [parts[0], to_right(parts[2], 2), apart(parts[1], 1), apart(parts[3], -1)]
         outs, *extra = call(
             drift_kernel,
             [shape((NY * NZ, 16, 128), BF), *extra],

time: 93.4 us -> 93.5 us (level)
    ppermute x9 -> x5, waiting for transfers between devices: 14 us -> 7.19 us  [to_right(): return lax.ppermute(x, 'x', [(i, (i + k) % NX) for i in range(NX)])]
    ppermute x0 -> x4, waiting for transfers between devices: none -> 6.65 us  [apart(): return lax.ppermute(x, ('x', 'c'), pairs)]
    ppermute x9 -> x5, starting transfers between devices: 14 us -> 7.53 us  [to_right(): return lax.ppermute(x, 'x', [(i, (i + k) % NX) for i in range(NX)])]
    ppermute x0 -> x4, starting transfers between devices: none -> 6.47 us  [apart(): return lax.ppermute(x, ('x', 'c'), pairs)]
where the time goes in v12:
time: 93.5 us; the launch traced here: 93 us
  blocking collectives  44.1 us (47%)
  waiting for transfers between devices  15.5 us (17%)
  Pallas kernels  15.4 us (16%)
  starting transfers between devices  15 us (16%)
  between operations  2.12 us (2%)
    all_to_all x2, blocking collectives, gathered_drifts(): got = lax.all_to_all(outs, ('y', 'z'), 0, 0, tiled=True)  35.2 us
    all_to_all x1, blocking collectives, local(): zg = lax.all_to_all(copies, ('x', 'c'), 0, 0, tiled=True)  8.89 us
    ppermute x5, starting transfers between devices, to_right(): return lax.ppermute(x, 'x', [(i, (i + k) % NX) for i in range(NX)])  7.53 us
    ppermute x5, waiting for transfers between devices, to_right(): return lax.ppermute(x, 'x', [(i, (i + k) % NX) for i in range(NX)])  7.19 us
    ppermute x4, waiting for transfers between devices, apart(): return lax.ppermute(x, ('x', 'c'), pairs)  6.65 us
    ppermute x4, starting transfers between devices, apart(): return lax.ppermute(x, ('x', 'c'), pairs)  6.47 us
    pallas_call x1, Pallas kernels, local(): call(second_kernel, [half, half], [VM] * 5, BLOCK_SCRATCH, limit=16)  3.66 us
    pallas_call x1, Pallas kernels, local(): call(first_kernel, [half, half], [VM] * 8, BLOCK_SCRATCH, limit=16)  3.65 us
  transfers between devices with their start and end apart: 14, of which 7 were waited for; matrix products, arithmetic and copies ran while one was open for 1% of the time, Pallas kernels for 9%

profile of v12, /device:TPU:32, one launch (start us, length us, event | category | flops | bytes accessed | tf_op | source)
XLA Modules:
  0.0 93.0 jit_solution(6307378873998933902)
XLA Ops:
  0.0 0.0 collective-permute-start.1
  0.0 0.7 bitcast_convert_fusion
  0.7 0.1 pad_maximum_fusion.z
  0.8 0.6 collective-permute-done.1.other
  1.4 0.1 shard_map.109.after.z0
  1.5 0.2 collective-permute-start.6
  1.6 2.8 %collective-permute-start.2 = (bf16[2,16,128]{2,1,0:T(8,128)(2,1)S(1)}, bf16[2,16,128]{2,1,0:T(8,128)(2,1)S(1)}, u32[]{:S(2)}, u32[]{:S(2)}) collective-permute-start(bf16[2,16,128]{2,1,0:T(8,128)(2,1)S(1)} %shard_map.109.after.z0), channel_id=1, source_target_pairs={{0,6},{2,0},{4,2},{6,4},{1,7},{3,1},{5,3},{7,5},{8,14},{10,8},{12,... | collective-permute-start | bytes 24584 | tf_op jit(solution)/shard_map/ppermute | solution.py:294
  4.4 0.8 collective-permute-start.3
  5.2 0.9 collective-permute-start.4
  6.7 3.3 %shard_map.110 = (f32[4,8,32,128]{3,2,1,0:T(8,128)S(1)}, bf16[128,3072]{1,0:T(8,128)(2,1)S(1)}, f32[8,3072]{1,0:T(8,128)S(1)}, bf16[64,3072]{1,0:T(8,128)(2,1)S(1)}, bf16[3072,1152]{1,0:T(8,128)(2,1)S(1)}) custom-call(s32[1]{0:T(128)S(6)} %copy.12.step, bf16[2,16,128]{2,1,0:T(8,128)(2,1)S(1)} %shard_map.109.after.z0, s32[2,256]{1,0:T(2,128)} %bitcast.10, ...), custom_call_target="tpu_custom_call" | custom-call | tf_op jit(solution)/shard_map/pallas_call | solution.py:315
  10.1 0.0 collective-permute-done.2.z1
  10.1 0.0 collective-permute-done.3.z2
  10.1 0.0 collective-permute-done.4.z3
  10.1 0.0 copy-start
  10.1 3.6 %shard_map.111 = (bf16[128,384]{1,0:T(8,128)(2,1)S(1)}, bf16[128,384]{1,0:T(8,128)(2,1)S(1)}) custom-call(bf16[2,16,128]{2,1,0:T(8,128)(2,1)S(1)} %shard_map.109.after.z0, bf16[2,16,128]{2,1,0:T(8,128)(2,1)S(1)} %collective-permute-done.2.z1, bf16[2,16,128]{2,1,0:T(8,128)(2,1)S(1)} %collective-permute-done.3.z2, ...), custom_call_target="tpu_custom_call" | custom-call | tf_op jit(solution)/shard_map/pallas_call | solution.py:333
  13.8 0.1 collective-permute-start.5
  13.9 0.0 copy-done
  13.9 0.7 shard_map.112
  14.6 0.0 copy-start.1
  14.6 0.0 copy-start.2
  14.6 0.5 collective-permute-done.5.peer
  15.1 0.0 collective-permute-done.6.w_peer
  15.1 0.6 shard_map.113
  15.7 1.9 %collective-permute-start.7 = (bf16[32,3072]{1,0:T(8,128)(2,1)S(1)}, bf16[32,3072]{1,0:T(8,128)(2,1)S(1)}, u32[]{:S(2)}, u32[]{:S(2)}) collective-permute-start(bf16[32,3072]{1,0:T(8,128)(2,1)S(1)} %get-tuple-element.42), channel_id=1, source_target_pairs={{0,4},{2,6},{4,0},{6,2},{1,5},{3,7},{5,1},{7,3},{8,12},{10,14},{12... | collective-permute-start | bytes 589832 | tf_op jit(solution)/shard_map/ppermute | solution.py:294
  17.7 1.4 %collective-permute-start.8 = (bf16[32,3072]{1,0:T(8,128)(2,1)S(1)}, bf16[32,3072]{1,0:T(8,128)(2,1)S(1)}, u32[]{:S(2)}, u32[]{:S(2)}) collective-permute-start(bf16[32,3072]{1,0:T(8,128)(2,1)S(1)} %get-tuple-element.43), channel_id=1, source_target_pairs={{0,2},{1,7},{2,4},{3,1},{4,6},{5,3},{6,0},{7,5},{8,10},{9,15},{10,... | collective-permute-start | bytes 589832 | tf_op jit(solution)/shard_map/ppermute | solution.py:299
  19.0 1.9 %collective-permute-start.9 = (bf16[32,3072]{1,0:T(8,128)(2,1)S(1)}, bf16[32,3072]{1,0:T(8,128)(2,1)S(1)}, u32[]{:S(2)}, u32[]{:S(2)}) collective-permute-start(bf16[32,3072]{1,0:T(8,128)(2,1)S(1)} %get-tuple-element.44), channel_id=1, source_target_pairs={{0,6},{1,3},{2,0},{3,5},{4,2},{5,7},{6,4},{7,1},{8,14},{9,11},{10,... | collective-permute-start | bytes 589832 | tf_op jit(solution)/shard_map/ppermute | solution.py:299
  20.9 0.6 collective-permute-start
  22.9 0.0 collective-permute-done.high
  22.9 2.2 %collective-permute-done.7.p1 = bf16[32,3072]{1,0:T(8,128)(2,1)S(1)} collective-permute-done((bf16[32,3072]{1,0:T(8,128)(2,1)S(1)}, bf16[32,3072]{1,0:T(8,128)(2,1)S(1)}, u32[]{:S(2)}, u32[]{:S(2)}) %collective-permute-start.7) | collective-permute-done | bytes 196640 | tf_op jit(solution)/shard_map/ppermute | solution.py:294
  25.1 3.4 %collective-permute-done.8.p2 = bf16[32,3072]{1,0:T(8,128)(2,1)S(1)} collective-permute-done((bf16[32,3072]{1,0:T(8,128)(2,1)S(1)}, bf16[32,3072]{1,0:T(8,128)(2,1)S(1)}, u32[]{:S(2)}, u32[]{:S(2)}) %collective-permute-start.8) | collective-permute-done | bytes 196640 | tf_op jit(solution)/shard_map/ppermute | solution.py:299
  28.4 0.0 collective-permute-done.9.p3
  28.4 0.0 copy-done.1
  28.4 0.0 copy-done.2
  28.4 0.7 shard_map.114
  29.1 21.1 %all_to_all.15.got = bf16[32,16,128]{2,1,0:T(8,128)(2,1)S(1)} all-to-all(bf16[32,16,128]{2,1,0:T(8,128)(2,1)S(1)} %shard_map.114), channel_id=1, replica_groups=mesh['y'=4,'z'=8,'x'=4,'c'=2] {'y','z'}, dimensions={0} | all-to-all | bytes 262144 | tf_op jit(solution)/shard_map/all_to_all | solution.py:350
  50.2 8.9 %all_to_all.16.zg = bf16[8,16,128]{2,1,0:T(8,128)(2,1)S(1)} all-to-all(bf16[8,16,128]{2,1,0:T(8,128)(2,1)S(1)} %get-tuple-element.45), channel_id=1, replica_groups=mesh['y'=4,'z'=8,'x'=4,'c'=2] {'x','c'}, dimensions={0} | all-to-all | bytes 65536 | tf_op jit(solution)/shard_map/all_to_all | solution.py:357
  59.1 3.7 %shard_map.116 = (bf16[128,384]{1,0:T(8,128)(2,1)S(1)}, bf16[128,384]{1,0:T(8,128)(2,1)S(1)}) custom-call(bf16[8,16,128]{2,1,0:T(8,128)(2,1)S(1)} %all_to_all.16.zg, f32[4,8,32,128]{3,2,1,0:T(8,128)S(1)} %get-tuple-element.31.rest_0_, bf16[128,3072]{1,0:T(8,128)(2,1)S(1)} %get-tuple-element.32.rest_1_, f32[8,3072]{1,0:T(8,128)S(1)} %get-tuple-element.33.rest_2_.gate, ...), custom_call_target="tpu_custom_call" | custom-call | tf_op jit(solution)/shard_map/pallas_call | solution.py:358
  62.8 0.1 collective-permute-start.10
  62.9 0.7 shard_map.117
  63.6 0.6 collective-permute-done.10.peer
  64.2 0.6 shard_map.118
  64.8 1.1 %collective-permute-start.11 = (bf16[32,3072]{1,0:T(8,128)(2,1)S(1)}, bf16[32,3072]{1,0:T(8,128)(2,1)S(1)}, u32[]{:S(2)}, u32[]{:S(2)}) collective-permute-start(bf16[32,3072]{1,0:T(8,128)(2,1)S(1)} %get-tuple-element.52), channel_id=1, source_target_pairs={{0,4},{2,6},{4,0},{6,2},{1,5},{3,7},{5,1},{7,3},{8,12},{10,14},{12... | collective-permute-start | bytes 589832 | tf_op jit(solution)/shard_map/ppermute | solution.py:294
  65.9 0.9 %collective-permute-start.12 = (bf16[32,3072]{1,0:T(8,128)(2,1)S(1)}, bf16[32,3072]{1,0:T(8,128)(2,1)S(1)}, u32[]{:S(2)}, u32[]{:S(2)}) collective-permute-start(bf16[32,3072]{1,0:T(8,128)(2,1)S(1)} %get-tuple-element.53), channel_id=1, source_target_pairs={{0,2},{1,7},{2,4},{3,1},{4,6},{5,3},{6,0},{7,5},{8,10},{9,15},{10,... | collective-permute-start | bytes 589832 | tf_op jit(solution)/shard_map/ppermute | solution.py:299
  66.9 2.3 %collective-permute-start.13 = (bf16[32,3072]{1,0:T(8,128)(2,1)S(1)}, bf16[32,3072]{1,0:T(8,128)(2,1)S(1)}, u32[]{:S(2)}, u32[]{:S(2)}) collective-permute-start(bf16[32,3072]{1,0:T(8,128)(2,1)S(1)} %get-tuple-element.54), channel_id=1, source_target_pairs={{0,6},{1,3},{2,0},{3,5},{4,2},{5,7},{6,4},{7,1},{8,14},{9,11},{10,... | collective-permute-start | bytes 589832 | tf_op jit(solution)/shard_map/ppermute | solution.py:299
  69.2 5.0 %collective-permute-done.11.p1 = bf16[32,3072]{1,0:T(8,128)(2,1)S(1)} collective-permute-done((bf16[32,3072]{1,0:T(8,128)(2,1)S(1)}, bf16[32,3072]{1,0:T(8,128)(2,1)S(1)}, u32[]{:S(2)}, u32[]{:S(2)}) %collective-permute-start.11) | collective-permute-done | bytes 196640 | tf_op jit(solution)/shard_map/ppermute | solution.py:294
  74.2 3.3 %collective-permute-done.12.p2 = bf16[32,3072]{1,0:T(8,128)(2,1)S(1)} collective-permute-done((bf16[32,3072]{1,0:T(8,128)(2,1)S(1)}, bf16[32,3072]{1,0:T(8,128)(2,1)S(1)}, u32[]{:S(2)}, u32[]{:S(2)}) %collective-permute-start.12) | collective-permute-done | bytes 196640 | tf_op jit(solution)/shard_map/ppermute | solution.py:299
  77.5 0.0 collective-permute-done.13.p3
  77.5 0.6 shard_map.119
  78.1 14.1 %all_to_all.17.got = bf16[32,16,128]{2,1,0:T(8,128)(2,1)S(1)} all-to-all(bf16[32,16,128]{2,1,0:T(8,128)(2,1)S(1)} %get-tuple-element.56), channel_id=1, replica_groups=mesh['y'=4,'z'=8,'x'=4,'c'=2] {'y','z'}, dimensions={0} | all-to-all | bytes 262144 | tf_op jit(solution)/shard_map/all_to_all | solution.py:350
  92.3 0.7 shard_map.120
  (2 shorter events, 0.0 us)
Async XLA Ops:
  0.0 1.4 %collective-permute-start.1 = (f32[1,32,64]{2,1,0:T(8,128)}, f32[1,32,64]{2,1,0:T(8,128)S(1)}, u32[]{:S(2)}, u32[]{:S(2)}) collective-permute-start(f32[1,32,64]{2,1,0:T(8,128)} %param.11), channel_id=1, source_target_pairs={{0,1},{1,0},{2,3},{3,2},{4,5},{5,4},{6,7},{7,6},{8,9},{9,8},{10,11... | collective-permute-start | bytes 24584 | tf_op jit(solution)/shard_map/ppermute | solution.py:303
  1.5 13.7 %collective-permute-start.6 = (bf16[384,3072]{1,0:T(8,128)(2,1)}, bf16[384,3072]{1,0:T(8,128)(2,1)S(1)}, u32[]{:S(2)}, u32[]{:S(2)}) collective-permute-start(bf16[384,3072]{1,0:T(8,128)(2,1)} %w_mine.3), channel_id=1, source_target_pairs={{0,1},{1,0},{2,3},{3,2},{4,5},{5,4},{6,7},{7,6},{8,9},{9,8},{10,11... | collective-permute-start | bytes 7077896 | tf_op jit(solution)/shard_map/ppermute | solution.py:303
  1.6 8.4 %collective-permute-start.2 = (bf16[2,16,128]{2,1,0:T(8,128)(2,1)S(1)}, bf16[2,16,128]{2,1,0:T(8,128)(2,1)S(1)}, u32[]{:S(2)}, u32[]{:S(2)}) collective-permute-start(bf16[2,16,128]{2,1,0:T(8,128)(2,1)S(1)} %shard_map.109.after.z0), channel_id=1, source_target_pairs={{0,6},{2,0},{4,2},{6,4},{1,7},{3,1},{5,3},{7,5},{8,14},{10,8},{12,... | collective-permute-start | bytes 24584 | tf_op jit(solution)/shard_map/ppermute | solution.py:294
  4.4 5.7 %collective-permute-start.3 = (bf16[2,16,128]{2,1,0:T(8,128)(2,1)S(1)}, bf16[2,16,128]{2,1,0:T(8,128)(2,1)S(1)}, u32[]{:S(2)}, u32[]{:S(2)}) collective-permute-start(bf16[2,16,128]{2,1,0:T(8,128)(2,1)S(1)} %shard_map.109.after.z0), channel_id=1, source_target_pairs={{0,4},{2,6},{4,0},{6,2},{1,5},{3,7},{5,1},{7,3},{8,12},{10,14},{12... | collective-permute-start | bytes 24584 | tf_op jit(solution)/shard_map/ppermute | solution.py:294
  5.2 4.9 %collective-permute-start.4 = (bf16[2,16,128]{2,1,0:T(8,128)(2,1)S(1)}, bf16[2,16,128]{2,1,0:T(8,128)(2,1)S(1)}, u32[]{:S(2)}, u32[]{:S(2)}) collective-permute-start(bf16[2,16,128]{2,1,0:T(8,128)(2,1)S(1)} %shard_map.109.after.z0), channel_id=1, source_target_pairs={{0,2},{2,4},{4,6},{6,0},{1,3},{3,5},{5,7},{7,1},{8,10},{10,12},{12... | collective-permute-start | bytes 24584 | tf_op jit(solution)/shard_map/ppermute | solution.py:294
  10.1 3.8 %copy-start = (bf16[384,3072]{1,0:T(8,128)(2,1)S(1)}, bf16[384,3072]{1,0:T(8,128)(2,1)}, u32[]{:S(2)}) copy-start(bf16[384,3072]{1,0:T(8,128)(2,1)} %w_mine.3) | copy-start | bytes 7077892
  13.8 1.4 %collective-permute-start.5 = (bf16[128,384]{1,0:T(8,128)(2,1)S(1)}, bf16[128,384]{1,0:T(8,128)(2,1)S(1)}, u32[]{:S(2)}, u32[]{:S(2)}) collective-permute-start(bf16[128,384]{1,0:T(8,128)(2,1)S(1)} %get-tuple-element.35.after), channel_id=1, source_target_pairs={{0,1},{1,0},{2,3},{3,2},{4,5},{5,4},{6,7},{7,6},{8,9},{9,8},{10,11... | collective-permute-start | bytes 294920 | tf_op jit(solution)/shard_map/ppermute | solution.py:303
  14.6 13.8 %copy-start.1 = (bf16[3072,64]{0,1:T(8,128)(2,1)S(1)}, bf16[3072,64]{0,1:T(8,128)(2,1)}, u32[]{:S(2)}) copy-start(bf16[3072,64]{0,1:T(8,128)(2,1)} %param.21) | copy-start | bytes 1179652
  14.6 13.8 %copy-start.2 = (f32[1,32,64]{2,1,0:T(8,128)S(1)}, f32[1,32,64]{2,1,0:T(8,128)}, u32[]{:S(2)}) copy-start(f32[1,32,64]{2,1,0:T(8,128)} %param.11) | copy-start | bytes 24580
  15.7 9.3 %collective-permute-start.7 = (bf16[32,3072]{1,0:T(8,128)(2,1)S(1)}, bf16[32,3072]{1,0:T(8,128)(2,1)S(1)}, u32[]{:S(2)}, u32[]{:S(2)}) collective-permute-start(bf16[32,3072]{1,0:T(8,128)(2,1)S(1)} %get-tuple-element.42), channel_id=1, source_target_pairs={{0,4},{2,6},{4,0},{6,2},{1,5},{3,7},{5,1},{7,3},{8,12},{10,14},{12... | collective-permute-start | bytes 589832 | tf_op jit(solution)/shard_map/ppermute | solution.py:294
  17.7 10.8 %collective-permute-start.8 = (bf16[32,3072]{1,0:T(8,128)(2,1)S(1)}, bf16[32,3072]{1,0:T(8,128)(2,1)S(1)}, u32[]{:S(2)}, u32[]{:S(2)}) collective-permute-start(bf16[32,3072]{1,0:T(8,128)(2,1)S(1)} %get-tuple-element.43), channel_id=1, source_target_pairs={{0,2},{1,7},{2,4},{3,1},{4,6},{5,3},{6,0},{7,5},{8,10},{9,15},{10,... | collective-permute-start | bytes 589832 | tf_op jit(solution)/shard_map/ppermute | solution.py:299
  19.0 9.4 %collective-permute-start.9 = (bf16[32,3072]{1,0:T(8,128)(2,1)S(1)}, bf16[32,3072]{1,0:T(8,128)(2,1)S(1)}, u32[]{:S(2)}, u32[]{:S(2)}) collective-permute-start(bf16[32,3072]{1,0:T(8,128)(2,1)S(1)} %get-tuple-element.44), channel_id=1, source_target_pairs={{0,6},{1,3},{2,0},{3,5},{4,2},{5,7},{6,4},{7,1},{8,14},{9,11},{10,... | collective-permute-start | bytes 589832 | tf_op jit(solution)/shard_map/ppermute | solution.py:299
  20.9 2.0 %collective-permute-start = (bf16[16,128]{1,0:T(8,128)(2,1)S(1)}, bf16[16,128]{1,0:T(8,128)(2,1)S(1)}, u32[]{:S(2)}, u32[]{:S(2)}) collective-permute-start(bf16[16,128]{1,0:T(8,128)(2,1)S(1)} %pad_maximum_fusion.z), channel_id=1, source_target_pairs={{0,248},{1,249},{2,250},{3,251},{4,252},{5,253},{6,254},{7,255}} | collective-permute-start | bytes 12296 | tf_op jit(solution)/shard_map/ppermute | solution.py:331
  62.8 1.4 %collective-permute-start.10 = (bf16[128,384]{1,0:T(8,128)(2,1)S(1)}, bf16[128,384]{1,0:T(8,128)(2,1)S(1)}, u32[]{:S(2)}, u32[]{:S(2)}) collective-permute-start(bf16[128,384]{1,0:T(8,128)(2,1)S(1)} %get-tuple-element.46.after), channel_id=1, source_target_pairs={{0,1},{1,0},{2,3},{3,2},{4,5},{5,4},{6,7},{7,6},{8,9},{9,8},{10,11... | collective-permute-start | bytes 294920 | tf_op jit(solution)/shard_map/ppermute | solution.py:303
  64.8 9.4 %collective-permute-start.11 = (bf16[32,3072]{1,0:T(8,128)(2,1)S(1)}, bf16[32,3072]{1,0:T(8,128)(2,1)S(1)}, u32[]{:S(2)}, u32[]{:S(2)}) collective-permute-start(bf16[32,3072]{1,0:T(8,128)(2,1)S(1)} %get-tuple-element.52), channel_id=1, source_target_pairs={{0,4},{2,6},{4,0},{6,2},{1,5},{3,7},{5,1},{7,3},{8,12},{10,14},{12... | collective-permute-start | bytes 589832 | tf_op jit(solution)/shard_map/ppermute | solution.py:294
  65.9 11.5 %collective-permute-start.12 = (bf16[32,3072]{1,0:T(8,128)(2,1)S(1)}, bf16[32,3072]{1,0:T(8,128)(2,1)S(1)}, u32[]{:S(2)}, u32[]{:S(2)}) collective-permute-start(bf16[32,3072]{1,0:T(8,128)(2,1)S(1)} %get-tuple-element.53), channel_id=1, source_target_pairs={{0,2},{1,7},{2,4},{3,1},{4,6},{5,3},{6,0},{7,5},{8,10},{9,15},{10,... | collective-permute-start | bytes 589832 | tf_op jit(solution)/shard_map/ppermute | solution.py:299
  66.9 10.6 %collective-permute-start.13 = (bf16[32,3072]{1,0:T(8,128)(2,1)S(1)}, bf16[32,3072]{1,0:T(8,128)(2,1)S(1)}, u32[]{:S(2)}, u32[]{:S(2)}) collective-permute-start(bf16[32,3072]{1,0:T(8,128)(2,1)S(1)} %get-tuple-element.54), channel_id=1, source_target_pairs={{0,6},{1,3},{2,0},{3,5},{4,2},{5,7},{6,4},{7,1},{8,14},{9,11},{10,... | collective-permute-start | bytes 589832 | tf_op jit(solution)/shard_map/ppermute | solution.py:299
